TPU v7x, 32 devices: a whole 2x2x4 slice. The times are simulated.
32 devices in a mesh: groups: 2 (over x), loop: 16 (over z, y, core).
Axes of the slice: x: 2, y: 2, z: 4, core: 2. Of those that a mesh axis runs over, the one named last changes fastest.
Arguments:
- hidden: bfloat16 [512, 5376], P(('groups', 'loop')), parts along dimension 0, may hold values from -6 to 6
- exit_depth: int32 [512], P(('groups', 'loop')), parts along dimension 0, may hold values from 0 to 3
- teacher: int32 [512], P(('groups', 'loop')), parts along dimension 0, may hold values from 0 to 16383
- normalizer: float32 [512], P(('groups', 'loop')), parts along dimension 0, as said below
- tied_head: bfloat16 [16384, 5376], P('loop'), may hold values from -0.25 to 0.25
- depth_gain: float32 [4, 5376], replicated, may hold values from 0.5 to 1.5
- depth_bias: float32 [4, 5376], replicated, may hold values from -1.75 to 1.75
Outputs:
- row_mass: float32 [512], P(('groups', 'loop')), parts along dimension 0
- grad_gain: float32 [8, 5376], P('groups'), parts along dimension 0
- grad_bias: float32 [8, 5376], P('groups'), parts along dimension 0
There are 2 independent parts, one for each index of `groups`. A program takes and returns all parts, laid end to end along the dimension named above; an argument that names none is the same for every part. Nothing has to cross between parts.
Inputs may be any that keep to these rules, and one draw needn't show every extreme that they name: A log-normalizer near that of the row's logits.
All inputs are finite; a program needn't handle non-finite values.
Results may differ from a plain program's by a relative error of at most 0.012.
The roundings to bfloat16 on the way count: a program that leaves them out, or rounds other values in their place, can miss the bound.
Values may be sent and summed in bfloat16 or wider, within the bound.
No kernel may reach another device: no remote copies, remote signals or barrier semaphores. Data moves between devices by JAX's collectives and lax.ppermute only.
A program may use at most 128 MiB of HBM per device.

v0:
```python
import jax
import jax.numpy as jnp
from jax import lax
from jax.sharding import PartitionSpec as P


def shards(hidden, exit_depth, teacher, normalizer, tied_head, depth_gain, depth_bias):
    rows_dev = hidden.shape[0]
    levels = depth_gain.shape[0]
    voc_local = tied_head.shape[0]
    own_pick = (exit_depth[:, None] == jnp.arange(levels, dtype=jnp.int32)[None, :]).astype(
        jnp.float32
    )
    all_hidden = lax.all_gather(hidden, "loop", axis=0, tiled=True)
    all_norm, all_teacher, all_pick = (
        lax.all_gather(normalizer, "loop", axis=0, tiled=True),
        lax.all_gather(teacher.astype(jnp.float32), "loop", axis=0, tiled=True),
        lax.all_gather(own_pick, "loop", axis=0, tiled=True),
    )
    widened = all_hidden.astype(jnp.float32)
    normed = widened * lax.rsqrt(jnp.mean(widened * widened, axis=-1, keepdims=True) + 1e-06)
    row_gain = jnp.dot(
        all_pick, depth_gain, precision=lax.Precision.HIGHEST, preferred_element_type=jnp.float32
    )
    row_bias = jnp.dot(
        all_pick, depth_bias, precision=lax.Precision.HIGHEST, preferred_element_type=jnp.float32
    )
    mapped = (normed * row_gain + row_bias).astype(jnp.bfloat16)
    logits = jnp.einsum("rd,vd->rv", mapped, tied_head, preferred_element_type=jnp.float32)
    prob_rows = jnp.exp(logits - all_norm[:, None])
    first_col = lax.axis_index("loop") * voc_local
    columns = first_col + jnp.arange(voc_local, dtype=jnp.int32)
    onehot = (all_teacher.astype(jnp.int32)[:, None] == columns[None, :]).astype(jnp.float32)
    slopes = (prob_rows - onehot).astype(jnp.bfloat16)
    row_mass = lax.psum_scatter(jnp.sum(prob_rows, axis=1), "loop", scatter_dimension=0, tiled=True)
    back_grad = lax.psum_scatter(
        jnp.dot(slopes, tied_head, preferred_element_type=jnp.float32),
        "loop",
        scatter_dimension=0,
        tiled=True,
    )
    own_normed = lax.dynamic_slice_in_dim(normed, lax.axis_index("loop") * rows_dev, rows_dev, 0)
    gain_total = jnp.dot(
        own_pick.T,
        back_grad * own_normed,
        precision=lax.Precision.HIGHEST,
        preferred_element_type=jnp.float32,
    )
    bias_total = jnp.dot(
        own_pick.T, back_grad, precision=lax.Precision.HIGHEST, preferred_element_type=jnp.float32
    )
    gain_total, bias_total = lax.psum((gain_total, bias_total), "loop")
    return (row_mass, gain_total, bias_total)


def solution(mesh):
    return jax.shard_map(
        shards,
        mesh=mesh,
        in_specs=(
            P(("groups", "loop"), None),
            P(("groups", "loop")),
            P(("groups", "loop")),
            P(("groups", "loop")),
            P("loop", None),
            P(),
            P(),
        ),
        out_specs=(P(("groups", "loop")), P("groups", None), P("groups", None)),
        check_vma=False,
    )
```

profile of v0, /device:TPU:0, one launch (start us, length us, event | category | flops | bytes accessed | tf_op | source)
XLA Modules:
  0.0 301.4 jit_solution(2330932905973686810)
XLA Ops:
  7.2 0.0 copy-start
  7.2 0.0 all-gather.3.cloned.1.call-start
  7.2 0.7 all-gather.3.cloned.1.call-update
  7.9 0.0 reduce-scatter.2.cloned.1.call-start
  8.0 0.7 convert_bitcast_fusion
  8.6 23.2 %all-gather = f32[16,16,4]{1,2,0:T(4,128)S(1)} all-gather(f32[1,16,4]{1,2,0:T(4,128)S(1)} %convert_bitcast_fusion), channel_id=1, replica_groups=mesh['groups'=2,'loop'=16] {'loop'}, dimensions={0}, use_global_device_ids=true | all-gather | bytes 4352 | tf_op jit(solution)/shard_map/all_gather | solution.py:18
  31.8 0.1 reshape.28
  31.9 1.3 fusion.13
  33.9 0.9 dynamic-update-slice
  34.7 30.2 %all-reduce = f32[256]{0:T(256)S(1)} all-reduce(f32[256]{0:T(256)S(1)} %dynamic-update-slice), channel_id=1, replica_groups=mesh['groups'=2,'loop'=16] {'loop'}, use_global_device_ids=true, to_apply=%add | all-reduce | flops 256 | bytes 2048
  64.9 0.7 convert_dynamic-update-slice_fusion
  65.7 0.0 copy-start.3
  65.7 0.0 all-gather.3.cloned.1.call-done
  65.7 2.4 fusion.1
  68.1 0.0 copy-done
  68.1 0.0 copy-start.2
  68.1 7.3 %convolution_multiply_fusion = f32[256,5376]{1,0:T(8,128)S(1)} fusion(f32[256,4]{0,1:T(4,128)S(1)} %reshape.28, f32[4,5376]{1,0:T(4,128)S(1)} %copy-done, f32[256]{0:T(256)S(1)} %add_rsqrt_fusion, bf16[256,5376]{1,0:T(8,128)(2,1)} %all-gather.3.cloned.1.call-done), kind=kOutput, calls=%fused_computation.1 | convolution fusion | flops 70189056 | bytes 8348672 | tf_op jit(solution)/shard_map/dot_general | solution.py:22
  75.5 0.0 copy-done.3
  75.5 5.0 %fusion = bf16[256,5376]{1,0:T(8,128)(2,1)S(1)} fusion(f32[256,5376]{1,0:T(8,128)S(1)} %convolution_multiply_fusion, f32[256,4]{0,1:T(4,128)S(1)} %reshape.28, f32[4,5376]{1,0:T(4,128)S(1)} %copy-done.3), kind=kOutput, calls=%fused_computation.2 | convolution fusion | flops 68812800 | bytes 8347648 | tf_op jit(solution)/shard_map/dot_general | solution.py:25
  80.5 0.0 copy-done.2
  80.5 3.1 %fusion.14 = (f32[256]{0:T(256)S(1)}, f32[256,1024]{1,0:T(8,128)S(1)}) fusion(f32[256]{0:T(256)S(1)} %all-reduce, bf16[256,5376]{1,0:T(8,128)(2,1)S(1)} %fusion, bf16[1024,5376]{1,0:T(8,128)(2,1)S(1)} %copy-done.2), kind=kOutput, calls=%fused_computation.25 | convolution fusion | flops 2819096320 | bytes 14813184 | tf_op jit(solution)/shard_map/rd,vd->rv/dot_general | solution.py:29
  83.6 29.7 %all-reduce.3 = (f32[256]{0:T(256)S(1)}, f32[256]{0:T(256)S(1)}) all-reduce(f32[256]{0:T(256)S(1)} %get-tuple-element.9, f32[256]{0:T(256)S(1)} %convert_dynamic-update-slice_fusion), channel_id=2, replica_groups=mesh['groups'=2,'loop'=16] {'loop'}, use_global_device_ids=true, to_apply=%region_2.0.clone | all-reduce | flops 512 | bytes 4096
  113.3 9.0 %fusion.3 = f32[256,5376]{1,0:T(8,128)} fusion(bf16[1024,5376]{1,0:T(8,128)(2,1)} %param.11, f32[256,1024]{1,0:T(8,128)S(1)} %get-tuple-element.10, s32[1024]{0:T(1024)S(1)} %iota_add_fusion, s32[256]{0:T(256)S(1)} %convert_element_type.25), kind=kOutput, calls=%fused_computation.9 | convolution fusion | flops 2819620864 | bytes 17568768 | tf_op jit(solution)/shard_map/dot_general | solution.py:37
  122.4 0.0 copy-start.1
  122.4 0.0 reduce-scatter.2.cloned.1.call-update
  122.4 0.0 copy-start.4
  122.4 0.0 all-reduce.7.cloned.1.call-start
  122.5 1.7 copy-done.1
  124.2 2.9 convert_multiply_fusion
  127.1 72.8 %reduce-scatter.2.cloned.1.call-done = f32[16,5376]{1,0:T(8,128)} async-done(((f32[256,5376]{1,0:T(8,128)}), f32[16,5376]{1,0:T(8,128)}) %reduce-scatter.2.cloned.1.call-update) | async-done | bytes 344080 | tf_op jit(solution)/shard_map/reduce_scatter | solution.py:36
  199.9 0.0 copy-done.4
  199.9 1.8 fusion.9
  201.8 2.0 fusion.6
  203.7 0.0 all-reduce.7.cloned.1.call-update
  204.4 0.6 dynamic-slice.3
  205.0 86.8 %all-reduce.7.cloned.1.call-done = (f32[4,5376]{1,0:T(4,128)}, f32[4,5376]{1,0:T(4,128)}) async-done(((f32[4,5376]{1,0:T(4,128)}, f32[4,5376]{1,0:T(4,128)}), (f32[4,5376]{1,0:T(4,128)}, f32[4,5376]{1,0:T(4,128)})) %all-reduce.7.cloned.1.call-update) | async-done | bytes 172048 | tf_op jit(solution)/shard_map/psum | solution.py:52
  291.8 1.5 copy.16
  293.3 1.5 copy.17
  (6 shorter events, 0.0 us)
Async XLA Ops:
  7.2 60.9 %copy-start = (f32[4,5376]{1,0:T(4,128)S(1)}, f32[4,5376]{1,0:T(4,128)}, u32[]{:S(2)}) copy-start(f32[4,5376]{1,0:T(4,128)} %param.12) | copy-start | bytes 258052
  7.2 58.5 %all-gather.3.cloned.1.call-start = ((), (), s32[]{:S(2)}) async-start(), calls=%async_computation.1 | async-start | bytes 2924544 | tf_op jit(solution)/shard_map/all_gather | solution.py:14
  7.9 192.0 %reduce-scatter.2.cloned.1.call-start = ((), (), s32[]{:S(2)}) async-start(), calls=%async_computation.2 | async-start | bytes 5849088 | tf_op jit(solution)/shard_map/reduce_scatter | solution.py:36
  65.7 9.8 %copy-start.3 = (f32[4,5376]{1,0:T(4,128)S(1)}, f32[4,5376]{1,0:T(4,128)}, u32[]{:S(2)}) copy-start(f32[4,5376]{1,0:T(4,128)} %param.13) | copy-start | bytes 258052
  68.1 12.4 %copy-start.2 = (bf16[1024,5376]{1,0:T(8,128)(2,1)S(1)}, bf16[1024,5376]{1,0:T(8,128)(2,1)}, u32[]{:S(2)}) copy-start(bf16[1024,5376]{1,0:T(8,128)(2,1)} %param.11) | copy-start | bytes 33030148
  122.4 1.8 copy-start.1
  122.4 77.5 %copy-start.4 = (s32[16]{0:T(128)S(1)}, s32[16]{0:T(128)}, u32[]{:S(2)}) copy-start(s32[16]{0:T(128)} %param.8) | copy-start | bytes 196
  122.4 169.4 %all-reduce.7.cloned.1.call-start = ((), (), s32[]{:S(2)}) async-start(), calls=%async_computation.3 | async-start | bytes 344064 | tf_op jit(solution)/shard_map/psum | solution.py:52
Sparse Core Ops, SparseCore 0:
  10.3 46.4 all-gather.2
  122.5 77.3 reduce-scatter.1
  204.4 87.3 all-reduce.6
where the time goes:
time: 302 us; the launch traced here: 301 us
  waiting for transfers between devices  160 us (53%)
  blocking collectives  83 us (27%)
  matrix products  28.3 us (9%)
  between operations  15.1 us (5%)
  local copies, waits for them, and re-layouts  7.62 us (3%)
  other arithmetic  6.78 us (2%)
    psum x1, waiting for transfers between devices, shards(): gain_total, bias_total = lax.psum((gain_total, bias_total), 'loop')  86.8 us
    reduce_scatter x1, waiting for transfers between devices, shards(): lax.psum_scatter(jnp.dot(slopes, tied_head, preferred_element_type=jnp.fl...  72.8 us
    unnamed x2, blocking collectives  59.9 us
    all_gather x1, blocking collectives, shards(): lax.all_gather(own_pick, 'loop', axis=0, tiled=True)  23.2 us
    dot_general x1, matrix products, shards(): jnp.dot(slopes, tied_head, preferred_element_type=jnp.float32)  9.04 us
    unnamed x18, local copies, waits for them, and re-layouts  7.62 us
    dot_general x1, matrix products, shards(): jnp.dot(all_pick, depth_gain, precision=lax.Precision.HIGHEST, preferred_...  7.32 us
  transfers between devices with their start and end apart: 3, of which 2 were waited for; matrix products, arithmetic and copies ran while one was open for 2% of the time, Pallas kernels for 0%

commit v1 on v0

v1 whole, which is shorter than its diff:
```python
import jax
import jax.numpy as jnp
from jax import lax
from jax.sharding import PartitionSpec as P

BF16 = jnp.bfloat16
F32 = jnp.float32


def ring_of(chips):
    order = list(range(0, chips, 2)) + list(range(chips - 1, 0, -2))
    return order if len(order) == chips else list(range(chips))


def ring_pairs(order):
    chips = len(order)
    return [
        (2 * order[i] + core, 2 * order[(i + 1) % chips] + core)
        for i in range(chips)
        for core in range(2)
    ]


def pieces(value):
    top = lax.reduce_precision(value, 8, 7)
    rest = value - top
    middle = lax.reduce_precision(rest, 8, 7)
    return [top, middle, rest - middle]


def digits(token):
    return [(token & 127), (token >> 7) & 127, token >> 14]


def pack(hidden, exit_depth, teacher, normalizer):
    columns = (
        pieces(normalizer)
        + [d.astype(F32) for d in digits(teacher)]
        + [exit_depth.astype(F32)]
    )
    meta = jnp.stack(columns, axis=1).astype(BF16)
    meta = jnp.pad(meta, ((0, 0), (0, 128 - meta.shape[1])))
    return jnp.concatenate([hidden, meta], axis=1)


def gather_rows(block, loop):
    chips = loop // 2
    order = ring_of(chips)
    right = ring_pairs(order)
    left = [(b, a) for a, b in right]
    swap = [(i, i ^ 1) for i in range(loop)]
    send = lambda x, pairs: lax.ppermute(x, "loop", pairs)
    mine = [None] * chips
    mine[0] = block
    from_left = from_right = block
    for step in range(1, (chips + 1) // 2):
        from_left, from_right = send(from_left, right), send(from_right, left)
        mine[chips - step], mine[step] = from_left, from_right
    if chips % 2 == 0:
        half = block.shape[1] // 256 * 128
        mine[chips // 2] = jnp.concatenate(
            [send(from_left[:, :half], right), send(from_right[:, half:], left)], axis=1
        )
    return mine + [send(x, swap) for x in mine]


def shards(loop, hidden, exit_depth, teacher, normalizer, tied_head, depth_gain, depth_bias):
    rows_dev, width = hidden.shape
    levels = depth_gain.shape[0]
    voc_local = tied_head.shape[0]
    chips = loop // 2
    rows = rows_dev * loop
    me = lax.axis_index("loop")
    order = jnp.array(ring_of(chips), jnp.int32)
    place = jnp.argmax(order == me // 2).astype(jnp.int32)
    core = me % 2

    every = jnp.concatenate(
        gather_rows(pack(hidden, exit_depth, teacher, normalizer), loop), axis=0
    )
    meta = every[:, width:].astype(F32)
    norm = (meta[:, 0] + meta[:, 1]) + meta[:, 2]
    target = (meta[:, 3] + 128.0 * meta[:, 4] + 16384.0 * meta[:, 5]).astype(jnp.int32)
    pick = (meta[:, 6:7] == jnp.arange(levels, dtype=F32)[None, :]).astype(F32)
    widened = every[:, :width].astype(F32)
    normed = widened * lax.rsqrt(jnp.mean(widened * widened, axis=-1, keepdims=True) + 1e-06)
    row_gain = jnp.dot(pick, depth_gain, precision=lax.Precision.HIGHEST)
    row_bias = jnp.dot(pick, depth_bias, precision=lax.Precision.HIGHEST)
    mapped = (normed * row_gain + row_bias).astype(BF16)
    logits = jnp.einsum("rd,vd->rv", mapped, tied_head, preferred_element_type=F32)
    prob_rows = jnp.exp(logits - norm[:, None])
    columns = me * voc_local + jnp.arange(voc_local, dtype=jnp.int32)
    onehot = (target[:, None] == columns[None, :]).astype(F32)
    slopes = (prob_rows - onehot).astype(BF16)
    back = jnp.dot(slopes, tied_head, preferred_element_type=F32)
    gain_part = jnp.dot(pick.T, back * normed, precision=lax.Precision.HIGHEST)
    bias_part = jnp.dot(pick.T, back, precision=lax.Precision.HIGHEST)
    mass = jnp.sum(prob_rows, axis=1).reshape(2, rows // 2)
    mass = jnp.roll(mass, place * rows_dev, axis=1)
    mass = jnp.where(core == 0, mass, mass[::-1]).reshape(rows)

    total = jnp.concatenate(
        [
            jnp.concatenate([gain_part, bias_part], axis=0),
            jnp.pad(mass[None, :], ((0, 2 * levels - 1), (0, 0))),
        ],
        axis=1,
    )
    total = total + lax.ppermute(total, "loop", [(i, i ^ 1) for i in range(loop)])
    bit = 2
    while bit < loop:
        pairs = [(i, i ^ bit) for i in range(loop)]
        total = lax.reduce_precision(total, 8, 7)
        total = total + lax.ppermute(total.astype(BF16), "loop", pairs).astype(F32)
        bit *= 2
    row_mass = lax.dynamic_slice(
        total[0, width:], (core * (rows // 2) + place * rows_dev,), (rows_dev,)
    )
    return row_mass, total[:levels, :width], total[levels:, :width]


def solution(mesh):
    loop = mesh.shape["loop"]

    def body(*args):
        return shards(loop, *args)

    return jax.shard_map(
        body,
        mesh=mesh,
        in_specs=(
            P(("groups", "loop"), None),
            P(("groups", "loop")),
            P(("groups", "loop")),
            P(("groups", "loop")),
            P("loop", None),
            P(),
            P(),
        ),
        out_specs=(P(("groups", "loop")), P("groups", None), P("groups", None)),
        check_vma=False,
    )
```

time: 302 us -> 75 us (0.25)
  waiting for transfers between devices: 160 us -> 31.2 us
  blocking collectives: 83 us -> 0 us
  starting transfers between devices: 0.12 us -> 16.5 us
  between operations: 15.1 us -> 1.59 us
  matrix products: 28.3 us -> 16.3 us
  local copies, waits for them, and re-layouts: 7.62 us -> 3.33 us
    psum x1 -> x0, waiting for transfers between devices: 86.8 us -> none  [shards(): gain_total, bias_total = lax.psum((gain_total, bias_total), 'loop')]
    reduce_scatter x1 -> x0, waiting for transfers between devices: 72.8 us -> none  [shards(): lax.psum_scatter(jnp.dot(slopes, tied_head, preferred_element_type=jnp.fl...]
    unnamed x2 -> x0, blocking collectives: 59.9 us -> none
    ppermute x0 -> x20, waiting for transfers between devices: none -> 31.2 us  [the longest x16 20.2 us: gather_rows(): send = lambda x, pairs: lax.ppermute(x, 'loop', pairs)]
    all_gather x1 -> x0, blocking collectives: 23.2 us -> none  [shards(): lax.all_gather(own_pick, 'loop', axis=0, tiled=True)]
    ppermute x0 -> x20, starting transfers between devices: none -> 16.5 us  [the longest x16 10.9 us: gather_rows(): send = lambda x, pairs: lax.ppermute(x, 'loop', pairs)]
    dot_general x6, matrix products: 28.3 us -> 16.3 us  [the longest x1 3.13 us: shards(): back = jnp.dot(slopes, tied_head, preferred_element_type=F32)]
    unnamed x18 -> x25, local copies, waits for them, and re-layouts: 7.62 us -> 1.22 us
  transfers between devices with their start and end apart: 3 -> 20, of which waited for: 2 -> 12; matrix products, arithmetic and copies ran while one was open for 2% -> 3% of each run, Pallas kernels for 0% -> 0%
where the time goes in v1:
time: 75 us; the launch traced here: 74.8 us
  waiting for transfers between devices  31.2 us (42%)
  starting transfers between devices  16.5 us (22%)
  matrix products  16.3 us (22%)
  other arithmetic  5.84 us (8%)
  local copies, waits for them, and re-layouts  3.33 us (4%)
  between operations  1.59 us (2%)
    ppermute x16, waiting for transfers between devices, gather_rows(): send = lambda x, pairs: lax.ppermute(x, 'loop', pairs)  20.2 us
    ppermute x16, starting transfers between devices, gather_rows(): send = lambda x, pairs: lax.ppermute(x, 'loop', pairs)  10.9 us
    ppermute x3, waiting for transfers between devices, shards(): total = total + lax.ppermute(total.astype(BF16), 'loop', pairs).astype(F32)  9.93 us
    ppermute x3, starting transfers between devices, shards(): total = total + lax.ppermute(total.astype(BF16), 'loop', pairs).astype(F32)  5.09 us
    dot_general x1, matrix products, shards(): back = jnp.dot(slopes, tied_head, preferred_element_type=F32)  3.13 us
    dot_general x1, matrix products, shards(): jnp.einsum('rd,vd->rv', mapped, tied_head, preferred_element_type=F32)  3.13 us
    dot_general x1, matrix products, shards(): row_gain = jnp.dot(pick, depth_gain, precision=lax.Precision.HIGHEST)  3.05 us
    dot_general x1, matrix products, shards(): gain_part = jnp.dot(pick.T, back * normed, precision=lax.Precision.HIGHEST)  2.64 us
  transfers between devices with their start and end apart: 20, of which 12 were waited for; matrix products, arithmetic and copies ran while one was open for 3% of the time, Pallas kernels for 0%

profile of v1, /device:TPU:0, one launch (start us, length us, event | category | flops | bytes accessed | tf_op | source)
XLA Modules:
  0.0 74.8 jit_solution(8565290418066255013)
XLA Ops:
  0.6 0.7 convert_bitcast_fusion
  1.3 0.7 convert_bitcast_fusion.1
  2.0 0.7 fusion.31
  2.7 0.1 copy.20
  2.8 0.1 copy.23
  2.9 0.1 copy.24
  3.2 0.1 copy.22
  3.3 0.1 stack.39
  3.4 0.9 %fusion.13 = (bf16[16,5504]{1,0:T(8,128)(2,1)S(1)}, bf16[256,5504]{1,0:T(8,128)(2,1)S(1)}) fusion(bf16[16,7]{1,0:T(8,128)(2,1)S(1)} %stack.39, bf16[16,5376]{1,0:T(8,128)(2,1)} %param.8), kind=kLoop, calls=%fused_computation.24 | loop fusion | flops 528383 | bytes 524512 | tf_op jit(solution)/shard_map/concatenate | solution.py:43
  4.4 3.1 %collective-permute-start.3 = (bf16[16,5504]{1,0:T(8,128)(2,1)S(1)}, bf16[16,5504]{1,0:T(8,128)(2,1)S(1)}, u32[]{:S(2)}, u32[]{:S(2)}) collective-permute-start(bf16[16,5504]{1,0:T(8,128)(2,1)S(1)} %get-tuple-element.11), channel_id=1, source_target_pairs={{0,4},{1,5},{4,8},{5,9},{8,12},{9,13},{12,14},{13,15},{14,10},{15,... | collective-permute-start | bytes 528392 | tf_op jit(solution)/shard_map/ppermute | solution.py:52
  7.5 1.3 %compare_reduce_fusion = (pred[]{:T(512)}, s32[]{:T(128)}) fusion(s32[8]{0:T(128)} %constant.84.clone, s32[]{:T(128)S(6)} %select_n.40), kind=kLoop, calls=%fused_computation.66 | loop fusion | flops 57 | bytes 41 | tf_op jit(solution)/shard_map/shards/reduce | solution.py:75
  9.5 2.4 %collective-permute-done.3 = bf16[16,5504]{1,0:T(8,128)(2,1)S(1)} collective-permute-done((bf16[16,5504]{1,0:T(8,128)(2,1)S(1)}, bf16[16,5504]{1,0:T(8,128)(2,1)S(1)}, u32[]{:S(2)}, u32[]{:S(2)}) %collective-permute-start.3) | collective-permute-done | bytes 176160 | tf_op jit(solution)/shard_map/ppermute | solution.py:52
  11.9 1.8 %collective-permute-start.4 = (bf16[16,5504]{1,0:T(8,128)(2,1)S(1)}, bf16[16,5504]{1,0:T(8,128)(2,1)S(1)}, u32[]{:S(2)}, u32[]{:S(2)}) collective-permute-start(bf16[16,5504]{1,0:T(8,128)(2,1)S(1)} %collective-permute-done.3), channel_id=1, source_target_pairs={{0,4},{1,5},{4,8},{5,9},{8,12},{9,13},{12,14},{13,15},{14,10},{15,... | collective-permute-start | bytes 528392 | tf_op jit(solution)/shard_map/ppermute | solution.py:52
  13.7 0.2 collective-permute-start.9
  13.9 0.2 collective-permute-start.1
  14.1 4.6 %collective-permute-done.4 = bf16[16,5504]{1,0:T(8,128)(2,1)S(1)} collective-permute-done((bf16[16,5504]{1,0:T(8,128)(2,1)S(1)}, bf16[16,5504]{1,0:T(8,128)(2,1)S(1)}, u32[]{:S(2)}, u32[]{:S(2)}) %collective-permute-start.4) | collective-permute-done | bytes 176160 | tf_op jit(solution)/shard_map/ppermute | solution.py:52
  18.7 1.8 %collective-permute-start.5 = (bf16[16,5504]{1,0:T(8,128)(2,1)S(1)}, bf16[16,5504]{1,0:T(8,128)(2,1)S(1)}, u32[]{:S(2)}, u32[]{:S(2)}) collective-permute-start(bf16[16,5504]{1,0:T(8,128)(2,1)S(1)} %collective-permute-done.4), channel_id=1, source_target_pairs={{0,4},{1,5},{4,8},{5,9},{8,12},{9,13},{12,14},{13,15},{14,10},{15,... | collective-permute-start | bytes 528392 | tf_op jit(solution)/shard_map/ppermute | solution.py:52
  20.6 0.3 collective-permute-start.2
  20.9 4.0 %collective-permute-done.5 = bf16[16,5504]{1,0:T(8,128)(2,1)S(1)} collective-permute-done((bf16[16,5504]{1,0:T(8,128)(2,1)S(1)}, bf16[16,5504]{1,0:T(8,128)(2,1)S(1)}, u32[]{:S(2)}, u32[]{:S(2)}) %collective-permute-start.5) | collective-permute-done | bytes 176160 | tf_op jit(solution)/shard_map/ppermute | solution.py:52
  24.9 1.5 %collective-permute-done.2 = bf16[16,5504]{1,0:T(8,128)(2,1)S(1)} collective-permute-done((bf16[16,5504]{1,0:T(8,128)(2,1)S(1)}, bf16[16,5504]{1,0:T(8,128)(2,1)S(1)}, u32[]{:S(2)}, u32[]{:S(2)}) %collective-permute-start.2) | collective-permute-done | bytes 176160 | tf_op jit(solution)/shard_map/ppermute | solution.py:52
  26.4 1.6 %collective-permute-start.6 = (bf16[16,2688]{1,0:T(8,128)(2,1)S(1)}, bf16[16,2688]{1,0:T(8,128)(2,1)S(1)}, u32[]{:S(2)}, u32[]{:S(2)}) collective-permute-start(bf16[16,2688]{1,0:T(8,128)(2,1)S(1)} %slice.56), channel_id=1, source_target_pairs={{0,4},{1,5},{4,8},{5,9},{8,12},{9,13},{12,14},{13,15},{14,10},{15,... | collective-permute-start | bytes 258056 | tf_op jit(solution)/shard_map/ppermute | solution.py:52
  28.0 2.9 %collective-permute-done.6 = bf16[16,2688]{1,0:T(8,128)(2,1)S(1)} collective-permute-done((bf16[16,2688]{1,0:T(8,128)(2,1)S(1)}, bf16[16,2688]{1,0:T(8,128)(2,1)S(1)}, u32[]{:S(2)}, u32[]{:S(2)}) %collective-permute-start.6) | collective-permute-done | bytes 86048 | tf_op jit(solution)/shard_map/ppermute | solution.py:52
  30.9 0.7 collective-permute-start.7
  31.6 3.8 %collective-permute-done.7 = bf16[16,2816]{1,0:T(8,128)(2,1)S(1)} collective-permute-done((bf16[16,2816]{1,0:T(8,128)(2,1)S(1)}, bf16[16,2816]{1,0:T(8,128)(2,1)S(1)}, u32[]{:S(2)}, u32[]{:S(2)}) %collective-permute-start.7) | collective-permute-done | bytes 90144 | tf_op jit(solution)/shard_map/ppermute | solution.py:52
  35.5 0.6 collective-permute-start.13
  36.1 0.9 %constant_dynamic-update-slice_fusion.7 = bf16[256,5504]{1,0:T(8,128)(2,1)S(1)} fusion(bf16[256,5504]{1,0:T(8,128)(2,1)S(1)} %constant_dynamic-update-slice_fusion.8, bf16[16,5504]{1,0:T(8,128)(2,1)} %collective-permute-done.8), kind=kLoop, calls=%fused_computation.53 | loop fusion | bytes 352256
  37.1 0.6 collective-permute-start.12
  37.7 0.8 %collective-permute-done.11 = bf16[16,5504]{1,0:T(8,128)(2,1)S(1)} collective-permute-done((bf16[16,5504]{1,0:T(8,128)(2,1)S(1)}, bf16[16,5504]{1,0:T(8,128)(2,1)S(1)}, u32[]{:S(2)}, u32[]{:S(2)}) %collective-permute-start.11) | collective-permute-done | bytes 176160 | tf_op jit(solution)/shard_map/ppermute | solution.py:52
  38.5 0.2 collective-permute-done.12
  38.9 0.6 fusion.5
  39.5 0.2 fusion.16
  39.8 0.3 fusion.18
  40.1 2.3 %fusion.20 = f32[256,5376]{1,0:T(8,128)S(1)} fusion(f32[4,5376]{1,0:T(4,128)S(1)} %copy-done, f32[256]{0:T(256)S(1)} %get-tuple-element.6), kind=kOutput, calls=%fused_computation.38 | convolution fusion | flops 66061312 | bytes 5592064 | tf_op jit(solution)/shard_map/dot_general | solution.py:88
  42.5 3.1 %fusion.1 = bf16[256,5376]{1,0:T(8,128)(2,1)S(1)} fusion(f32[256,5376]{1,0:T(8,128)S(1)} %fusion.20, f32[4,5376]{1,0:T(4,128)S(1)} %copy-done.1, f32[256]{0:T(256)S(1)} %add_rsqrt_fusion, bf16[256,5504]{1,0:T(8,128)(2,1)S(1)} %constant_dynamic-update-slice_fusion, f32[256]{0:T(256)S(1)} %get-tuple-element.6), kind=kOutput, calls=%fused_computation.2 | convolution fusion | flops 72942592 | bytes 11098112 | tf_op jit(solution)/shard_map/dot_general | solution.py:87
  45.6 3.1 %fusion.35 = (f32[256]{0:T(256)S(1)}, f32[256,1024]{1,0:T(8,128)S(1)}) fusion(f32[256]{0:T(256)S(1)} %get-tuple-element.5, bf16[256,5376]{1,0:T(8,128)(2,1)S(1)} %fusion.1, bf16[1024,5376]{1,0:T(8,128)(2,1)S(1)} %bitcast.25), kind=kOutput, calls=%fused_computation.86 | convolution fusion | flops 2819096320 | bytes 14813184 | tf_op jit(solution)/shard_map/rd,vd->rv/dot_general | solution.py:90
  48.7 3.1 %fusion.9 = f32[256,5376]{1,0:T(8,128)S(1)} fusion(bf16[1024,5376]{1,0:T(8,128)(2,1)S(1)} %bitcast.25, f32[256,1024]{1,0:T(8,128)S(1)} %get-tuple-element.20, s32[1024]{0:T(1024)S(1)} %iota_add_fusion, s32[256]{0:T(256)S(1)} %fusion.16), kind=kOutput, calls=%fused_computation.13 | convolution fusion | flops 2819620864 | bytes 17568768 | tf_op jit(solution)/shard_map/dot_general | solution.py:95
  51.9 2.6 %fusion.3 = f32[4,5376]{1,0:T(4,128)S(1)} fusion(f32[256,5376]{1,0:T(8,128)S(1)} %fusion.9, f32[256]{0:T(256)S(1)} %add_rsqrt_fusion, bf16[256,5504]{1,0:T(8,128)(2,1)S(1)} %constant_dynamic-update-slice_fusion, f32[256]{0:T(256)S(1)} %get-tuple-element.6), kind=kOutput, calls=%fused_computation.6 | convolution fusion | flops 70190080 | bytes 8345600 | tf_op jit(solution)/shard_map/dot_general | solution.py:96
  54.5 2.0 %fusion.19 = f32[4,5376]{1,0:T(4,128)S(1)} fusion(f32[256,5376]{1,0:T(8,128)S(1)} %fusion.9, f32[256]{0:T(256)S(1)} %get-tuple-element.6), kind=kOutput, calls=%fused_computation.37 | convolution fusion | flops 66061312 | bytes 5592064 | tf_op jit(solution)/shard_map/dot_general | solution.py:97
  56.8 0.4 collective-permute-start.16
  57.2 1.1 %collective-permute-done.16 = f32[8,5632]{1,0:T(8,128)S(1)} collective-permute-done((f32[8,5632]{1,0:T(8,128)S(1)}, f32[8,5632]{1,0:T(8,128)S(1)}, u32[]{:S(2)}, u32[]{:S(2)}) %collective-permute-start.16) | collective-permute-done | bytes 180256 | tf_op jit(solution)/shard_map/ppermute | solution.py:109
  58.3 0.8 %collective-permute-start.17 = (bf16[8,5632]{1,0:T(8,128)(2,1)S(1)}, bf16[8,5632]{1,0:T(8,128)(2,1)S(1)}, u32[]{:S(2)}, u32[]{:S(2)}) collective-permute-start(bf16[8,5632]{1,0:T(8,128)(2,1)S(1)} %get-tuple-element.7), channel_id=1, source_target_pairs={{0,2},{1,3},{2,0},{3,1},{4,6},{5,7},{6,4},{7,5},{8,10},{9,11},{10,... | collective-permute-start | bytes 270344 | tf_op jit(solution)/shard_map/ppermute | solution.py:114
  59.1 4.1 %collective-permute-done.17 = bf16[8,5632]{1,0:T(8,128)(2,1)S(1)} collective-permute-done((bf16[8,5632]{1,0:T(8,128)(2,1)S(1)}, bf16[8,5632]{1,0:T(8,128)(2,1)S(1)}, u32[]{:S(2)}, u32[]{:S(2)}) %collective-permute-start.17) | collective-permute-done | bytes 90144 | tf_op jit(solution)/shard_map/ppermute | solution.py:114
  63.3 1.6 %collective-permute-start.18 = (bf16[8,5632]{1,0:T(8,128)(2,1)S(1)}, bf16[8,5632]{1,0:T(8,128)(2,1)S(1)}, u32[]{:S(2)}, u32[]{:S(2)}) collective-permute-start(bf16[8,5632]{1,0:T(8,128)(2,1)S(1)} %fusion.21), channel_id=1, source_target_pairs={{0,4},{1,5},{2,6},{3,7},{4,0},{5,1},{6,2},{7,3},{8,12},{9,13},{10,... | collective-permute-start | bytes 270344 | tf_op jit(solution)/shard_map/ppermute | solution.py:114
  64.9 3.0 %collective-permute-done.18 = bf16[8,5632]{1,0:T(8,128)(2,1)S(1)} collective-permute-done((bf16[8,5632]{1,0:T(8,128)(2,1)S(1)}, bf16[8,5632]{1,0:T(8,128)(2,1)S(1)}, u32[]{:S(2)}, u32[]{:S(2)}) %collective-permute-start.18) | collective-permute-done | bytes 90144 | tf_op jit(solution)/shard_map/ppermute | solution.py:114
  67.9 2.7 %collective-permute-start.19 = (bf16[8,5632]{1,0:T(8,128)(2,1)S(1)}, bf16[8,5632]{1,0:T(8,128)(2,1)S(1)}, u32[]{:S(2)}, u32[]{:S(2)}) collective-permute-start(bf16[8,5632]{1,0:T(8,128)(2,1)S(1)} %fusion.26), channel_id=1, source_target_pairs={{0,8},{1,9},{2,10},{3,11},{4,12},{5,13},{6,14},{7,15},{8,0},{9,1},... | collective-permute-start | bytes 270344 | tf_op jit(solution)/shard_map/ppermute | solution.py:114
  70.6 2.8 %collective-permute-done.19 = bf16[8,5632]{1,0:T(8,128)(2,1)S(1)} collective-permute-done((bf16[8,5632]{1,0:T(8,128)(2,1)S(1)}, bf16[8,5632]{1,0:T(8,128)(2,1)S(1)}, u32[]{:S(2)}, u32[]{:S(2)}) %collective-permute-start.19) | collective-permute-done | bytes 90144 | tf_op jit(solution)/shard_map/ppermute | solution.py:114
  73.5 0.7 fusion.34
  74.2 0.6 fusion.32
  (58 shorter events, 1.2 us)
Async XLA Ops:
  0.6 39.5 %copy-start = (f32[4,5376]{1,0:T(4,128)S(1)}, f32[4,5376]{1,0:T(4,128)}, u32[]{:S(2)}) copy-start(f32[4,5376]{1,0:T(4,128)} %param.14) | copy-start | bytes 258052
  4.4 7.5 %collective-permute-start.3 = (bf16[16,5504]{1,0:T(8,128)(2,1)S(1)}, bf16[16,5504]{1,0:T(8,128)(2,1)S(1)}, u32[]{:S(2)}, u32[]{:S(2)}) collective-permute-start(bf16[16,5504]{1,0:T(8,128)(2,1)S(1)} %get-tuple-element.11), channel_id=1, source_target_pairs={{0,4},{1,5},{4,8},{5,9},{8,12},{9,13},{12,14},{13,15},{14,10},{15,... | collective-permute-start | bytes 528392 | tf_op jit(solution)/shard_map/ppermute | solution.py:52
  7.5 6.2 %collective-permute-start = (bf16[16,5504]{1,0:T(8,128)(2,1)S(1)}, bf16[16,5504]{1,0:T(8,128)(2,1)S(1)}, u32[]{:S(2)}, u32[]{:S(2)}) collective-permute-start(bf16[16,5504]{1,0:T(8,128)(2,1)S(1)} %get-tuple-element.11), channel_id=1, source_target_pairs={{4,0},{5,1},{8,4},{9,5},{12,8},{13,9},{14,12},{15,13},{10,14},{11,... | collective-permute-start | bytes 528392 | tf_op jit(solution)/shard_map/ppermute | solution.py:52
  7.5 28.0 %collective-permute-start.8 = (bf16[16,5504]{1,0:T(8,128)(2,1)S(1)}, bf16[16,5504]{1,0:T(8,128)(2,1)}, u32[]{:S(2)}, u32[]{:S(2)}) collective-permute-start(bf16[16,5504]{1,0:T(8,128)(2,1)S(1)} %get-tuple-element.11), channel_id=1, source_target_pairs={{0,1},{1,0},{2,3},{3,2},{4,5},{5,4},{6,7},{7,6},{8,9},{9,8},{10,11... | collective-permute-start | bytes 528392 | tf_op jit(solution)/shard_map/ppermute | solution.py:52
  11.9 27.0 %collective-permute-start.15 = (bf16[16,5504]{1,0:T(8,128)(2,1)S(1)}, bf16[16,5504]{1,0:T(8,128)(2,1)S(1)}, u32[]{:S(2)}, u32[]{:S(2)}) collective-permute-start(bf16[16,5504]{1,0:T(8,128)(2,1)S(1)} %collective-permute-done.3), channel_id=1, source_target_pairs={{0,1},{1,0},{2,3},{3,2},{4,5},{5,4},{6,7},{7,6},{8,9},{9,8},{10,11... | collective-permute-start | bytes 528392 | tf_op jit(solution)/shard_map/ppermute | solution.py:52
  11.9 6.9 %collective-permute-start.4 = (bf16[16,5504]{1,0:T(8,128)(2,1)S(1)}, bf16[16,5504]{1,0:T(8,128)(2,1)S(1)}, u32[]{:S(2)}, u32[]{:S(2)}) collective-permute-start(bf16[16,5504]{1,0:T(8,128)(2,1)S(1)} %collective-permute-done.3), channel_id=1, source_target_pairs={{0,4},{1,5},{4,8},{5,9},{8,12},{9,13},{12,14},{13,15},{14,10},{15,... | collective-permute-start | bytes 528392 | tf_op jit(solution)/shard_map/ppermute | solution.py:52
  13.7 23.4 %collective-permute-start.9 = (bf16[16,5504]{1,0:T(8,128)(2,1)S(1)}, bf16[16,5504]{1,0:T(8,128)(2,1)S(1)}, u32[]{:S(2)}, u32[]{:S(2)}) collective-permute-start(bf16[16,5504]{1,0:T(8,128)(2,1)S(1)} %collective-permute-done), channel_id=1, source_target_pairs={{0,1},{1,0},{2,3},{3,2},{4,5},{5,4},{6,7},{7,6},{8,9},{9,8},{10,11... | collective-permute-start | bytes 528392 | tf_op jit(solution)/shard_map/ppermute | solution.py:52
  13.9 6.7 %collective-permute-start.1 = (bf16[16,5504]{1,0:T(8,128)(2,1)S(1)}, bf16[16,5504]{1,0:T(8,128)(2,1)S(1)}, u32[]{:S(2)}, u32[]{:S(2)}) collective-permute-start(bf16[16,5504]{1,0:T(8,128)(2,1)S(1)} %collective-permute-done), channel_id=1, source_target_pairs={{4,0},{5,1},{8,4},{9,5},{12,8},{13,9},{14,12},{15,13},{10,14},{11,... | collective-permute-start | bytes 528392 | tf_op jit(solution)/shard_map/ppermute | solution.py:52
  18.7 6.1 %collective-permute-start.5 = (bf16[16,5504]{1,0:T(8,128)(2,1)S(1)}, bf16[16,5504]{1,0:T(8,128)(2,1)S(1)}, u32[]{:S(2)}, u32[]{:S(2)}) collective-permute-start(bf16[16,5504]{1,0:T(8,128)(2,1)S(1)} %collective-permute-done.4), channel_id=1, source_target_pairs={{0,4},{1,5},{4,8},{5,9},{8,12},{9,13},{12,14},{13,15},{14,10},{15,... | collective-permute-start | bytes 528392 | tf_op jit(solution)/shard_map/ppermute | solution.py:52
  20.6 5.8 %collective-permute-start.2 = (bf16[16,5504]{1,0:T(8,128)(2,1)S(1)}, bf16[16,5504]{1,0:T(8,128)(2,1)S(1)}, u32[]{:S(2)}, u32[]{:S(2)}) collective-permute-start(bf16[16,5504]{1,0:T(8,128)(2,1)S(1)} %collective-permute-done.1), channel_id=1, source_target_pairs={{4,0},{5,1},{8,4},{9,5},{12,8},{13,9},{14,12},{15,13},{10,14},{11,... | collective-permute-start | bytes 528392 | tf_op jit(solution)/shard_map/ppermute | solution.py:52
  24.8 14.0 %collective-permute-start.14 = (bf16[16,5504]{1,0:T(8,128)(2,1)S(1)}, bf16[16,5504]{1,0:T(8,128)(2,1)S(1)}, u32[]{:S(2)}, u32[]{:S(2)}) collective-permute-start(bf16[16,5504]{1,0:T(8,128)(2,1)S(1)} %collective-permute-done.4), channel_id=1, source_target_pairs={{0,1},{1,0},{2,3},{3,2},{4,5},{5,4},{6,7},{7,6},{8,9},{9,8},{10,11... | collective-permute-start | bytes 528392 | tf_op jit(solution)/shard_map/ppermute | solution.py:52
  26.4 4.5 %collective-permute-start.6 = (bf16[16,2688]{1,0:T(8,128)(2,1)S(1)}, bf16[16,2688]{1,0:T(8,128)(2,1)S(1)}, u32[]{:S(2)}, u32[]{:S(2)}) collective-permute-start(bf16[16,2688]{1,0:T(8,128)(2,1)S(1)} %slice.56), channel_id=1, source_target_pairs={{0,4},{1,5},{4,8},{5,9},{8,12},{9,13},{12,14},{13,15},{14,10},{15,... | collective-permute-start | bytes 258056 | tf_op jit(solution)/shard_map/ppermute | solution.py:52
  30.9 4.5 %collective-permute-start.7 = (bf16[16,2816]{1,0:T(8,128)(2,1)S(1)}, bf16[16,2816]{1,0:T(8,128)(2,1)S(1)}, u32[]{:S(2)}, u32[]{:S(2)}) collective-permute-start(bf16[16,2816]{1,0:T(8,128)(2,1)S(1)} %slice.57), channel_id=1, source_target_pairs={{4,0},{5,1},{8,4},{9,5},{12,8},{13,9},{14,12},{15,13},{10,14},{11,... | collective-permute-start | bytes 270344 | tf_op jit(solution)/shard_map/ppermute | solution.py:52
  35.4 1.7 %collective-permute-start.10 = (bf16[16,5504]{1,0:T(8,128)(2,1)S(1)}, bf16[16,5504]{1,0:T(8,128)(2,1)S(1)}, u32[]{:S(2)}, u32[]{:S(2)}) collective-permute-start(bf16[16,5504]{1,0:T(8,128)(2,1)S(1)} %collective-permute-done.1), channel_id=1, source_target_pairs={{0,1},{1,0},{2,3},{3,2},{4,5},{5,4},{6,7},{7,6},{8,9},{9,8},{10,11... | collective-permute-start | bytes 528392 | tf_op jit(solution)/shard_map/ppermute | solution.py:52
  35.5 3.3 %collective-permute-start.13 = (bf16[16,5504]{1,0:T(8,128)(2,1)S(1)}, bf16[16,5504]{1,0:T(8,128)(2,1)S(1)}, u32[]{:S(2)}, u32[]{:S(2)}) collective-permute-start(bf16[16,5504]{1,0:T(8,128)(2,1)S(1)} %collective-permute-done.5), channel_id=1, source_target_pairs={{0,1},{1,0},{2,3},{3,2},{4,5},{5,4},{6,7},{7,6},{8,9},{9,8},{10,11... | collective-permute-start | bytes 528392 | tf_op jit(solution)/shard_map/ppermute | solution.py:52
  37.0 1.5 %collective-permute-start.11 = (bf16[16,5504]{1,0:T(8,128)(2,1)S(1)}, bf16[16,5504]{1,0:T(8,128)(2,1)S(1)}, u32[]{:S(2)}, u32[]{:S(2)}) collective-permute-start(bf16[16,5504]{1,0:T(8,128)(2,1)S(1)} %collective-permute-done.2), channel_id=1, source_target_pairs={{0,1},{1,0},{2,3},{3,2},{4,5},{5,4},{6,7},{7,6},{8,9},{9,8},{10,11... | collective-permute-start | bytes 528392 | tf_op jit(solution)/shard_map/ppermute | solution.py:52
  37.1 1.6 %collective-permute-start.12 = (bf16[16,5504]{1,0:T(8,128)(2,1)S(1)}, bf16[16,5504]{1,0:T(8,128)(2,1)S(1)}, u32[]{:S(2)}, u32[]{:S(2)}) collective-permute-start(bf16[16,5504]{1,0:T(8,128)(2,1)S(1)} %pad_maximum_fusion), channel_id=1, source_target_pairs={{0,1},{1,0},{2,3},{3,2},{4,5},{5,4},{6,7},{7,6},{8,9},{9,8},{10,11... | collective-permute-start | bytes 528392 | tf_op jit(solution)/shard_map/ppermute | solution.py:52
  38.9 6.7 %slice-start = ((s8[11010048]{0:T(1024)(128)(4,1)}), s8[4194304]{0:T(1024)(128)(4,1)S(1)}, s32[]{:S(2)}) async-start(s8[11010048]{0:T(1024)(128)(4,1)} %bitcast.24), calls=%async_computation | async-start | bytes 8388608
  40.1 2.4 %copy-start.1 = (f32[4,5376]{1,0:T(4,128)S(1)}, f32[4,5376]{1,0:T(4,128)}, u32[]{:S(2)}) copy-start(f32[4,5376]{1,0:T(4,128)} %param.13) | copy-start | bytes 258052
  40.1 5.5 %slice-start.1 = ((s8[11010048]{0:T(1024)(128)(4,1)}), s8[4194304]{0:T(1024)(128)(4,1)S(1)}, s32[]{:S(2)}) async-start(s8[11010048]{0:T(1024)(128)(4,1)} %bitcast.24), calls=%async_computation.1 | async-start | bytes 8388608
  42.5 3.1 %slice-start.2 = ((s8[11010048]{0:T(1024)(128)(4,1)}), s8[2621440]{0:T(1024)(128)(4,1)S(1)}, s32[]{:S(2)}) async-start(s8[11010048]{0:T(1024)(128)(4,1)} %bitcast.24), calls=%async_computation.2 | async-start | bytes 5242880
  56.8 1.5 %collective-permute-start.16 = (f32[8,5632]{1,0:T(8,128)S(1)}, f32[8,5632]{1,0:T(8,128)S(1)}, u32[]{:S(2)}, u32[]{:S(2)}) collective-permute-start(f32[8,5632]{1,0:T(8,128)S(1)} %select_maximum_fusion), channel_id=1, source_target_pairs={{0,1},{1,0},{2,3},{3,2},{4,5},{5,4},{6,7},{7,6},{8,9},{9,8},{10,11... | collective-permute-start | bytes 540680 | tf_op jit(solution)/shard_map/ppermute | solution.py:109
  58.3 4.9 %collective-permute-start.17 = (bf16[8,5632]{1,0:T(8,128)(2,1)S(1)}, bf16[8,5632]{1,0:T(8,128)(2,1)S(1)}, u32[]{:S(2)}, u32[]{:S(2)}) collective-permute-start(bf16[8,5632]{1,0:T(8,128)(2,1)S(1)} %get-tuple-element.7), channel_id=1, source_target_pairs={{0,2},{1,3},{2,0},{3,1},{4,6},{5,7},{6,4},{7,5},{8,10},{9,11},{10,... | collective-permute-start | bytes 270344 | tf_op jit(solution)/shard_map/ppermute | solution.py:114
  63.3 4.6 %collective-permute-start.18 = (bf16[8,5632]{1,0:T(8,128)(2,1)S(1)}, bf16[8,5632]{1,0:T(8,128)(2,1)S(1)}, u32[]{:S(2)}, u32[]{:S(2)}) collective-permute-start(bf16[8,5632]{1,0:T(8,128)(2,1)S(1)} %fusion.21), channel_id=1, source_target_pairs={{0,4},{1,5},{2,6},{3,7},{4,0},{5,1},{6,2},{7,3},{8,12},{9,13},{10,... | collective-permute-start | bytes 270344 | tf_op jit(solution)/shard_map/ppermute | solution.py:114
  67.9 5.5 %collective-permute-start.19 = (bf16[8,5632]{1,0:T(8,128)(2,1)S(1)}, bf16[8,5632]{1,0:T(8,128)(2,1)S(1)}, u32[]{:S(2)}, u32[]{:S(2)}) collective-permute-start(bf16[8,5632]{1,0:T(8,128)(2,1)S(1)} %fusion.26), channel_id=1, source_target_pairs={{0,8},{1,9},{2,10},{3,11},{4,12},{5,13},{6,14},{7,15},{8,0},{9,1},... | collective-permute-start | bytes 270344 | tf_op jit(solution)/shard_map/ppermute | solution.py:114

commit v2 on v0

v2 whole, which is shorter than its diff:
```python
import functools

import jax
import jax.numpy as jnp
from jax import lax
from jax.experimental import pallas as pl
from jax.experimental.pallas import tpu as pltpu
from jax.sharding import PartitionSpec as P

BF16 = jnp.bfloat16
F32 = jnp.float32
LANES = 128
NT = (((1,), (1,)), ((), ()))
VMEM = pl.BlockSpec(memory_space=pltpu.VMEM)


def ring_of(chips):
    return list(range(0, chips, 2)) + list(range(chips - 1, 0, -2))


def chip_at(place, chips):
    return jnp.where(place < chips // 2, 2 * place, 2 * (chips - 1 - place) + 1)


def place_of(chip, chips):
    return jnp.where(chip % 2 == 0, chip // 2, chips - 1 - chip // 2)


def pieces(value):
    top = value.astype(BF16).astype(F32)
    rest = value - top
    middle = rest.astype(BF16).astype(F32)
    return [top, middle, rest - middle]


def prep_kernel(hidden, exit_depth, teacher, normalizer, out):
    rows, width = hidden.shape
    block = hidden[...]
    out[:, :width] = block
    wide = block.astype(F32)
    mean = jnp.sum(wide * wide, axis=1, keepdims=True) * (1.0 / width)
    scale = lax.rsqrt(mean + 1e-06)
    down = lax.broadcasted_iota(jnp.int32, (rows, rows), 0)
    across = lax.broadcasted_iota(jnp.int32, (rows, rows), 1)

    def column(line):
        square = jnp.broadcast_to(line, (rows, rows))
        return jnp.sum(jnp.where(down == across, square, 0.0), axis=1, keepdims=True)

    token = teacher[...]
    columns = pieces(scale) + pieces(column(normalizer[...]))
    for digit in (token & 127, (token >> 7) & 127, token >> 14):
        columns.append(column(digit.astype(F32)))
    columns.append(column(exit_depth[...].astype(F32)))
    lane = lax.broadcasted_iota(jnp.int32, (rows, LANES), 1)
    meta = jnp.zeros((rows, LANES), F32)
    for i, value in enumerate(columns):
        meta = jnp.where(lane == i, value, meta)
    out[:, width:] = meta.astype(BF16)


def prep(hidden, exit_depth, teacher, normalizer):
    rows, width = hidden.shape
    line = pl.BlockSpec((1, rows), lambda i: (0, 0))
    return pl.pallas_call(
        prep_kernel,
        grid=(1,),
        out_shape=jax.ShapeDtypeStruct((rows, width + LANES), BF16),
        in_specs=[pl.BlockSpec((rows, width), lambda i: (0, 0)), line, line, line],
        out_specs=VMEM,
        compiler_params=pltpu.CompilerParams(vmem_limit_bytes=8 << 20),
    )(
        hidden,
        exit_depth.reshape(1, rows),
        teacher.reshape(1, rows),
        normalizer.reshape(1, rows),
    )


def gather_blocks(block, loop):
    chips = loop // 2
    order = ring_of(chips)
    pairs = []
    for i in range(chips):
        here, after = order[i], order[(i + 1) % chips]
        pairs += [(2 * here, 2 * after), (2 * after + 1, 2 * here + 1)]
    swap_pairs = [(i, i ^ 1) for i in range(loop)]
    swap = lambda x: lax.ppermute(x, "loop", swap_pairs)
    hop = lambda x: lax.ppermute(x, "loop", pairs)
    same, other = [None] * chips, [None] * chips
    same[0], other[0] = block, swap(block)
    half = chips // 2
    for step in range(1, half + 1):
        same[step] = hop(same[step - 1])
        if step < half:
            other[step] = hop(other[step - 1])
            other[chips - step] = swap(same[step])
            same[chips - step] = swap(other[step])
        else:
            other[step] = swap(same[step])
    return same + other


def main_kernel(loop, levels, count, *refs):
    blocks = refs[:count]
    head, gain, bias, out, mapped, slopes = refs[count:]
    voc, width = head.shape
    rows = mapped.shape[0]
    rows_dev = rows // loop
    chips = loop // 2
    me = lax.axis_index("loop")
    meta = jnp.concatenate([b[:, width:] for b in blocks], axis=0).astype(F32)
    col = lambda i: meta[:, i : i + 1]
    scale = (col(0) + col(1)) + col(2)
    norm = (col(3) + col(4)) + col(5)
    target = (col(6) + 128.0 * col(7) + 16384.0 * col(8)).astype(jnp.int32)
    depth = col(9)

    cut = width // 3
    logits = None
    for k in range(3):
        at = slice(k * cut, (k + 1) * cut)
        row = 0
        for b in blocks:
            part = slice(row, row + b.shape[0])
            g, c = gain[0:1, at], bias[0:1, at]
            for level in range(1, levels):
                here = depth[part] == float(level)
                g = jnp.where(here, gain[level : level + 1, at], g)
                c = jnp.where(here, bias[level : level + 1, at], c)
            mapped[part, at] = ((b[:, at].astype(F32) * scale[part]) * g + c).astype(BF16)
            row += b.shape[0]
        term = lax.dot_general(mapped[:, at], head[:, at], NT, preferred_element_type=F32)
        logits = term if logits is None else logits + term
    prob = jnp.exp(logits - norm)
    columns = me * voc + lax.broadcasted_iota(jnp.int32, (rows, voc), 1)
    slopes[:rows, :] = jnp.where(columns == target, prob - 1.0, prob).astype(BF16)

    mass = prob[:, :LANES]
    for j in range(1, voc // LANES):
        mass = mass + prob[:, j * LANES : (j + 1) * LANES]
    mass = jnp.sum(mass.T, axis=0, keepdims=True)
    index = lax.broadcasted_iota(jnp.int32, (rows, rows), 0)
    flip = index // (rows // 2)
    relative = (index - flip * (rows // 2)) // rows_dev
    core = me % 2
    place = place_of(me // 2, chips) + jnp.where(core == 0, chips - relative, relative)
    place = jnp.where(place >= chips, place - chips, place)
    owner = 2 * chip_at(place, chips) + jnp.where(flip == 0, core, 1 - core)
    goes_to = owner * rows_dev + index % rows_dev
    move = goes_to == lax.broadcasted_iota(jnp.int32, (rows, rows), 1)
    move = jnp.where(move, 1.0, 0.0).astype(BF16)
    lines = jnp.concatenate(pieces(mass) + [jnp.zeros((13, rows), F32)], axis=0)
    moved = jnp.dot(lines.astype(BF16), move, preferred_element_type=F32)
    moved = (moved[0:1] + moved[1:2]) + moved[2:3]
    out[:, width:] = jnp.broadcast_to(moved, (2 * levels, rows))

    lane = lax.broadcasted_iota(jnp.int32, (rows, LANES), 1).astype(F32)
    pick = jnp.where(lane == depth, 1.0, 0.0).T[:levels]
    scaled = pick * jnp.broadcast_to(scale, (rows, LANES)).T[:levels]
    none = jnp.zeros((16 - 3 * levels, rows), F32)
    scaled = jnp.concatenate(pieces(scaled) + [none], axis=0).astype(BF16)
    sums = jnp.dot(pick.astype(BF16), slopes[:rows, :], preferred_element_type=F32)
    none = jnp.zeros((16 - 3 * levels, voc), F32)
    slopes[rows:, :] = jnp.concatenate(pieces(sums) + [none], axis=0).astype(BF16)
    add3 = lambda x: (x[:levels] + x[levels : 2 * levels]) + x[2 * levels : 3 * levels]
    for k in range(width // 256):
        at = slice(k * 256, (k + 1) * 256)
        back = jnp.dot(slopes[...], head[:, at], preferred_element_type=F32)
        wide = jnp.concatenate([b[:, at] for b in blocks], axis=0).astype(F32)
        mapped[:, at] = (back[:rows] * wide).astype(BF16)
        out[levels : 2 * levels, at] = add3(back[rows:])
    out[:levels, :width] = add3(jnp.dot(scaled, mapped[...], preferred_element_type=F32))


def main(blocks, tied_head, depth_gain, depth_bias, loop):
    levels = depth_gain.shape[0]
    voc, width = tied_head.shape
    rows = sum(b.shape[0] for b in blocks)
    return pl.pallas_call(
        functools.partial(main_kernel, loop, levels, len(blocks)),
        out_shape=jax.ShapeDtypeStruct((2 * levels, width + rows), F32),
        in_specs=[VMEM] * (len(blocks) + 3),
        out_specs=VMEM,
        scratch_shapes=[
            pltpu.VMEM((rows, width), BF16),
            pltpu.VMEM((rows + 16, voc), BF16),
        ],
        compiler_params=pltpu.CompilerParams(vmem_limit_bytes=24 << 20),
        cost_estimate=pl.CostEstimate(
            flops=4 * rows * voc * width,
            bytes_accessed=2 * voc * width,
            transcendentals=rows * voc,
        ),
    )(*blocks, tied_head, depth_gain, depth_bias)


def shards(loop, hidden, exit_depth, teacher, normalizer, tied_head, depth_gain, depth_bias):
    rows_dev, width = hidden.shape
    levels = depth_gain.shape[0]
    me = lax.axis_index("loop")
    blocks = gather_blocks(prep(hidden, exit_depth, teacher, normalizer), loop)
    if rows_dev % 16:
        whole = jnp.concatenate(blocks, axis=0)
        blocks = [whole[i : i + 16] for i in range(0, whole.shape[0], 16)]
    total = main(blocks, tied_head, depth_gain, depth_bias, loop)
    total = total + lax.ppermute(total, "loop", [(i, i ^ 1) for i in range(loop)])
    bit = 2
    while bit < loop:
        pairs = [(i, i ^ bit) for i in range(loop)]
        total = lax.reduce_precision(total, 8, 7)
        total = total + lax.ppermute(total.astype(BF16), "loop", pairs).astype(F32)
        bit *= 2
    row_mass = lax.dynamic_slice(total[0], (width + me * rows_dev,), (rows_dev,))
    return row_mass, total[:levels, :width], total[levels:, :width]


def solution(mesh):
    loop = mesh.shape["loop"]

    def body(*args):
        return shards(loop, *args)

    return jax.shard_map(
        body,
        mesh=mesh,
        in_specs=(
            P(("groups", "loop"), None),
            P(("groups", "loop")),
            P(("groups", "loop")),
            P(("groups", "loop")),
            P("loop", None),
            P(),
            P(),
        ),
        out_specs=(P(("groups", "loop")), P("groups", None), P("groups", None)),
        check_vma=False,
    )
```

time: 302 us -> 62.3 us (0.21)
  waiting for transfers between devices: 160 us -> 20.1 us
  blocking collectives: 83 us -> 0 us
  matrix products: 28.3 us -> 0 us
  starting transfers between devices: 0.12 us -> 22.5 us
  between operations: 15.1 us -> 0.72 us
  Pallas kernels: 0 us -> 8.47 us
  other arithmetic: 6.78 us -> 0.14 us
    psum x1 -> x0, waiting for transfers between devices: 86.8 us -> none  [shards(): gain_total, bias_total = lax.psum((gain_total, bias_total), 'loop')]
    reduce_scatter x1 -> x0, waiting for transfers between devices: 72.8 us -> none  [shards(): lax.psum_scatter(jnp.dot(slopes, tied_head, preferred_element_type=jnp.fl...]
    unnamed x2 -> x0, blocking collectives: 59.9 us -> none
    dot_general x6 -> x0, matrix products: 28.3 us -> none  [the longest x1 9.04 us: shards(): jnp.dot(slopes, tied_head, preferred_element_type=jnp.float32)]
    all_gather x1 -> x0, blocking collectives: 23.2 us -> none  [shards(): lax.all_gather(own_pick, 'loop', axis=0, tiled=True)]
    ppermute x0 -> x19, starting transfers between devices: none -> 22.5 us  [the longest x7 14.6 us: gather_blocks(): hop = lambda x: lax.ppermute(x, 'loop', pairs)]
    ppermute x0 -> x19, waiting for transfers between devices: none -> 20.1 us  [the longest x7 9.12 us: gather_blocks(): hop = lambda x: lax.ppermute(x, 'loop', pairs)]
    pallas_call x0 -> x2, Pallas kernels: none -> 8.47 us  [the longest x1 8.33 us: main(): pl.pallas_call(functools.partial(main_kernel, loop, levels, len(blocks)),...]
  transfers between devices with their start and end apart: 3 -> 19, of which waited for: 2 -> 10; matrix products, arithmetic and copies ran while one was open for 2% -> 0% of each run, Pallas kernels for 0% -> 0%
where the time goes in v2:
time: 62.3 us; the launch traced here: 62 us
  starting transfers between devices  22.5 us (36%)
  waiting for transfers between devices  20.1 us (32%)
  local copies, waits for them, and re-layouts  10.1 us (16%)
  Pallas kernels  8.47 us (14%)
  between operations  0.72 us (1%)
    ppermute x7, starting transfers between devices, gather_blocks(): hop = lambda x: lax.ppermute(x, 'loop', pairs)  14.6 us
    ppermute x7, waiting for transfers between devices, gather_blocks(): hop = lambda x: lax.ppermute(x, 'loop', pairs)  9.12 us
    unnamed x14, local copies, waits for them, and re-layouts  8.78 us
    pallas_call x1, Pallas kernels, main(): pl.pallas_call(functools.partial(main_kernel, loop, levels, len(blocks)),...  8.33 us
    ppermute x3, waiting for transfers between devices, shards(): total = total + lax.ppermute(total.astype(BF16), 'loop', pairs).astype(F32)  8.29 us
    ppermute x3, starting transfers between devices, shards(): total = total + lax.ppermute(total.astype(BF16), 'loop', pairs).astype(F32)  6.58 us
    ppermute x8, waiting for transfers between devices, gather_blocks(): swap = lambda x: lax.ppermute(x, 'loop', swap_pairs)  1.4 us
    ppermute x1, waiting for transfers between devices, shards(): lax.ppermute(total, 'loop', [(i, i ^ 1) for i in range(loop)])  1.31 us
  transfers between devices with their start and end apart: 19, of which 10 were waited for; matrix products, arithmetic and copies ran while one was open for 0% of the time, Pallas kernels for 0%

profile of v2, /device:TPU:0, one launch (start us, length us, event | category | flops | bytes accessed | tf_op | source)
XLA Modules:
  0.0 62.0 jit_solution(4433465411437879403)
XLA Ops:
  0.6 0.9 %copy-done = bf16[16,5376]{1,0:T(8,128)(2,1)S(1)} copy-done((bf16[16,5376]{1,0:T(8,128)(2,1)S(1)}, bf16[16,5376]{1,0:T(8,128)(2,1)}, u32[]{:S(2)}) %copy-start) | copy-done | bytes 172056
  1.6 0.7 %copy-done.1 = s32[16]{0:T(128)S(1)} copy-done((s32[16]{0:T(128)S(1)}, s32[16]{0:T(128)}, u32[]{:S(2)}) %copy-start.1) | copy-done | bytes 88
  2.2 0.7 %copy-done.2 = s32[16]{0:T(128)S(1)} copy-done((s32[16]{0:T(128)S(1)}, s32[16]{0:T(128)}, u32[]{:S(2)}) %copy-start.2) | copy-done | bytes 88
  2.9 0.7 %copy-done.3 = f32[16]{0:T(128)S(1)} copy-done((f32[16]{0:T(128)S(1)}, f32[16]{0:T(128)}, u32[]{:S(2)}) %copy-start.3) | copy-done | bytes 88
  3.5 0.1 shard_map.94.refs_0_
  3.7 3.1 %collective-permute-start = (bf16[16,5504]{1,0:T(8,128)(2,1)S(1)}, bf16[16,5504]{1,0:T(8,128)(2,1)S(1)}, u32[]{:S(2)}, u32[]{:S(2)}) collective-permute-start(bf16[16,5504]{1,0:T(8,128)(2,1)S(1)} %shard_map.94.refs_0_), channel_id=1, source_target_pairs={{0,4},{5,1},{4,8},{9,5},{8,12},{13,9},{12,14},{15,13},{14,10},{11,... | collective-permute-start | bytes 528392 | tf_op jit(solution)/shard_map/ppermute | solution.py:89
  6.7 0.0 collective-permute-start.4
  6.7 3.4 %collective-permute-done.refs_1_ = bf16[16,5504]{1,0:T(8,128)(2,1)S(1)} collective-permute-done((bf16[16,5504]{1,0:T(8,128)(2,1)S(1)}, bf16[16,5504]{1,0:T(8,128)(2,1)S(1)}, u32[]{:S(2)}, u32[]{:S(2)}) %collective-permute-start) | collective-permute-done | bytes 176160 | tf_op jit(solution)/shard_map/ppermute | solution.py:89
  10.1 2.1 %collective-permute-start.1 = (bf16[16,5504]{1,0:T(8,128)(2,1)S(1)}, bf16[16,5504]{1,0:T(8,128)(2,1)S(1)}, u32[]{:S(2)}, u32[]{:S(2)}) collective-permute-start(bf16[16,5504]{1,0:T(8,128)(2,1)S(1)} %collective-permute-done.refs_1_), channel_id=1, source_target_pairs={{0,4},{5,1},{4,8},{9,5},{8,12},{13,9},{12,14},{15,13},{14,10},{11,... | collective-permute-start | bytes 528392 | tf_op jit(solution)/shard_map/ppermute | solution.py:89
  12.2 0.0 collective-permute-done.4.refs_8_
  12.2 1.6 %collective-permute-start.5 = (bf16[16,5504]{1,0:T(8,128)(2,1)S(1)}, bf16[16,5504]{1,0:T(8,128)(2,1)S(1)}, u32[]{:S(2)}, u32[]{:S(2)}) collective-permute-start(bf16[16,5504]{1,0:T(8,128)(2,1)S(1)} %collective-permute-done.4.refs_8_), channel_id=1, source_target_pairs={{0,4},{5,1},{4,8},{9,5},{8,12},{13,9},{12,14},{15,13},{14,10},{11,... | collective-permute-start | bytes 528392 | tf_op jit(solution)/shard_map/ppermute | solution.py:89
  13.8 1.8 %collective-permute-done.1.refs_2_ = bf16[16,5504]{1,0:T(8,128)(2,1)S(1)} collective-permute-done((bf16[16,5504]{1,0:T(8,128)(2,1)S(1)}, bf16[16,5504]{1,0:T(8,128)(2,1)S(1)}, u32[]{:S(2)}, u32[]{:S(2)}) %collective-permute-start.1) | collective-permute-done | bytes 176160 | tf_op jit(solution)/shard_map/ppermute | solution.py:89
  15.6 2.1 %collective-permute-start.2 = (bf16[16,5504]{1,0:T(8,128)(2,1)S(1)}, bf16[16,5504]{1,0:T(8,128)(2,1)S(1)}, u32[]{:S(2)}, u32[]{:S(2)}) collective-permute-start(bf16[16,5504]{1,0:T(8,128)(2,1)S(1)} %collective-permute-done.1.refs_2_), channel_id=1, source_target_pairs={{0,4},{5,1},{4,8},{9,5},{8,12},{13,9},{12,14},{15,13},{14,10},{11,... | collective-permute-start | bytes 528392 | tf_op jit(solution)/shard_map/ppermute | solution.py:89
  17.6 0.0 collective-permute-done.5.refs_9_
  17.6 1.9 %collective-permute-start.6 = (bf16[16,5504]{1,0:T(8,128)(2,1)S(1)}, bf16[16,5504]{1,0:T(8,128)(2,1)S(1)}, u32[]{:S(2)}, u32[]{:S(2)}) collective-permute-start(bf16[16,5504]{1,0:T(8,128)(2,1)S(1)} %collective-permute-done.5.refs_9_), channel_id=1, source_target_pairs={{0,4},{5,1},{4,8},{9,5},{8,12},{13,9},{12,14},{15,13},{14,10},{11,... | collective-permute-start | bytes 528392 | tf_op jit(solution)/shard_map/ppermute | solution.py:89
  19.5 0.0 collective-permute-start.14
  19.5 0.5 collective-permute-start.13
  20.0 1.0 %collective-permute-done.2.refs_3_ = bf16[16,5504]{1,0:T(8,128)(2,1)S(1)} collective-permute-done((bf16[16,5504]{1,0:T(8,128)(2,1)S(1)}, bf16[16,5504]{1,0:T(8,128)(2,1)S(1)}, u32[]{:S(2)}, u32[]{:S(2)}) %collective-permute-start.2) | collective-permute-done | bytes 176160 | tf_op jit(solution)/shard_map/ppermute | solution.py:89
  21.0 2.1 %collective-permute-start.3 = (bf16[16,5504]{1,0:T(8,128)(2,1)S(1)}, bf16[16,5504]{1,0:T(8,128)(2,1)S(1)}, u32[]{:S(2)}, u32[]{:S(2)}) collective-permute-start(bf16[16,5504]{1,0:T(8,128)(2,1)S(1)} %collective-permute-done.2.refs_3_), channel_id=1, source_target_pairs={{0,4},{5,1},{4,8},{9,5},{8,12},{13,9},{12,14},{15,13},{14,10},{11,... | collective-permute-start | bytes 528392 | tf_op jit(solution)/shard_map/ppermute | solution.py:89
  23.1 0.0 collective-permute-done.6.refs_10_
  23.1 1.9 %collective-permute-start.7 = (bf16[16,5504]{1,0:T(8,128)(2,1)S(1)}, bf16[16,5504]{1,0:T(8,128)(2,1)S(1)}, u32[]{:S(2)}, u32[]{:S(2)}) collective-permute-start(bf16[16,5504]{1,0:T(8,128)(2,1)S(1)} %collective-permute-done.6.refs_10_), channel_id=1, source_target_pairs={{0,4},{5,1},{4,8},{9,5},{8,12},{13,9},{12,14},{15,13},{14,10},{11,... | collective-permute-start | bytes 528392 | tf_op jit(solution)/shard_map/ppermute | solution.py:89
  25.0 0.0 collective-permute-start.10
  25.0 0.0 collective-permute-done.14.refs_15_
  25.0 0.5 collective-permute-start.12
  25.5 0.0 collective-permute-done.13.refs_14_
  25.5 0.1 collective-permute-start.9
  25.6 0.9 %collective-permute-done.3.refs_4_ = bf16[16,5504]{1,0:T(8,128)(2,1)S(1)} collective-permute-done((bf16[16,5504]{1,0:T(8,128)(2,1)S(1)}, bf16[16,5504]{1,0:T(8,128)(2,1)S(1)}, u32[]{:S(2)}, u32[]{:S(2)}) %collective-permute-start.3) | collective-permute-done | bytes 176160 | tf_op jit(solution)/shard_map/ppermute | solution.py:89
  26.5 2.1 %collective-permute-done.7.refs_11_ = bf16[16,5504]{1,0:T(8,128)(2,1)S(1)} collective-permute-done((bf16[16,5504]{1,0:T(8,128)(2,1)S(1)}, bf16[16,5504]{1,0:T(8,128)(2,1)S(1)}, u32[]{:S(2)}, u32[]{:S(2)}) %collective-permute-start.7) | collective-permute-done | bytes 176160 | tf_op jit(solution)/shard_map/ppermute | solution.py:89
  28.6 0.0 collective-permute-start.8
  28.6 0.0 collective-permute-done.10.refs_7_
  28.6 0.0 collective-permute-done.12.refs_13_
  28.6 0.0 collective-permute-done.11.refs_12_
  28.6 1.4 %collective-permute-done.8.refs_5_ = bf16[16,5504]{1,0:T(8,128)(2,1)S(1)} collective-permute-done((bf16[16,5504]{1,0:T(8,128)(2,1)S(1)}, bf16[16,5504]{1,0:T(8,128)(2,1)S(1)}, u32[]{:S(2)}, u32[]{:S(2)}) %collective-permute-start.8) | collective-permute-done | bytes 176160 | tf_op jit(solution)/shard_map/ppermute | solution.py:88
  30.0 4.1 %copy-done.4 = bf16[1024,5376]{1,0:T(8,128)(2,1)S(1)} copy-done((bf16[1024,5376]{1,0:T(8,128)(2,1)S(1)}, bf16[1024,5376]{1,0:T(8,128)(2,1)}, u32[]{:S(2)}) %copy-start.4) | copy-done | bytes 11010072
  34.1 0.9 %copy-done.5 = f32[4,5376]{1,0:T(4,128)S(1)} copy-done((f32[4,5376]{1,0:T(4,128)S(1)}, f32[4,5376]{1,0:T(4,128)}, u32[]{:S(2)}) %copy-start.5) | copy-done | bytes 86040
  35.0 0.9 %copy-done.6 = f32[4,5376]{1,0:T(4,128)S(1)} copy-done((f32[4,5376]{1,0:T(4,128)S(1)}, f32[4,5376]{1,0:T(4,128)}, u32[]{:S(2)}) %copy-start.6) | copy-done | bytes 86040
  35.9 8.3 %shard_map.95 = f32[8,5632]{1,0:T(8,128)S(1)} custom-call(bf16[16,5504]{1,0:T(8,128)(2,1)S(1)} %shard_map.94.refs_0_, bf16[16,5504]{1,0:T(8,128)(2,1)S(1)} %collective-permute-done.refs_1_, bf16[16,5504]{1,0:T(8,128)(2,1)S(1)} %collective-permute-done.1.refs_2_, bf16[16,5504]{1,0:T(8,128)(2,1)S(1)} %collective-permute-done.2.refs_3_, ...), custom_call_target="tpu_custom_call" | custom-call | flops 5637144576 | bytes 11010048 | tf_op jit(solution)/shard_map/pallas_call | solution.py:180
  44.2 0.2 collective-permute-start.15
  44.4 1.3 %collective-permute-done.15 = f32[8,5632]{1,0:T(8,128)S(1)} collective-permute-done((f32[8,5632]{1,0:T(8,128)S(1)}, f32[8,5632]{1,0:T(8,128)S(1)}, u32[]{:S(2)}, u32[]{:S(2)}) %collective-permute-start.15) | collective-permute-done | bytes 180256 | tf_op jit(solution)/shard_map/ppermute | solution.py:207
  45.7 1.9 %collective-permute-start.16 = (bf16[8,5632]{1,0:T(8,128)(2,1)S(1)}, bf16[8,5632]{1,0:T(8,128)(2,1)S(1)}, u32[]{:S(2)}, u32[]{:S(2)}) collective-permute-start(bf16[8,5632]{1,0:T(8,128)(2,1)S(1)} %get-tuple-element.3), channel_id=1, source_target_pairs={{0,2},{1,3},{2,0},{3,1},{4,6},{5,7},{6,4},{7,5},{8,10},{9,11},{10,... | collective-permute-start | bytes 270344 | tf_op jit(solution)/shard_map/ppermute | solution.py:212
  47.6 2.9 %collective-permute-done.16 = bf16[8,5632]{1,0:T(8,128)(2,1)S(1)} collective-permute-done((bf16[8,5632]{1,0:T(8,128)(2,1)S(1)}, bf16[8,5632]{1,0:T(8,128)(2,1)S(1)}, u32[]{:S(2)}, u32[]{:S(2)}) %collective-permute-start.16) | collective-permute-done | bytes 90144 | tf_op jit(solution)/shard_map/ppermute | solution.py:212
  50.5 1.9 %collective-permute-start.17 = (bf16[8,5632]{1,0:T(8,128)(2,1)S(1)}, bf16[8,5632]{1,0:T(8,128)(2,1)S(1)}, u32[]{:S(2)}, u32[]{:S(2)}) collective-permute-start(bf16[8,5632]{1,0:T(8,128)(2,1)S(1)} %fusion), channel_id=1, source_target_pairs={{0,4},{1,5},{2,6},{3,7},{4,0},{5,1},{6,2},{7,3},{8,12},{9,13},{10,... | collective-permute-start | bytes 270344 | tf_op jit(solution)/shard_map/ppermute | solution.py:212
  52.4 2.7 %collective-permute-done.17 = bf16[8,5632]{1,0:T(8,128)(2,1)S(1)} collective-permute-done((bf16[8,5632]{1,0:T(8,128)(2,1)S(1)}, bf16[8,5632]{1,0:T(8,128)(2,1)S(1)}, u32[]{:S(2)}, u32[]{:S(2)}) %collective-permute-start.17) | collective-permute-done | bytes 90144 | tf_op jit(solution)/shard_map/ppermute | solution.py:212
  55.2 2.9 %collective-permute-start.18 = (bf16[8,5632]{1,0:T(8,128)(2,1)S(1)}, bf16[8,5632]{1,0:T(8,128)(2,1)S(1)}, u32[]{:S(2)}, u32[]{:S(2)}) collective-permute-start(bf16[8,5632]{1,0:T(8,128)(2,1)S(1)} %fusion.1), channel_id=1, source_target_pairs={{0,8},{1,9},{2,10},{3,11},{4,12},{5,13},{6,14},{7,15},{8,0},{9,1},... | collective-permute-start | bytes 270344 | tf_op jit(solution)/shard_map/ppermute | solution.py:212
  58.0 2.6 %collective-permute-done.18 = bf16[8,5632]{1,0:T(8,128)(2,1)S(1)} collective-permute-done((bf16[8,5632]{1,0:T(8,128)(2,1)S(1)}, bf16[8,5632]{1,0:T(8,128)(2,1)S(1)}, u32[]{:S(2)}, u32[]{:S(2)}) %collective-permute-start.18) | collective-permute-done | bytes 90144 | tf_op jit(solution)/shard_map/ppermute | solution.py:212
  60.7 0.1 convert_add_fusion
  60.7 0.7 %fusion.3 = (f32[4,5376]{1,0:T(4,128)}, f32[4,5376]{1,0:T(4,128)}) fusion(f32[8,5632]{1,0:T(8,128)S(1)} %convert_add_fusion), kind=kLoop, calls=%fused_computation.8 | loop fusion | bytes 344064 | tf_op jit(solution)/shard_map/slice | solution.py:215
  61.4 0.6 dynamic-slice_bitcast_fusion
  (13 shorter events, 0.1 us)
Async XLA Ops:
  0.6 0.9 %copy-start = (bf16[16,5376]{1,0:T(8,128)(2,1)S(1)}, bf16[16,5376]{1,0:T(8,128)(2,1)}, u32[]{:S(2)}) copy-start(bf16[16,5376]{1,0:T(8,128)(2,1)} %hidden.1) | copy-start | bytes 516100
  1.6 0.7 %copy-start.1 = (s32[16]{0:T(128)S(1)}, s32[16]{0:T(128)}, u32[]{:S(2)}) copy-start(s32[16]{0:T(128)} %param.8) | copy-start | bytes 196
  2.2 0.7 %copy-start.2 = (s32[16]{0:T(128)S(1)}, s32[16]{0:T(128)}, u32[]{:S(2)}) copy-start(s32[16]{0:T(128)} %param.9) | copy-start | bytes 196
  2.9 0.7 %copy-start.3 = (f32[16]{0:T(128)S(1)}, f32[16]{0:T(128)}, u32[]{:S(2)}) copy-start(f32[16]{0:T(128)} %param.10) | copy-start | bytes 196
  3.7 6.4 %collective-permute-start = (bf16[16,5504]{1,0:T(8,128)(2,1)S(1)}, bf16[16,5504]{1,0:T(8,128)(2,1)S(1)}, u32[]{:S(2)}, u32[]{:S(2)}) collective-permute-start(bf16[16,5504]{1,0:T(8,128)(2,1)S(1)} %shard_map.94.refs_0_), channel_id=1, source_target_pairs={{0,4},{5,1},{4,8},{9,5},{8,12},{13,9},{12,14},{15,13},{14,10},{11,... | collective-permute-start | bytes 528392 | tf_op jit(solution)/shard_map/ppermute | solution.py:89
  6.7 5.5 %collective-permute-start.4 = (bf16[16,5504]{1,0:T(8,128)(2,1)S(1)}, bf16[16,5504]{1,0:T(8,128)(2,1)S(1)}, u32[]{:S(2)}, u32[]{:S(2)}) collective-permute-start(bf16[16,5504]{1,0:T(8,128)(2,1)S(1)} %shard_map.94.refs_0_), channel_id=1, source_target_pairs={{0,1},{1,0},{2,3},{3,2},{4,5},{5,4},{6,7},{7,6},{8,9},{9,8},{10,11... | collective-permute-start | bytes 528392 | tf_op jit(solution)/shard_map/ppermute | solution.py:88
  10.1 5.5 %collective-permute-start.1 = (bf16[16,5504]{1,0:T(8,128)(2,1)S(1)}, bf16[16,5504]{1,0:T(8,128)(2,1)S(1)}, u32[]{:S(2)}, u32[]{:S(2)}) collective-permute-start(bf16[16,5504]{1,0:T(8,128)(2,1)S(1)} %collective-permute-done.refs_1_), channel_id=1, source_target_pairs={{0,4},{5,1},{4,8},{9,5},{8,12},{13,9},{12,14},{15,13},{14,10},{11,... | collective-permute-start | bytes 528392 | tf_op jit(solution)/shard_map/ppermute | solution.py:89
  12.2 5.5 %collective-permute-start.5 = (bf16[16,5504]{1,0:T(8,128)(2,1)S(1)}, bf16[16,5504]{1,0:T(8,128)(2,1)S(1)}, u32[]{:S(2)}, u32[]{:S(2)}) collective-permute-start(bf16[16,5504]{1,0:T(8,128)(2,1)S(1)} %collective-permute-done.4.refs_8_), channel_id=1, source_target_pairs={{0,4},{5,1},{4,8},{9,5},{8,12},{13,9},{12,14},{15,13},{14,10},{11,... | collective-permute-start | bytes 528392 | tf_op jit(solution)/shard_map/ppermute | solution.py:89
  15.6 5.5 %collective-permute-start.2 = (bf16[16,5504]{1,0:T(8,128)(2,1)S(1)}, bf16[16,5504]{1,0:T(8,128)(2,1)S(1)}, u32[]{:S(2)}, u32[]{:S(2)}) collective-permute-start(bf16[16,5504]{1,0:T(8,128)(2,1)S(1)} %collective-permute-done.1.refs_2_), channel_id=1, source_target_pairs={{0,4},{5,1},{4,8},{9,5},{8,12},{13,9},{12,14},{15,13},{14,10},{11,... | collective-permute-start | bytes 528392 | tf_op jit(solution)/shard_map/ppermute | solution.py:89
  17.6 5.5 %collective-permute-start.6 = (bf16[16,5504]{1,0:T(8,128)(2,1)S(1)}, bf16[16,5504]{1,0:T(8,128)(2,1)S(1)}, u32[]{:S(2)}, u32[]{:S(2)}) collective-permute-start(bf16[16,5504]{1,0:T(8,128)(2,1)S(1)} %collective-permute-done.5.refs_9_), channel_id=1, source_target_pairs={{0,4},{5,1},{4,8},{9,5},{8,12},{13,9},{12,14},{15,13},{14,10},{11,... | collective-permute-start | bytes 528392 | tf_op jit(solution)/shard_map/ppermute | solution.py:89
  19.5 5.5 %collective-permute-start.14 = (bf16[16,5504]{1,0:T(8,128)(2,1)S(1)}, bf16[16,5504]{1,0:T(8,128)(2,1)S(1)}, u32[]{:S(2)}, u32[]{:S(2)}) collective-permute-start(bf16[16,5504]{1,0:T(8,128)(2,1)S(1)} %collective-permute-done.refs_1_), channel_id=1, source_target_pairs={{0,1},{1,0},{2,3},{3,2},{4,5},{5,4},{6,7},{7,6},{8,9},{9,8},{10,11... | collective-permute-start | bytes 528392 | tf_op jit(solution)/shard_map/ppermute | solution.py:88
  19.5 6.0 %collective-permute-start.13 = (bf16[16,5504]{1,0:T(8,128)(2,1)S(1)}, bf16[16,5504]{1,0:T(8,128)(2,1)S(1)}, u32[]{:S(2)}, u32[]{:S(2)}) collective-permute-start(bf16[16,5504]{1,0:T(8,128)(2,1)S(1)} %collective-permute-done.1.refs_2_), channel_id=1, source_target_pairs={{0,1},{1,0},{2,3},{3,2},{4,5},{5,4},{6,7},{7,6},{8,9},{9,8},{10,11... | collective-permute-start | bytes 528392 | tf_op jit(solution)/shard_map/ppermute | solution.py:88
  21.0 5.5 %collective-permute-start.3 = (bf16[16,5504]{1,0:T(8,128)(2,1)S(1)}, bf16[16,5504]{1,0:T(8,128)(2,1)S(1)}, u32[]{:S(2)}, u32[]{:S(2)}) collective-permute-start(bf16[16,5504]{1,0:T(8,128)(2,1)S(1)} %collective-permute-done.2.refs_3_), channel_id=1, source_target_pairs={{0,4},{5,1},{4,8},{9,5},{8,12},{13,9},{12,14},{15,13},{14,10},{11,... | collective-permute-start | bytes 528392 | tf_op jit(solution)/shard_map/ppermute | solution.py:89
  23.1 5.5 %collective-permute-start.7 = (bf16[16,5504]{1,0:T(8,128)(2,1)S(1)}, bf16[16,5504]{1,0:T(8,128)(2,1)S(1)}, u32[]{:S(2)}, u32[]{:S(2)}) collective-permute-start(bf16[16,5504]{1,0:T(8,128)(2,1)S(1)} %collective-permute-done.6.refs_10_), channel_id=1, source_target_pairs={{0,4},{5,1},{4,8},{9,5},{8,12},{13,9},{12,14},{15,13},{14,10},{11,... | collective-permute-start | bytes 528392 | tf_op jit(solution)/shard_map/ppermute | solution.py:89
  25.0 3.6 %collective-permute-start.10 = (bf16[16,5504]{1,0:T(8,128)(2,1)S(1)}, bf16[16,5504]{1,0:T(8,128)(2,1)S(1)}, u32[]{:S(2)}, u32[]{:S(2)}) collective-permute-start(bf16[16,5504]{1,0:T(8,128)(2,1)S(1)} %collective-permute-done.5.refs_9_), channel_id=1, source_target_pairs={{0,1},{1,0},{2,3},{3,2},{4,5},{5,4},{6,7},{7,6},{8,9},{9,8},{10,11... | collective-permute-start | bytes 528392 | tf_op jit(solution)/shard_map/ppermute | solution.py:88
  25.0 3.6 %collective-permute-start.12 = (bf16[16,5504]{1,0:T(8,128)(2,1)S(1)}, bf16[16,5504]{1,0:T(8,128)(2,1)S(1)}, u32[]{:S(2)}, u32[]{:S(2)}) collective-permute-start(bf16[16,5504]{1,0:T(8,128)(2,1)S(1)} %collective-permute-done.2.refs_3_), channel_id=1, source_target_pairs={{0,1},{1,0},{2,3},{3,2},{4,5},{5,4},{6,7},{7,6},{8,9},{9,8},{10,11... | collective-permute-start | bytes 528392 | tf_op jit(solution)/shard_map/ppermute | solution.py:88
  25.5 3.1 %collective-permute-start.9 = (bf16[16,5504]{1,0:T(8,128)(2,1)S(1)}, bf16[16,5504]{1,0:T(8,128)(2,1)S(1)}, u32[]{:S(2)}, u32[]{:S(2)}) collective-permute-start(bf16[16,5504]{1,0:T(8,128)(2,1)S(1)} %collective-permute-done.6.refs_10_), channel_id=1, source_target_pairs={{0,1},{1,0},{2,3},{3,2},{4,5},{5,4},{6,7},{7,6},{8,9},{9,8},{10,11... | collective-permute-start | bytes 528392 | tf_op jit(solution)/shard_map/ppermute | solution.py:88
  26.5 2.1 %collective-permute-start.11 = (bf16[16,5504]{1,0:T(8,128)(2,1)S(1)}, bf16[16,5504]{1,0:T(8,128)(2,1)S(1)}, u32[]{:S(2)}, u32[]{:S(2)}) collective-permute-start(bf16[16,5504]{1,0:T(8,128)(2,1)S(1)} %collective-permute-done.3.refs_4_), channel_id=1, source_target_pairs={{0,1},{1,0},{2,3},{3,2},{4,5},{5,4},{6,7},{7,6},{8,9},{9,8},{10,11... | collective-permute-start | bytes 528392 | tf_op jit(solution)/shard_map/ppermute | solution.py:88
  28.6 1.4 %collective-permute-start.8 = (bf16[16,5504]{1,0:T(8,128)(2,1)S(1)}, bf16[16,5504]{1,0:T(8,128)(2,1)S(1)}, u32[]{:S(2)}, u32[]{:S(2)}) collective-permute-start(bf16[16,5504]{1,0:T(8,128)(2,1)S(1)} %collective-permute-done.7.refs_11_), channel_id=1, source_target_pairs={{0,1},{1,0},{2,3},{3,2},{4,5},{5,4},{6,7},{7,6},{8,9},{9,8},{10,11... | collective-permute-start | bytes 528392 | tf_op jit(solution)/shard_map/ppermute | solution.py:88
  30.0 4.1 %copy-start.4 = (bf16[1024,5376]{1,0:T(8,128)(2,1)S(1)}, bf16[1024,5376]{1,0:T(8,128)(2,1)}, u32[]{:S(2)}) copy-start(bf16[1024,5376]{1,0:T(8,128)(2,1)} %refs_16_.1) | copy-start | bytes 33030148
  34.1 0.9 %copy-start.5 = (f32[4,5376]{1,0:T(4,128)S(1)}, f32[4,5376]{1,0:T(4,128)}, u32[]{:S(2)}) copy-start(f32[4,5376]{1,0:T(4,128)} %refs_17_.1) | copy-start | bytes 258052
  35.0 0.9 %copy-start.6 = (f32[4,5376]{1,0:T(4,128)S(1)}, f32[4,5376]{1,0:T(4,128)}, u32[]{:S(2)}) copy-start(f32[4,5376]{1,0:T(4,128)} %refs_18_.1) | copy-start | bytes 258052
  44.2 1.5 %collective-permute-start.15 = (f32[8,5632]{1,0:T(8,128)S(1)}, f32[8,5632]{1,0:T(8,128)S(1)}, u32[]{:S(2)}, u32[]{:S(2)}) collective-permute-start(f32[8,5632]{1,0:T(8,128)S(1)} %shard_map.95), channel_id=1, source_target_pairs={{0,1},{1,0},{2,3},{3,2},{4,5},{5,4},{6,7},{7,6},{8,9},{9,8},{10,11... | collective-permute-start | bytes 540680 | tf_op jit(solution)/shard_map/ppermute | solution.py:207
  45.7 4.8 %collective-permute-start.16 = (bf16[8,5632]{1,0:T(8,128)(2,1)S(1)}, bf16[8,5632]{1,0:T(8,128)(2,1)S(1)}, u32[]{:S(2)}, u32[]{:S(2)}) collective-permute-start(bf16[8,5632]{1,0:T(8,128)(2,1)S(1)} %get-tuple-element.3), channel_id=1, source_target_pairs={{0,2},{1,3},{2,0},{3,1},{4,6},{5,7},{6,4},{7,5},{8,10},{9,11},{10,... | collective-permute-start | bytes 270344 | tf_op jit(solution)/shard_map/ppermute | solution.py:212
  50.5 4.6 %collective-permute-start.17 = (bf16[8,5632]{1,0:T(8,128)(2,1)S(1)}, bf16[8,5632]{1,0:T(8,128)(2,1)S(1)}, u32[]{:S(2)}, u32[]{:S(2)}) collective-permute-start(bf16[8,5632]{1,0:T(8,128)(2,1)S(1)} %fusion), channel_id=1, source_target_pairs={{0,4},{1,5},{2,6},{3,7},{4,0},{5,1},{6,2},{7,3},{8,12},{9,13},{10,... | collective-permute-start | bytes 270344 | tf_op jit(solution)/shard_map/ppermute | solution.py:212
  55.2 5.5 %collective-permute-start.18 = (bf16[8,5632]{1,0:T(8,128)(2,1)S(1)}, bf16[8,5632]{1,0:T(8,128)(2,1)S(1)}, u32[]{:S(2)}, u32[]{:S(2)}) collective-permute-start(bf16[8,5632]{1,0:T(8,128)(2,1)S(1)} %fusion.1), channel_id=1, source_target_pairs={{0,8},{1,9},{2,10},{3,11},{4,12},{5,13},{6,14},{7,15},{8,0},{9,1},... | collective-permute-start | bytes 270344 | tf_op jit(solution)/shard_map/ppermute | solution.py:212

commit v3 on v2

--- a/solution.py
+++ b/solution.py
@@ -12,6 +12,11 @@
 LANES = 128
 NT = (((1,), (1,)), ((), ()))
 VMEM = pl.BlockSpec(memory_space=pltpu.VMEM)
+HBM = pl.BlockSpec(memory_space=pl.ANY)
+
+
+def in_hbm(x):
+    return pltpu.with_memory_space_constraint(x, pltpu.HBM)
 
 
 def ring_of(chips):
@@ -33,9 +38,24 @@
     return [top, middle, rest - middle]
 
 
-def prep_kernel(hidden, exit_depth, teacher, normalizer, out):
+def prep_kernel(
+    hidden, exit_depth, teacher, normalizer, depth_gain, depth_bias,
+    out, gain_out, bias_out, row_buf, int_buf, float_buf, sems,
+):
     rows, width = hidden.shape
-    block = hidden[...]
+    copies = [
+        pltpu.make_async_copy(hidden, row_buf, sems.at[0]),
+        pltpu.make_async_copy(exit_depth, int_buf.at[0], sems.at[1]),
+        pltpu.make_async_copy(teacher, int_buf.at[1], sems.at[2]),
+        pltpu.make_async_copy(normalizer, float_buf, sems.at[3]),
+        pltpu.make_async_copy(depth_gain, gain_out, sems.at[4]),
+        pltpu.make_async_copy(depth_bias, bias_out, sems.at[5]),
+    ]
+    for copy in copies:
+        copy.start()
+    for copy in copies[:4]:
+        copy.wait()
+    block = row_buf[...]
     out[:, :width] = block
     wide = block.astype(F32)
     mean = jnp.sum(wide * wide, axis=1, keepdims=True) * (1.0 / width)
@@ -47,53 +67,70 @@
         square = jnp.broadcast_to(line, (rows, rows))
         return jnp.sum(jnp.where(down == across, square, 0.0), axis=1, keepdims=True)
 
-    token = teacher[...]
-    columns = pieces(scale) + pieces(column(normalizer[...]))
+    token = int_buf[1]
+    columns = pieces(scale) + pieces(column(float_buf[...]))
     for digit in (token & 127, (token >> 7) & 127, token >> 14):
         columns.append(column(digit.astype(F32)))
-    columns.append(column(exit_depth[...].astype(F32)))
+    columns.append(column(int_buf[0].astype(F32)))
     lane = lax.broadcasted_iota(jnp.int32, (rows, LANES), 1)
     meta = jnp.zeros((rows, LANES), F32)
     for i, value in enumerate(columns):
         meta = jnp.where(lane == i, value, meta)
     out[:, width:] = meta.astype(BF16)
-
-
-def prep(hidden, exit_depth, teacher, normalizer):
+    for copy in copies[4:]:
+        copy.wait()
+
+
+def prep(hidden, exit_depth, teacher, normalizer, depth_gain, depth_bias):
     rows, width = hidden.shape
-    line = pl.BlockSpec((1, rows), lambda i: (0, 0))
     return pl.pallas_call(
         prep_kernel,
-        grid=(1,),
-        out_shape=jax.ShapeDtypeStruct((rows, width + LANES), BF16),
-        in_specs=[pl.BlockSpec((rows, width), lambda i: (0, 0)), line, line, line],
-        out_specs=VMEM,
+        out_shape=(
+            pltpu.VMEM((rows, width + LANES), BF16),
+            pltpu.VMEM(depth_gain.shape, F32),
+            pltpu.VMEM(depth_bias.shape, F32),
+        ),
+        in_specs=[HBM] * 6,
+        out_specs=(VMEM, VMEM, VMEM),
+        scratch_shapes=[
+            pltpu.VMEM((rows, width), BF16),
+            pltpu.VMEM((2, 1, rows), jnp.int32),
+            pltpu.VMEM((1, rows), F32),
+            pltpu.SemaphoreType.DMA((6,)),
+        ],
         compiler_params=pltpu.CompilerParams(vmem_limit_bytes=8 << 20),
     )(
-        hidden,
-        exit_depth.reshape(1, rows),
-        teacher.reshape(1, rows),
-        normalizer.reshape(1, rows),
+        in_hbm(hidden),
+        in_hbm(exit_depth.reshape(1, rows)),
+        in_hbm(teacher.reshape(1, rows)),
+        in_hbm(normalizer.reshape(1, rows)),
+        in_hbm(depth_gain),
+        in_hbm(depth_bias),
     )
 
 
 def gather_blocks(block, loop):
     chips = loop // 2
     order = ring_of(chips)
-    pairs = []
+    pairs, cross_pairs = [], []
     for i in range(chips):
         here, after = order[i], order[(i + 1) % chips]
         pairs += [(2 * here, 2 * after), (2 * after + 1, 2 * here + 1)]
+        cross_pairs += [(2 * here + 1, 2 * after), (2 * after, 2 * here + 1)]
     swap_pairs = [(i, i ^ 1) for i in range(loop)]
     swap = lambda x: lax.ppermute(x, "loop", swap_pairs)
     hop = lambda x: lax.ppermute(x, "loop", pairs)
     same, other = [None] * chips, [None] * chips
-    same[0], other[0] = block, swap(block)
+    same[0] = block
     half = chips // 2
     for step in range(1, half + 1):
         same[step] = hop(same[step - 1])
+        if step == 1:
+            other[step] = lax.ppermute(block, "loop", cross_pairs)
+            other[0] = swap(block)
+        elif step < half:
+            other[step] = hop(other[step - 1])
         if step < half:
-            other[step] = hop(other[step - 1])
             other[chips - step] = swap(same[step])
             same[chips - step] = swap(other[step])
         else:
@@ -103,8 +140,16 @@
 
 def main_kernel(loop, levels, count, *refs):
     blocks = refs[:count]
-    head, gain, bias, out, mapped, slopes = refs[count:]
+    head_hbm, gain, bias, out, head, mapped, slopes, sems = refs[count:]
     voc, width = head.shape
+    cuts = 7 if width % (7 * LANES) == 0 else 1
+    cut = width // cuts
+    copies = []
+    for k in range(cuts):
+        at = pl.ds(k * cut, cut)
+        copies.append(pltpu.make_async_copy(head_hbm.at[:, at], head.at[:, at], sems.at[k]))
+    for copy in copies:
+        copy.start()
     rows = mapped.shape[0]
     rows_dev = rows // loop
     chips = loop // 2
@@ -116,9 +161,8 @@
     target = (col(6) + 128.0 * col(7) + 16384.0 * col(8)).astype(jnp.int32)
     depth = col(9)
 
-    cut = width // 3
     logits = None
-    for k in range(3):
+    for k in range(cuts):
         at = slice(k * cut, (k + 1) * cut)
         row = 0
         for b in blocks:
@@ -130,6 +174,7 @@
                 c = jnp.where(here, bias[level : level + 1, at], c)
             mapped[part, at] = ((b[:, at].astype(F32) * scale[part]) * g + c).astype(BF16)
             row += b.shape[0]
+        copies[k].wait()
         term = lax.dot_general(mapped[:, at], head[:, at], NT, preferred_element_type=F32)
         logits = term if logits is None else logits + term
     prob = jnp.exp(logits - norm)
@@ -179,40 +224,90 @@
     rows = sum(b.shape[0] for b in blocks)
     return pl.pallas_call(
         functools.partial(main_kernel, loop, levels, len(blocks)),
-        out_shape=jax.ShapeDtypeStruct((2 * levels, width + rows), F32),
-        in_specs=[VMEM] * (len(blocks) + 3),
+        out_shape=pltpu.VMEM((2 * levels, width + rows), F32),
+        in_specs=[VMEM] * len(blocks) + [HBM, VMEM, VMEM],
         out_specs=VMEM,
         scratch_shapes=[
+            pltpu.VMEM((voc, width), BF16),
             pltpu.VMEM((rows, width), BF16),
             pltpu.VMEM((rows + 16, voc), BF16),
+            pltpu.SemaphoreType.DMA((7,)),
         ],
-        compiler_params=pltpu.CompilerParams(vmem_limit_bytes=24 << 20),
+        compiler_params=pltpu.CompilerParams(vmem_limit_bytes=32 << 20),
         cost_estimate=pl.CostEstimate(
             flops=4 * rows * voc * width,
             bytes_accessed=2 * voc * width,
             transcendentals=rows * voc,
         ),
-    )(*blocks, tied_head, depth_gain, depth_bias)
+    )(*blocks, in_hbm(tied_head), depth_gain, depth_bias)
+
+
+def sum_over_loop(part, loop):
+    send = lambda x, pairs: lax.ppermute(x, "loop", pairs)
+    odd = range(1, loop, 2)
+    total = part + send(part, [(i - 1, i) for i in odd])
+    bits = [1 << k for k in range(1, loop.bit_length() - 1)]
+    rounds = [bits[:1]] + [bits[k : k + 2] for k in range(1, len(bits), 2)]
+    for dims in rounds:
+        mine = lax.reduce_precision(total, 8, 7)
+        sent = mine.astype(BF16)
+        take = lambda mask: send(sent, [(i, i ^ mask) for i in odd]).astype(F32)
+        total = mine + take(dims[0])
+        if len(dims) == 2:
+            total = total + (take(dims[1]) + take(dims[0] ^ dims[1]))
+    return total, send(total, [(i, i - 1) for i in odd])
+
+
+def last_kernel(levels, rows, total, arrived, mass_out, gain_out, bias_out, buf, line, sems):
+    width = gain_out.shape[1]
+    me = lax.axis_index("loop")
+    buf[...] = jnp.where(me % 2 == 0, arrived[...], total[...])
+    every = buf[0:1, width:]
+    spread = lax.broadcasted_iota(jnp.int32, (every.shape[1], LANES), 0)
+    target = lax.broadcasted_iota(jnp.int32, (every.shape[1], LANES), 1)
+    move = jnp.where(spread - me * rows == target, 1.0, 0.0).astype(BF16)
+    lines = jnp.concatenate(pieces(every) + [jnp.zeros((13, every.shape[1]), F32)], axis=0)
+    own = jnp.dot(lines.astype(BF16), move, preferred_element_type=F32)
+    line[...] = ((own[0:1] + own[1:2]) + own[2:3])[:, :rows]
+    copies = [
+        pltpu.make_async_copy(buf.at[pl.ds(0, levels), pl.ds(0, width)], gain_out, sems.at[0]),
+        pltpu.make_async_copy(buf.at[pl.ds(levels, levels), pl.ds(0, width)], bias_out, sems.at[1]),
+        pltpu.make_async_copy(line, mass_out, sems.at[2]),
+    ]
+    for copy in copies:
+        copy.start()
+    for copy in copies:
+        copy.wait()
+
+
+def last(total, arrived, levels, width, rows):
+    grad = pltpu.HBM((levels, width), F32)
+    mass, gain, bias = pl.pallas_call(
+        functools.partial(last_kernel, levels, rows),
+        out_shape=(pltpu.HBM((1, rows), F32), grad, grad),
+        in_specs=[VMEM, VMEM],
+        out_specs=(HBM, HBM, HBM),
+        scratch_shapes=[
+            pltpu.VMEM(total.shape, F32),
+            pltpu.VMEM((1, rows), F32),
+            pltpu.SemaphoreType.DMA((3,)),
+        ],
+        compiler_params=pltpu.CompilerParams(vmem_limit_bytes=8 << 20),
+    )(total, arrived)
+    return mass.reshape(rows), gain, bias
 
 
 def shards(loop, hidden, exit_depth, teacher, normalizer, tied_head, depth_gain, depth_bias):
     rows_dev, width = hidden.shape
     levels = depth_gain.shape[0]
-    me = lax.axis_index("loop")
-    blocks = gather_blocks(prep(hidden, exit_depth, teacher, normalizer), loop)
+    block, gain, bias = prep(hidden, exit_depth, teacher, normalizer, depth_gain, depth_bias)
+    blocks = gather_blocks(block, loop)
     if rows_dev % 16:
         whole = jnp.concatenate(blocks, axis=0)
         blocks = [whole[i : i + 16] for i in range(0, whole.shape[0], 16)]
-    total = main(blocks, tied_head, depth_gain, depth_bias, loop)
-    total = total + lax.ppermute(total, "loop", [(i, i ^ 1) for i in range(loop)])
-    bit = 2
-    while bit < loop:
-        pairs = [(i, i ^ bit) for i in range(loop)]
-        total = lax.reduce_precision(total, 8, 7)
-        total = total + lax.ppermute(total.astype(BF16), "loop", pairs).astype(F32)
-        bit *= 2
-    row_mass = lax.dynamic_slice(total[0], (width + me * rows_dev,), (rows_dev,))
-    return row_mass, total[:levels, :width], total[levels:, :width]
+    part = main(blocks, tied_head, gain, bias, loop)
+    total, arrived = sum_over_loop(part, loop)
+    return last(total, arrived, levels, width, rows_dev)
 
 
 def solution(mesh):

time: 62.3 us -> 64.7 us (1.039)
  waiting for transfers between devices: 20.1 us -> 30.9 us
  local copies, waits for them, and re-layouts: 10.1 us -> 0 us
  Pallas kernels: 8.47 us -> 14 us
  starting transfers between devices: 22.5 us -> 18.6 us
    unnamed x14 -> x0, local copies, waits for them, and re-layouts: 8.78 us -> none
    ppermute x4 -> x7, waiting for transfers between devices: 9.6 us -> 17.4 us  [the longest x6 17.4 us: sum_over_loop(): send = lambda x, pairs: lax.ppermute(x, 'loop', pairs)]
    ppermute x7 -> x6, starting transfers between devices: 14.6 us -> 10.6 us  [gather_blocks(): hop = lambda x: lax.ppermute(x, 'loop', pairs)]
    pallas_call x1, Pallas kernels: 8.33 us -> 12.2 us  [main(): pl.pallas_call(functools.partial(main_kernel, loop, levels, len(blocks)),...]
    ppermute x7 -> x6, waiting for transfers between devices: 9.12 us -> 12.1 us  [gather_blocks(): hop = lambda x: lax.ppermute(x, 'loop', pairs)]
    pallas_call x1 -> x2, Pallas kernels: 0.14 us -> 1.87 us  [the longest x1 1.13 us: prep(): pl.pallas_call(prep_kernel, out_shape=(pltpu.VMEM((rows, width + LANES),...]
    slice x2 -> x0, local copies, waits for them, and re-layouts: 0.71 us -> none  [the longest x1 0.69 us: shards(): return (row_mass, total[:levels, :width], total[levels:, :width])]
    ppermute x4 -> x7, starting transfers between devices: 6.75 us -> 6.69 us  [the longest x6 6.02 us: sum_over_loop(): send = lambda x, pairs: lax.ppermute(x, 'loop', pairs)]
  transfers between devices with their start and end apart: 19 -> 21, of which waited for: 10 -> 9; matrix products, arithmetic and copies ran while one was open for 0% -> 0% of each run, Pallas kernels for 0% -> 0%
where the time goes in v3:
time: 64.7 us; the launch traced here: 64.4 us
  waiting for transfers between devices  30.9 us (48%)
  starting transfers between devices  18.6 us (29%)
  Pallas kernels  14 us (22%)
  between operations  0.77 us (1%)
    ppermute x6, waiting for transfers between devices, sum_over_loop(): send = lambda x, pairs: lax.ppermute(x, 'loop', pairs)  17.4 us
    pallas_call x1, Pallas kernels, main(): pl.pallas_call(functools.partial(main_kernel, loop, levels, len(blocks)),...  12.2 us
    ppermute x6, waiting for transfers between devices, gather_blocks(): hop = lambda x: lax.ppermute(x, 'loop', pairs)  12.1 us
    ppermute x6, starting transfers between devices, gather_blocks(): hop = lambda x: lax.ppermute(x, 'loop', pairs)  10.6 us
    ppermute x6, starting transfers between devices, sum_over_loop(): send = lambda x, pairs: lax.ppermute(x, 'loop', pairs)  6.02 us
    ppermute x8, waiting for transfers between devices, gather_blocks(): swap = lambda x: lax.ppermute(x, 'loop', swap_pairs)  1.4 us
    ppermute x8, starting transfers between devices, gather_blocks(): swap = lambda x: lax.ppermute(x, 'loop', swap_pairs)  1.32 us
  transfers between devices with their start and end apart: 21, of which 9 were waited for; matrix products, arithmetic and copies ran while one was open for 0% of the time, Pallas kernels for 0%

profile of v3, /device:TPU:0, one launch (start us, length us, event | category | flops | bytes accessed | tf_op | source)
XLA Modules:
  0.0 64.4 jit_solution(7993574893487214280)
XLA Ops:
  0.6 1.1 %shard_map.94 = (bf16[16,5504]{1,0:T(8,128)(2,1)S(1)}, f32[4,5376]{1,0:T(4,128)S(1)}, f32[4,5376]{1,0:T(4,128)S(1)}) custom-call(bf16[16,5376]{1,0:T(8,128)(2,1)} %hidden.1, s32[1,16]{1,0:T(1,128)} %bitcast.4, s32[1,16]{1,0:T(1,128)} %bitcast.5, f32[1,16]{1,0:T(1,128)} %bitcast.6, f32[4,5376]{1,0:T(4,128)} %depth_gain.1, f32[4,5376]{1,0:T(4,128)} %depth_bias.1), custom_call_target="tpu_custom_call" | custom-call | tf_op jit(solution)/shard_map/pallas_call | solution.py:86
  1.8 3.1 %collective-permute-start = (bf16[16,5504]{1,0:T(8,128)(2,1)S(1)}, bf16[16,5504]{1,0:T(8,128)(2,1)S(1)}, u32[]{:S(2)}, u32[]{:S(2)}) collective-permute-start(bf16[16,5504]{1,0:T(8,128)(2,1)S(1)} %get-tuple-element.9.refs_0_), channel_id=1, source_target_pairs={{0,4},{5,1},{4,8},{9,5},{8,12},{13,9},{12,14},{15,13},{14,10},{11,... | collective-permute-start | bytes 528392 | tf_op jit(solution)/shard_map/ppermute | solution.py:122
  4.8 0.7 %collective-permute-start.4 = (bf16[16,5504]{1,0:T(8,128)(2,1)S(1)}, bf16[16,5504]{1,0:T(8,128)(2,1)S(1)}, u32[]{:S(2)}, u32[]{:S(2)}) collective-permute-start(bf16[16,5504]{1,0:T(8,128)(2,1)S(1)} %get-tuple-element.9.refs_0_), channel_id=1, source_target_pairs={{1,4},{4,1},{5,8},{8,5},{9,12},{12,9},{13,14},{14,13},{15,10},{10,... | collective-permute-start | bytes 528392 | tf_op jit(solution)/shard_map/ppermute | solution.py:129
  5.5 3.2 %collective-permute-done.refs_1_ = bf16[16,5504]{1,0:T(8,128)(2,1)S(1)} collective-permute-done((bf16[16,5504]{1,0:T(8,128)(2,1)S(1)}, bf16[16,5504]{1,0:T(8,128)(2,1)S(1)}, u32[]{:S(2)}, u32[]{:S(2)}) %collective-permute-start) | collective-permute-done | bytes 176160 | tf_op jit(solution)/shard_map/ppermute | solution.py:122
  8.7 2.5 %collective-permute-start.1 = (bf16[16,5504]{1,0:T(8,128)(2,1)S(1)}, bf16[16,5504]{1,0:T(8,128)(2,1)S(1)}, u32[]{:S(2)}, u32[]{:S(2)}) collective-permute-start(bf16[16,5504]{1,0:T(8,128)(2,1)S(1)} %collective-permute-done.refs_1_), channel_id=1, source_target_pairs={{0,4},{5,1},{4,8},{9,5},{8,12},{13,9},{12,14},{15,13},{14,10},{11,... | collective-permute-start | bytes 528392 | tf_op jit(solution)/shard_map/ppermute | solution.py:122
  11.2 0.0 collective-permute-done.4.refs_9_
  11.2 1.6 %collective-permute-start.5 = (bf16[16,5504]{1,0:T(8,128)(2,1)S(1)}, bf16[16,5504]{1,0:T(8,128)(2,1)S(1)}, u32[]{:S(2)}, u32[]{:S(2)}) collective-permute-start(bf16[16,5504]{1,0:T(8,128)(2,1)S(1)} %collective-permute-done.4.refs_9_), channel_id=1, source_target_pairs={{0,4},{5,1},{4,8},{9,5},{8,12},{13,9},{12,14},{15,13},{14,10},{11,... | collective-permute-start | bytes 528392 | tf_op jit(solution)/shard_map/ppermute | solution.py:122
  12.8 2.8 %collective-permute-done.1.refs_2_ = bf16[16,5504]{1,0:T(8,128)(2,1)S(1)} collective-permute-done((bf16[16,5504]{1,0:T(8,128)(2,1)S(1)}, bf16[16,5504]{1,0:T(8,128)(2,1)S(1)}, u32[]{:S(2)}, u32[]{:S(2)}) %collective-permute-start.1) | collective-permute-done | bytes 176160 | tf_op jit(solution)/shard_map/ppermute | solution.py:122
  15.6 1.1 %collective-permute-start.2 = (bf16[16,5504]{1,0:T(8,128)(2,1)S(1)}, bf16[16,5504]{1,0:T(8,128)(2,1)S(1)}, u32[]{:S(2)}, u32[]{:S(2)}) collective-permute-start(bf16[16,5504]{1,0:T(8,128)(2,1)S(1)} %collective-permute-done.1.refs_2_), channel_id=1, source_target_pairs={{0,4},{5,1},{4,8},{9,5},{8,12},{13,9},{12,14},{15,13},{14,10},{11,... | collective-permute-start | bytes 528392 | tf_op jit(solution)/shard_map/ppermute | solution.py:122
  16.6 0.0 collective-permute-start.10
  16.6 0.5 collective-permute-start.9
  17.1 0.0 collective-permute-start.14
  17.1 0.3 collective-permute-done.5.refs_10_
  17.4 1.3 %collective-permute-start.6 = (bf16[16,5504]{1,0:T(8,128)(2,1)S(1)}, bf16[16,5504]{1,0:T(8,128)(2,1)S(1)}, u32[]{:S(2)}, u32[]{:S(2)}) collective-permute-start(bf16[16,5504]{1,0:T(8,128)(2,1)S(1)} %collective-permute-done.5.refs_10_), channel_id=1, source_target_pairs={{0,4},{5,1},{4,8},{9,5},{8,12},{13,9},{12,14},{15,13},{14,10},{11,... | collective-permute-start | bytes 528392 | tf_op jit(solution)/shard_map/ppermute | solution.py:122
  18.7 2.3 %collective-permute-done.2.refs_3_ = bf16[16,5504]{1,0:T(8,128)(2,1)S(1)} collective-permute-done((bf16[16,5504]{1,0:T(8,128)(2,1)S(1)}, bf16[16,5504]{1,0:T(8,128)(2,1)S(1)}, u32[]{:S(2)}, u32[]{:S(2)}) %collective-permute-start.2) | collective-permute-done | bytes 176160 | tf_op jit(solution)/shard_map/ppermute | solution.py:122
  21.0 1.1 %collective-permute-start.3 = (bf16[16,5504]{1,0:T(8,128)(2,1)S(1)}, bf16[16,5504]{1,0:T(8,128)(2,1)S(1)}, u32[]{:S(2)}, u32[]{:S(2)}) collective-permute-start(bf16[16,5504]{1,0:T(8,128)(2,1)S(1)} %collective-permute-done.2.refs_3_), channel_id=1, source_target_pairs={{0,4},{5,1},{4,8},{9,5},{8,12},{13,9},{12,14},{15,13},{14,10},{11,... | collective-permute-start | bytes 528392 | tf_op jit(solution)/shard_map/ppermute | solution.py:122
  22.1 0.0 collective-permute-done.10.refs_8_
  22.1 0.0 collective-permute-start.8
  22.1 0.0 collective-permute-done.9.refs_7_
  22.1 0.5 collective-permute-start.13
  22.6 0.0 collective-permute-done.14.refs_15_
  22.6 0.1 collective-permute-start.12
  22.7 0.2 collective-permute-done.6.refs_11_
  22.9 0.2 collective-permute-start.7
  23.1 3.3 %collective-permute-done.3.refs_4_ = bf16[16,5504]{1,0:T(8,128)(2,1)S(1)} collective-permute-done((bf16[16,5504]{1,0:T(8,128)(2,1)S(1)}, bf16[16,5504]{1,0:T(8,128)(2,1)S(1)}, u32[]{:S(2)}, u32[]{:S(2)}) %collective-permute-start.3) | collective-permute-done | bytes 176160 | tf_op jit(solution)/shard_map/ppermute | solution.py:122
  26.5 0.0 collective-permute-start.11
  26.5 0.0 collective-permute-done.8.refs_6_
  26.5 0.0 collective-permute-done.13.refs_14_
  26.5 0.0 collective-permute-done.7.refs_5_
  26.5 0.0 collective-permute-done.12.refs_13_
  26.5 1.4 %collective-permute-done.11.refs_12_ = bf16[16,5504]{1,0:T(8,128)(2,1)S(1)} collective-permute-done((bf16[16,5504]{1,0:T(8,128)(2,1)S(1)}, bf16[16,5504]{1,0:T(8,128)(2,1)S(1)}, u32[]{:S(2)}, u32[]{:S(2)}) %collective-permute-start.11) | collective-permute-done | bytes 176160 | tf_op jit(solution)/shard_map/ppermute | solution.py:121
  27.9 12.2 %shard_map.95 = f32[8,5632]{1,0:T(8,128)S(1)} custom-call(bf16[16,5504]{1,0:T(8,128)(2,1)S(1)} %get-tuple-element.9.refs_0_, bf16[16,5504]{1,0:T(8,128)(2,1)S(1)} %collective-permute-done.refs_1_, bf16[16,5504]{1,0:T(8,128)(2,1)S(1)} %collective-permute-done.1.refs_2_, bf16[16,5504]{1,0:T(8,128)(2,1)S(1)} %collective-permute-done.2.refs_3_, ...), custom_call_target="tpu_custom_call" | custom-call | flops 5637144576 | bytes 11010048 | tf_op jit(solution)/shard_map/pallas_call | solution.py:225
  40.1 2.1 %collective-permute-start.15 = (f32[8,5632]{1,0:T(8,128)S(1)}, f32[8,5632]{1,0:T(8,128)S(1)}, u32[]{:S(2)}, u32[]{:S(2)}) collective-permute-start(f32[8,5632]{1,0:T(8,128)S(1)} %shard_map.95), channel_id=1, source_target_pairs={{0,1},{2,3},{4,5},{6,7},{8,9},{10,11},{12,13},{14,15},{16,17},{18,... | collective-permute-start | bytes 540680 | tf_op jit(solution)/shard_map/ppermute | solution.py:246
  42.1 1.0 %collective-permute-done.15 = f32[8,5632]{1,0:T(8,128)S(1)} collective-permute-done((f32[8,5632]{1,0:T(8,128)S(1)}, f32[8,5632]{1,0:T(8,128)S(1)}, u32[]{:S(2)}, u32[]{:S(2)}) %collective-permute-start.15) | collective-permute-done | bytes 180256 | tf_op jit(solution)/shard_map/ppermute | solution.py:246
  43.2 0.7 %collective-permute-start.16 = (bf16[8,5632]{1,0:T(8,128)(2,1)S(1)}, bf16[8,5632]{1,0:T(8,128)(2,1)S(1)}, u32[]{:S(2)}, u32[]{:S(2)}) collective-permute-start(bf16[8,5632]{1,0:T(8,128)(2,1)S(1)} %fusion.1), channel_id=1, source_target_pairs={{1,3},{3,1},{5,7},{7,5},{9,11},{11,9},{13,15},{15,13},{17,19},{19,... | collective-permute-start | bytes 270344 | tf_op jit(solution)/shard_map/ppermute | solution.py:246
  43.8 0.0 collective-permute-done.16
  43.9 0.7 %collective-permute-start.19 = (bf16[8,5632]{1,0:T(8,128)(2,1)S(1)}, bf16[8,5632]{1,0:T(8,128)(2,1)S(1)}, u32[]{:S(2)}, u32[]{:S(2)}) collective-permute-start(bf16[8,5632]{1,0:T(8,128)(2,1)S(1)} %fusion), channel_id=1, source_target_pairs={{1,13},{3,15},{5,9},{7,11},{9,5},{11,7},{13,1},{15,3},{17,29},{19,... | collective-permute-start | bytes 270344 | tf_op jit(solution)/shard_map/ppermute | solution.py:246
  44.6 0.7 %collective-permute-start.18 = (bf16[8,5632]{1,0:T(8,128)(2,1)S(1)}, bf16[8,5632]{1,0:T(8,128)(2,1)S(1)}, u32[]{:S(2)}, u32[]{:S(2)}) collective-permute-start(bf16[8,5632]{1,0:T(8,128)(2,1)S(1)} %fusion), channel_id=1, source_target_pairs={{1,9},{3,11},{5,13},{7,15},{9,1},{11,3},{13,5},{15,7},{17,25},{19,... | collective-permute-start | bytes 270344 | tf_op jit(solution)/shard_map/ppermute | solution.py:246
  45.2 0.7 %collective-permute-start.17 = (bf16[8,5632]{1,0:T(8,128)(2,1)S(1)}, bf16[8,5632]{1,0:T(8,128)(2,1)S(1)}, u32[]{:S(2)}, u32[]{:S(2)}) collective-permute-start(bf16[8,5632]{1,0:T(8,128)(2,1)S(1)} %fusion), channel_id=1, source_target_pairs={{1,5},{3,7},{5,1},{7,3},{9,13},{11,15},{13,9},{15,11},{17,21},{19,... | collective-permute-start | bytes 270344 | tf_op jit(solution)/shard_map/ppermute | solution.py:246
  45.9 0.0 collective-permute-done.19
  45.9 0.0 collective-permute-done.18
  45.9 0.0 collective-permute-done.17
  45.9 0.1 add_add_fusion.total
  46.0 1.3 %collective-permute-start.20 = (f32[8,5632]{1,0:T(8,128)S(1)}, f32[8,5632]{1,0:T(8,128)S(1)}, u32[]{:S(2)}, u32[]{:S(2)}) collective-permute-start(f32[8,5632]{1,0:T(8,128)S(1)} %add_add_fusion.total), channel_id=1, source_target_pairs={{1,0},{3,2},{5,4},{7,6},{9,8},{11,10},{13,12},{15,14},{17,16},{19,... | collective-permute-start | bytes 540680 | tf_op jit(solution)/shard_map/ppermute | solution.py:246
  47.3 16.4 %collective-permute-done.20.arrived = f32[8,5632]{1,0:T(8,128)S(1)} collective-permute-done((f32[8,5632]{1,0:T(8,128)S(1)}, f32[8,5632]{1,0:T(8,128)S(1)}, u32[]{:S(2)}, u32[]{:S(2)}) %collective-permute-start.20) | collective-permute-done | bytes 180256 | tf_op jit(solution)/shard_map/ppermute | solution.py:246
  63.7 0.7 %shard_map.96 = (f32[1,16]{1,0:T(1,128)}, f32[4,5376]{1,0:T(4,128)}, f32[4,5376]{1,0:T(4,128)}) custom-call(f32[8,5632]{1,0:T(8,128)S(1)} %add_add_fusion.total, f32[8,5632]{1,0:T(8,128)S(1)} %collective-permute-done.20.arrived), custom_call_target="tpu_custom_call" | custom-call | tf_op jit(solution)/shard_map/pallas_call | solution.py:285
  (2 shorter events, 0.1 us)
Async XLA Ops:
  1.8 6.9 %collective-permute-start = (bf16[16,5504]{1,0:T(8,128)(2,1)S(1)}, bf16[16,5504]{1,0:T(8,128)(2,1)S(1)}, u32[]{:S(2)}, u32[]{:S(2)}) collective-permute-start(bf16[16,5504]{1,0:T(8,128)(2,1)S(1)} %get-tuple-element.9.refs_0_), channel_id=1, source_target_pairs={{0,4},{5,1},{4,8},{9,5},{8,12},{13,9},{12,14},{15,13},{14,10},{11,... | collective-permute-start | bytes 528392 | tf_op jit(solution)/shard_map/ppermute | solution.py:122
  4.8 6.3 %collective-permute-start.4 = (bf16[16,5504]{1,0:T(8,128)(2,1)S(1)}, bf16[16,5504]{1,0:T(8,128)(2,1)S(1)}, u32[]{:S(2)}, u32[]{:S(2)}) collective-permute-start(bf16[16,5504]{1,0:T(8,128)(2,1)S(1)} %get-tuple-element.9.refs_0_), channel_id=1, source_target_pairs={{1,4},{4,1},{5,8},{8,5},{9,12},{12,9},{13,14},{14,13},{15,10},{10,... | collective-permute-start | bytes 528392 | tf_op jit(solution)/shard_map/ppermute | solution.py:129
  8.7 6.9 %collective-permute-start.1 = (bf16[16,5504]{1,0:T(8,128)(2,1)S(1)}, bf16[16,5504]{1,0:T(8,128)(2,1)S(1)}, u32[]{:S(2)}, u32[]{:S(2)}) collective-permute-start(bf16[16,5504]{1,0:T(8,128)(2,1)S(1)} %collective-permute-done.refs_1_), channel_id=1, source_target_pairs={{0,4},{5,1},{4,8},{9,5},{8,12},{13,9},{12,14},{15,13},{14,10},{11,... | collective-permute-start | bytes 528392 | tf_op jit(solution)/shard_map/ppermute | solution.py:122
  11.2 6.3 %collective-permute-start.5 = (bf16[16,5504]{1,0:T(8,128)(2,1)S(1)}, bf16[16,5504]{1,0:T(8,128)(2,1)S(1)}, u32[]{:S(2)}, u32[]{:S(2)}) collective-permute-start(bf16[16,5504]{1,0:T(8,128)(2,1)S(1)} %collective-permute-done.4.refs_9_), channel_id=1, source_target_pairs={{0,4},{5,1},{4,8},{9,5},{8,12},{13,9},{12,14},{15,13},{14,10},{11,... | collective-permute-start | bytes 528392 | tf_op jit(solution)/shard_map/ppermute | solution.py:122
  15.6 5.5 %collective-permute-start.2 = (bf16[16,5504]{1,0:T(8,128)(2,1)S(1)}, bf16[16,5504]{1,0:T(8,128)(2,1)S(1)}, u32[]{:S(2)}, u32[]{:S(2)}) collective-permute-start(bf16[16,5504]{1,0:T(8,128)(2,1)S(1)} %collective-permute-done.1.refs_2_), channel_id=1, source_target_pairs={{0,4},{5,1},{4,8},{9,5},{8,12},{13,9},{12,14},{15,13},{14,10},{11,... | collective-permute-start | bytes 528392 | tf_op jit(solution)/shard_map/ppermute | solution.py:122
  16.6 5.5 %collective-permute-start.10 = (bf16[16,5504]{1,0:T(8,128)(2,1)S(1)}, bf16[16,5504]{1,0:T(8,128)(2,1)S(1)}, u32[]{:S(2)}, u32[]{:S(2)}) collective-permute-start(bf16[16,5504]{1,0:T(8,128)(2,1)S(1)} %get-tuple-element.9.refs_0_), channel_id=1, source_target_pairs={{0,1},{1,0},{2,3},{3,2},{4,5},{5,4},{6,7},{7,6},{8,9},{9,8},{10,11... | collective-permute-start | bytes 528392 | tf_op jit(solution)/shard_map/ppermute | solution.py:121
  16.6 5.5 %collective-permute-start.9 = (bf16[16,5504]{1,0:T(8,128)(2,1)S(1)}, bf16[16,5504]{1,0:T(8,128)(2,1)S(1)}, u32[]{:S(2)}, u32[]{:S(2)}) collective-permute-start(bf16[16,5504]{1,0:T(8,128)(2,1)S(1)} %collective-permute-done.4.refs_9_), channel_id=1, source_target_pairs={{0,1},{1,0},{2,3},{3,2},{4,5},{5,4},{6,7},{7,6},{8,9},{9,8},{10,11... | collective-permute-start | bytes 528392 | tf_op jit(solution)/shard_map/ppermute | solution.py:121
  17.1 5.5 %collective-permute-start.14 = (bf16[16,5504]{1,0:T(8,128)(2,1)S(1)}, bf16[16,5504]{1,0:T(8,128)(2,1)S(1)}, u32[]{:S(2)}, u32[]{:S(2)}) collective-permute-start(bf16[16,5504]{1,0:T(8,128)(2,1)S(1)} %collective-permute-done.refs_1_), channel_id=1, source_target_pairs={{0,1},{1,0},{2,3},{3,2},{4,5},{5,4},{6,7},{7,6},{8,9},{9,8},{10,11... | collective-permute-start | bytes 528392 | tf_op jit(solution)/shard_map/ppermute | solution.py:121
  17.4 5.5 %collective-permute-start.6 = (bf16[16,5504]{1,0:T(8,128)(2,1)S(1)}, bf16[16,5504]{1,0:T(8,128)(2,1)S(1)}, u32[]{:S(2)}, u32[]{:S(2)}) collective-permute-start(bf16[16,5504]{1,0:T(8,128)(2,1)S(1)} %collective-permute-done.5.refs_10_), channel_id=1, source_target_pairs={{0,4},{5,1},{4,8},{9,5},{8,12},{13,9},{12,14},{15,13},{14,10},{11,... | collective-permute-start | bytes 528392 | tf_op jit(solution)/shard_map/ppermute | solution.py:122
  21.0 5.5 %collective-permute-start.3 = (bf16[16,5504]{1,0:T(8,128)(2,1)S(1)}, bf16[16,5504]{1,0:T(8,128)(2,1)S(1)}, u32[]{:S(2)}, u32[]{:S(2)}) collective-permute-start(bf16[16,5504]{1,0:T(8,128)(2,1)S(1)} %collective-permute-done.2.refs_3_), channel_id=1, source_target_pairs={{0,4},{5,1},{4,8},{9,5},{8,12},{13,9},{12,14},{15,13},{14,10},{11,... | collective-permute-start | bytes 528392 | tf_op jit(solution)/shard_map/ppermute | solution.py:122
  22.1 4.4 %collective-permute-start.8 = (bf16[16,5504]{1,0:T(8,128)(2,1)S(1)}, bf16[16,5504]{1,0:T(8,128)(2,1)S(1)}, u32[]{:S(2)}, u32[]{:S(2)}) collective-permute-start(bf16[16,5504]{1,0:T(8,128)(2,1)S(1)} %collective-permute-done.5.refs_10_), channel_id=1, source_target_pairs={{0,1},{1,0},{2,3},{3,2},{4,5},{5,4},{6,7},{7,6},{8,9},{9,8},{10,11... | collective-permute-start | bytes 528392 | tf_op jit(solution)/shard_map/ppermute | solution.py:121
  22.1 4.4 %collective-permute-start.13 = (bf16[16,5504]{1,0:T(8,128)(2,1)S(1)}, bf16[16,5504]{1,0:T(8,128)(2,1)S(1)}, u32[]{:S(2)}, u32[]{:S(2)}) collective-permute-start(bf16[16,5504]{1,0:T(8,128)(2,1)S(1)} %collective-permute-done.1.refs_2_), channel_id=1, source_target_pairs={{0,1},{1,0},{2,3},{3,2},{4,5},{5,4},{6,7},{7,6},{8,9},{9,8},{10,11... | collective-permute-start | bytes 528392 | tf_op jit(solution)/shard_map/ppermute | solution.py:121
  22.6 3.9 %collective-permute-start.12 = (bf16[16,5504]{1,0:T(8,128)(2,1)S(1)}, bf16[16,5504]{1,0:T(8,128)(2,1)S(1)}, u32[]{:S(2)}, u32[]{:S(2)}) collective-permute-start(bf16[16,5504]{1,0:T(8,128)(2,1)S(1)} %collective-permute-done.2.refs_3_), channel_id=1, source_target_pairs={{0,1},{1,0},{2,3},{3,2},{4,5},{5,4},{6,7},{7,6},{8,9},{9,8},{10,11... | collective-permute-start | bytes 528392 | tf_op jit(solution)/shard_map/ppermute | solution.py:121
  22.9 3.6 %collective-permute-start.7 = (bf16[16,5504]{1,0:T(8,128)(2,1)S(1)}, bf16[16,5504]{1,0:T(8,128)(2,1)S(1)}, u32[]{:S(2)}, u32[]{:S(2)}) collective-permute-start(bf16[16,5504]{1,0:T(8,128)(2,1)S(1)} %collective-permute-done.6.refs_11_), channel_id=1, source_target_pairs={{0,1},{1,0},{2,3},{3,2},{4,5},{5,4},{6,7},{7,6},{8,9},{9,8},{10,11... | collective-permute-start | bytes 528392 | tf_op jit(solution)/shard_map/ppermute | solution.py:121
  26.5 1.4 %collective-permute-start.11 = (bf16[16,5504]{1,0:T(8,128)(2,1)S(1)}, bf16[16,5504]{1,0:T(8,128)(2,1)S(1)}, u32[]{:S(2)}, u32[]{:S(2)}) collective-permute-start(bf16[16,5504]{1,0:T(8,128)(2,1)S(1)} %collective-permute-done.3.refs_4_), channel_id=1, source_target_pairs={{0,1},{1,0},{2,3},{3,2},{4,5},{5,4},{6,7},{7,6},{8,9},{9,8},{10,11... | collective-permute-start | bytes 528392 | tf_op jit(solution)/shard_map/ppermute | solution.py:121
  40.1 3.1 %collective-permute-start.15 = (f32[8,5632]{1,0:T(8,128)S(1)}, f32[8,5632]{1,0:T(8,128)S(1)}, u32[]{:S(2)}, u32[]{:S(2)}) collective-permute-start(f32[8,5632]{1,0:T(8,128)S(1)} %shard_map.95), channel_id=1, source_target_pairs={{0,1},{2,3},{4,5},{6,7},{8,9},{10,11},{12,13},{14,15},{16,17},{18,... | collective-permute-start | bytes 540680 | tf_op jit(solution)/shard_map/ppermute | solution.py:246
  43.2 0.7 %collective-permute-start.16 = (bf16[8,5632]{1,0:T(8,128)(2,1)S(1)}, bf16[8,5632]{1,0:T(8,128)(2,1)S(1)}, u32[]{:S(2)}, u32[]{:S(2)}) collective-permute-start(bf16[8,5632]{1,0:T(8,128)(2,1)S(1)} %fusion.1), channel_id=1, source_target_pairs={{1,3},{3,1},{5,7},{7,5},{9,11},{11,9},{13,15},{15,13},{17,19},{19,... | collective-permute-start | bytes 270344 | tf_op jit(solution)/shard_map/ppermute | solution.py:246
  43.9 2.0 %collective-permute-start.19 = (bf16[8,5632]{1,0:T(8,128)(2,1)S(1)}, bf16[8,5632]{1,0:T(8,128)(2,1)S(1)}, u32[]{:S(2)}, u32[]{:S(2)}) collective-permute-start(bf16[8,5632]{1,0:T(8,128)(2,1)S(1)} %fusion), channel_id=1, source_target_pairs={{1,13},{3,15},{5,9},{7,11},{9,5},{11,7},{13,1},{15,3},{17,29},{19,... | collective-permute-start | bytes 270344 | tf_op jit(solution)/shard_map/ppermute | solution.py:246
  44.6 1.4 %collective-permute-start.18 = (bf16[8,5632]{1,0:T(8,128)(2,1)S(1)}, bf16[8,5632]{1,0:T(8,128)(2,1)S(1)}, u32[]{:S(2)}, u32[]{:S(2)}) collective-permute-start(bf16[8,5632]{1,0:T(8,128)(2,1)S(1)} %fusion), channel_id=1, source_target_pairs={{1,9},{3,11},{5,13},{7,15},{9,1},{11,3},{13,5},{15,7},{17,25},{19,... | collective-permute-start | bytes 270344 | tf_op jit(solution)/shard_map/ppermute | solution.py:246
  45.2 0.7 %collective-permute-start.17 = (bf16[8,5632]{1,0:T(8,128)(2,1)S(1)}, bf16[8,5632]{1,0:T(8,128)(2,1)S(1)}, u32[]{:S(2)}, u32[]{:S(2)}) collective-permute-start(bf16[8,5632]{1,0:T(8,128)(2,1)S(1)} %fusion), channel_id=1, source_target_pairs={{1,5},{3,7},{5,1},{7,3},{9,13},{11,15},{13,9},{15,11},{17,21},{19,... | collective-permute-start | bytes 270344 | tf_op jit(solution)/shard_map/ppermute | solution.py:246
  46.0 17.7 %collective-permute-start.20 = (f32[8,5632]{1,0:T(8,128)S(1)}, f32[8,5632]{1,0:T(8,128)S(1)}, u32[]{:S(2)}, u32[]{:S(2)}) collective-permute-start(f32[8,5632]{1,0:T(8,128)S(1)} %add_add_fusion.total), channel_id=1, source_target_pairs={{1,0},{3,2},{5,4},{7,6},{9,8},{11,10},{13,12},{15,14},{17,16},{19,... | collective-permute-start | bytes 540680 | tf_op jit(solution)/shard_map/ppermute | solution.py:246

commit v4 on v3

--- a/solution.py
+++ b/solution.py
@@ -109,47 +109,82 @@
     )
 
 
-def gather_blocks(block, loop):
+def hop_pairs(order, step, cross):
+    chips = len(order)
+    first = 1 - step % 2
+    pairs = []
+    for i in range(chips):
+        here, after = 2 * order[i], 2 * order[(i + 1) % chips]
+        if cross:
+            pairs += [(here + first, after + 1 - first), (after + 1 - first, here + first)]
+        else:
+            pairs += [(here + 1 - first, after + 1 - first), (after + first, here + first)]
+    return pairs
+
+
+def gather_blocks(block, loop, beside):
     chips = loop // 2
     order = ring_of(chips)
-    pairs, cross_pairs = [], []
-    for i in range(chips):
-        here, after = order[i], order[(i + 1) % chips]
-        pairs += [(2 * here, 2 * after), (2 * after + 1, 2 * here + 1)]
-        cross_pairs += [(2 * here + 1, 2 * after), (2 * after, 2 * here + 1)]
+    half = chips // 2
     swap_pairs = [(i, i ^ 1) for i in range(loop)]
-    swap = lambda x: lax.ppermute(x, "loop", swap_pairs)
-    hop = lambda x: lax.ppermute(x, "loop", pairs)
+    send = lambda x, pairs: lax.ppermute(x, "loop", pairs)
     same, other = [None] * chips, [None] * chips
-    same[0] = block
-    half = chips // 2
+    same[0], other[0] = block, send(block, swap_pairs)
+    crossed = plain = block
     for step in range(1, half + 1):
-        same[step] = hop(same[step - 1])
+        crossed = send(crossed, hop_pairs(order, step, True))
+        if step < half:
+            plain = send(plain, hop_pairs(order, step, step > 1))
         if step == 1:
-            other[step] = lax.ppermute(block, "loop", cross_pairs)
-            other[0] = swap(block)
-        elif step < half:
-            other[step] = hop(other[step - 1])
+            crossed, beside = lax.optimization_barrier((crossed, beside))
+        far = step if step % 2 else chips - step
+        near = chips - far
+        mine, theirs = (other, same) if step % 2 else (same, other)
+        mine[far] = crossed
         if step < half:
-            other[chips - step] = swap(same[step])
-            same[chips - step] = swap(other[step])
+            theirs[far] = plain
+            theirs[near] = send(crossed, swap_pairs)
+            mine[near] = send(plain, swap_pairs)
         else:
-            other[step] = swap(same[step])
-    return same + other
+            theirs[far] = send(crossed, swap_pairs)
+    return same + other, beside
+
+
+def load_kernel(head_hbm, head, sems):
+    parts = sems.shape[0]
+    size = head.shape[0] // parts
+    copies = [
+        pltpu.make_async_copy(
+            head_hbm.at[pl.ds(k * size, size)], head.at[pl.ds(k * size, size)], sems.at[k]
+        )
+        for k in range(parts)
+    ]
+    for copy in copies:
+        copy.start()
+    for copy in copies:
+        copy.wait()
+
+
+def load(tied_head):
+    return pl.pallas_call(
+        load_kernel,
+        out_shape=pltpu.VMEM(tied_head.shape, BF16),
+        in_specs=[HBM],
+        out_specs=VMEM,
+        scratch_shapes=[pltpu.SemaphoreType.DMA((4,))],
+        compiler_params=pltpu.CompilerParams(vmem_limit_bytes=16 << 20),
+        cost_estimate=pl.CostEstimate(
+            flops=0, bytes_accessed=4 * tied_head.shape[0] * tied_head.shape[1], transcendentals=0
+        ),
+    )(in_hbm(tied_head))
 
 
 def main_kernel(loop, levels, count, *refs):
     blocks = refs[:count]
-    head_hbm, gain, bias, out, head, mapped, slopes, sems = refs[count:]
+    head, gain, bias, out, mapped, slopes = refs[count:]
     voc, width = head.shape
-    cuts = 7 if width % (7 * LANES) == 0 else 1
+    cuts = 3 if width % (3 * LANES) == 0 else 1
     cut = width // cuts
-    copies = []
-    for k in range(cuts):
-        at = pl.ds(k * cut, cut)
-        copies.append(pltpu.make_async_copy(head_hbm.at[:, at], head.at[:, at], sems.at[k]))
-    for copy in copies:
-        copy.start()
     rows = mapped.shape[0]
     rows_dev = rows // loop
     chips = loop // 2
@@ -174,7 +209,6 @@
                 c = jnp.where(here, bias[level : level + 1, at], c)
             mapped[part, at] = ((b[:, at].astype(F32) * scale[part]) * g + c).astype(BF16)
             row += b.shape[0]
-        copies[k].wait()
         term = lax.dot_general(mapped[:, at], head[:, at], NT, preferred_element_type=F32)
         logits = term if logits is None else logits + term
     prob = jnp.exp(logits - norm)
@@ -189,7 +223,7 @@
     flip = index // (rows // 2)
     relative = (index - flip * (rows // 2)) // rows_dev
     core = me % 2
-    place = place_of(me // 2, chips) + jnp.where(core == 0, chips - relative, relative)
+    place = place_of(me // 2, chips) + jnp.where(core == 0, relative, chips - relative)
     place = jnp.where(place >= chips, place - chips, place)
     owner = 2 * chip_at(place, chips) + jnp.where(flip == 0, core, 1 - core)
     goes_to = owner * rows_dev + index % rows_dev
@@ -225,43 +259,35 @@
     return pl.pallas_call(
         functools.partial(main_kernel, loop, levels, len(blocks)),
         out_shape=pltpu.VMEM((2 * levels, width + rows), F32),
-        in_specs=[VMEM] * len(blocks) + [HBM, VMEM, VMEM],
+        in_specs=[VMEM] * (len(blocks) + 3),
         out_specs=VMEM,
         scratch_shapes=[
-            pltpu.VMEM((voc, width), BF16),
             pltpu.VMEM((rows, width), BF16),
             pltpu.VMEM((rows + 16, voc), BF16),
-            pltpu.SemaphoreType.DMA((7,)),
         ],
-        compiler_params=pltpu.CompilerParams(vmem_limit_bytes=32 << 20),
+        compiler_params=pltpu.CompilerParams(vmem_limit_bytes=20 << 20),
         cost_estimate=pl.CostEstimate(
             flops=4 * rows * voc * width,
             bytes_accessed=2 * voc * width,
             transcendentals=rows * voc,
         ),
-    )(*blocks, in_hbm(tied_head), depth_gain, depth_bias)
-
-
-def sum_over_loop(part, loop):
-    send = lambda x, pairs: lax.ppermute(x, "loop", pairs)
-    odd = range(1, loop, 2)
-    total = part + send(part, [(i - 1, i) for i in odd])
-    bits = [1 << k for k in range(1, loop.bit_length() - 1)]
-    rounds = [bits[:1]] + [bits[k : k + 2] for k in range(1, len(bits), 2)]
-    for dims in rounds:
-        mine = lax.reduce_precision(total, 8, 7)
-        sent = mine.astype(BF16)
-        take = lambda mask: send(sent, [(i, i ^ mask) for i in odd]).astype(F32)
-        total = mine + take(dims[0])
-        if len(dims) == 2:
-            total = total + (take(dims[1]) + take(dims[0] ^ dims[1]))
-    return total, send(total, [(i, i - 1) for i in odd])
-
-
-def last_kernel(levels, rows, total, arrived, mass_out, gain_out, bias_out, buf, line, sems):
+    )(*blocks, tied_head, depth_gain, depth_bias)
+
+
+def sum_over_loop(total, loop):
+    total = total + lax.ppermute(total, "loop", [(i, i ^ 1) for i in range(loop)])
+    bit = 2
+    while bit < loop:
+        pairs = [(i, i ^ bit) for i in range(loop)]
+        total = lax.reduce_precision(total, 8, 7)
+        total = total + lax.ppermute(total.astype(BF16), "loop", pairs).astype(F32)
+        bit *= 2
+    return total
+
+
+def last_kernel(levels, rows, buf, mass_out, gain_out, bias_out, line, sems):
     width = gain_out.shape[1]
     me = lax.axis_index("loop")
-    buf[...] = jnp.where(me % 2 == 0, arrived[...], total[...])
     every = buf[0:1, width:]
     spread = lax.broadcasted_iota(jnp.int32, (every.shape[1], LANES), 0)
     target = lax.broadcasted_iota(jnp.int32, (every.shape[1], LANES), 1)
@@ -280,20 +306,19 @@
         copy.wait()
 
 
-def last(total, arrived, levels, width, rows):
+def last(total, levels, width, rows):
     grad = pltpu.HBM((levels, width), F32)
     mass, gain, bias = pl.pallas_call(
         functools.partial(last_kernel, levels, rows),
         out_shape=(pltpu.HBM((1, rows), F32), grad, grad),
-        in_specs=[VMEM, VMEM],
+        in_specs=[VMEM],
         out_specs=(HBM, HBM, HBM),
         scratch_shapes=[
-            pltpu.VMEM(total.shape, F32),
             pltpu.VMEM((1, rows), F32),
             pltpu.SemaphoreType.DMA((3,)),
         ],
         compiler_params=pltpu.CompilerParams(vmem_limit_bytes=8 << 20),
-    )(total, arrived)
+    )(total)
     return mass.reshape(rows), gain, bias
 
 
@@ -301,13 +326,12 @@
     rows_dev, width = hidden.shape
     levels = depth_gain.shape[0]
     block, gain, bias = prep(hidden, exit_depth, teacher, normalizer, depth_gain, depth_bias)
-    blocks = gather_blocks(block, loop)
+    blocks, head = gather_blocks(block, loop, load(tied_head))
     if rows_dev % 16:
         whole = jnp.concatenate(blocks, axis=0)
         blocks = [whole[i : i + 16] for i in range(0, whole.shape[0], 16)]
-    part = main(blocks, tied_head, gain, bias, loop)
-    total, arrived = sum_over_loop(part, loop)
-    return last(total, arrived, levels, width, rows_dev)
+    part = main(blocks, head, gain, bias, loop)
+    return last(sum_over_loop(part, loop), levels, width, rows_dev)
 
 
 def solution(mesh):

time: 64.7 us -> 52.1 us (0.81)
  waiting for transfers between devices: 30.9 us -> 16.9 us
  starting transfers between devices: 18.6 us -> 19.5 us
  Pallas kernels: 14 us -> 14.7 us
    ppermute x21 -> x19, waiting for transfers between devices: 30.9 us -> 16.9 us  [the longest x3 8.28 us: sum_over_loop(): total = total + lax.ppermute(total.astype(BF16), 'loop', pairs).astype(F32)]
    pallas_call x0 -> x1, Pallas kernels: none -> 4.24 us  [load(): pl.pallas_call(load_kernel, out_shape=pltpu.VMEM(tied_head.shape, BF16),...]
    pallas_call x1, Pallas kernels: 12.2 us -> 8.58 us  [main(): pl.pallas_call(functools.partial(main_kernel, loop, levels, len(blocks)),...]
    ppermute x21 -> x19, starting transfers between devices: 18.6 us -> 19.5 us  [the longest x15 12.5 us: gather_blocks(): send = lambda x, pairs: lax.ppermute(x, 'loop', pairs)]
  transfers between devices with their start and end apart: 21 -> 19, of which waited for: 9 -> 9; matrix products, arithmetic and copies ran while one was open for 0% -> 0% of each run, Pallas kernels for 0% -> 8%
where the time goes in v4:
time: 52.1 us; the launch traced here: 51.9 us
  starting transfers between devices  19.5 us (37%)
  waiting for transfers between devices  16.9 us (32%)
  Pallas kernels  14.7 us (28%)
  between operations  0.7 us (1%)
    ppermute x15, starting transfers between devices, gather_blocks(): send = lambda x, pairs: lax.ppermute(x, 'loop', pairs)  12.5 us
    pallas_call x1, Pallas kernels, main(): pl.pallas_call(functools.partial(main_kernel, loop, levels, len(blocks)),...  8.58 us
    ppermute x3, waiting for transfers between devices, sum_over_loop(): total = total + lax.ppermute(total.astype(BF16), 'loop', pairs).astype(F32)  8.28 us
    ppermute x15, waiting for transfers between devices, gather_blocks(): send = lambda x, pairs: lax.ppermute(x, 'loop', pairs)  7.35 us
    ppermute x3, starting transfers between devices, sum_over_loop(): total = total + lax.ppermute(total.astype(BF16), 'loop', pairs).astype(F32)  6.83 us
    pallas_call x1, Pallas kernels, load(): pl.pallas_call(load_kernel, out_shape=pltpu.VMEM(tied_head.shape, BF16),...  4.24 us
    ppermute x1, waiting for transfers between devices, sum_over_loop(): lax.ppermute(total, 'loop', [(i, i ^ 1) for i in range(loop)])  1.28 us
    pallas_call x1, Pallas kernels, prep(): pl.pallas_call(prep_kernel, out_shape=(pltpu.VMEM((rows, width + LANES),...  1.13 us
  transfers between devices with their start and end apart: 19, of which 9 were waited for; matrix products, arithmetic and copies ran while one was open for 0% of the time, Pallas kernels for 8%

profile of v4, /device:TPU:0, one launch (start us, length us, event | category | flops | bytes accessed | tf_op | source)
XLA Modules:
  0.0 51.9 jit_solution(14670615245501977541)
XLA Ops:
  0.6 1.1 %shard_map.94 = (bf16[16,5504]{1,0:T(8,128)(2,1)S(1)}, f32[4,5376]{1,0:T(4,128)S(1)}, f32[4,5376]{1,0:T(4,128)S(1)}) custom-call(bf16[16,5376]{1,0:T(8,128)(2,1)} %hidden.1, s32[1,16]{1,0:T(1,128)} %bitcast.4, s32[1,16]{1,0:T(1,128)} %bitcast.5, f32[1,16]{1,0:T(1,128)} %bitcast.6, f32[4,5376]{1,0:T(4,128)} %depth_gain.1, f32[4,5376]{1,0:T(4,128)} %depth_bias.1), custom_call_target="tpu_custom_call" | custom-call | tf_op jit(solution)/shard_map/pallas_call | solution.py:86
  1.8 2.5 %collective-permute-start.4 = (bf16[16,5504]{1,0:T(8,128)(2,1)S(1)}, bf16[16,5504]{1,0:T(8,128)(2,1)S(1)}, u32[]{:S(2)}, u32[]{:S(2)}) collective-permute-start(bf16[16,5504]{1,0:T(8,128)(2,1)S(1)} %get-tuple-element.11.refs_0_), channel_id=1, source_target_pairs={{0,5},{5,0},{4,9},{9,4},{8,13},{13,8},{12,15},{15,12},{14,11},{11,... | collective-permute-start | bytes 528392 | tf_op jit(solution)/shard_map/ppermute | solution.py:130
  4.3 0.6 %collective-permute-start = (bf16[16,5504]{1,0:T(8,128)(2,1)S(1)}, bf16[16,5504]{1,0:T(8,128)(2,1)S(1)}, u32[]{:S(2)}, u32[]{:S(2)}) collective-permute-start(bf16[16,5504]{1,0:T(8,128)(2,1)S(1)} %get-tuple-element.11.refs_0_), channel_id=1, source_target_pairs={{1,5},{4,0},{5,9},{8,4},{9,13},{12,8},{13,15},{14,12},{15,11},{10,... | collective-permute-start | bytes 528392 | tf_op jit(solution)/shard_map/ppermute | solution.py:130
  4.9 4.2 %shard_map.95.refs_16_ = bf16[1024,5376]{1,0:T(8,128)(2,1)S(1)} custom-call(bf16[1024,5376]{1,0:T(8,128)(2,1)} %head_hbm.1), custom_call_target="tpu_custom_call" | custom-call | bytes 22020096 | tf_op jit(solution)/shard_map/pallas_call | solution.py:169
  9.1 0.0 collective-permute-done.4.refs_9_
  9.1 1.5 %collective-permute-start.5 = (bf16[16,5504]{1,0:T(8,128)(2,1)S(1)}, bf16[16,5504]{1,0:T(8,128)(2,1)S(1)}, u32[]{:S(2)}, u32[]{:S(2)}) collective-permute-start(bf16[16,5504]{1,0:T(8,128)(2,1)S(1)} %collective-permute-done.4.refs_9_), channel_id=1, source_target_pairs={{1,4},{4,1},{5,8},{8,5},{9,12},{12,9},{13,14},{14,13},{15,10},{10,... | collective-permute-start | bytes 528392 | tf_op jit(solution)/shard_map/ppermute | solution.py:130
  10.6 0.0 collective-permute-done.refs_1_
  10.6 0.7 %collective-permute-start.1 = (bf16[16,5504]{1,0:T(8,128)(2,1)S(1)}, bf16[16,5504]{1,0:T(8,128)(2,1)S(1)}, u32[]{:S(2)}, u32[]{:S(2)}) collective-permute-start(bf16[16,5504]{1,0:T(8,128)(2,1)S(1)} %collective-permute-done.refs_1_), channel_id=1, source_target_pairs={{1,4},{4,1},{5,8},{8,5},{9,12},{12,9},{13,14},{14,13},{15,10},{10,... | collective-permute-start | bytes 528392 | tf_op jit(solution)/shard_map/ppermute | solution.py:130
  11.3 2.8 %collective-permute-done.5.refs_6_ = bf16[16,5504]{1,0:T(8,128)(2,1)S(1)} collective-permute-done((bf16[16,5504]{1,0:T(8,128)(2,1)S(1)}, bf16[16,5504]{1,0:T(8,128)(2,1)S(1)}, u32[]{:S(2)}, u32[]{:S(2)}) %collective-permute-start.5) | collective-permute-done | bytes 176160 | tf_op jit(solution)/shard_map/ppermute | solution.py:130
  14.1 2.4 %collective-permute-start.6 = (bf16[16,5504]{1,0:T(8,128)(2,1)S(1)}, bf16[16,5504]{1,0:T(8,128)(2,1)S(1)}, u32[]{:S(2)}, u32[]{:S(2)}) collective-permute-start(bf16[16,5504]{1,0:T(8,128)(2,1)S(1)} %collective-permute-done.5.refs_6_), channel_id=1, source_target_pairs={{0,5},{5,0},{4,9},{9,4},{8,13},{13,8},{12,15},{15,12},{14,11},{11,... | collective-permute-start | bytes 528392 | tf_op jit(solution)/shard_map/ppermute | solution.py:130
  16.5 0.0 collective-permute-start.10
  16.5 0.5 collective-permute-start.14
  17.0 0.0 collective-permute-start.9
  17.0 0.0 collective-permute-done.1.refs_14_
  17.0 1.6 %collective-permute-start.3 = (bf16[16,5504]{1,0:T(8,128)(2,1)S(1)}, bf16[16,5504]{1,0:T(8,128)(2,1)S(1)}, u32[]{:S(2)}, u32[]{:S(2)}) collective-permute-start(bf16[16,5504]{1,0:T(8,128)(2,1)S(1)} %collective-permute-done.1.refs_14_), channel_id=1, source_target_pairs={{0,5},{5,0},{4,9},{9,4},{8,13},{13,8},{12,15},{15,12},{14,11},{11,... | collective-permute-start | bytes 528392 | tf_op jit(solution)/shard_map/ppermute | solution.py:130
  18.6 1.0 %collective-permute-done.6.refs_11_ = bf16[16,5504]{1,0:T(8,128)(2,1)S(1)} collective-permute-done((bf16[16,5504]{1,0:T(8,128)(2,1)S(1)}, bf16[16,5504]{1,0:T(8,128)(2,1)S(1)}, u32[]{:S(2)}, u32[]{:S(2)}) %collective-permute-start.6) | collective-permute-done | bytes 176160 | tf_op jit(solution)/shard_map/ppermute | solution.py:130
  19.6 1.3 %collective-permute-start.7 = (bf16[16,5504]{1,0:T(8,128)(2,1)S(1)}, bf16[16,5504]{1,0:T(8,128)(2,1)S(1)}, u32[]{:S(2)}, u32[]{:S(2)}) collective-permute-start(bf16[16,5504]{1,0:T(8,128)(2,1)S(1)} %collective-permute-done.6.refs_11_), channel_id=1, source_target_pairs={{1,4},{4,1},{5,8},{8,5},{9,12},{12,9},{13,14},{14,13},{15,10},{10,... | collective-permute-start | bytes 528392 | tf_op jit(solution)/shard_map/ppermute | solution.py:130
  20.9 0.0 collective-permute-done.10.refs_8_
  20.9 0.3 collective-permute-start.2
  21.2 0.0 collective-permute-done.14.refs_15_
  21.2 0.3 collective-permute-start.11
  21.5 0.0 collective-permute-done.9.refs_7_
  21.5 0.3 collective-permute-start.8
  21.7 0.1 collective-permute-done.3.refs_3_
  21.9 0.5 collective-permute-start.13
  22.4 2.1 %collective-permute-done.7.refs_4_ = bf16[16,5504]{1,0:T(8,128)(2,1)S(1)} collective-permute-done((bf16[16,5504]{1,0:T(8,128)(2,1)S(1)}, bf16[16,5504]{1,0:T(8,128)(2,1)S(1)}, u32[]{:S(2)}, u32[]{:S(2)}) %collective-permute-start.7) | collective-permute-done | bytes 176160 | tf_op jit(solution)/shard_map/ppermute | solution.py:130
  24.5 0.1 collective-permute-start.12
  24.6 0.0 collective-permute-done.2.refs_2_
  24.6 0.0 collective-permute-done.11.refs_10_
  24.6 0.0 collective-permute-done.13.refs_13_
  24.6 0.0 collective-permute-done.8.refs_5_
  24.6 1.3 %collective-permute-done.12.refs_12_ = bf16[16,5504]{1,0:T(8,128)(2,1)S(1)} collective-permute-done((bf16[16,5504]{1,0:T(8,128)(2,1)S(1)}, bf16[16,5504]{1,0:T(8,128)(2,1)S(1)}, u32[]{:S(2)}, u32[]{:S(2)}) %collective-permute-start.12) | collective-permute-done | bytes 176160 | tf_op jit(solution)/shard_map/ppermute | solution.py:130
  25.9 8.6 %shard_map.96 = f32[8,5632]{1,0:T(8,128)S(1)} custom-call(bf16[16,5504]{1,0:T(8,128)(2,1)S(1)} %get-tuple-element.11.refs_0_, bf16[16,5504]{1,0:T(8,128)(2,1)S(1)} %collective-permute-done.refs_1_, bf16[16,5504]{1,0:T(8,128)(2,1)S(1)} %collective-permute-done.2.refs_2_, bf16[16,5504]{1,0:T(8,128)(2,1)S(1)} %collective-permute-done.3.refs_3_, ...), custom_call_target="tpu_custom_call" | custom-call | flops 5637144576 | bytes 11010048 | tf_op jit(solution)/shard_map/pallas_call | solution.py:259
  34.5 0.2 collective-permute-start.15
  34.7 1.3 %collective-permute-done.15 = f32[8,5632]{1,0:T(8,128)S(1)} collective-permute-done((f32[8,5632]{1,0:T(8,128)S(1)}, f32[8,5632]{1,0:T(8,128)S(1)}, u32[]{:S(2)}, u32[]{:S(2)}) %collective-permute-start.15) | collective-permute-done | bytes 180256 | tf_op jit(solution)/shard_map/ppermute | solution.py:278
  36.0 1.5 %collective-permute-start.16 = (bf16[8,5632]{1,0:T(8,128)(2,1)S(1)}, bf16[8,5632]{1,0:T(8,128)(2,1)S(1)}, u32[]{:S(2)}, u32[]{:S(2)}) collective-permute-start(bf16[8,5632]{1,0:T(8,128)(2,1)S(1)} %get-tuple-element.19), channel_id=1, source_target_pairs={{0,2},{1,3},{2,0},{3,1},{4,6},{5,7},{6,4},{7,5},{8,10},{9,11},{10,... | collective-permute-start | bytes 270344 | tf_op jit(solution)/shard_map/ppermute | solution.py:283
  37.5 3.3 %collective-permute-done.16 = bf16[8,5632]{1,0:T(8,128)(2,1)S(1)} collective-permute-done((bf16[8,5632]{1,0:T(8,128)(2,1)S(1)}, bf16[8,5632]{1,0:T(8,128)(2,1)S(1)}, u32[]{:S(2)}, u32[]{:S(2)}) %collective-permute-start.16) | collective-permute-done | bytes 90144 | tf_op jit(solution)/shard_map/ppermute | solution.py:283
  40.7 2.4 %collective-permute-start.17 = (bf16[8,5632]{1,0:T(8,128)(2,1)S(1)}, bf16[8,5632]{1,0:T(8,128)(2,1)S(1)}, u32[]{:S(2)}, u32[]{:S(2)}) collective-permute-start(bf16[8,5632]{1,0:T(8,128)(2,1)S(1)} %fusion), channel_id=1, source_target_pairs={{0,4},{1,5},{2,6},{3,7},{4,0},{5,1},{6,2},{7,3},{8,12},{9,13},{10,... | collective-permute-start | bytes 270344 | tf_op jit(solution)/shard_map/ppermute | solution.py:283
  43.1 2.5 %collective-permute-done.17 = bf16[8,5632]{1,0:T(8,128)(2,1)S(1)} collective-permute-done((bf16[8,5632]{1,0:T(8,128)(2,1)S(1)}, bf16[8,5632]{1,0:T(8,128)(2,1)S(1)}, u32[]{:S(2)}, u32[]{:S(2)}) %collective-permute-start.17) | collective-permute-done | bytes 90144 | tf_op jit(solution)/shard_map/ppermute | solution.py:283
  45.7 3.0 %collective-permute-start.18 = (bf16[8,5632]{1,0:T(8,128)(2,1)S(1)}, bf16[8,5632]{1,0:T(8,128)(2,1)S(1)}, u32[]{:S(2)}, u32[]{:S(2)}) collective-permute-start(bf16[8,5632]{1,0:T(8,128)(2,1)S(1)} %fusion.1), channel_id=1, source_target_pairs={{0,8},{1,9},{2,10},{3,11},{4,12},{5,13},{6,14},{7,15},{8,0},{9,1},... | collective-permute-start | bytes 270344 | tf_op jit(solution)/shard_map/ppermute | solution.py:283
  48.7 2.5 %collective-permute-done.18 = bf16[8,5632]{1,0:T(8,128)(2,1)S(1)} collective-permute-done((bf16[8,5632]{1,0:T(8,128)(2,1)S(1)}, bf16[8,5632]{1,0:T(8,128)(2,1)S(1)}, u32[]{:S(2)}, u32[]{:S(2)}) %collective-permute-start.18) | collective-permute-done | bytes 90144 | tf_op jit(solution)/shard_map/ppermute | solution.py:283
  51.2 0.1 convert_add_fusion.buf
  51.2 0.7 %shard_map.97 = (f32[1,16]{1,0:T(1,128)}, f32[4,5376]{1,0:T(4,128)}, f32[4,5376]{1,0:T(4,128)}) custom-call(f32[8,5632]{1,0:T(8,128)S(1)} %convert_add_fusion.buf), custom_call_target="tpu_custom_call" | custom-call | tf_op jit(solution)/shard_map/pallas_call | solution.py:311
  (3 shorter events, 0.1 us)
Async XLA Ops:
  1.8 7.4 %collective-permute-start.4 = (bf16[16,5504]{1,0:T(8,128)(2,1)S(1)}, bf16[16,5504]{1,0:T(8,128)(2,1)S(1)}, u32[]{:S(2)}, u32[]{:S(2)}) collective-permute-start(bf16[16,5504]{1,0:T(8,128)(2,1)S(1)} %get-tuple-element.11.refs_0_), channel_id=1, source_target_pairs={{0,5},{5,0},{4,9},{9,4},{8,13},{13,8},{12,15},{15,12},{14,11},{11,... | collective-permute-start | bytes 528392 | tf_op jit(solution)/shard_map/ppermute | solution.py:130
  4.3 6.3 %collective-permute-start = (bf16[16,5504]{1,0:T(8,128)(2,1)S(1)}, bf16[16,5504]{1,0:T(8,128)(2,1)S(1)}, u32[]{:S(2)}, u32[]{:S(2)}) collective-permute-start(bf16[16,5504]{1,0:T(8,128)(2,1)S(1)} %get-tuple-element.11.refs_0_), channel_id=1, source_target_pairs={{1,5},{4,0},{5,9},{8,4},{9,13},{12,8},{13,15},{14,12},{15,11},{10,... | collective-permute-start | bytes 528392 | tf_op jit(solution)/shard_map/ppermute | solution.py:130
  9.1 4.9 %collective-permute-start.5 = (bf16[16,5504]{1,0:T(8,128)(2,1)S(1)}, bf16[16,5504]{1,0:T(8,128)(2,1)S(1)}, u32[]{:S(2)}, u32[]{:S(2)}) collective-permute-start(bf16[16,5504]{1,0:T(8,128)(2,1)S(1)} %collective-permute-done.4.refs_9_), channel_id=1, source_target_pairs={{1,4},{4,1},{5,8},{8,5},{9,12},{12,9},{13,14},{14,13},{15,10},{10,... | collective-permute-start | bytes 528392 | tf_op jit(solution)/shard_map/ppermute | solution.py:130
  10.6 6.4 %collective-permute-start.1 = (bf16[16,5504]{1,0:T(8,128)(2,1)S(1)}, bf16[16,5504]{1,0:T(8,128)(2,1)S(1)}, u32[]{:S(2)}, u32[]{:S(2)}) collective-permute-start(bf16[16,5504]{1,0:T(8,128)(2,1)S(1)} %collective-permute-done.refs_1_), channel_id=1, source_target_pairs={{1,4},{4,1},{5,8},{8,5},{9,12},{12,9},{13,14},{14,13},{15,10},{10,... | collective-permute-start | bytes 528392 | tf_op jit(solution)/shard_map/ppermute | solution.py:130
  14.1 5.5 %collective-permute-start.6 = (bf16[16,5504]{1,0:T(8,128)(2,1)S(1)}, bf16[16,5504]{1,0:T(8,128)(2,1)S(1)}, u32[]{:S(2)}, u32[]{:S(2)}) collective-permute-start(bf16[16,5504]{1,0:T(8,128)(2,1)S(1)} %collective-permute-done.5.refs_6_), channel_id=1, source_target_pairs={{0,5},{5,0},{4,9},{9,4},{8,13},{13,8},{12,15},{15,12},{14,11},{11,... | collective-permute-start | bytes 528392 | tf_op jit(solution)/shard_map/ppermute | solution.py:130
  16.5 4.5 %collective-permute-start.10 = (bf16[16,5504]{1,0:T(8,128)(2,1)S(1)}, bf16[16,5504]{1,0:T(8,128)(2,1)S(1)}, u32[]{:S(2)}, u32[]{:S(2)}) collective-permute-start(bf16[16,5504]{1,0:T(8,128)(2,1)S(1)} %get-tuple-element.11.refs_0_), channel_id=1, source_target_pairs={{0,1},{1,0},{2,3},{3,2},{4,5},{5,4},{6,7},{7,6},{8,9},{9,8},{10,11... | collective-permute-start | bytes 528392 | tf_op jit(solution)/shard_map/ppermute | solution.py:130
  16.5 4.7 %collective-permute-start.14 = (bf16[16,5504]{1,0:T(8,128)(2,1)S(1)}, bf16[16,5504]{1,0:T(8,128)(2,1)S(1)}, u32[]{:S(2)}, u32[]{:S(2)}) collective-permute-start(bf16[16,5504]{1,0:T(8,128)(2,1)S(1)} %collective-permute-done.refs_1_), channel_id=1, source_target_pairs={{0,1},{1,0},{2,3},{3,2},{4,5},{5,4},{6,7},{7,6},{8,9},{9,8},{10,11... | collective-permute-start | bytes 528392 | tf_op jit(solution)/shard_map/ppermute | solution.py:130
  17.0 4.5 %collective-permute-start.9 = (bf16[16,5504]{1,0:T(8,128)(2,1)S(1)}, bf16[16,5504]{1,0:T(8,128)(2,1)S(1)}, u32[]{:S(2)}, u32[]{:S(2)}) collective-permute-start(bf16[16,5504]{1,0:T(8,128)(2,1)S(1)} %collective-permute-done.4.refs_9_), channel_id=1, source_target_pairs={{0,1},{1,0},{2,3},{3,2},{4,5},{5,4},{6,7},{7,6},{8,9},{9,8},{10,11... | collective-permute-start | bytes 528392 | tf_op jit(solution)/shard_map/ppermute | solution.py:130
  17.0 4.9 %collective-permute-start.3 = (bf16[16,5504]{1,0:T(8,128)(2,1)S(1)}, bf16[16,5504]{1,0:T(8,128)(2,1)S(1)}, u32[]{:S(2)}, u32[]{:S(2)}) collective-permute-start(bf16[16,5504]{1,0:T(8,128)(2,1)S(1)} %collective-permute-done.1.refs_14_), channel_id=1, source_target_pairs={{0,5},{5,0},{4,9},{9,4},{8,13},{13,8},{12,15},{15,12},{14,11},{11,... | collective-permute-start | bytes 528392 | tf_op jit(solution)/shard_map/ppermute | solution.py:130
  19.6 4.9 %collective-permute-start.7 = (bf16[16,5504]{1,0:T(8,128)(2,1)S(1)}, bf16[16,5504]{1,0:T(8,128)(2,1)S(1)}, u32[]{:S(2)}, u32[]{:S(2)}) collective-permute-start(bf16[16,5504]{1,0:T(8,128)(2,1)S(1)} %collective-permute-done.6.refs_11_), channel_id=1, source_target_pairs={{1,4},{4,1},{5,8},{8,5},{9,12},{12,9},{13,14},{14,13},{15,10},{10,... | collective-permute-start | bytes 528392 | tf_op jit(solution)/shard_map/ppermute | solution.py:130
  20.9 3.6 %collective-permute-start.2 = (bf16[16,5504]{1,0:T(8,128)(2,1)S(1)}, bf16[16,5504]{1,0:T(8,128)(2,1)S(1)}, u32[]{:S(2)}, u32[]{:S(2)}) collective-permute-start(bf16[16,5504]{1,0:T(8,128)(2,1)S(1)} %collective-permute-done.1.refs_14_), channel_id=1, source_target_pairs={{0,1},{1,0},{2,3},{3,2},{4,5},{5,4},{6,7},{7,6},{8,9},{9,8},{10,11... | collective-permute-start | bytes 528392 | tf_op jit(solution)/shard_map/ppermute | solution.py:130
  21.2 3.4 %collective-permute-start.11 = (bf16[16,5504]{1,0:T(8,128)(2,1)S(1)}, bf16[16,5504]{1,0:T(8,128)(2,1)S(1)}, u32[]{:S(2)}, u32[]{:S(2)}) collective-permute-start(bf16[16,5504]{1,0:T(8,128)(2,1)S(1)} %collective-permute-done.5.refs_6_), channel_id=1, source_target_pairs={{0,1},{1,0},{2,3},{3,2},{4,5},{5,4},{6,7},{7,6},{8,9},{9,8},{10,11... | collective-permute-start | bytes 528392 | tf_op jit(solution)/shard_map/ppermute | solution.py:130
  21.5 3.1 %collective-permute-start.8 = (bf16[16,5504]{1,0:T(8,128)(2,1)S(1)}, bf16[16,5504]{1,0:T(8,128)(2,1)S(1)}, u32[]{:S(2)}, u32[]{:S(2)}) collective-permute-start(bf16[16,5504]{1,0:T(8,128)(2,1)S(1)} %collective-permute-done.6.refs_11_), channel_id=1, source_target_pairs={{0,1},{1,0},{2,3},{3,2},{4,5},{5,4},{6,7},{7,6},{8,9},{9,8},{10,11... | collective-permute-start | bytes 528392 | tf_op jit(solution)/shard_map/ppermute | solution.py:130
  21.9 2.7 %collective-permute-start.13 = (bf16[16,5504]{1,0:T(8,128)(2,1)S(1)}, bf16[16,5504]{1,0:T(8,128)(2,1)S(1)}, u32[]{:S(2)}, u32[]{:S(2)}) collective-permute-start(bf16[16,5504]{1,0:T(8,128)(2,1)S(1)} %collective-permute-done.3.refs_3_), channel_id=1, source_target_pairs={{0,1},{1,0},{2,3},{3,2},{4,5},{5,4},{6,7},{7,6},{8,9},{9,8},{10,11... | collective-permute-start | bytes 528392 | tf_op jit(solution)/shard_map/ppermute | solution.py:130
  24.5 1.4 %collective-permute-start.12 = (bf16[16,5504]{1,0:T(8,128)(2,1)S(1)}, bf16[16,5504]{1,0:T(8,128)(2,1)S(1)}, u32[]{:S(2)}, u32[]{:S(2)}) collective-permute-start(bf16[16,5504]{1,0:T(8,128)(2,1)S(1)} %collective-permute-done.7.refs_4_), channel_id=1, source_target_pairs={{0,1},{1,0},{2,3},{3,2},{4,5},{5,4},{6,7},{7,6},{8,9},{9,8},{10,11... | collective-permute-start | bytes 528392 | tf_op jit(solution)/shard_map/ppermute | solution.py:130
  34.5 1.5 %collective-permute-start.15 = (f32[8,5632]{1,0:T(8,128)S(1)}, f32[8,5632]{1,0:T(8,128)S(1)}, u32[]{:S(2)}, u32[]{:S(2)}) collective-permute-start(f32[8,5632]{1,0:T(8,128)S(1)} %shard_map.96), channel_id=1, source_target_pairs={{0,1},{1,0},{2,3},{3,2},{4,5},{5,4},{6,7},{7,6},{8,9},{9,8},{10,11... | collective-permute-start | bytes 540680 | tf_op jit(solution)/shard_map/ppermute | solution.py:278
  36.0 4.7 %collective-permute-start.16 = (bf16[8,5632]{1,0:T(8,128)(2,1)S(1)}, bf16[8,5632]{1,0:T(8,128)(2,1)S(1)}, u32[]{:S(2)}, u32[]{:S(2)}) collective-permute-start(bf16[8,5632]{1,0:T(8,128)(2,1)S(1)} %get-tuple-element.19), channel_id=1, source_target_pairs={{0,2},{1,3},{2,0},{3,1},{4,6},{5,7},{6,4},{7,5},{8,10},{9,11},{10,... | collective-permute-start | bytes 270344 | tf_op jit(solution)/shard_map/ppermute | solution.py:283
  40.7 4.9 %collective-permute-start.17 = (bf16[8,5632]{1,0:T(8,128)(2,1)S(1)}, bf16[8,5632]{1,0:T(8,128)(2,1)S(1)}, u32[]{:S(2)}, u32[]{:S(2)}) collective-permute-start(bf16[8,5632]{1,0:T(8,128)(2,1)S(1)} %fusion), channel_id=1, source_target_pairs={{0,4},{1,5},{2,6},{3,7},{4,0},{5,1},{6,2},{7,3},{8,12},{9,13},{10,... | collective-permute-start | bytes 270344 | tf_op jit(solution)/shard_map/ppermute | solution.py:283
  45.7 5.5 %collective-permute-start.18 = (bf16[8,5632]{1,0:T(8,128)(2,1)S(1)}, bf16[8,5632]{1,0:T(8,128)(2,1)S(1)}, u32[]{:S(2)}, u32[]{:S(2)}) collective-permute-start(bf16[8,5632]{1,0:T(8,128)(2,1)S(1)} %fusion.1), channel_id=1, source_target_pairs={{0,8},{1,9},{2,10},{3,11},{4,12},{5,13},{6,14},{7,15},{8,0},{9,1},... | collective-permute-start | bytes 270344 | tf_op jit(solution)/shard_map/ppermute | solution.py:283

commit v5 on v4

--- a/solution.py
+++ b/solution.py
@@ -122,32 +122,89 @@
     return pairs
 
 
-def gather_blocks(block, loop, beside):
+def gather_blocks(block, loop, head, mapper):
     chips = loop // 2
     order = ring_of(chips)
     half = chips // 2
-    swap_pairs = [(i, i ^ 1) for i in range(loop)]
+    tie = lambda *xs: lax.optimization_barrier(xs)
     send = lambda x, pairs: lax.ppermute(x, "loop", pairs)
-    same, other = [None] * chips, [None] * chips
-    same[0], other[0] = block, send(block, swap_pairs)
+    swap = lambda x: send(x, [(i, i ^ 1) for i in range(loop)])
+    blocks = [None] * loop
+    first = swap(block)
+    blocks[0], blocks[chips] = block, first
     crossed = plain = block
+    ready = [0, chips]
+    mapped = None
     for step in range(1, half + 1):
         crossed = send(crossed, hop_pairs(order, step, True))
         if step < half:
             plain = send(plain, hop_pairs(order, step, step > 1))
         if step == 1:
-            crossed, beside = lax.optimization_barrier((crossed, beside))
+            crossed, plain, head, first = tie(crossed, plain, head, first)
+            blocks[chips] = first
+        if mapper is not None and step == 3:
+            mapped = mapper(None, {i: blocks[i] for i in ready[:6]})
+            plain, mapped = tie(plain, mapped)
+        if mapper is not None and step == half:
+            mapped = mapper(mapped, {i: blocks[i] for i in ready[6:12]})
+            crossed, mapped = tie(crossed, mapped)
         far = step if step % 2 else chips - step
         near = chips - far
-        mine, theirs = (other, same) if step % 2 else (same, other)
-        mine[far] = crossed
+        mine, theirs = (chips, 0) if step % 2 else (0, chips)
+        blocks[mine + far] = crossed
         if step < half:
-            theirs[far] = plain
-            theirs[near] = send(crossed, swap_pairs)
-            mine[near] = send(plain, swap_pairs)
+            blocks[theirs + far] = plain
+            blocks[theirs + near] = swap(crossed)
+            blocks[mine + near] = swap(plain)
+            ready += [mine + far, theirs + far, theirs + near, mine + near]
         else:
-            theirs[far] = send(crossed, swap_pairs)
-    return same + other, beside
+            blocks[theirs + far] = swap(crossed)
+            ready += [mine + far, theirs + far]
+    return blocks, head, mapped, ready[12:] if mapper is not None else ready
+
+
+def map_rows(block, gain, bias, mapped, first):
+    rows, width = block.shape[0], mapped.shape[1]
+    levels = gain.shape[0]
+    meta = block[:, width:].astype(F32)
+    scale = (meta[:, 0:1] + meta[:, 1:2]) + meta[:, 2:3]
+    depth = meta[:, 9:10]
+    cuts = 3 if width % (3 * LANES) == 0 else 1
+    cut = width // cuts
+    for k in range(cuts):
+        at = slice(k * cut, (k + 1) * cut)
+        g, c = gain[0:1, at], bias[0:1, at]
+        for level in range(1, levels):
+            here = depth == float(level)
+            g = jnp.where(here, gain[level : level + 1, at], g)
+            c = jnp.where(here, bias[level : level + 1, at], c)
+        value = (block[:, at].astype(F32) * scale) * g + c
+        mapped[first : first + rows, at] = value.astype(BF16)
+
+
+def map_kernel(places, *refs):
+    blocks = refs[: len(places)]
+    gain, bias = refs[len(places) : len(places) + 2]
+    for place, block in zip(places, blocks):
+        map_rows(block, gain, bias, refs[-1], place * block.shape[0])
+
+
+def map_early(rows, gain, bias, mapped, blocks):
+    places, blocks = list(blocks), list(blocks.values())
+    width = gain.shape[1]
+    operands = blocks + [gain, bias] + ([] if mapped is None else [mapped])
+    count = len(blocks) * blocks[0].shape[0]
+    return pl.pallas_call(
+        functools.partial(map_kernel, places),
+        out_shape=pltpu.VMEM((rows, width), BF16),
+        in_specs=[VMEM] * len(operands),
+        out_specs=VMEM,
+        input_output_aliases={} if mapped is None else {len(operands) - 1: 0},
+        compiler_params=pltpu.CompilerParams(vmem_limit_bytes=8 << 20),
+        cost_estimate=pl.CostEstimate(
+            flops=20 * count * width, bytes_accessed=4 * count * width, transcendentals=0
+        ),
+    )(*operands)
 
 
 def load_kernel(head_hbm, head, sems):
@@ -179,12 +236,11 @@
     )(in_hbm(tied_head))
 
 
-def main_kernel(loop, levels, count, *refs):
+def main_kernel(loop, levels, count, late, *refs):
     blocks = refs[:count]
-    head, gain, bias, out, mapped, slopes = refs[count:]
+    head, gain, bias = refs[count : count + 3]
+    keep, give, mapped, out, slopes = refs[-5:]
     voc, width = head.shape
-    cuts = 3 if width % (3 * LANES) == 0 else 1
-    cut = width // cuts
     rows = mapped.shape[0]
     rows_dev = rows // loop
     chips = loop // 2
@@ -196,21 +252,9 @@
     target = (col(6) + 128.0 * col(7) + 16384.0 * col(8)).astype(jnp.int32)
     depth = col(9)
 
-    logits = None
-    for k in range(cuts):
-        at = slice(k * cut, (k + 1) * cut)
-        row = 0
-        for b in blocks:
-            part = slice(row, row + b.shape[0])
-            g, c = gain[0:1, at], bias[0:1, at]
-            for level in range(1, levels):
-                here = depth[part] == float(level)
-                g = jnp.where(here, gain[level : level + 1, at], g)
-                c = jnp.where(here, bias[level : level + 1, at], c)
-            mapped[part, at] = ((b[:, at].astype(F32) * scale[part]) * g + c).astype(BF16)
-            row += b.shape[0]
-        term = lax.dot_general(mapped[:, at], head[:, at], NT, preferred_element_type=F32)
-        logits = term if logits is None else logits + term
+    for i in late:
+        map_rows(blocks[i], gain, bias, mapped, i * blocks[i].shape[0])
+    logits = lax.dot_general(mapped[...], head[...], NT, preferred_element_type=F32)
     prob = jnp.exp(logits - norm)
     columns = me * voc + lax.broadcasted_iota(jnp.int32, (rows, voc), 1)
     slopes[:rows, :] = jnp.where(columns == target, prob - 1.0, prob).astype(BF16)
@@ -250,19 +294,27 @@
         mapped[:, at] = (back[:rows] * wide).astype(BF16)
         out[levels : 2 * levels, at] = add3(back[rows:])
     out[:levels, :width] = add3(jnp.dot(scaled, mapped[...], preferred_element_type=F32))
-
-
-def main(blocks, tied_head, depth_gain, depth_bias, loop):
-    levels = depth_gain.shape[0]
-    voc, width = tied_head.shape
+    middle = out.shape[1] // 2
+    low, high = out[:, :middle], out[:, middle:]
+    keep[...] = jnp.where(core == 0, low, high)
+    give[...] = jnp.where(core == 0, high, low)
+
+
+def main(blocks, head, gain, bias, mapped, late, loop):
+    levels = gain.shape[0]
+    voc, width = head.shape
     rows = sum(b.shape[0] for b in blocks)
+    columns = width + rows
+    half = pltpu.VMEM((2 * levels, columns // 2), F32)
+    operands = list(blocks) + [head, gain, bias] + ([] if mapped is None else [mapped])
     return pl.pallas_call(
-        functools.partial(main_kernel, loop, levels, len(blocks)),
-        out_shape=pltpu.VMEM((2 * levels, width + rows), F32),
-        in_specs=[VMEM] * (len(blocks) + 3),
-        out_specs=VMEM,
+        functools.partial(main_kernel, loop, levels, len(blocks), late),
+        out_shape=(half, half, pltpu.VMEM((rows, width), BF16)),
+        in_specs=[VMEM] * len(operands),
+        out_specs=(VMEM, VMEM, VMEM),
+        input_output_aliases={} if mapped is None else {len(operands) - 1: 2},
         scratch_shapes=[
-            pltpu.VMEM((rows, width), BF16),
+            pltpu.VMEM((2 * levels, columns), F32),
             pltpu.VMEM((rows + 16, voc), BF16),
         ],
         compiler_params=pltpu.CompilerParams(vmem_limit_bytes=20 << 20),
@@ -271,23 +323,27 @@
             bytes_accessed=2 * voc * width,
             transcendentals=rows * voc,
         ),
-    )(*blocks, tied_head, depth_gain, depth_bias)
-
-
-def sum_over_loop(total, loop):
-    total = total + lax.ppermute(total, "loop", [(i, i ^ 1) for i in range(loop)])
+    )(*operands)[:2]
+
+
+def sum_over_loop(keep, give, loop):
+    swap = lambda x: lax.ppermute(x, "loop", [(i, i ^ 1) for i in range(loop)])
+    total = keep + swap(give)
     bit = 2
     while bit < loop:
         pairs = [(i, i ^ bit) for i in range(loop)]
         total = lax.reduce_precision(total, 8, 7)
         total = total + lax.ppermute(total.astype(BF16), "loop", pairs).astype(F32)
         bit *= 2
-    return total
-
-
-def last_kernel(levels, rows, buf, mass_out, gain_out, bias_out, line, sems):
+    return total, swap(total)
+
+
+def last_kernel(levels, rows, kept, given, mass_out, gain_out, bias_out, buf, line, sems):
     width = gain_out.shape[1]
     me = lax.axis_index("loop")
+    middle = kept.shape[1]
+    buf[:, :middle] = jnp.where(me % 2 == 0, kept[...], given[...])
+    buf[:, middle:] = jnp.where(me % 2 == 0, given[...], kept[...])
     every = buf[0:1, width:]
     spread = lax.broadcasted_iota(jnp.int32, (every.shape[1], LANES), 0)
     target = lax.broadcasted_iota(jnp.int32, (every.shape[1], LANES), 1)
@@ -306,19 +362,20 @@
         copy.wait()
 
 
-def last(total, levels, width, rows):
+def last(kept, given, levels, width, rows):
     grad = pltpu.HBM((levels, width), F32)
     mass, gain, bias = pl.pallas_call(
         functools.partial(last_kernel, levels, rows),
         out_shape=(pltpu.HBM((1, rows), F32), grad, grad),
-        in_specs=[VMEM],
+        in_specs=[VMEM, VMEM],
         out_specs=(HBM, HBM, HBM),
         scratch_shapes=[
+            pltpu.VMEM((kept.shape[0], 2 * kept.shape[1]), F32),
             pltpu.VMEM((1, rows), F32),
             pltpu.SemaphoreType.DMA((3,)),
         ],
         compiler_params=pltpu.CompilerParams(vmem_limit_bytes=8 << 20),
-    )(total)
+    )(kept, given)
     return mass.reshape(rows), gain, bias
 
 
@@ -326,12 +383,16 @@
     rows_dev, width = hidden.shape
     levels = depth_gain.shape[0]
     block, gain, bias = prep(hidden, exit_depth, teacher, normalizer, depth_gain, depth_bias)
-    blocks, head = gather_blocks(block, loop, load(tied_head))
+    rows = rows_dev * loop
+    early = rows_dev % 16 == 0 and loop == 16
+    mapper = functools.partial(map_early, rows, gain, bias) if early else None
+    blocks, head, mapped, late = gather_blocks(block, loop, load(tied_head), mapper)
     if rows_dev % 16:
         whole = jnp.concatenate(blocks, axis=0)
-        blocks = [whole[i : i + 16] for i in range(0, whole.shape[0], 16)]
-    part = main(blocks, head, gain, bias, loop)
-    return last(sum_over_loop(part, loop), levels, width, rows_dev)
+        blocks = [whole[i : i + 16] for i in range(0, rows, 16)]
+        late = range(len(blocks))
+    keep, give = main(blocks, head, gain, bias, mapped, late, loop)
+    return last(*sum_over_loop(keep, give, loop), levels, width, rows_dev)
 
 
 def solution(mesh):

time: 52.1 us -> 51.2 us (0.983)
  waiting for transfers between devices: 16.9 us -> 15.9 us
    ppermute x15, waiting for transfers between devices: 7.35 us -> 5.72 us  [gather_blocks(): send = lambda x, pairs: lax.ppermute(x, 'loop', pairs)]
    ppermute x3, starting transfers between devices: 6.83 us -> 5.27 us  [sum_over_loop(): total = total + lax.ppermute(total.astype(BF16), 'loop', pairs).astype(F32)]
    ppermute x1 -> x2, waiting for transfers between devices: 1.28 us -> 2.21 us  [sum_over_loop(): swap = lambda x: lax.ppermute(x, 'loop', [(i, i ^ 1) for i in range(loop)])]
    ppermute x15, starting transfers between devices: 12.5 us -> 13.4 us  [gather_blocks(): send = lambda x, pairs: lax.ppermute(x, 'loop', pairs)]
    pallas_call x1 -> x3, Pallas kernels: 8.58 us -> 9.02 us  [the longest x1 7.02 us: main(): pl.pallas_call(functools.partial(main_kernel, loop, levels, len(blocks),...]
  transfers between devices with their start and end apart: 19 -> 20, of which waited for: 9 -> 10; matrix products, arithmetic and copies ran while one was open for 0% -> 0% of each run, Pallas kernels for 8% -> 12%
where the time goes in v5:
time: 51.2 us; the launch traced here: 51 us
  starting transfers between devices  19.1 us (37%)
  waiting for transfers between devices  15.9 us (31%)
  Pallas kernels  15.1 us (29%)
  between operations  0.75 us (1%)
    ppermute x15, starting transfers between devices, gather_blocks(): send = lambda x, pairs: lax.ppermute(x, 'loop', pairs)  13.4 us
    ppermute x3, waiting for transfers between devices, sum_over_loop(): total = total + lax.ppermute(total.astype(BF16), 'loop', pairs).astype(F32)  7.96 us
    pallas_call x1, Pallas kernels, main(): pl.pallas_call(functools.partial(main_kernel, loop, levels, len(blocks),...  7.02 us
    ppermute x15, waiting for transfers between devices, gather_blocks(): send = lambda x, pairs: lax.ppermute(x, 'loop', pairs)  5.72 us
    ppermute x3, starting transfers between devices, sum_over_loop(): total = total + lax.ppermute(total.astype(BF16), 'loop', pairs).astype(F32)  5.27 us
    pallas_call x1, Pallas kernels, load(): pl.pallas_call(load_kernel, out_shape=pltpu.VMEM(tied_head.shape, BF16),...  4.24 us
    ppermute x2, waiting for transfers between devices, sum_over_loop(): swap = lambda x: lax.ppermute(x, 'loop', [(i, i ^ 1) for i in range(loop)])  2.21 us
    pallas_call x2, Pallas kernels, map_early(): pl.pallas_call(functools.partial(map_kernel, places), out_shape=pltpu.VME...  2 us
  transfers between devices with their start and end apart: 20, of which 10 were waited for; matrix products, arithmetic and copies ran while one was open for 0% of the time, Pallas kernels for 12%

profile of v5, /device:TPU:0, one launch (start us, length us, event | category | flops | bytes accessed | tf_op | source)
XLA Modules:
  0.0 51.0 jit_solution(1586435634283868654)
XLA Ops:
  0.6 1.1 %shard_map.94 = (bf16[16,5504]{1,0:T(8,128)(2,1)S(1)}, f32[4,5376]{1,0:T(4,128)S(1)}, f32[4,5376]{1,0:T(4,128)S(1)}) custom-call(bf16[16,5376]{1,0:T(8,128)(2,1)} %hidden.1, s32[1,16]{1,0:T(1,128)} %bitcast.4, s32[1,16]{1,0:T(1,128)} %bitcast.5, f32[1,16]{1,0:T(1,128)} %bitcast.6, f32[4,5376]{1,0:T(4,128)} %depth_gain.1, f32[4,5376]{1,0:T(4,128)} %depth_bias.1), custom_call_target="tpu_custom_call" | custom-call | tf_op jit(solution)/shard_map/pallas_call | solution.py:86
  1.8 0.5 %collective-permute-start.2 = (bf16[16,5504]{1,0:T(8,128)(2,1)S(1)}, bf16[16,5504]{1,0:T(8,128)(2,1)S(1)}, u32[]{:S(2)}, u32[]{:S(2)}) collective-permute-start(bf16[16,5504]{1,0:T(8,128)(2,1)S(1)} %get-tuple-element.19.refs_0_), channel_id=1, source_target_pairs={{0,1},{1,0},{2,3},{3,2},{4,5},{5,4},{6,7},{7,6},{8,9},{9,8},{10,11... | collective-permute-start | bytes 528392 | tf_op jit(solution)/shard_map/ppermute | solution.py:130
  2.3 2.6 %collective-permute-start.1 = (bf16[16,5504]{1,0:T(8,128)(2,1)S(1)}, bf16[16,5504]{1,0:T(8,128)(2,1)S(1)}, u32[]{:S(2)}, u32[]{:S(2)}) collective-permute-start(bf16[16,5504]{1,0:T(8,128)(2,1)S(1)} %get-tuple-element.19.refs_0_), channel_id=1, source_target_pairs={{1,5},{4,0},{5,9},{8,4},{9,13},{12,8},{13,15},{14,12},{15,11},{10,... | collective-permute-start | bytes 528392 | tf_op jit(solution)/shard_map/ppermute | solution.py:130
  4.9 1.4 %collective-permute-start = (bf16[16,5504]{1,0:T(8,128)(2,1)S(1)}, bf16[16,5504]{1,0:T(8,128)(2,1)S(1)}, u32[]{:S(2)}, u32[]{:S(2)}) collective-permute-start(bf16[16,5504]{1,0:T(8,128)(2,1)S(1)} %get-tuple-element.19.refs_0_), channel_id=1, source_target_pairs={{0,5},{5,0},{4,9},{9,4},{8,13},{13,8},{12,15},{15,12},{14,11},{11,... | collective-permute-start | bytes 528392 | tf_op jit(solution)/shard_map/ppermute | solution.py:130
  6.3 4.2 %shard_map.95.refs_16_ = bf16[1024,5376]{1,0:T(8,128)(2,1)S(1)} custom-call(bf16[1024,5376]{1,0:T(8,128)(2,1)} %head_hbm.1), custom_call_target="tpu_custom_call" | custom-call | bytes 22020096 | tf_op jit(solution)/shard_map/pallas_call | solution.py:226
  10.5 0.0 collective-permute-done.2.refs_1_.refs_8_
  10.5 0.0 collective-permute-done.1.refs_3_.refs_1_
  10.5 0.0 collective-permute-done.refs_2_.refs_9_
  10.6 1.5 %collective-permute-start.8 = (bf16[16,5504]{1,0:T(8,128)(2,1)S(1)}, bf16[16,5504]{1,0:T(8,128)(2,1)S(1)}, u32[]{:S(2)}, u32[]{:S(2)}) collective-permute-start(bf16[16,5504]{1,0:T(8,128)(2,1)S(1)} %collective-permute-done.refs_2_.refs_9_), channel_id=1, source_target_pairs={{1,4},{4,1},{5,8},{8,5},{9,12},{12,9},{13,14},{14,13},{15,10},{10,... | collective-permute-start | bytes 528392 | tf_op jit(solution)/shard_map/ppermute | solution.py:130
  12.1 0.3 collective-permute-start.3
  12.4 0.3 collective-permute-start.7
  12.7 2.8 %collective-permute-done.8.refs_0_.refs_6_ = bf16[16,5504]{1,0:T(8,128)(2,1)S(1)} collective-permute-done((bf16[16,5504]{1,0:T(8,128)(2,1)S(1)}, bf16[16,5504]{1,0:T(8,128)(2,1)S(1)}, u32[]{:S(2)}, u32[]{:S(2)}) %collective-permute-start.8) | collective-permute-done | bytes 176160 | tf_op jit(solution)/shard_map/ppermute | solution.py:130
  15.5 1.5 %collective-permute-start.9 = (bf16[16,5504]{1,0:T(8,128)(2,1)S(1)}, bf16[16,5504]{1,0:T(8,128)(2,1)S(1)}, u32[]{:S(2)}, u32[]{:S(2)}) collective-permute-start(bf16[16,5504]{1,0:T(8,128)(2,1)S(1)} %collective-permute-done.8.refs_0_.refs_6_), channel_id=1, source_target_pairs={{0,5},{5,0},{4,9},{9,4},{8,13},{13,8},{12,15},{15,12},{14,11},{11,... | collective-permute-start | bytes 528392 | tf_op jit(solution)/shard_map/ppermute | solution.py:130
  17.0 0.2 collective-permute-start.6
  17.2 0.2 collective-permute-done.3.refs_1_.refs_14_
  17.4 1.4 %collective-permute-start.5 = (bf16[16,5504]{1,0:T(8,128)(2,1)S(1)}, bf16[16,5504]{1,0:T(8,128)(2,1)S(1)}, u32[]{:S(2)}, u32[]{:S(2)}) collective-permute-start(bf16[16,5504]{1,0:T(8,128)(2,1)S(1)} %collective-permute-done.3.refs_1_.refs_14_), channel_id=1, source_target_pairs={{0,5},{5,0},{4,9},{9,4},{8,13},{13,8},{12,15},{15,12},{14,11},{11,... | collective-permute-start | bytes 528392 | tf_op jit(solution)/shard_map/ppermute | solution.py:130
  18.8 0.3 collective-permute-start.4
  19.1 0.0 collective-permute-done.7.refs_5_.refs_15_
  19.1 0.2 collective-permute-start.11
  19.3 1.1 %collective-permute-done.9.refs_4_.refs_11_ = bf16[16,5504]{1,0:T(8,128)(2,1)S(1)} collective-permute-done((bf16[16,5504]{1,0:T(8,128)(2,1)S(1)}, bf16[16,5504]{1,0:T(8,128)(2,1)S(1)}, u32[]{:S(2)}, u32[]{:S(2)}) %collective-permute-start.9) | collective-permute-done | bytes 176160 | tf_op jit(solution)/shard_map/ppermute | solution.py:130
  20.4 2.1 %collective-permute-start.10 = (bf16[16,5504]{1,0:T(8,128)(2,1)S(1)}, bf16[16,5504]{1,0:T(8,128)(2,1)S(1)}, u32[]{:S(2)}, u32[]{:S(2)}) collective-permute-start(bf16[16,5504]{1,0:T(8,128)(2,1)S(1)} %collective-permute-done.9.refs_4_.refs_11_), channel_id=1, source_target_pairs={{1,4},{4,1},{5,8},{8,5},{9,12},{12,9},{13,14},{14,13},{15,10},{10,... | collective-permute-start | bytes 528392 | tf_op jit(solution)/shard_map/ppermute | solution.py:130
  22.4 0.0 collective-permute-done.6.refs_4_.refs_7_
  22.4 1.0 %shard_map.96.refs_8_ = bf16[256,5376]{1,0:T(8,128)(2,1)S(1)} custom-call(bf16[16,5504]{1,0:T(8,128)(2,1)S(1)} %get-tuple-element.19.refs_0_, bf16[16,5504]{1,0:T(8,128)(2,1)S(1)} %collective-permute-done.2.refs_1_.refs_8_, bf16[16,5504]{1,0:T(8,128)(2,1)S(1)} %collective-permute-done.refs_2_.refs_9_, ...), custom_call_target="tpu_custom_call" | custom-call | flops 10321920 | bytes 2064384 | tf_op jit(solution)/shard_map/pallas_call | solution.py:197
  23.4 0.0 collective-permute-done.5.refs_5_.refs_3_
  23.5 0.1 collective-permute-start.14
  23.5 0.5 collective-permute-start.12
  24.0 0.0 collective-permute-done.4.refs_3_.refs_2_
  24.0 0.0 collective-permute-done.11.refs_2_.refs_10_
  24.0 1.0 %shard_map.97.refs_19_ = bf16[256,5376]{1,0:T(8,128)(2,1)S(1)} custom-call(bf16[16,5504]{1,0:T(8,128)(2,1)S(1)} %collective-permute-done.8.refs_0_.refs_6_, bf16[16,5504]{1,0:T(8,128)(2,1)S(1)} %collective-permute-done.3.refs_1_.refs_14_, bf16[16,5504]{1,0:T(8,128)(2,1)S(1)} %collective-permute-done.11.refs_2_.refs_10_, ...), custom_call_target="tpu_custom_call", output_to_operand_aliasing={{}: (8, {})} | custom-call | flops 10321920 | bytes 2064384 | tf_op jit(solution)/shard_map/pallas_call | solution.py:197
  25.0 0.5 %collective-permute-done.10.refs_4_ = bf16[16,5504]{1,0:T(8,128)(2,1)S(1)} collective-permute-done((bf16[16,5504]{1,0:T(8,128)(2,1)S(1)}, bf16[16,5504]{1,0:T(8,128)(2,1)S(1)}, u32[]{:S(2)}, u32[]{:S(2)}) %collective-permute-start.10) | collective-permute-done | bytes 176160 | tf_op jit(solution)/shard_map/ppermute | solution.py:130
  25.6 0.6 %collective-permute-start.13 = (bf16[16,5504]{1,0:T(8,128)(2,1)S(1)}, bf16[16,5504]{1,0:T(8,128)(2,1)S(1)}, u32[]{:S(2)}, u32[]{:S(2)}) collective-permute-start(bf16[16,5504]{1,0:T(8,128)(2,1)S(1)} %collective-permute-done.10.refs_4_), channel_id=1, source_target_pairs={{0,1},{1,0},{2,3},{3,2},{4,5},{5,4},{6,7},{7,6},{8,9},{9,8},{10,11... | collective-permute-start | bytes 528392 | tf_op jit(solution)/shard_map/ppermute | solution.py:130
  26.1 0.0 collective-permute-done.12.refs_5_
  26.1 0.0 collective-permute-done.14.refs_13_
  26.1 1.0 %collective-permute-done.13.refs_12_ = bf16[16,5504]{1,0:T(8,128)(2,1)S(1)} collective-permute-done((bf16[16,5504]{1,0:T(8,128)(2,1)S(1)}, bf16[16,5504]{1,0:T(8,128)(2,1)S(1)}, u32[]{:S(2)}, u32[]{:S(2)}) %collective-permute-start.13) | collective-permute-done | bytes 176160 | tf_op jit(solution)/shard_map/ppermute | solution.py:130
  27.2 7.0 %shard_map.98 = (f32[8,2816]{1,0:T(8,128)S(1)}, f32[8,2816]{1,0:T(8,128)S(1)}, bf16[256,5376]{1,0:T(8,128)(2,1)S(1)}) custom-call(bf16[16,5504]{1,0:T(8,128)(2,1)S(1)} %get-tuple-element.19.refs_0_, bf16[16,5504]{1,0:T(8,128)(2,1)S(1)} %collective-permute-done.1.refs_3_.refs_1_, ...), custom_call_target="tpu_custom_call", output_to_operand_aliasing={{2}: (19, {})} | custom-call | flops 5637144576 | bytes 11010048 | tf_op jit(solution)/shard_map/pallas_call | solution.py:310
  34.2 0.4 collective-permute-start.15
  34.6 0.9 %collective-permute-done.15 = f32[8,2816]{1,0:T(8,128)S(1)} collective-permute-done((f32[8,2816]{1,0:T(8,128)S(1)}, f32[8,2816]{1,0:T(8,128)S(1)}, u32[]{:S(2)}, u32[]{:S(2)}) %collective-permute-start.15) | collective-permute-done | bytes 90144 | tf_op jit(solution)/shard_map/ppermute | solution.py:330
  35.6 1.6 %collective-permute-start.16 = (bf16[8,2816]{1,0:T(8,128)(2,1)S(1)}, bf16[8,2816]{1,0:T(8,128)(2,1)S(1)}, u32[]{:S(2)}, u32[]{:S(2)}) collective-permute-start(bf16[8,2816]{1,0:T(8,128)(2,1)S(1)} %get-tuple-element.35), channel_id=1, source_target_pairs={{0,2},{1,3},{2,0},{3,1},{4,6},{5,7},{6,4},{7,5},{8,10},{9,11},{10,... | collective-permute-start | bytes 135176 | tf_op jit(solution)/shard_map/ppermute | solution.py:336
  37.2 2.5 %collective-permute-done.16 = bf16[8,2816]{1,0:T(8,128)(2,1)S(1)} collective-permute-done((bf16[8,2816]{1,0:T(8,128)(2,1)S(1)}, bf16[8,2816]{1,0:T(8,128)(2,1)S(1)}, u32[]{:S(2)}, u32[]{:S(2)}) %collective-permute-start.16) | collective-permute-done | bytes 45088 | tf_op jit(solution)/shard_map/ppermute | solution.py:336
  39.7 1.4 %collective-permute-start.17 = (bf16[8,2816]{1,0:T(8,128)(2,1)S(1)}, bf16[8,2816]{1,0:T(8,128)(2,1)S(1)}, u32[]{:S(2)}, u32[]{:S(2)}) collective-permute-start(bf16[8,2816]{1,0:T(8,128)(2,1)S(1)} %fusion), channel_id=1, source_target_pairs={{0,4},{1,5},{2,6},{3,7},{4,0},{5,1},{6,2},{7,3},{8,12},{9,13},{10,... | collective-permute-start | bytes 135176 | tf_op jit(solution)/shard_map/ppermute | solution.py:336
  41.1 2.7 %collective-permute-done.17 = bf16[8,2816]{1,0:T(8,128)(2,1)S(1)} collective-permute-done((bf16[8,2816]{1,0:T(8,128)(2,1)S(1)}, bf16[8,2816]{1,0:T(8,128)(2,1)S(1)}, u32[]{:S(2)}, u32[]{:S(2)}) %collective-permute-start.17) | collective-permute-done | bytes 45088 | tf_op jit(solution)/shard_map/ppermute | solution.py:336
  43.9 2.3 %collective-permute-start.18 = (bf16[8,2816]{1,0:T(8,128)(2,1)S(1)}, bf16[8,2816]{1,0:T(8,128)(2,1)S(1)}, u32[]{:S(2)}, u32[]{:S(2)}) collective-permute-start(bf16[8,2816]{1,0:T(8,128)(2,1)S(1)} %fusion.1), channel_id=1, source_target_pairs={{0,8},{1,9},{2,10},{3,11},{4,12},{5,13},{6,14},{7,15},{8,0},{9,1},... | collective-permute-start | bytes 135176 | tf_op jit(solution)/shard_map/ppermute | solution.py:336
  46.1 2.8 %collective-permute-done.18 = bf16[8,2816]{1,0:T(8,128)(2,1)S(1)} collective-permute-done((bf16[8,2816]{1,0:T(8,128)(2,1)S(1)}, bf16[8,2816]{1,0:T(8,128)(2,1)S(1)}, u32[]{:S(2)}, u32[]{:S(2)}) %collective-permute-start.18) | collective-permute-done | bytes 45088 | tf_op jit(solution)/shard_map/ppermute | solution.py:336
  48.9 0.1 collective-permute-start.19
  49.0 1.3 %collective-permute-done.19.given = f32[8,2816]{1,0:T(8,128)S(1)} collective-permute-done((f32[8,2816]{1,0:T(8,128)S(1)}, f32[8,2816]{1,0:T(8,128)S(1)}, u32[]{:S(2)}, u32[]{:S(2)}) %collective-permute-start.19) | collective-permute-done | bytes 90144 | tf_op jit(solution)/shard_map/ppermute | solution.py:330
  50.3 0.7 %shard_map.99 = (f32[1,16]{1,0:T(1,128)}, f32[4,5376]{1,0:T(4,128)}, f32[4,5376]{1,0:T(4,128)}) custom-call(f32[8,2816]{1,0:T(8,128)S(1)} %convert_add_fusion.kept, f32[8,2816]{1,0:T(8,128)S(1)} %collective-permute-done.19.given), custom_call_target="tpu_custom_call" | custom-call | tf_op jit(solution)/shard_map/pallas_call | solution.py:367
  (4 shorter events, 0.1 us)
Async XLA Ops:
  1.8 8.8 %collective-permute-start.2 = (bf16[16,5504]{1,0:T(8,128)(2,1)S(1)}, bf16[16,5504]{1,0:T(8,128)(2,1)S(1)}, u32[]{:S(2)}, u32[]{:S(2)}) collective-permute-start(bf16[16,5504]{1,0:T(8,128)(2,1)S(1)} %get-tuple-element.19.refs_0_), channel_id=1, source_target_pairs={{0,1},{1,0},{2,3},{3,2},{4,5},{5,4},{6,7},{7,6},{8,9},{9,8},{10,11... | collective-permute-start | bytes 528392 | tf_op jit(solution)/shard_map/ppermute | solution.py:130
  2.3 8.2 %collective-permute-start.1 = (bf16[16,5504]{1,0:T(8,128)(2,1)S(1)}, bf16[16,5504]{1,0:T(8,128)(2,1)S(1)}, u32[]{:S(2)}, u32[]{:S(2)}) collective-permute-start(bf16[16,5504]{1,0:T(8,128)(2,1)S(1)} %get-tuple-element.19.refs_0_), channel_id=1, source_target_pairs={{1,5},{4,0},{5,9},{8,4},{9,13},{12,8},{13,15},{14,12},{15,11},{10,... | collective-permute-start | bytes 528392 | tf_op jit(solution)/shard_map/ppermute | solution.py:130
  4.9 5.7 %collective-permute-start = (bf16[16,5504]{1,0:T(8,128)(2,1)S(1)}, bf16[16,5504]{1,0:T(8,128)(2,1)S(1)}, u32[]{:S(2)}, u32[]{:S(2)}) collective-permute-start(bf16[16,5504]{1,0:T(8,128)(2,1)S(1)} %get-tuple-element.19.refs_0_), channel_id=1, source_target_pairs={{0,5},{5,0},{4,9},{9,4},{8,13},{13,8},{12,15},{15,12},{14,11},{11,... | collective-permute-start | bytes 528392 | tf_op jit(solution)/shard_map/ppermute | solution.py:130
  10.6 4.9 %collective-permute-start.8 = (bf16[16,5504]{1,0:T(8,128)(2,1)S(1)}, bf16[16,5504]{1,0:T(8,128)(2,1)S(1)}, u32[]{:S(2)}, u32[]{:S(2)}) collective-permute-start(bf16[16,5504]{1,0:T(8,128)(2,1)S(1)} %collective-permute-done.refs_2_.refs_9_), channel_id=1, source_target_pairs={{1,4},{4,1},{5,8},{8,5},{9,12},{12,9},{13,14},{14,13},{15,10},{10,... | collective-permute-start | bytes 528392 | tf_op jit(solution)/shard_map/ppermute | solution.py:130
  12.1 5.3 %collective-permute-start.3 = (bf16[16,5504]{1,0:T(8,128)(2,1)S(1)}, bf16[16,5504]{1,0:T(8,128)(2,1)S(1)}, u32[]{:S(2)}, u32[]{:S(2)}) collective-permute-start(bf16[16,5504]{1,0:T(8,128)(2,1)S(1)} %collective-permute-done.1.refs_3_.refs_1_), channel_id=1, source_target_pairs={{1,4},{4,1},{5,8},{8,5},{9,12},{12,9},{13,14},{14,13},{15,10},{10,... | collective-permute-start | bytes 528392 | tf_op jit(solution)/shard_map/ppermute | solution.py:130
  12.4 6.7 %collective-permute-start.7 = (bf16[16,5504]{1,0:T(8,128)(2,1)S(1)}, bf16[16,5504]{1,0:T(8,128)(2,1)S(1)}, u32[]{:S(2)}, u32[]{:S(2)}) collective-permute-start(bf16[16,5504]{1,0:T(8,128)(2,1)S(1)} %collective-permute-done.1.refs_3_.refs_1_), channel_id=1, source_target_pairs={{0,1},{1,0},{2,3},{3,2},{4,5},{5,4},{6,7},{7,6},{8,9},{9,8},{10,11... | collective-permute-start | bytes 528392 | tf_op jit(solution)/shard_map/ppermute | solution.py:130
  15.5 4.9 %collective-permute-start.9 = (bf16[16,5504]{1,0:T(8,128)(2,1)S(1)}, bf16[16,5504]{1,0:T(8,128)(2,1)S(1)}, u32[]{:S(2)}, u32[]{:S(2)}) collective-permute-start(bf16[16,5504]{1,0:T(8,128)(2,1)S(1)} %collective-permute-done.8.refs_0_.refs_6_), channel_id=1, source_target_pairs={{0,5},{5,0},{4,9},{9,4},{8,13},{13,8},{12,15},{15,12},{14,11},{11,... | collective-permute-start | bytes 528392 | tf_op jit(solution)/shard_map/ppermute | solution.py:130
  17.0 5.4 %collective-permute-start.6 = (bf16[16,5504]{1,0:T(8,128)(2,1)S(1)}, bf16[16,5504]{1,0:T(8,128)(2,1)S(1)}, u32[]{:S(2)}, u32[]{:S(2)}) collective-permute-start(bf16[16,5504]{1,0:T(8,128)(2,1)S(1)} %collective-permute-done.refs_2_.refs_9_), channel_id=1, source_target_pairs={{0,1},{1,0},{2,3},{3,2},{4,5},{5,4},{6,7},{7,6},{8,9},{9,8},{10,11... | collective-permute-start | bytes 528392 | tf_op jit(solution)/shard_map/ppermute | solution.py:130
  17.4 6.1 %collective-permute-start.5 = (bf16[16,5504]{1,0:T(8,128)(2,1)S(1)}, bf16[16,5504]{1,0:T(8,128)(2,1)S(1)}, u32[]{:S(2)}, u32[]{:S(2)}) collective-permute-start(bf16[16,5504]{1,0:T(8,128)(2,1)S(1)} %collective-permute-done.3.refs_1_.refs_14_), channel_id=1, source_target_pairs={{0,5},{5,0},{4,9},{9,4},{8,13},{13,8},{12,15},{15,12},{14,11},{11,... | collective-permute-start | bytes 528392 | tf_op jit(solution)/shard_map/ppermute | solution.py:130
  18.8 5.3 %collective-permute-start.4 = (bf16[16,5504]{1,0:T(8,128)(2,1)S(1)}, bf16[16,5504]{1,0:T(8,128)(2,1)S(1)}, u32[]{:S(2)}, u32[]{:S(2)}) collective-permute-start(bf16[16,5504]{1,0:T(8,128)(2,1)S(1)} %collective-permute-done.3.refs_1_.refs_14_), channel_id=1, source_target_pairs={{0,1},{1,0},{2,3},{3,2},{4,5},{5,4},{6,7},{7,6},{8,9},{9,8},{10,11... | collective-permute-start | bytes 528392 | tf_op jit(solution)/shard_map/ppermute | solution.py:130
  19.1 4.9 %collective-permute-start.11 = (bf16[16,5504]{1,0:T(8,128)(2,1)S(1)}, bf16[16,5504]{1,0:T(8,128)(2,1)S(1)}, u32[]{:S(2)}, u32[]{:S(2)}) collective-permute-start(bf16[16,5504]{1,0:T(8,128)(2,1)S(1)} %collective-permute-done.8.refs_0_.refs_6_), channel_id=1, source_target_pairs={{0,1},{1,0},{2,3},{3,2},{4,5},{5,4},{6,7},{7,6},{8,9},{9,8},{10,11... | collective-permute-start | bytes 528392 | tf_op jit(solution)/shard_map/ppermute | solution.py:130
  20.4 5.2 %collective-permute-start.10 = (bf16[16,5504]{1,0:T(8,128)(2,1)S(1)}, bf16[16,5504]{1,0:T(8,128)(2,1)S(1)}, u32[]{:S(2)}, u32[]{:S(2)}) collective-permute-start(bf16[16,5504]{1,0:T(8,128)(2,1)S(1)} %collective-permute-done.9.refs_4_.refs_11_), channel_id=1, source_target_pairs={{1,4},{4,1},{5,8},{8,5},{9,12},{12,9},{13,14},{14,13},{15,10},{10,... | collective-permute-start | bytes 528392 | tf_op jit(solution)/shard_map/ppermute | solution.py:130
  23.5 2.7 %collective-permute-start.14 = (bf16[16,5504]{1,0:T(8,128)(2,1)S(1)}, bf16[16,5504]{1,0:T(8,128)(2,1)S(1)}, u32[]{:S(2)}, u32[]{:S(2)}) collective-permute-start(bf16[16,5504]{1,0:T(8,128)(2,1)S(1)} %collective-permute-done.5.refs_5_.refs_3_), channel_id=1, source_target_pairs={{0,1},{1,0},{2,3},{3,2},{4,5},{5,4},{6,7},{7,6},{8,9},{9,8},{10,11... | collective-permute-start | bytes 528392 | tf_op jit(solution)/shard_map/ppermute | solution.py:130
  23.5 2.6 %collective-permute-start.12 = (bf16[16,5504]{1,0:T(8,128)(2,1)S(1)}, bf16[16,5504]{1,0:T(8,128)(2,1)S(1)}, u32[]{:S(2)}, u32[]{:S(2)}) collective-permute-start(bf16[16,5504]{1,0:T(8,128)(2,1)S(1)} %collective-permute-done.9.refs_4_.refs_11_), channel_id=1, source_target_pairs={{0,1},{1,0},{2,3},{3,2},{4,5},{5,4},{6,7},{7,6},{8,9},{9,8},{10,11... | collective-permute-start | bytes 528392 | tf_op jit(solution)/shard_map/ppermute | solution.py:130
  25.6 1.6 %collective-permute-start.13 = (bf16[16,5504]{1,0:T(8,128)(2,1)S(1)}, bf16[16,5504]{1,0:T(8,128)(2,1)S(1)}, u32[]{:S(2)}, u32[]{:S(2)}) collective-permute-start(bf16[16,5504]{1,0:T(8,128)(2,1)S(1)} %collective-permute-done.10.refs_4_), channel_id=1, source_target_pairs={{0,1},{1,0},{2,3},{3,2},{4,5},{5,4},{6,7},{7,6},{8,9},{9,8},{10,11... | collective-permute-start | bytes 528392 | tf_op jit(solution)/shard_map/ppermute | solution.py:130
  34.2 1.4 %collective-permute-start.15 = (f32[8,2816]{1,0:T(8,128)S(1)}, f32[8,2816]{1,0:T(8,128)S(1)}, u32[]{:S(2)}, u32[]{:S(2)}) collective-permute-start(f32[8,2816]{1,0:T(8,128)S(1)} %get-tuple-element.31), channel_id=1, source_target_pairs={{0,1},{1,0},{2,3},{3,2},{4,5},{5,4},{6,7},{7,6},{8,9},{9,8},{10,11... | collective-permute-start | bytes 270344 | tf_op jit(solution)/shard_map/ppermute | solution.py:330
  35.6 4.1 %collective-permute-start.16 = (bf16[8,2816]{1,0:T(8,128)(2,1)S(1)}, bf16[8,2816]{1,0:T(8,128)(2,1)S(1)}, u32[]{:S(2)}, u32[]{:S(2)}) collective-permute-start(bf16[8,2816]{1,0:T(8,128)(2,1)S(1)} %get-tuple-element.35), channel_id=1, source_target_pairs={{0,2},{1,3},{2,0},{3,1},{4,6},{5,7},{6,4},{7,5},{8,10},{9,11},{10,... | collective-permute-start | bytes 135176 | tf_op jit(solution)/shard_map/ppermute | solution.py:336
  39.7 4.1 %collective-permute-start.17 = (bf16[8,2816]{1,0:T(8,128)(2,1)S(1)}, bf16[8,2816]{1,0:T(8,128)(2,1)S(1)}, u32[]{:S(2)}, u32[]{:S(2)}) collective-permute-start(bf16[8,2816]{1,0:T(8,128)(2,1)S(1)} %fusion), channel_id=1, source_target_pairs={{0,4},{1,5},{2,6},{3,7},{4,0},{5,1},{6,2},{7,3},{8,12},{9,13},{10,... | collective-permute-start | bytes 135176 | tf_op jit(solution)/shard_map/ppermute | solution.py:336
  43.9 5.0 %collective-permute-start.18 = (bf16[8,2816]{1,0:T(8,128)(2,1)S(1)}, bf16[8,2816]{1,0:T(8,128)(2,1)S(1)}, u32[]{:S(2)}, u32[]{:S(2)}) collective-permute-start(bf16[8,2816]{1,0:T(8,128)(2,1)S(1)} %fusion.1), channel_id=1, source_target_pairs={{0,8},{1,9},{2,10},{3,11},{4,12},{5,13},{6,14},{7,15},{8,0},{9,1},... | collective-permute-start | bytes 135176 | tf_op jit(solution)/shard_map/ppermute | solution.py:336
  48.9 1.4 %collective-permute-start.19 = (f32[8,2816]{1,0:T(8,128)S(1)}, f32[8,2816]{1,0:T(8,128)S(1)}, u32[]{:S(2)}, u32[]{:S(2)}) collective-permute-start(f32[8,2816]{1,0:T(8,128)S(1)} %convert_add_fusion.kept), channel_id=1, source_target_pairs={{0,1},{1,0},{2,3},{3,2},{4,5},{5,4},{6,7},{7,6},{8,9},{9,8},{10,11... | collective-permute-start | bytes 270344 | tf_op jit(solution)/shard_map/ppermute | solution.py:330

commit v6 on v5

--- a/solution.py
+++ b/solution.py
@@ -122,7 +122,7 @@
     return pairs
 
 
-def gather_blocks(block, loop, head, mapper):
+def gather_blocks(block, loop, tied_head, mapper):
     chips = loop // 2
     order = ring_of(chips)
     half = chips // 2
@@ -140,6 +140,10 @@
         if step < half:
             plain = send(plain, hop_pairs(order, step, step > 1))
         if step == 1:
+            head = load(tied_head, 0, 2)
+            crossed, plain, head = tie(crossed, plain, head)
+        if step == min(2, half):
+            head = load(tied_head, 1, 2, head)
             crossed, plain, head, first = tie(crossed, plain, head, first)
             blocks[chips] = first
         if mapper is not None and step == 3:
@@ -207,44 +211,66 @@
     )(*operands)
 
 
-def load_kernel(head_hbm, head, sems):
-    parts = sems.shape[0]
-    size = head.shape[0] // parts
-    copies = [
-        pltpu.make_async_copy(
-            head_hbm.at[pl.ds(k * size, size)], head.at[pl.ds(k * size, size)], sems.at[k]
-        )
-        for k in range(parts)
-    ]
+def load_kernel(part, parts, head_hbm, *refs):
+    head, sems = refs[-2:]
+    count = sems.shape[0]
+    size = head.shape[0] // (parts * count)
+    copies = []
+    for k in range(count):
+        at = pl.ds((part * count + k) * size, size)
+        copies.append(pltpu.make_async_copy(head_hbm.at[at], head.at[at], sems.at[k]))
     for copy in copies:
         copy.start()
     for copy in copies:
         copy.wait()
 
 
-def load(tied_head):
+def load(tied_head, part, parts, loaded=None):
+    operands = [in_hbm(tied_head)] + ([] if loaded is None else [loaded])
+    voc, width = tied_head.shape
     return pl.pallas_call(
-        load_kernel,
+        functools.partial(load_kernel, part, parts),
         out_shape=pltpu.VMEM(tied_head.shape, BF16),
-        in_specs=[HBM],
+        in_specs=[HBM] + [VMEM] * (len(operands) - 1),
         out_specs=VMEM,
+        input_output_aliases={} if loaded is None else {1: 0},
         scratch_shapes=[pltpu.SemaphoreType.DMA((4,))],
         compiler_params=pltpu.CompilerParams(vmem_limit_bytes=16 << 20),
         cost_estimate=pl.CostEstimate(
-            flops=0, bytes_accessed=4 * tied_head.shape[0] * tied_head.shape[1], transcendentals=0
+            flops=0, bytes_accessed=4 * voc * width // parts, transcendentals=0
         ),
-    )(in_hbm(tied_head))
-
-
-def main_kernel(loop, levels, count, late, *refs):
+    )(*operands)
+
+
+def half_sums(blocks, head, slopes, scaled, mass, which, work, out):
+    levels = out.shape[0] // 2
+    rows = sum(b.shape[0] for b in blocks)
+    half = head.shape[1] // 2
+    add3 = lambda x: (x[:levels] + x[levels : 2 * levels]) + x[2 * levels : 3 * levels]
+    done = 0
+    while done < half:
+        size = min(256, half - done)
+        here = slice(done, done + size)
+        at = pl.ds(pl.multiple_of(which * half + done, LANES), size)
+        back = jnp.dot(slopes[...], head[:, at], preferred_element_type=F32)
+        wide = jnp.concatenate([b[:, at] for b in blocks], axis=0).astype(F32)
+        work[:, here] = (back[:rows] * wide).astype(BF16)
+        out[levels:, here] = add3(back[rows:])
+        done += size
+    out[:levels, :half] = add3(jnp.dot(scaled, work[:, :half], preferred_element_type=F32))
+    out[:, half:] = jnp.broadcast_to(mass, (2 * levels, mass.shape[1]))
+
+
+def front_kernel(loop, levels, count, late, *refs):
     blocks = refs[:count]
     head, gain, bias = refs[count : count + 3]
-    keep, give, mapped, out, slopes = refs[-5:]
+    give, slopes, scaled_out, mass_out, mapped = refs[-5:]
     voc, width = head.shape
     rows = mapped.shape[0]
     rows_dev = rows // loop
     chips = loop // 2
     me = lax.axis_index("loop")
+    core = me % 2
     meta = jnp.concatenate([b[:, width:] for b in blocks], axis=0).astype(F32)
     col = lambda i: meta[:, i : i + 1]
     scale = (col(0) + col(1)) + col(2)
@@ -266,7 +292,6 @@
     index = lax.broadcasted_iota(jnp.int32, (rows, rows), 0)
     flip = index // (rows // 2)
     relative = (index - flip * (rows // 2)) // rows_dev
-    core = me % 2
     place = place_of(me // 2, chips) + jnp.where(core == 0, relative, chips - relative)
     place = jnp.where(place >= chips, place - chips, place)
     owner = 2 * chip_at(place, chips) + jnp.where(flip == 0, core, 1 - core)
@@ -276,74 +301,92 @@
     lines = jnp.concatenate(pieces(mass) + [jnp.zeros((13, rows), F32)], axis=0)
     moved = jnp.dot(lines.astype(BF16), move, preferred_element_type=F32)
     moved = (moved[0:1] + moved[1:2]) + moved[2:3]
-    out[:, width:] = jnp.broadcast_to(moved, (2 * levels, rows))
+    low, high = moved[:, : rows // 2], moved[:, rows // 2 :]
+    mass_out[...] = jnp.where(core == 0, low, high)
 
     lane = lax.broadcasted_iota(jnp.int32, (rows, LANES), 1).astype(F32)
     pick = jnp.where(lane == depth, 1.0, 0.0).T[:levels]
     scaled = pick * jnp.broadcast_to(scale, (rows, LANES)).T[:levels]
     none = jnp.zeros((16 - 3 * levels, rows), F32)
     scaled = jnp.concatenate(pieces(scaled) + [none], axis=0).astype(BF16)
+    scaled_out[...] = scaled
     sums = jnp.dot(pick.astype(BF16), slopes[:rows, :], preferred_element_type=F32)
     none = jnp.zeros((16 - 3 * levels, voc), F32)
     slopes[rows:, :] = jnp.concatenate(pieces(sums) + [none], axis=0).astype(BF16)
-    add3 = lambda x: (x[:levels] + x[levels : 2 * levels]) + x[2 * levels : 3 * levels]
-    for k in range(width // 256):
-        at = slice(k * 256, (k + 1) * 256)
-        back = jnp.dot(slopes[...], head[:, at], preferred_element_type=F32)
-        wide = jnp.concatenate([b[:, at] for b in blocks], axis=0).astype(F32)
-        mapped[:, at] = (back[:rows] * wide).astype(BF16)
-        out[levels : 2 * levels, at] = add3(back[rows:])
-    out[:levels, :width] = add3(jnp.dot(scaled, mapped[...], preferred_element_type=F32))
-    middle = out.shape[1] // 2
-    low, high = out[:, :middle], out[:, middle:]
-    keep[...] = jnp.where(core == 0, low, high)
-    give[...] = jnp.where(core == 0, high, low)
+    other = jnp.where(core == 0, high, low)
+    half_sums(blocks, head, slopes, scaled, other, 1 - core, mapped, give)
+
+
+def back_kernel(count, *refs):
+    blocks = refs[:count]
+    head, slopes, scaled, mass, keep, work = refs[count:]
+    core = lax.axis_index("loop") % 2
+    half_sums(blocks, head, slopes, scaled[...], mass[...], core, work, keep)
 
 
 def main(blocks, head, gain, bias, mapped, late, loop):
     levels = gain.shape[0]
     voc, width = head.shape
     rows = sum(b.shape[0] for b in blocks)
-    columns = width + rows
-    half = pltpu.VMEM((2 * levels, columns // 2), F32)
+    half = pltpu.VMEM((2 * levels, (width + rows) // 2), F32)
     operands = list(blocks) + [head, gain, bias] + ([] if mapped is None else [mapped])
-    return pl.pallas_call(
-        functools.partial(main_kernel, loop, levels, len(blocks), late),
-        out_shape=(half, half, pltpu.VMEM((rows, width), BF16)),
+    cost = lambda passes: pl.CostEstimate(
+        flops=passes * rows * voc * width, bytes_accessed=voc * width, transcendentals=0
+    )
+    give, slopes, scaled, mass, _ = pl.pallas_call(
+        functools.partial(front_kernel, loop, levels, len(blocks), late),
+        out_shape=(
+            half,
+            pltpu.VMEM((rows + 16, voc), BF16),
+            pltpu.VMEM((16, rows), BF16),
+            pltpu.VMEM((1, rows // 2), F32),
+            pltpu.VMEM((rows, width), BF16),
+        ),
         in_specs=[VMEM] * len(operands),
-        out_specs=(VMEM, VMEM, VMEM),
-        input_output_aliases={} if mapped is None else {len(operands) - 1: 2},
-        scratch_shapes=[
-            pltpu.VMEM((2 * levels, columns), F32),
-            pltpu.VMEM((rows + 16, voc), BF16),
-        ],
-        compiler_params=pltpu.CompilerParams(vmem_limit_bytes=20 << 20),
-        cost_estimate=pl.CostEstimate(
-            flops=4 * rows * voc * width,
-            bytes_accessed=2 * voc * width,
-            transcendentals=rows * voc,
-        ),
-    )(*operands)[:2]
+        out_specs=(VMEM,) * 5,
+        input_output_aliases={} if mapped is None else {len(operands) - 1: 4},
+        compiler_params=pltpu.CompilerParams(vmem_limit_bytes=16 << 20),
+        cost_estimate=cost(3),
+    )(*operands)
+    operands = list(blocks) + [head, slopes, scaled, mass]
+    keep = pl.pallas_call(
+        functools.partial(back_kernel, len(blocks)),
+        out_shape=half,
+        in_specs=[VMEM] * len(operands),
+        out_specs=VMEM,
+        scratch_shapes=[pltpu.VMEM((rows, width // 2), BF16)],
+        compiler_params=pltpu.CompilerParams(vmem_limit_bytes=16 << 20),
+        cost_estimate=cost(1),
+    )(*operands)
+    return keep, give
 
 
 def sum_over_loop(keep, give, loop):
-    swap = lambda x: lax.ppermute(x, "loop", [(i, i ^ 1) for i in range(loop)])
-    total = keep + swap(give)
-    bit = 2
-    while bit < loop:
-        pairs = [(i, i ^ bit) for i in range(loop)]
+    send = lambda x, mask: lax.ppermute(x, "loop", [(i, i ^ mask) for i in range(loop)])
+    total = keep + send(give, 1)
+    bits = [1 << k for k in range(1, loop.bit_length() - 1)]
+    for k in range(0, len(bits) - 1, 2):
+        dims = bits[:-1][k : k + 2]
         total = lax.reduce_precision(total, 8, 7)
-        total = total + lax.ppermute(total.astype(BF16), "loop", pairs).astype(F32)
-        bit *= 2
-    return total, swap(total)
+        sent = total.astype(BF16)
+        take = lambda mask: send(sent, mask).astype(F32)
+        total = total + take(dims[0])
+        if len(dims) == 2:
+            total = total + (take(dims[1]) + take(dims[0] ^ dims[1]))
+    total = lax.reduce_precision(total, 8, 7)
+    sent = total.astype(BF16)
+    take = lambda mask: send(sent, mask).astype(F32)
+    return total + take(bits[-1]), take(1) + take(bits[-1] ^ 1)
 
 
 def last_kernel(levels, rows, kept, given, mass_out, gain_out, bias_out, buf, line, sems):
     width = gain_out.shape[1]
     me = lax.axis_index("loop")
-    middle = kept.shape[1]
-    buf[:, :middle] = jnp.where(me % 2 == 0, kept[...], given[...])
-    buf[:, middle:] = jnp.where(me % 2 == 0, given[...], kept[...])
+    cut = width // 2
+    low = jnp.where(me % 2 == 0, kept[...], given[...])
+    high = jnp.where(me % 2 == 0, given[...], kept[...])
+    buf[:, :cut], buf[:, cut:width] = low[:, :cut], high[:, :cut]
+    buf[:, width:] = jnp.concatenate([low[:, cut:], high[:, cut:]], axis=1)
     every = buf[0:1, width:]
     spread = lax.broadcasted_iota(jnp.int32, (every.shape[1], LANES), 0)
     target = lax.broadcasted_iota(jnp.int32, (every.shape[1], LANES), 1)
@@ -386,7 +429,7 @@
     rows = rows_dev * loop
     early = rows_dev % 16 == 0 and loop == 16
     mapper = functools.partial(map_early, rows, gain, bias) if early else None
-    blocks, head, mapped, late = gather_blocks(block, loop, load(tied_head), mapper)
+    blocks, head, mapped, late = gather_blocks(block, loop, tied_head, mapper)
     if rows_dev % 16:
         whole = jnp.concatenate(blocks, axis=0)
         blocks = [whole[i : i + 16] for i in range(0, rows, 16)]

time: 51.2 us -> 52.6 us (1.027)
  waiting for transfers between devices: 15.9 us -> 14 us
  Pallas kernels: 15.1 us -> 16.9 us
  starting transfers between devices: 19.1 us -> 20.8 us
    pallas_call x2 -> x4, Pallas kernels: 11.3 us -> 13 us  [the longest x1 5.6 us: main(): pl.pallas_call(functools.partial(front_kernel, loop, levels, len(blocks),...]
    ppermute x5 -> x7, waiting for transfers between devices: 10.2 us -> 8.5 us  [sum_over_loop(): lax.ppermute(x, 'loop', [(i, i ^ mask) for i in range(loop)])]
    ppermute x5 -> x7, starting transfers between devices: 5.78 us -> 7.01 us  [sum_over_loop(): lax.ppermute(x, 'loop', [(i, i ^ mask) for i in range(loop)])]
  transfers between devices with their start and end apart: 20 -> 22, of which waited for: 10 -> 11; matrix products, arithmetic and copies ran while one was open for 0% -> 0% of each run, Pallas kernels for 12% -> 18%
where the time goes in v6:
time: 52.6 us; the launch traced here: 52.5 us
  starting transfers between devices  20.8 us (40%)
  Pallas kernels  16.9 us (32%)
  waiting for transfers between devices  14 us (27%)
  between operations  0.73 us (1%)
    ppermute x15, starting transfers between devices, gather_blocks(): send = lambda x, pairs: lax.ppermute(x, 'loop', pairs)  13.8 us
    ppermute x7, waiting for transfers between devices, sum_over_loop(): lax.ppermute(x, 'loop', [(i, i ^ mask) for i in range(loop)])  8.5 us
    ppermute x7, starting transfers between devices, sum_over_loop(): lax.ppermute(x, 'loop', [(i, i ^ mask) for i in range(loop)])  7.01 us
    pallas_call x1, Pallas kernels, main(): pl.pallas_call(functools.partial(front_kernel, loop, levels, len(blocks),...  5.6 us
    ppermute x15, waiting for transfers between devices, gather_blocks(): send = lambda x, pairs: lax.ppermute(x, 'loop', pairs)  5.53 us
    pallas_call x2, Pallas kernels, load(): pl.pallas_call(functools.partial(load_kernel, part, parts), out_shape=plt...  5.23 us
    pallas_call x1, Pallas kernels, main(): pl.pallas_call(functools.partial(back_kernel, len(blocks)), out_shape=hal...  2.13 us
    pallas_call x2, Pallas kernels, map_early(): pl.pallas_call(functools.partial(map_kernel, places), out_shape=pltpu.VME...  2.04 us
  transfers between devices with their start and end apart: 22, of which 11 were waited for; matrix products, arithmetic and copies ran while one was open for 0% of the time, Pallas kernels for 18%

profile of v6, /device:TPU:0, one launch (start us, length us, event | category | flops | bytes accessed | tf_op | source)
XLA Modules:
  0.0 52.5 jit_solution(2097491642731913099)
XLA Ops:
  0.6 1.1 %shard_map.94 = (bf16[16,5504]{1,0:T(8,128)(2,1)S(1)}, f32[4,5376]{1,0:T(4,128)S(1)}, f32[4,5376]{1,0:T(4,128)S(1)}) custom-call(bf16[16,5376]{1,0:T(8,128)(2,1)} %hidden.1, s32[1,16]{1,0:T(1,128)} %bitcast.4, s32[1,16]{1,0:T(1,128)} %bitcast.5, f32[1,16]{1,0:T(1,128)} %bitcast.6, f32[4,5376]{1,0:T(4,128)} %depth_gain.1, f32[4,5376]{1,0:T(4,128)} %depth_bias.1), custom_call_target="tpu_custom_call" | custom-call | tf_op jit(solution)/shard_map/pallas_call | solution.py:86
  1.8 3.0 %collective-permute-start.1 = (bf16[16,5504]{1,0:T(8,128)(2,1)S(1)}, bf16[16,5504]{1,0:T(8,128)(2,1)S(1)}, u32[]{:S(2)}, u32[]{:S(2)}) collective-permute-start(bf16[16,5504]{1,0:T(8,128)(2,1)S(1)} %get-tuple-element.24.refs_0_), channel_id=1, source_target_pairs={{1,5},{4,0},{5,9},{8,4},{9,13},{12,8},{13,15},{14,12},{15,11},{10,... | collective-permute-start | bytes 528392 | tf_op jit(solution)/shard_map/ppermute | solution.py:130
  4.8 0.8 %collective-permute-start = (bf16[16,5504]{1,0:T(8,128)(2,1)S(1)}, bf16[16,5504]{1,0:T(8,128)(2,1)S(1)}, u32[]{:S(2)}, u32[]{:S(2)}) collective-permute-start(bf16[16,5504]{1,0:T(8,128)(2,1)S(1)} %get-tuple-element.24.refs_0_), channel_id=1, source_target_pairs={{0,5},{5,0},{4,9},{9,4},{8,13},{13,8},{12,15},{15,12},{14,11},{11,... | collective-permute-start | bytes 528392 | tf_op jit(solution)/shard_map/ppermute | solution.py:130
  5.6 0.9 %collective-permute-start.4 = (bf16[16,5504]{1,0:T(8,128)(2,1)S(1)}, bf16[16,5504]{1,0:T(8,128)(2,1)S(1)}, u32[]{:S(2)}, u32[]{:S(2)}) collective-permute-start(bf16[16,5504]{1,0:T(8,128)(2,1)S(1)} %get-tuple-element.24.refs_0_), channel_id=1, source_target_pairs={{0,1},{1,0},{2,3},{3,2},{4,5},{5,4},{6,7},{7,6},{8,9},{9,8},{10,11... | collective-permute-start | bytes 528392 | tf_op jit(solution)/shard_map/ppermute | solution.py:130
  6.5 2.6 %shard_map.95.refs_0_ = bf16[1024,5376]{1,0:T(8,128)(2,1)S(1)} custom-call(bf16[1024,5376]{1,0:T(8,128)(2,1)} %head_hbm.3), custom_call_target="tpu_custom_call" | custom-call | bytes 11010048 | tf_op jit(solution)/shard_map/pallas_call | solution.py:231
  9.1 0.0 collective-permute-done.1.refs_3_.refs_1_
  9.1 1.0 %collective-permute-done.refs_2_.refs_9_ = bf16[16,5504]{1,0:T(8,128)(2,1)S(1)} collective-permute-done((bf16[16,5504]{1,0:T(8,128)(2,1)S(1)}, bf16[16,5504]{1,0:T(8,128)(2,1)S(1)}, u32[]{:S(2)}, u32[]{:S(2)}) %collective-permute-start) | collective-permute-done | bytes 176160 | tf_op jit(solution)/shard_map/ppermute | solution.py:130
  10.2 0.9 %collective-permute-start.3 = (bf16[16,5504]{1,0:T(8,128)(2,1)S(1)}, bf16[16,5504]{1,0:T(8,128)(2,1)S(1)}, u32[]{:S(2)}, u32[]{:S(2)}) collective-permute-start(bf16[16,5504]{1,0:T(8,128)(2,1)S(1)} %collective-permute-done.1.refs_3_.refs_1_), channel_id=1, source_target_pairs={{1,4},{4,1},{5,8},{8,5},{9,12},{12,9},{13,14},{14,13},{15,10},{10,... | collective-permute-start | bytes 528392 | tf_op jit(solution)/shard_map/ppermute | solution.py:130
  11.1 0.8 %collective-permute-start.2 = (bf16[16,5504]{1,0:T(8,128)(2,1)S(1)}, bf16[16,5504]{1,0:T(8,128)(2,1)S(1)}, u32[]{:S(2)}, u32[]{:S(2)}) collective-permute-start(bf16[16,5504]{1,0:T(8,128)(2,1)S(1)} %collective-permute-done.refs_2_.refs_9_), channel_id=1, source_target_pairs={{1,4},{4,1},{5,8},{8,5},{9,12},{12,9},{13,14},{14,13},{15,10},{10,... | collective-permute-start | bytes 528392 | tf_op jit(solution)/shard_map/ppermute | solution.py:130
  11.9 0.4 collective-permute-start.8
  12.3 2.6 %shard_map.96.refs_16_ = bf16[1024,5376]{1,0:T(8,128)(2,1)S(1)} custom-call(bf16[1024,5376]{1,0:T(8,128)(2,1)} %head_hbm.3, bf16[1024,5376]{1,0:T(8,128)(2,1)S(1)} %shard_map.95.refs_0_), custom_call_target="tpu_custom_call", output_to_operand_aliasing={{}: (1, {})} | custom-call | bytes 11010048 | tf_op jit(solution)/shard_map/pallas_call | solution.py:231
  15.0 0.0 collective-permute-done.4.refs_1_.refs_8_
  15.0 0.1 collective-permute-done.3.refs_1_.refs_14_
  15.0 1.9 %collective-permute-done.2.refs_0_.refs_6_ = bf16[16,5504]{1,0:T(8,128)(2,1)S(1)} collective-permute-done((bf16[16,5504]{1,0:T(8,128)(2,1)S(1)}, bf16[16,5504]{1,0:T(8,128)(2,1)S(1)}, u32[]{:S(2)}, u32[]{:S(2)}) %collective-permute-start.2) | collective-permute-done | bytes 176160 | tf_op jit(solution)/shard_map/ppermute | solution.py:130
  16.9 1.7 %collective-permute-start.9 = (bf16[16,5504]{1,0:T(8,128)(2,1)S(1)}, bf16[16,5504]{1,0:T(8,128)(2,1)S(1)}, u32[]{:S(2)}, u32[]{:S(2)}) collective-permute-start(bf16[16,5504]{1,0:T(8,128)(2,1)S(1)} %collective-permute-done.2.refs_0_.refs_6_), channel_id=1, source_target_pairs={{0,5},{5,0},{4,9},{9,4},{8,13},{13,8},{12,15},{15,12},{14,11},{11,... | collective-permute-start | bytes 528392 | tf_op jit(solution)/shard_map/ppermute | solution.py:130
  18.7 0.3 collective-permute-start.7
  19.0 1.3 %collective-permute-start.6 = (bf16[16,5504]{1,0:T(8,128)(2,1)S(1)}, bf16[16,5504]{1,0:T(8,128)(2,1)S(1)}, u32[]{:S(2)}, u32[]{:S(2)}) collective-permute-start(bf16[16,5504]{1,0:T(8,128)(2,1)S(1)} %collective-permute-done.3.refs_1_.refs_14_), channel_id=1, source_target_pairs={{0,5},{5,0},{4,9},{9,4},{8,13},{13,8},{12,15},{15,12},{14,11},{11,... | collective-permute-start | bytes 528392 | tf_op jit(solution)/shard_map/ppermute | solution.py:130
  20.3 0.4 collective-permute-start.5
  20.7 0.0 collective-permute-done.8.refs_5_.refs_15_
  20.7 0.1 collective-permute-start.11
  20.8 1.0 %collective-permute-done.9.refs_4_.refs_11_ = bf16[16,5504]{1,0:T(8,128)(2,1)S(1)} collective-permute-done((bf16[16,5504]{1,0:T(8,128)(2,1)S(1)}, bf16[16,5504]{1,0:T(8,128)(2,1)S(1)}, u32[]{:S(2)}, u32[]{:S(2)}) %collective-permute-start.9) | collective-permute-done | bytes 176160 | tf_op jit(solution)/shard_map/ppermute | solution.py:130
  21.8 1.8 %collective-permute-start.10 = (bf16[16,5504]{1,0:T(8,128)(2,1)S(1)}, bf16[16,5504]{1,0:T(8,128)(2,1)S(1)}, u32[]{:S(2)}, u32[]{:S(2)}) collective-permute-start(bf16[16,5504]{1,0:T(8,128)(2,1)S(1)} %collective-permute-done.9.refs_4_.refs_11_), channel_id=1, source_target_pairs={{1,4},{4,1},{5,8},{8,5},{9,12},{12,9},{13,14},{14,13},{15,10},{10,... | collective-permute-start | bytes 528392 | tf_op jit(solution)/shard_map/ppermute | solution.py:130
  23.6 0.0 collective-permute-done.7.refs_4_.refs_7_
  23.6 1.0 %shard_map.97.refs_8_ = bf16[256,5376]{1,0:T(8,128)(2,1)S(1)} custom-call(bf16[16,5504]{1,0:T(8,128)(2,1)S(1)} %get-tuple-element.24.refs_0_, bf16[16,5504]{1,0:T(8,128)(2,1)S(1)} %collective-permute-done.4.refs_1_.refs_8_, bf16[16,5504]{1,0:T(8,128)(2,1)S(1)} %collective-permute-done.refs_2_.refs_9_, ...), custom_call_target="tpu_custom_call" | custom-call | flops 10321920 | bytes 2064384 | tf_op jit(solution)/shard_map/pallas_call | solution.py:201
  24.7 0.4 collective-permute-start.14
  25.0 0.2 collective-permute-start.12
  25.2 1.0 %shard_map.98.refs_19_ = bf16[256,5376]{1,0:T(8,128)(2,1)S(1)} custom-call(bf16[16,5504]{1,0:T(8,128)(2,1)S(1)} %collective-permute-done.2.refs_0_.refs_6_, bf16[16,5504]{1,0:T(8,128)(2,1)S(1)} %collective-permute-done.3.refs_1_.refs_14_, bf16[16,5504]{1,0:T(8,128)(2,1)S(1)} %collective-permute-done.11.refs_2_.refs_10_, ...), custom_call_target="tpu_custom_call", output_to_operand_aliasing={{}: (8, {})} | custom-call | flops 10321920 | bytes 2064384 | tf_op jit(solution)/shard_map/pallas_call | solution.py:201
  26.3 0.5 collective-permute-done.10.refs_4_
  26.8 0.6 %collective-permute-start.13 = (bf16[16,5504]{1,0:T(8,128)(2,1)S(1)}, bf16[16,5504]{1,0:T(8,128)(2,1)S(1)}, u32[]{:S(2)}, u32[]{:S(2)}) collective-permute-start(bf16[16,5504]{1,0:T(8,128)(2,1)S(1)} %collective-permute-done.10.refs_4_), channel_id=1, source_target_pairs={{0,1},{1,0},{2,3},{3,2},{4,5},{5,4},{6,7},{7,6},{8,9},{9,8},{10,11... | collective-permute-start | bytes 528392 | tf_op jit(solution)/shard_map/ppermute | solution.py:130
  27.4 0.0 collective-permute-done.14.refs_13_
  27.4 1.0 %collective-permute-done.13.refs_12_ = bf16[16,5504]{1,0:T(8,128)(2,1)S(1)} collective-permute-done((bf16[16,5504]{1,0:T(8,128)(2,1)S(1)}, bf16[16,5504]{1,0:T(8,128)(2,1)S(1)}, u32[]{:S(2)}, u32[]{:S(2)}) %collective-permute-start.13) | collective-permute-done | bytes 176160 | tf_op jit(solution)/shard_map/ppermute | solution.py:130
  28.4 5.6 %shard_map.99 = (f32[8,2816]{1,0:T(8,128)S(1)}, bf16[272,1024]{1,0:T(8,128)(2,1)S(1)}, bf16[16,256]{1,0:T(8,128)(2,1)S(1)}, f32[1,128]{1,0:T(1,128)S(1)}, bf16[256,5376]{1,0:T(8,128)(2,1)S(1)}) custom-call(bf16[16,5504]{1,0:T(8,128)(2,1)S(1)} %get-tuple-element.24.refs_0_, ...), custom_call_target="tpu_custom_call", output_to_operand_aliasing={{4}: (19, {})} | custom-call | flops 4227858432 | bytes 5505024 | tf_op jit(solution)/shard_map/pallas_call | solution.py:336
  34.0 0.4 collective-permute-start.15
  34.4 2.1 %shard_map.100 = f32[8,2816]{1,0:T(8,128)S(1)} custom-call(bf16[16,5504]{1,0:T(8,128)(2,1)S(1)} %get-tuple-element.24.refs_0_, bf16[16,5504]{1,0:T(8,128)(2,1)S(1)} %collective-permute-done.1.refs_3_.refs_1_, bf16[16,5504]{1,0:T(8,128)(2,1)S(1)} %collective-permute-done.5.refs_3_.refs_2_, bf16[16,5504]{1,0:T(8,128)(2,1)S(1)} %collective-permute-done.6.refs_5_.refs_3_, ...), custom_call_target="tpu_custom_call" | custom-call | flops 1409286144 | bytes 5505024 | tf_op jit(solution)/shard_map/pallas_call | solution.py:352
  36.5 0.0 collective-permute-done.15
  36.5 2.6 %collective-permute-start.18 = (bf16[8,2816]{1,0:T(8,128)(2,1)S(1)}, bf16[8,2816]{1,0:T(8,128)(2,1)S(1)}, u32[]{:S(2)}, u32[]{:S(2)}) collective-permute-start(bf16[8,2816]{1,0:T(8,128)(2,1)S(1)} %fusion), channel_id=1, source_target_pairs={{0,6},{1,7},{2,4},{3,5},{4,2},{5,3},{6,0},{7,1},{8,14},{9,15},{10,... | collective-permute-start | bytes 135176 | tf_op jit(solution)/shard_map/ppermute | solution.py:365
  39.1 0.4 collective-permute-start.17
  39.6 0.5 collective-permute-start.16
  40.1 1.5 %collective-permute-done.18 = bf16[8,2816]{1,0:T(8,128)(2,1)S(1)} collective-permute-done((bf16[8,2816]{1,0:T(8,128)(2,1)S(1)}, bf16[8,2816]{1,0:T(8,128)(2,1)S(1)}, u32[]{:S(2)}, u32[]{:S(2)}) %collective-permute-start.18) | collective-permute-done | bytes 45088 | tf_op jit(solution)/shard_map/ppermute | solution.py:365
  41.5 1.6 %collective-permute-done.17 = bf16[8,2816]{1,0:T(8,128)(2,1)S(1)} collective-permute-done((bf16[8,2816]{1,0:T(8,128)(2,1)S(1)}, bf16[8,2816]{1,0:T(8,128)(2,1)S(1)}, u32[]{:S(2)}, u32[]{:S(2)}) %collective-permute-start.17) | collective-permute-done | bytes 45088 | tf_op jit(solution)/shard_map/ppermute | solution.py:365
  43.2 0.4 collective-permute-done.16
  43.7 0.8 %collective-permute-start.21 = (bf16[8,2816]{1,0:T(8,128)(2,1)S(1)}, bf16[8,2816]{1,0:T(8,128)(2,1)S(1)}, u32[]{:S(2)}, u32[]{:S(2)}) collective-permute-start(bf16[8,2816]{1,0:T(8,128)(2,1)S(1)} %get-tuple-element.45), channel_id=1, source_target_pairs={{0,9},{1,8},{2,11},{3,10},{4,13},{5,12},{6,15},{7,14},{8,1},{9,0},... | collective-permute-start | bytes 135176 | tf_op jit(solution)/shard_map/ppermute | solution.py:365
  44.5 1.9 %collective-permute-start.20 = (bf16[8,2816]{1,0:T(8,128)(2,1)S(1)}, bf16[8,2816]{1,0:T(8,128)(2,1)S(1)}, u32[]{:S(2)}, u32[]{:S(2)}) collective-permute-start(bf16[8,2816]{1,0:T(8,128)(2,1)S(1)} %get-tuple-element.45), channel_id=1, source_target_pairs={{0,1},{1,0},{2,3},{3,2},{4,5},{5,4},{6,7},{7,6},{8,9},{9,8},{10,11... | collective-permute-start | bytes 135176 | tf_op jit(solution)/shard_map/ppermute | solution.py:365
  46.4 0.4 collective-permute-start.19
  46.8 1.6 %collective-permute-done.21 = bf16[8,2816]{1,0:T(8,128)(2,1)S(1)} collective-permute-done((bf16[8,2816]{1,0:T(8,128)(2,1)S(1)}, bf16[8,2816]{1,0:T(8,128)(2,1)S(1)}, u32[]{:S(2)}, u32[]{:S(2)}) %collective-permute-start.21) | collective-permute-done | bytes 45088 | tf_op jit(solution)/shard_map/ppermute | solution.py:365
  48.4 0.0 collective-permute-done.20
  48.4 3.3 %collective-permute-done.19 = bf16[8,2816]{1,0:T(8,128)(2,1)S(1)} collective-permute-done((bf16[8,2816]{1,0:T(8,128)(2,1)S(1)}, bf16[8,2816]{1,0:T(8,128)(2,1)S(1)}, u32[]{:S(2)}, u32[]{:S(2)}) %collective-permute-start.19) | collective-permute-done | bytes 45088 | tf_op jit(solution)/shard_map/ppermute | solution.py:365
  51.8 0.7 %shard_map.101 = (f32[1,16]{1,0:T(1,128)}, f32[4,5376]{1,0:T(4,128)}, f32[4,5376]{1,0:T(4,128)}) custom-call(f32[8,2816]{1,0:T(8,128)S(1)} %convert_add_fusion.1.kept, f32[8,2816]{1,0:T(8,128)S(1)} %convert_add_fusion.given), custom_call_target="tpu_custom_call" | custom-call | tf_op jit(solution)/shard_map/pallas_call | solution.py:410
  (8 shorter events, 0.1 us)
Async XLA Ops:
  1.8 7.3 %collective-permute-start.1 = (bf16[16,5504]{1,0:T(8,128)(2,1)S(1)}, bf16[16,5504]{1,0:T(8,128)(2,1)S(1)}, u32[]{:S(2)}, u32[]{:S(2)}) collective-permute-start(bf16[16,5504]{1,0:T(8,128)(2,1)S(1)} %get-tuple-element.24.refs_0_), channel_id=1, source_target_pairs={{1,5},{4,0},{5,9},{8,4},{9,13},{12,8},{13,15},{14,12},{15,11},{10,... | collective-permute-start | bytes 528392 | tf_op jit(solution)/shard_map/ppermute | solution.py:130
  4.8 5.4 %collective-permute-start = (bf16[16,5504]{1,0:T(8,128)(2,1)S(1)}, bf16[16,5504]{1,0:T(8,128)(2,1)S(1)}, u32[]{:S(2)}, u32[]{:S(2)}) collective-permute-start(bf16[16,5504]{1,0:T(8,128)(2,1)S(1)} %get-tuple-element.24.refs_0_), channel_id=1, source_target_pairs={{0,5},{5,0},{4,9},{9,4},{8,13},{13,8},{12,15},{15,12},{14,11},{11,... | collective-permute-start | bytes 528392 | tf_op jit(solution)/shard_map/ppermute | solution.py:130
  5.6 9.4 %collective-permute-start.4 = (bf16[16,5504]{1,0:T(8,128)(2,1)S(1)}, bf16[16,5504]{1,0:T(8,128)(2,1)S(1)}, u32[]{:S(2)}, u32[]{:S(2)}) collective-permute-start(bf16[16,5504]{1,0:T(8,128)(2,1)S(1)} %get-tuple-element.24.refs_0_), channel_id=1, source_target_pairs={{0,1},{1,0},{2,3},{3,2},{4,5},{5,4},{6,7},{7,6},{8,9},{9,8},{10,11... | collective-permute-start | bytes 528392 | tf_op jit(solution)/shard_map/ppermute | solution.py:130
  10.2 4.9 %collective-permute-start.3 = (bf16[16,5504]{1,0:T(8,128)(2,1)S(1)}, bf16[16,5504]{1,0:T(8,128)(2,1)S(1)}, u32[]{:S(2)}, u32[]{:S(2)}) collective-permute-start(bf16[16,5504]{1,0:T(8,128)(2,1)S(1)} %collective-permute-done.1.refs_3_.refs_1_), channel_id=1, source_target_pairs={{1,4},{4,1},{5,8},{8,5},{9,12},{12,9},{13,14},{14,13},{15,10},{10,... | collective-permute-start | bytes 528392 | tf_op jit(solution)/shard_map/ppermute | solution.py:130
  11.1 5.8 %collective-permute-start.2 = (bf16[16,5504]{1,0:T(8,128)(2,1)S(1)}, bf16[16,5504]{1,0:T(8,128)(2,1)S(1)}, u32[]{:S(2)}, u32[]{:S(2)}) collective-permute-start(bf16[16,5504]{1,0:T(8,128)(2,1)S(1)} %collective-permute-done.refs_2_.refs_9_), channel_id=1, source_target_pairs={{1,4},{4,1},{5,8},{8,5},{9,12},{12,9},{13,14},{14,13},{15,10},{10,... | collective-permute-start | bytes 528392 | tf_op jit(solution)/shard_map/ppermute | solution.py:130
  11.9 8.8 %collective-permute-start.8 = (bf16[16,5504]{1,0:T(8,128)(2,1)S(1)}, bf16[16,5504]{1,0:T(8,128)(2,1)S(1)}, u32[]{:S(2)}, u32[]{:S(2)}) collective-permute-start(bf16[16,5504]{1,0:T(8,128)(2,1)S(1)} %collective-permute-done.1.refs_3_.refs_1_), channel_id=1, source_target_pairs={{0,1},{1,0},{2,3},{3,2},{4,5},{5,4},{6,7},{7,6},{8,9},{9,8},{10,11... | collective-permute-start | bytes 528392 | tf_op jit(solution)/shard_map/ppermute | solution.py:130
  16.9 4.9 %collective-permute-start.9 = (bf16[16,5504]{1,0:T(8,128)(2,1)S(1)}, bf16[16,5504]{1,0:T(8,128)(2,1)S(1)}, u32[]{:S(2)}, u32[]{:S(2)}) collective-permute-start(bf16[16,5504]{1,0:T(8,128)(2,1)S(1)} %collective-permute-done.2.refs_0_.refs_6_), channel_id=1, source_target_pairs={{0,5},{5,0},{4,9},{9,4},{8,13},{13,8},{12,15},{15,12},{14,11},{11,... | collective-permute-start | bytes 528392 | tf_op jit(solution)/shard_map/ppermute | solution.py:130
  18.7 5.0 %collective-permute-start.7 = (bf16[16,5504]{1,0:T(8,128)(2,1)S(1)}, bf16[16,5504]{1,0:T(8,128)(2,1)S(1)}, u32[]{:S(2)}, u32[]{:S(2)}) collective-permute-start(bf16[16,5504]{1,0:T(8,128)(2,1)S(1)} %collective-permute-done.refs_2_.refs_9_), channel_id=1, source_target_pairs={{0,1},{1,0},{2,3},{3,2},{4,5},{5,4},{6,7},{7,6},{8,9},{9,8},{10,11... | collective-permute-start | bytes 528392 | tf_op jit(solution)/shard_map/ppermute | solution.py:130
  19.0 5.6 %collective-permute-start.6 = (bf16[16,5504]{1,0:T(8,128)(2,1)S(1)}, bf16[16,5504]{1,0:T(8,128)(2,1)S(1)}, u32[]{:S(2)}, u32[]{:S(2)}) collective-permute-start(bf16[16,5504]{1,0:T(8,128)(2,1)S(1)} %collective-permute-done.3.refs_1_.refs_14_), channel_id=1, source_target_pairs={{0,5},{5,0},{4,9},{9,4},{8,13},{13,8},{12,15},{15,12},{14,11},{11,... | collective-permute-start | bytes 528392 | tf_op jit(solution)/shard_map/ppermute | solution.py:130
  20.3 4.9 %collective-permute-start.5 = (bf16[16,5504]{1,0:T(8,128)(2,1)S(1)}, bf16[16,5504]{1,0:T(8,128)(2,1)S(1)}, u32[]{:S(2)}, u32[]{:S(2)}) collective-permute-start(bf16[16,5504]{1,0:T(8,128)(2,1)S(1)} %collective-permute-done.3.refs_1_.refs_14_), channel_id=1, source_target_pairs={{0,1},{1,0},{2,3},{3,2},{4,5},{5,4},{6,7},{7,6},{8,9},{9,8},{10,11... | collective-permute-start | bytes 528392 | tf_op jit(solution)/shard_map/ppermute | solution.py:130
  20.7 4.5 %collective-permute-start.11 = (bf16[16,5504]{1,0:T(8,128)(2,1)S(1)}, bf16[16,5504]{1,0:T(8,128)(2,1)S(1)}, u32[]{:S(2)}, u32[]{:S(2)}) collective-permute-start(bf16[16,5504]{1,0:T(8,128)(2,1)S(1)} %collective-permute-done.2.refs_0_.refs_6_), channel_id=1, source_target_pairs={{0,1},{1,0},{2,3},{3,2},{4,5},{5,4},{6,7},{7,6},{8,9},{9,8},{10,11... | collective-permute-start | bytes 528392 | tf_op jit(solution)/shard_map/ppermute | solution.py:130
  21.8 4.9 %collective-permute-start.10 = (bf16[16,5504]{1,0:T(8,128)(2,1)S(1)}, bf16[16,5504]{1,0:T(8,128)(2,1)S(1)}, u32[]{:S(2)}, u32[]{:S(2)}) collective-permute-start(bf16[16,5504]{1,0:T(8,128)(2,1)S(1)} %collective-permute-done.9.refs_4_.refs_11_), channel_id=1, source_target_pairs={{1,4},{4,1},{5,8},{8,5},{9,12},{12,9},{13,14},{14,13},{15,10},{10,... | collective-permute-start | bytes 528392 | tf_op jit(solution)/shard_map/ppermute | solution.py:130
  24.7 2.7 %collective-permute-start.14 = (bf16[16,5504]{1,0:T(8,128)(2,1)S(1)}, bf16[16,5504]{1,0:T(8,128)(2,1)S(1)}, u32[]{:S(2)}, u32[]{:S(2)}) collective-permute-start(bf16[16,5504]{1,0:T(8,128)(2,1)S(1)} %collective-permute-done.6.refs_5_.refs_3_), channel_id=1, source_target_pairs={{0,1},{1,0},{2,3},{3,2},{4,5},{5,4},{6,7},{7,6},{8,9},{9,8},{10,11... | collective-permute-start | bytes 528392 | tf_op jit(solution)/shard_map/ppermute | solution.py:130
  25.0 2.3 %collective-permute-start.12 = (bf16[16,5504]{1,0:T(8,128)(2,1)S(1)}, bf16[16,5504]{1,0:T(8,128)(2,1)S(1)}, u32[]{:S(2)}, u32[]{:S(2)}) collective-permute-start(bf16[16,5504]{1,0:T(8,128)(2,1)S(1)} %collective-permute-done.9.refs_4_.refs_11_), channel_id=1, source_target_pairs={{0,1},{1,0},{2,3},{3,2},{4,5},{5,4},{6,7},{7,6},{8,9},{9,8},{10,11... | collective-permute-start | bytes 528392 | tf_op jit(solution)/shard_map/ppermute | solution.py:130
  26.8 1.7 %collective-permute-start.13 = (bf16[16,5504]{1,0:T(8,128)(2,1)S(1)}, bf16[16,5504]{1,0:T(8,128)(2,1)S(1)}, u32[]{:S(2)}, u32[]{:S(2)}) collective-permute-start(bf16[16,5504]{1,0:T(8,128)(2,1)S(1)} %collective-permute-done.10.refs_4_), channel_id=1, source_target_pairs={{0,1},{1,0},{2,3},{3,2},{4,5},{5,4},{6,7},{7,6},{8,9},{9,8},{10,11... | collective-permute-start | bytes 528392 | tf_op jit(solution)/shard_map/ppermute | solution.py:130
  34.0 2.5 %collective-permute-start.15 = (f32[8,2816]{1,0:T(8,128)S(1)}, f32[8,2816]{1,0:T(8,128)S(1)}, u32[]{:S(2)}, u32[]{:S(2)}) collective-permute-start(f32[8,2816]{1,0:T(8,128)S(1)} %get-tuple-element.41), channel_id=1, source_target_pairs={{0,1},{1,0},{2,3},{3,2},{4,5},{5,4},{6,7},{7,6},{8,9},{9,8},{10,11... | collective-permute-start | bytes 270344 | tf_op jit(solution)/shard_map/ppermute | solution.py:365
  36.5 5.0 %collective-permute-start.18 = (bf16[8,2816]{1,0:T(8,128)(2,1)S(1)}, bf16[8,2816]{1,0:T(8,128)(2,1)S(1)}, u32[]{:S(2)}, u32[]{:S(2)}) collective-permute-start(bf16[8,2816]{1,0:T(8,128)(2,1)S(1)} %fusion), channel_id=1, source_target_pairs={{0,6},{1,7},{2,4},{3,5},{4,2},{5,3},{6,0},{7,1},{8,14},{9,15},{10,... | collective-permute-start | bytes 135176 | tf_op jit(solution)/shard_map/ppermute | solution.py:365
  39.1 4.0 %collective-permute-start.17 = (bf16[8,2816]{1,0:T(8,128)(2,1)S(1)}, bf16[8,2816]{1,0:T(8,128)(2,1)S(1)}, u32[]{:S(2)}, u32[]{:S(2)}) collective-permute-start(bf16[8,2816]{1,0:T(8,128)(2,1)S(1)} %fusion), channel_id=1, source_target_pairs={{0,4},{1,5},{2,6},{3,7},{4,0},{5,1},{6,2},{7,3},{8,12},{9,13},{10,... | collective-permute-start | bytes 135176 | tf_op jit(solution)/shard_map/ppermute | solution.py:365
  39.6 4.0 %collective-permute-start.16 = (bf16[8,2816]{1,0:T(8,128)(2,1)S(1)}, bf16[8,2816]{1,0:T(8,128)(2,1)S(1)}, u32[]{:S(2)}, u32[]{:S(2)}) collective-permute-start(bf16[8,2816]{1,0:T(8,128)(2,1)S(1)} %fusion), channel_id=1, source_target_pairs={{0,2},{1,3},{2,0},{3,1},{4,6},{5,7},{6,4},{7,5},{8,10},{9,11},{10,... | collective-permute-start | bytes 135176 | tf_op jit(solution)/shard_map/ppermute | solution.py:365
  43.7 4.7 %collective-permute-start.21 = (bf16[8,2816]{1,0:T(8,128)(2,1)S(1)}, bf16[8,2816]{1,0:T(8,128)(2,1)S(1)}, u32[]{:S(2)}, u32[]{:S(2)}) collective-permute-start(bf16[8,2816]{1,0:T(8,128)(2,1)S(1)} %get-tuple-element.45), channel_id=1, source_target_pairs={{0,9},{1,8},{2,11},{3,10},{4,13},{5,12},{6,15},{7,14},{8,1},{9,0},... | collective-permute-start | bytes 135176 | tf_op jit(solution)/shard_map/ppermute | solution.py:365
  44.5 3.9 %collective-permute-start.20 = (bf16[8,2816]{1,0:T(8,128)(2,1)S(1)}, bf16[8,2816]{1,0:T(8,128)(2,1)S(1)}, u32[]{:S(2)}, u32[]{:S(2)}) collective-permute-start(bf16[8,2816]{1,0:T(8,128)(2,1)S(1)} %get-tuple-element.45), channel_id=1, source_target_pairs={{0,1},{1,0},{2,3},{3,2},{4,5},{5,4},{6,7},{7,6},{8,9},{9,8},{10,11... | collective-permute-start | bytes 135176 | tf_op jit(solution)/shard_map/ppermute | solution.py:365
  46.4 5.4 %collective-permute-start.19 = (bf16[8,2816]{1,0:T(8,128)(2,1)S(1)}, bf16[8,2816]{1,0:T(8,128)(2,1)S(1)}, u32[]{:S(2)}, u32[]{:S(2)}) collective-permute-start(bf16[8,2816]{1,0:T(8,128)(2,1)S(1)} %get-tuple-element.45), channel_id=1, source_target_pairs={{0,8},{1,9},{2,10},{3,11},{4,12},{5,13},{6,14},{7,15},{8,0},{9,1},... | collective-permute-start | bytes 135176 | tf_op jit(solution)/shard_map/ppermute | solution.py:365

commit v7 on v6

--- a/solution.py
+++ b/solution.py
@@ -130,8 +130,7 @@
     send = lambda x, pairs: lax.ppermute(x, "loop", pairs)
     swap = lambda x: send(x, [(i, i ^ 1) for i in range(loop)])
     blocks = [None] * loop
-    first = swap(block)
-    blocks[0], blocks[chips] = block, first
+    blocks[0], blocks[chips] = block, swap(block)
     crossed = plain = block
     ready = [0, chips]
     mapped = None
@@ -141,11 +140,10 @@
             plain = send(plain, hop_pairs(order, step, step > 1))
         if step == 1:
             head = load(tied_head, 0, 2)
-            crossed, plain, head = tie(crossed, plain, head)
+            crossed, head = tie(crossed, head)
         if step == min(2, half):
             head = load(tied_head, 1, 2, head)
-            crossed, plain, head, first = tie(crossed, plain, head, first)
-            blocks[chips] = first
+            plain, head = tie(plain, head)
         if mapper is not None and step == 3:
             mapped = mapper(None, {i: blocks[i] for i in ready[:6]})
             plain, mapped = tie(plain, mapped)
@@ -374,9 +372,8 @@
         if len(dims) == 2:
             total = total + (take(dims[1]) + take(dims[0] ^ dims[1]))
     total = lax.reduce_precision(total, 8, 7)
-    sent = total.astype(BF16)
-    take = lambda mask: send(sent, mask).astype(F32)
-    return total + take(bits[-1]), take(1) + take(bits[-1] ^ 1)
+    total = total + send(total.astype(BF16), bits[-1]).astype(F32)
+    return total, send(total, 1)
 
 
 def last_kernel(levels, rows, kept, given, mass_out, gain_out, bias_out, buf, line, sems):

time: 52.6 us -> 50 us (0.951)
  waiting for transfers between devices: 14 us -> 12.1 us
  starting transfers between devices: 20.8 us -> 20.1 us
    ppermute x7 -> x6, waiting for transfers between devices: 8.5 us -> 5.86 us  [sum_over_loop(): lax.ppermute(x, 'loop', [(i, i ^ mask) for i in range(loop)])]
    ppermute x15, starting transfers between devices: 13.8 us -> 12.7 us  [gather_blocks(): send = lambda x, pairs: lax.ppermute(x, 'loop', pairs)]
    ppermute x15, waiting for transfers between devices: 5.53 us -> 6.23 us  [gather_blocks(): send = lambda x, pairs: lax.ppermute(x, 'loop', pairs)]
    ppermute x7 -> x6, starting transfers between devices: 7.01 us -> 7.43 us  [sum_over_loop(): lax.ppermute(x, 'loop', [(i, i ^ mask) for i in range(loop)])]
  transfers between devices with their start and end apart: 22 -> 21, of which waited for: 11 -> 10; matrix products, arithmetic and copies ran while one was open for 0% -> 0% of each run, Pallas kernels for 18% -> 19%
where the time goes in v7:
time: 50 us; the launch traced here: 49.9 us
  starting transfers between devices  20.1 us (40%)
  Pallas kernels  16.9 us (34%)
  waiting for transfers between devices  12.1 us (24%)
  between operations  0.72 us (1%)
    ppermute x15, starting transfers between devices, gather_blocks(): send = lambda x, pairs: lax.ppermute(x, 'loop', pairs)  12.7 us
    ppermute x6, starting transfers between devices, sum_over_loop(): lax.ppermute(x, 'loop', [(i, i ^ mask) for i in range(loop)])  7.43 us
    ppermute x15, waiting for transfers between devices, gather_blocks(): send = lambda x, pairs: lax.ppermute(x, 'loop', pairs)  6.23 us
    ppermute x6, waiting for transfers between devices, sum_over_loop(): lax.ppermute(x, 'loop', [(i, i ^ mask) for i in range(loop)])  5.86 us
    pallas_call x1, Pallas kernels, main(): pl.pallas_call(functools.partial(front_kernel, loop, levels, len(blocks),...  5.62 us
    pallas_call x2, Pallas kernels, load(): pl.pallas_call(functools.partial(load_kernel, part, parts), out_shape=plt...  5.23 us
    pallas_call x1, Pallas kernels, main(): pl.pallas_call(functools.partial(back_kernel, len(blocks)), out_shape=hal...  2.13 us
    pallas_call x2, Pallas kernels, map_early(): pl.pallas_call(functools.partial(map_kernel, places), out_shape=pltpu.VME...  2.04 us
  transfers between devices with their start and end apart: 21, of which 10 were waited for; matrix products, arithmetic and copies ran while one was open for 0% of the time, Pallas kernels for 19%

profile of v7, /device:TPU:0, one launch (start us, length us, event | category | flops | bytes accessed | tf_op | source)
XLA Modules:
  0.0 49.9 jit_solution(2373821010092636216)
XLA Ops:
  0.6 1.1 %shard_map.94 = (bf16[16,5504]{1,0:T(8,128)(2,1)S(1)}, f32[4,5376]{1,0:T(4,128)S(1)}, f32[4,5376]{1,0:T(4,128)S(1)}) custom-call(bf16[16,5376]{1,0:T(8,128)(2,1)} %hidden.1, s32[1,16]{1,0:T(1,128)} %bitcast.4, s32[1,16]{1,0:T(1,128)} %bitcast.5, f32[1,16]{1,0:T(1,128)} %bitcast.6, f32[4,5376]{1,0:T(4,128)} %depth_gain.1, f32[4,5376]{1,0:T(4,128)} %depth_bias.1), custom_call_target="tpu_custom_call" | custom-call | tf_op jit(solution)/shard_map/pallas_call | solution.py:86
  1.8 2.5 %collective-permute-start.2 = (bf16[16,5504]{1,0:T(8,128)(2,1)S(1)}, bf16[16,5504]{1,0:T(8,128)(2,1)S(1)}, u32[]{:S(2)}, u32[]{:S(2)}) collective-permute-start(bf16[16,5504]{1,0:T(8,128)(2,1)S(1)} %get-tuple-element.21.refs_0_), channel_id=1, source_target_pairs={{0,5},{5,0},{4,9},{9,4},{8,13},{13,8},{12,15},{15,12},{14,11},{11,... | collective-permute-start | bytes 528392 | tf_op jit(solution)/shard_map/ppermute | solution.py:130
  4.3 0.6 %collective-permute-start = (bf16[16,5504]{1,0:T(8,128)(2,1)S(1)}, bf16[16,5504]{1,0:T(8,128)(2,1)S(1)}, u32[]{:S(2)}, u32[]{:S(2)}) collective-permute-start(bf16[16,5504]{1,0:T(8,128)(2,1)S(1)} %get-tuple-element.21.refs_0_), channel_id=1, source_target_pairs={{1,5},{4,0},{5,9},{8,4},{9,13},{12,8},{13,15},{14,12},{15,11},{10,... | collective-permute-start | bytes 528392 | tf_op jit(solution)/shard_map/ppermute | solution.py:130
  4.9 2.6 %shard_map.95.refs_0_ = bf16[1024,5376]{1,0:T(8,128)(2,1)S(1)} custom-call(bf16[1024,5376]{1,0:T(8,128)(2,1)} %head_hbm.3), custom_call_target="tpu_custom_call" | custom-call | bytes 11010048 | tf_op jit(solution)/shard_map/pallas_call | solution.py:229
  7.5 1.6 %collective-permute-done.2.refs_2_.refs_9_ = bf16[16,5504]{1,0:T(8,128)(2,1)S(1)} collective-permute-done((bf16[16,5504]{1,0:T(8,128)(2,1)S(1)}, bf16[16,5504]{1,0:T(8,128)(2,1)S(1)}, u32[]{:S(2)}, u32[]{:S(2)}) %collective-permute-start.2) | collective-permute-done | bytes 176160 | tf_op jit(solution)/shard_map/ppermute | solution.py:130
  9.1 1.1 %collective-permute-start.8 = (bf16[16,5504]{1,0:T(8,128)(2,1)S(1)}, bf16[16,5504]{1,0:T(8,128)(2,1)S(1)}, u32[]{:S(2)}, u32[]{:S(2)}) collective-permute-start(bf16[16,5504]{1,0:T(8,128)(2,1)S(1)} %collective-permute-done.2.refs_2_.refs_9_), channel_id=1, source_target_pairs={{1,4},{4,1},{5,8},{8,5},{9,12},{12,9},{13,14},{14,13},{15,10},{10,... | collective-permute-start | bytes 528392 | tf_op jit(solution)/shard_map/ppermute | solution.py:130
  10.2 0.0 collective-permute-done.refs_3_.refs_1_
  10.2 1.1 %collective-permute-start.1 = (bf16[16,5504]{1,0:T(8,128)(2,1)S(1)}, bf16[16,5504]{1,0:T(8,128)(2,1)S(1)}, u32[]{:S(2)}, u32[]{:S(2)}) collective-permute-start(bf16[16,5504]{1,0:T(8,128)(2,1)S(1)} %collective-permute-done.refs_3_.refs_1_), channel_id=1, source_target_pairs={{1,4},{4,1},{5,8},{8,5},{9,12},{12,9},{13,14},{14,13},{15,10},{10,... | collective-permute-start | bytes 528392 | tf_op jit(solution)/shard_map/ppermute | solution.py:130
  11.3 0.5 collective-permute-start.5
  11.7 0.1 collective-permute-start.6
  11.8 2.2 %collective-permute-done.8.refs_0_.refs_6_ = bf16[16,5504]{1,0:T(8,128)(2,1)S(1)} collective-permute-done((bf16[16,5504]{1,0:T(8,128)(2,1)S(1)}, bf16[16,5504]{1,0:T(8,128)(2,1)S(1)}, u32[]{:S(2)}, u32[]{:S(2)}) %collective-permute-start.8) | collective-permute-done | bytes 176160 | tf_op jit(solution)/shard_map/ppermute | solution.py:130
  14.0 2.5 %collective-permute-start.9 = (bf16[16,5504]{1,0:T(8,128)(2,1)S(1)}, bf16[16,5504]{1,0:T(8,128)(2,1)S(1)}, u32[]{:S(2)}, u32[]{:S(2)}) collective-permute-start(bf16[16,5504]{1,0:T(8,128)(2,1)S(1)} %collective-permute-done.8.refs_0_.refs_6_), channel_id=1, source_target_pairs={{0,5},{5,0},{4,9},{9,4},{8,13},{13,8},{12,15},{15,12},{14,11},{11,... | collective-permute-start | bytes 528392 | tf_op jit(solution)/shard_map/ppermute | solution.py:130
  16.5 0.0 collective-permute-start.7
  16.5 2.6 %shard_map.96.refs_16_ = bf16[1024,5376]{1,0:T(8,128)(2,1)S(1)} custom-call(bf16[1024,5376]{1,0:T(8,128)(2,1)} %head_hbm.3, bf16[1024,5376]{1,0:T(8,128)(2,1)S(1)} %shard_map.95.refs_0_), custom_call_target="tpu_custom_call", output_to_operand_aliasing={{}: (1, {})} | custom-call | bytes 11010048 | tf_op jit(solution)/shard_map/pallas_call | solution.py:229
  19.1 0.0 collective-permute-done.1.refs_1_.refs_14_
  19.1 1.7 %collective-permute-start.4 = (bf16[16,5504]{1,0:T(8,128)(2,1)S(1)}, bf16[16,5504]{1,0:T(8,128)(2,1)S(1)}, u32[]{:S(2)}, u32[]{:S(2)}) collective-permute-start(bf16[16,5504]{1,0:T(8,128)(2,1)S(1)} %collective-permute-done.1.refs_1_.refs_14_), channel_id=1, source_target_pairs={{0,5},{5,0},{4,9},{9,4},{8,13},{13,8},{12,15},{15,12},{14,11},{11,... | collective-permute-start | bytes 528392 | tf_op jit(solution)/shard_map/ppermute | solution.py:130
  20.8 0.0 collective-permute-done.5.refs_1_.refs_8_
  20.8 0.0 collective-permute-start.3
  20.8 0.0 collective-permute-done.6.refs_4_.refs_7_
  20.8 0.5 %collective-permute-start.11 = (bf16[16,5504]{1,0:T(8,128)(2,1)S(1)}, bf16[16,5504]{1,0:T(8,128)(2,1)S(1)}, u32[]{:S(2)}, u32[]{:S(2)}) collective-permute-start(bf16[16,5504]{1,0:T(8,128)(2,1)S(1)} %collective-permute-done.8.refs_0_.refs_6_), channel_id=1, source_target_pairs={{0,1},{1,0},{2,3},{3,2},{4,5},{5,4},{6,7},{7,6},{8,9},{9,8},{10,11... | collective-permute-start | bytes 528392 | tf_op jit(solution)/shard_map/ppermute | solution.py:130
  21.3 0.8 %collective-permute-start.10 = (bf16[16,5504]{1,0:T(8,128)(2,1)S(1)}, bf16[16,5504]{1,0:T(8,128)(2,1)S(1)}, u32[]{:S(2)}, u32[]{:S(2)}) collective-permute-start(bf16[16,5504]{1,0:T(8,128)(2,1)S(1)} %collective-permute-done.9.refs_4_.refs_11_), channel_id=1, source_target_pairs={{1,4},{4,1},{5,8},{8,5},{9,12},{12,9},{13,14},{14,13},{15,10},{10,... | collective-permute-start | bytes 528392 | tf_op jit(solution)/shard_map/ppermute | solution.py:130
  22.1 0.0 collective-permute-done.7.refs_5_.refs_15_
  22.1 1.0 %shard_map.97.refs_8_ = bf16[256,5376]{1,0:T(8,128)(2,1)S(1)} custom-call(bf16[16,5504]{1,0:T(8,128)(2,1)S(1)} %get-tuple-element.21.refs_0_, bf16[16,5504]{1,0:T(8,128)(2,1)S(1)} %collective-permute-done.5.refs_1_.refs_8_, bf16[16,5504]{1,0:T(8,128)(2,1)S(1)} %collective-permute-done.2.refs_2_.refs_9_, ...), custom_call_target="tpu_custom_call" | custom-call | flops 10321920 | bytes 2064384 | tf_op jit(solution)/shard_map/pallas_call | solution.py:199
  23.1 0.9 %collective-permute-done.4.refs_5_.refs_3_ = bf16[16,5504]{1,0:T(8,128)(2,1)S(1)} collective-permute-done((bf16[16,5504]{1,0:T(8,128)(2,1)S(1)}, bf16[16,5504]{1,0:T(8,128)(2,1)S(1)}, u32[]{:S(2)}, u32[]{:S(2)}) %collective-permute-start.4) | collective-permute-done | bytes 176160 | tf_op jit(solution)/shard_map/ppermute | solution.py:130
  24.0 1.2 %collective-permute-start.14 = (bf16[16,5504]{1,0:T(8,128)(2,1)S(1)}, bf16[16,5504]{1,0:T(8,128)(2,1)S(1)}, u32[]{:S(2)}, u32[]{:S(2)}) collective-permute-start(bf16[16,5504]{1,0:T(8,128)(2,1)S(1)} %collective-permute-done.4.refs_5_.refs_3_), channel_id=1, source_target_pairs={{0,1},{1,0},{2,3},{3,2},{4,5},{5,4},{6,7},{7,6},{8,9},{9,8},{10,11... | collective-permute-start | bytes 528392 | tf_op jit(solution)/shard_map/ppermute | solution.py:130
  25.2 0.0 collective-permute-start.12
  25.2 0.0 collective-permute-done.3.refs_3_.refs_2_
  25.2 0.0 collective-permute-done.11.refs_2_.refs_10_
  25.2 1.0 %shard_map.98.refs_19_ = bf16[256,5376]{1,0:T(8,128)(2,1)S(1)} custom-call(bf16[16,5504]{1,0:T(8,128)(2,1)S(1)} %collective-permute-done.8.refs_0_.refs_6_, bf16[16,5504]{1,0:T(8,128)(2,1)S(1)} %collective-permute-done.1.refs_1_.refs_14_, bf16[16,5504]{1,0:T(8,128)(2,1)S(1)} %collective-permute-done.11.refs_2_.refs_10_, ...), custom_call_target="tpu_custom_call", output_to_operand_aliasing={{}: (8, {})} | custom-call | flops 10321920 | bytes 2064384 | tf_op jit(solution)/shard_map/pallas_call | solution.py:199
  26.3 0.3 collective-permute-done.10.refs_4_
  26.6 0.2 collective-permute-start.13
  26.9 0.0 collective-permute-done.12.refs_5_
  26.9 0.0 collective-permute-done.14.refs_13_
  26.9 1.2 %collective-permute-done.13.refs_12_ = bf16[16,5504]{1,0:T(8,128)(2,1)S(1)} collective-permute-done((bf16[16,5504]{1,0:T(8,128)(2,1)S(1)}, bf16[16,5504]{1,0:T(8,128)(2,1)S(1)}, u32[]{:S(2)}, u32[]{:S(2)}) %collective-permute-start.13) | collective-permute-done | bytes 176160 | tf_op jit(solution)/shard_map/ppermute | solution.py:130
  28.0 5.6 %shard_map.99 = (f32[8,2816]{1,0:T(8,128)S(1)}, bf16[272,1024]{1,0:T(8,128)(2,1)S(1)}, bf16[16,256]{1,0:T(8,128)(2,1)S(1)}, f32[1,128]{1,0:T(1,128)S(1)}, bf16[256,5376]{1,0:T(8,128)(2,1)S(1)}) custom-call(bf16[16,5504]{1,0:T(8,128)(2,1)S(1)} %get-tuple-element.21.refs_0_, ...), custom_call_target="tpu_custom_call", output_to_operand_aliasing={{4}: (19, {})} | custom-call | flops 4227858432 | bytes 5505024 | tf_op jit(solution)/shard_map/pallas_call | solution.py:334
  33.6 0.2 collective-permute-start.15
  33.9 2.1 %shard_map.100 = f32[8,2816]{1,0:T(8,128)S(1)} custom-call(bf16[16,5504]{1,0:T(8,128)(2,1)S(1)} %get-tuple-element.21.refs_0_, bf16[16,5504]{1,0:T(8,128)(2,1)S(1)} %collective-permute-done.refs_3_.refs_1_, bf16[16,5504]{1,0:T(8,128)(2,1)S(1)} %collective-permute-done.3.refs_3_.refs_2_, bf16[16,5504]{1,0:T(8,128)(2,1)S(1)} %collective-permute-done.4.refs_5_.refs_3_, ...), custom_call_target="tpu_custom_call" | custom-call | flops 1409286144 | bytes 5505024 | tf_op jit(solution)/shard_map/pallas_call | solution.py:350
  36.0 1.6 %collective-permute-start.18 = (bf16[8,2816]{1,0:T(8,128)(2,1)S(1)}, bf16[8,2816]{1,0:T(8,128)(2,1)S(1)}, u32[]{:S(2)}, u32[]{:S(2)}) collective-permute-start(bf16[8,2816]{1,0:T(8,128)(2,1)S(1)} %fusion), channel_id=1, source_target_pairs={{0,6},{1,7},{2,4},{3,5},{4,2},{5,3},{6,0},{7,1},{8,14},{9,15},{10,... | collective-permute-start | bytes 135176 | tf_op jit(solution)/shard_map/ppermute | solution.py:363
  37.6 0.4 collective-permute-start.17
  38.0 1.5 %collective-permute-start.16 = (bf16[8,2816]{1,0:T(8,128)(2,1)S(1)}, bf16[8,2816]{1,0:T(8,128)(2,1)S(1)}, u32[]{:S(2)}, u32[]{:S(2)}) collective-permute-start(bf16[8,2816]{1,0:T(8,128)(2,1)S(1)} %fusion), channel_id=1, source_target_pairs={{0,2},{1,3},{2,0},{3,1},{4,6},{5,7},{6,4},{7,5},{8,10},{9,11},{10,... | collective-permute-start | bytes 135176 | tf_op jit(solution)/shard_map/ppermute | solution.py:363
  39.6 1.6 %collective-permute-done.18 = bf16[8,2816]{1,0:T(8,128)(2,1)S(1)} collective-permute-done((bf16[8,2816]{1,0:T(8,128)(2,1)S(1)}, bf16[8,2816]{1,0:T(8,128)(2,1)S(1)}, u32[]{:S(2)}, u32[]{:S(2)}) %collective-permute-start.18) | collective-permute-done | bytes 45088 | tf_op jit(solution)/shard_map/ppermute | solution.py:363
  41.1 0.5 collective-permute-done.17
  41.6 0.4 collective-permute-done.16
  42.1 3.6 %collective-permute-start.19 = (bf16[8,2816]{1,0:T(8,128)(2,1)S(1)}, bf16[8,2816]{1,0:T(8,128)(2,1)S(1)}, u32[]{:S(2)}, u32[]{:S(2)}) collective-permute-start(bf16[8,2816]{1,0:T(8,128)(2,1)S(1)} %get-tuple-element.39), channel_id=1, source_target_pairs={{0,8},{1,9},{2,10},{3,11},{4,12},{5,13},{6,14},{7,15},{8,0},{9,1},... | collective-permute-start | bytes 135176 | tf_op jit(solution)/shard_map/ppermute | solution.py:363
  45.7 2.1 %collective-permute-done.19 = bf16[8,2816]{1,0:T(8,128)(2,1)S(1)} collective-permute-done((bf16[8,2816]{1,0:T(8,128)(2,1)S(1)}, bf16[8,2816]{1,0:T(8,128)(2,1)S(1)}, u32[]{:S(2)}, u32[]{:S(2)}) %collective-permute-start.19) | collective-permute-done | bytes 45088 | tf_op jit(solution)/shard_map/ppermute | solution.py:363
  47.8 0.1 collective-permute-start.20
  47.9 1.3 %collective-permute-done.20.given = f32[8,2816]{1,0:T(8,128)S(1)} collective-permute-done((f32[8,2816]{1,0:T(8,128)S(1)}, f32[8,2816]{1,0:T(8,128)S(1)}, u32[]{:S(2)}, u32[]{:S(2)}) %collective-permute-start.20) | collective-permute-done | bytes 90144 | tf_op jit(solution)/shard_map/ppermute | solution.py:363
  49.2 0.7 %shard_map.101 = (f32[1,16]{1,0:T(1,128)}, f32[4,5376]{1,0:T(4,128)}, f32[4,5376]{1,0:T(4,128)}) custom-call(f32[8,2816]{1,0:T(8,128)S(1)} %convert_add_fusion.kept, f32[8,2816]{1,0:T(8,128)S(1)} %collective-permute-done.20.given), custom_call_target="tpu_custom_call" | custom-call | tf_op jit(solution)/shard_map/pallas_call | solution.py:407
  (5 shorter events, 0.1 us)
Async XLA Ops:
  1.8 7.3 %collective-permute-start.2 = (bf16[16,5504]{1,0:T(8,128)(2,1)S(1)}, bf16[16,5504]{1,0:T(8,128)(2,1)S(1)}, u32[]{:S(2)}, u32[]{:S(2)}) collective-permute-start(bf16[16,5504]{1,0:T(8,128)(2,1)S(1)} %get-tuple-element.21.refs_0_), channel_id=1, source_target_pairs={{0,5},{5,0},{4,9},{9,4},{8,13},{13,8},{12,15},{15,12},{14,11},{11,... | collective-permute-start | bytes 528392 | tf_op jit(solution)/shard_map/ppermute | solution.py:130
  4.3 5.9 %collective-permute-start = (bf16[16,5504]{1,0:T(8,128)(2,1)S(1)}, bf16[16,5504]{1,0:T(8,128)(2,1)S(1)}, u32[]{:S(2)}, u32[]{:S(2)}) collective-permute-start(bf16[16,5504]{1,0:T(8,128)(2,1)S(1)} %get-tuple-element.21.refs_0_), channel_id=1, source_target_pairs={{1,5},{4,0},{5,9},{8,4},{9,13},{12,8},{13,15},{14,12},{15,11},{10,... | collective-permute-start | bytes 528392 | tf_op jit(solution)/shard_map/ppermute | solution.py:130
  9.1 4.9 %collective-permute-start.8 = (bf16[16,5504]{1,0:T(8,128)(2,1)S(1)}, bf16[16,5504]{1,0:T(8,128)(2,1)S(1)}, u32[]{:S(2)}, u32[]{:S(2)}) collective-permute-start(bf16[16,5504]{1,0:T(8,128)(2,1)S(1)} %collective-permute-done.2.refs_2_.refs_9_), channel_id=1, source_target_pairs={{1,4},{4,1},{5,8},{8,5},{9,12},{12,9},{13,14},{14,13},{15,10},{10,... | collective-permute-start | bytes 528392 | tf_op jit(solution)/shard_map/ppermute | solution.py:130
  10.2 8.9 %collective-permute-start.1 = (bf16[16,5504]{1,0:T(8,128)(2,1)S(1)}, bf16[16,5504]{1,0:T(8,128)(2,1)S(1)}, u32[]{:S(2)}, u32[]{:S(2)}) collective-permute-start(bf16[16,5504]{1,0:T(8,128)(2,1)S(1)} %collective-permute-done.refs_3_.refs_1_), channel_id=1, source_target_pairs={{1,4},{4,1},{5,8},{8,5},{9,12},{12,9},{13,14},{14,13},{15,10},{10,... | collective-permute-start | bytes 528392 | tf_op jit(solution)/shard_map/ppermute | solution.py:130
  11.3 9.5 %collective-permute-start.5 = (bf16[16,5504]{1,0:T(8,128)(2,1)S(1)}, bf16[16,5504]{1,0:T(8,128)(2,1)S(1)}, u32[]{:S(2)}, u32[]{:S(2)}) collective-permute-start(bf16[16,5504]{1,0:T(8,128)(2,1)S(1)} %get-tuple-element.21.refs_0_), channel_id=1, source_target_pairs={{0,1},{1,0},{2,3},{3,2},{4,5},{5,4},{6,7},{7,6},{8,9},{9,8},{10,11... | collective-permute-start | bytes 528392 | tf_op jit(solution)/shard_map/ppermute | solution.py:130
  11.7 9.0 %collective-permute-start.6 = (bf16[16,5504]{1,0:T(8,128)(2,1)S(1)}, bf16[16,5504]{1,0:T(8,128)(2,1)S(1)}, u32[]{:S(2)}, u32[]{:S(2)}) collective-permute-start(bf16[16,5504]{1,0:T(8,128)(2,1)S(1)} %collective-permute-done.2.refs_2_.refs_9_), channel_id=1, source_target_pairs={{0,1},{1,0},{2,3},{3,2},{4,5},{5,4},{6,7},{7,6},{8,9},{9,8},{10,11... | collective-permute-start | bytes 528392 | tf_op jit(solution)/shard_map/ppermute | solution.py:130
  14.0 7.3 %collective-permute-start.9 = (bf16[16,5504]{1,0:T(8,128)(2,1)S(1)}, bf16[16,5504]{1,0:T(8,128)(2,1)S(1)}, u32[]{:S(2)}, u32[]{:S(2)}) collective-permute-start(bf16[16,5504]{1,0:T(8,128)(2,1)S(1)} %collective-permute-done.8.refs_0_.refs_6_), channel_id=1, source_target_pairs={{0,5},{5,0},{4,9},{9,4},{8,13},{13,8},{12,15},{15,12},{14,11},{11,... | collective-permute-start | bytes 528392 | tf_op jit(solution)/shard_map/ppermute | solution.py:130
  16.5 5.6 %collective-permute-start.7 = (bf16[16,5504]{1,0:T(8,128)(2,1)S(1)}, bf16[16,5504]{1,0:T(8,128)(2,1)S(1)}, u32[]{:S(2)}, u32[]{:S(2)}) collective-permute-start(bf16[16,5504]{1,0:T(8,128)(2,1)S(1)} %collective-permute-done.refs_3_.refs_1_), channel_id=1, source_target_pairs={{0,1},{1,0},{2,3},{3,2},{4,5},{5,4},{6,7},{7,6},{8,9},{9,8},{10,11... | collective-permute-start | bytes 528392 | tf_op jit(solution)/shard_map/ppermute | solution.py:130
  19.1 4.9 %collective-permute-start.4 = (bf16[16,5504]{1,0:T(8,128)(2,1)S(1)}, bf16[16,5504]{1,0:T(8,128)(2,1)S(1)}, u32[]{:S(2)}, u32[]{:S(2)}) collective-permute-start(bf16[16,5504]{1,0:T(8,128)(2,1)S(1)} %collective-permute-done.1.refs_1_.refs_14_), channel_id=1, source_target_pairs={{0,5},{5,0},{4,9},{9,4},{8,13},{13,8},{12,15},{15,12},{14,11},{11,... | collective-permute-start | bytes 528392 | tf_op jit(solution)/shard_map/ppermute | solution.py:130
  20.8 4.5 %collective-permute-start.3 = (bf16[16,5504]{1,0:T(8,128)(2,1)S(1)}, bf16[16,5504]{1,0:T(8,128)(2,1)S(1)}, u32[]{:S(2)}, u32[]{:S(2)}) collective-permute-start(bf16[16,5504]{1,0:T(8,128)(2,1)S(1)} %collective-permute-done.1.refs_1_.refs_14_), channel_id=1, source_target_pairs={{0,1},{1,0},{2,3},{3,2},{4,5},{5,4},{6,7},{7,6},{8,9},{9,8},{10,11... | collective-permute-start | bytes 528392 | tf_op jit(solution)/shard_map/ppermute | solution.py:130
  20.8 4.5 %collective-permute-start.11 = (bf16[16,5504]{1,0:T(8,128)(2,1)S(1)}, bf16[16,5504]{1,0:T(8,128)(2,1)S(1)}, u32[]{:S(2)}, u32[]{:S(2)}) collective-permute-start(bf16[16,5504]{1,0:T(8,128)(2,1)S(1)} %collective-permute-done.8.refs_0_.refs_6_), channel_id=1, source_target_pairs={{0,1},{1,0},{2,3},{3,2},{4,5},{5,4},{6,7},{7,6},{8,9},{9,8},{10,11... | collective-permute-start | bytes 528392 | tf_op jit(solution)/shard_map/ppermute | solution.py:130
  21.3 5.3 %collective-permute-start.10 = (bf16[16,5504]{1,0:T(8,128)(2,1)S(1)}, bf16[16,5504]{1,0:T(8,128)(2,1)S(1)}, u32[]{:S(2)}, u32[]{:S(2)}) collective-permute-start(bf16[16,5504]{1,0:T(8,128)(2,1)S(1)} %collective-permute-done.9.refs_4_.refs_11_), channel_id=1, source_target_pairs={{1,4},{4,1},{5,8},{8,5},{9,12},{12,9},{13,14},{14,13},{15,10},{10,... | collective-permute-start | bytes 528392 | tf_op jit(solution)/shard_map/ppermute | solution.py:130
  24.0 2.8 %collective-permute-start.14 = (bf16[16,5504]{1,0:T(8,128)(2,1)S(1)}, bf16[16,5504]{1,0:T(8,128)(2,1)S(1)}, u32[]{:S(2)}, u32[]{:S(2)}) collective-permute-start(bf16[16,5504]{1,0:T(8,128)(2,1)S(1)} %collective-permute-done.4.refs_5_.refs_3_), channel_id=1, source_target_pairs={{0,1},{1,0},{2,3},{3,2},{4,5},{5,4},{6,7},{7,6},{8,9},{9,8},{10,11... | collective-permute-start | bytes 528392 | tf_op jit(solution)/shard_map/ppermute | solution.py:130
  25.2 1.6 %collective-permute-start.12 = (bf16[16,5504]{1,0:T(8,128)(2,1)S(1)}, bf16[16,5504]{1,0:T(8,128)(2,1)S(1)}, u32[]{:S(2)}, u32[]{:S(2)}) collective-permute-start(bf16[16,5504]{1,0:T(8,128)(2,1)S(1)} %collective-permute-done.9.refs_4_.refs_11_), channel_id=1, source_target_pairs={{0,1},{1,0},{2,3},{3,2},{4,5},{5,4},{6,7},{7,6},{8,9},{9,8},{10,11... | collective-permute-start | bytes 528392 | tf_op jit(solution)/shard_map/ppermute | solution.py:130
  26.6 1.4 %collective-permute-start.13 = (bf16[16,5504]{1,0:T(8,128)(2,1)S(1)}, bf16[16,5504]{1,0:T(8,128)(2,1)S(1)}, u32[]{:S(2)}, u32[]{:S(2)}) collective-permute-start(bf16[16,5504]{1,0:T(8,128)(2,1)S(1)} %collective-permute-done.10.refs_4_), channel_id=1, source_target_pairs={{0,1},{1,0},{2,3},{3,2},{4,5},{5,4},{6,7},{7,6},{8,9},{9,8},{10,11... | collective-permute-start | bytes 528392 | tf_op jit(solution)/shard_map/ppermute | solution.py:130
  33.6 2.4 %collective-permute-start.15 = (f32[8,2816]{1,0:T(8,128)S(1)}, f32[8,2816]{1,0:T(8,128)S(1)}, u32[]{:S(2)}, u32[]{:S(2)}) collective-permute-start(f32[8,2816]{1,0:T(8,128)S(1)} %get-tuple-element.35), channel_id=1, source_target_pairs={{0,1},{1,0},{2,3},{3,2},{4,5},{5,4},{6,7},{7,6},{8,9},{9,8},{10,11... | collective-permute-start | bytes 270344 | tf_op jit(solution)/shard_map/ppermute | solution.py:363
  36.0 5.1 %collective-permute-start.18 = (bf16[8,2816]{1,0:T(8,128)(2,1)S(1)}, bf16[8,2816]{1,0:T(8,128)(2,1)S(1)}, u32[]{:S(2)}, u32[]{:S(2)}) collective-permute-start(bf16[8,2816]{1,0:T(8,128)(2,1)S(1)} %fusion), channel_id=1, source_target_pairs={{0,6},{1,7},{2,4},{3,5},{4,2},{5,3},{6,0},{7,1},{8,14},{9,15},{10,... | collective-permute-start | bytes 135176 | tf_op jit(solution)/shard_map/ppermute | solution.py:363
  37.6 4.0 %collective-permute-start.17 = (bf16[8,2816]{1,0:T(8,128)(2,1)S(1)}, bf16[8,2816]{1,0:T(8,128)(2,1)S(1)}, u32[]{:S(2)}, u32[]{:S(2)}) collective-permute-start(bf16[8,2816]{1,0:T(8,128)(2,1)S(1)} %fusion), channel_id=1, source_target_pairs={{0,4},{1,5},{2,6},{3,7},{4,0},{5,1},{6,2},{7,3},{8,12},{9,13},{10,... | collective-permute-start | bytes 135176 | tf_op jit(solution)/shard_map/ppermute | solution.py:363
  38.0 4.0 %collective-permute-start.16 = (bf16[8,2816]{1,0:T(8,128)(2,1)S(1)}, bf16[8,2816]{1,0:T(8,128)(2,1)S(1)}, u32[]{:S(2)}, u32[]{:S(2)}) collective-permute-start(bf16[8,2816]{1,0:T(8,128)(2,1)S(1)} %fusion), channel_id=1, source_target_pairs={{0,2},{1,3},{2,0},{3,1},{4,6},{5,7},{6,4},{7,5},{8,10},{9,11},{10,... | collective-permute-start | bytes 135176 | tf_op jit(solution)/shard_map/ppermute | solution.py:363
  42.1 5.7 %collective-permute-start.19 = (bf16[8,2816]{1,0:T(8,128)(2,1)S(1)}, bf16[8,2816]{1,0:T(8,128)(2,1)S(1)}, u32[]{:S(2)}, u32[]{:S(2)}) collective-permute-start(bf16[8,2816]{1,0:T(8,128)(2,1)S(1)} %get-tuple-element.39), channel_id=1, source_target_pairs={{0,8},{1,9},{2,10},{3,11},{4,12},{5,13},{6,14},{7,15},{8,0},{9,1},... | collective-permute-start | bytes 135176 | tf_op jit(solution)/shard_map/ppermute | solution.py:363
  47.8 1.4 %collective-permute-start.20 = (f32[8,2816]{1,0:T(8,128)S(1)}, f32[8,2816]{1,0:T(8,128)S(1)}, u32[]{:S(2)}, u32[]{:S(2)}) collective-permute-start(f32[8,2816]{1,0:T(8,128)S(1)} %convert_add_fusion.kept), channel_id=1, source_target_pairs={{0,1},{1,0},{2,3},{3,2},{4,5},{5,4},{6,7},{7,6},{8,9},{9,8},{10,11... | collective-permute-start | bytes 270344 | tf_op jit(solution)/shard_map/ppermute | solution.py:363

commit v8 on v7

--- a/solution.py
+++ b/solution.py
@@ -139,11 +139,8 @@
         if step < half:
             plain = send(plain, hop_pairs(order, step, step > 1))
         if step == 1:
-            head = load(tied_head, 0, 2)
+            head = load(tied_head)
             crossed, head = tie(crossed, head)
-        if step == min(2, half):
-            head = load(tied_head, 1, 2, head)
-            plain, head = tie(plain, head)
         if mapper is not None and step == 3:
             mapped = mapper(None, {i: blocks[i] for i in ready[:6]})
             plain, mapped = tie(plain, mapped)
@@ -209,13 +206,12 @@
     )(*operands)
 
 
-def load_kernel(part, parts, head_hbm, *refs):
-    head, sems = refs[-2:]
+def load_kernel(head_hbm, head, sems):
     count = sems.shape[0]
-    size = head.shape[0] // (parts * count)
+    size = head.shape[0] // count
     copies = []
     for k in range(count):
-        at = pl.ds((part * count + k) * size, size)
+        at = pl.ds(k * size, size)
         copies.append(pltpu.make_async_copy(head_hbm.at[at], head.at[at], sems.at[k]))
     for copy in copies:
         copy.start()
@@ -223,21 +219,19 @@
         copy.wait()
 
 
-def load(tied_head, part, parts, loaded=None):
-    operands = [in_hbm(tied_head)] + ([] if loaded is None else [loaded])
+def load(tied_head):
     voc, width = tied_head.shape
     return pl.pallas_call(
-        functools.partial(load_kernel, part, parts),
+        load_kernel,
         out_shape=pltpu.VMEM(tied_head.shape, BF16),
-        in_specs=[HBM] + [VMEM] * (len(operands) - 1),
+        in_specs=[HBM],
         out_specs=VMEM,
-        input_output_aliases={} if loaded is None else {1: 0},
         scratch_shapes=[pltpu.SemaphoreType.DMA((4,))],
         compiler_params=pltpu.CompilerParams(vmem_limit_bytes=16 << 20),
         cost_estimate=pl.CostEstimate(
-            flops=0, bytes_accessed=4 * voc * width // parts, transcendentals=0
+            flops=0, bytes_accessed=4 * voc * width, transcendentals=0
         ),
-    )(*operands)
+    )(in_hbm(tied_head))
 
 
 def half_sums(blocks, head, slopes, scaled, mass, which, work, out):

time: 50 us -> 48.2 us (0.964)
  starting transfers between devices: 20.1 us -> 19 us
  Pallas kernels: 16.9 us -> 15.9 us
    ppermute x6, waiting for transfers between devices: 5.86 us -> 6.91 us  [sum_over_loop(): lax.ppermute(x, 'loop', [(i, i ^ mask) for i in range(loop)])]
    pallas_call x2 -> x1, Pallas kernels: 5.23 us -> 4.24 us  [load(): pl.pallas_call(load_kernel, out_shape=pltpu.VMEM(tied_head.shape, BF16),...]
    ppermute x15, waiting for transfers between devices: 6.23 us -> 5.48 us  [gather_blocks(): send = lambda x, pairs: lax.ppermute(x, 'loop', pairs)]
    ppermute x6, starting transfers between devices: 7.43 us -> 6.74 us  [sum_over_loop(): lax.ppermute(x, 'loop', [(i, i ^ mask) for i in range(loop)])]
  transfers between devices with their start and end apart: 21 -> 21, of which waited for: 10 -> 9; matrix products, arithmetic and copies ran while one was open for 0% -> 0% of each run, Pallas kernels for 19% -> 17%
where the time goes in v8:
time: 48.2 us; the launch traced here: 48.1 us
  starting transfers between devices  19 us (39%)
  Pallas kernels  15.9 us (33%)
  waiting for transfers between devices  12.4 us (26%)
  between operations  0.72 us (1%)
    ppermute x15, starting transfers between devices, gather_blocks(): send = lambda x, pairs: lax.ppermute(x, 'loop', pairs)  12.3 us
    ppermute x6, waiting for transfers between devices, sum_over_loop(): lax.ppermute(x, 'loop', [(i, i ^ mask) for i in range(loop)])  6.91 us
    ppermute x6, starting transfers between devices, sum_over_loop(): lax.ppermute(x, 'loop', [(i, i ^ mask) for i in range(loop)])  6.74 us
    pallas_call x1, Pallas kernels, main(): pl.pallas_call(functools.partial(front_kernel, loop, levels, len(blocks),...  5.6 us
    ppermute x15, waiting for transfers between devices, gather_blocks(): send = lambda x, pairs: lax.ppermute(x, 'loop', pairs)  5.48 us
    pallas_call x1, Pallas kernels, load(): pl.pallas_call(load_kernel, out_shape=pltpu.VMEM(tied_head.shape, BF16),...  4.24 us
    pallas_call x1, Pallas kernels, main(): pl.pallas_call(functools.partial(back_kernel, len(blocks)), out_shape=hal...  2.13 us
    pallas_call x2, Pallas kernels, map_early(): pl.pallas_call(functools.partial(map_kernel, places), out_shape=pltpu.VME...  2.04 us
  transfers between devices with their start and end apart: 21, of which 9 were waited for; matrix products, arithmetic and copies ran while one was open for 0% of the time, Pallas kernels for 17%

profile of v8, /device:TPU:0, one launch (start us, length us, event | category | flops | bytes accessed | tf_op | source)
XLA Modules:
  0.0 48.1 jit_solution(8659528463495607490)
XLA Ops:
  0.6 1.1 %shard_map.94 = (bf16[16,5504]{1,0:T(8,128)(2,1)S(1)}, f32[4,5376]{1,0:T(4,128)S(1)}, f32[4,5376]{1,0:T(4,128)S(1)}) custom-call(bf16[16,5376]{1,0:T(8,128)(2,1)} %hidden.1, s32[1,16]{1,0:T(1,128)} %bitcast.4, s32[1,16]{1,0:T(1,128)} %bitcast.5, f32[1,16]{1,0:T(1,128)} %bitcast.6, f32[4,5376]{1,0:T(4,128)} %depth_gain.1, f32[4,5376]{1,0:T(4,128)} %depth_bias.1), custom_call_target="tpu_custom_call" | custom-call | tf_op jit(solution)/shard_map/pallas_call | solution.py:86
  1.8 2.5 %collective-permute-start.5 = (bf16[16,5504]{1,0:T(8,128)(2,1)S(1)}, bf16[16,5504]{1,0:T(8,128)(2,1)S(1)}, u32[]{:S(2)}, u32[]{:S(2)}) collective-permute-start(bf16[16,5504]{1,0:T(8,128)(2,1)S(1)} %get-tuple-element.19.refs_0_), channel_id=1, source_target_pairs={{0,5},{5,0},{4,9},{9,4},{8,13},{13,8},{12,15},{15,12},{14,11},{11,... | collective-permute-start | bytes 528392 | tf_op jit(solution)/shard_map/ppermute | solution.py:130
  4.3 0.6 %collective-permute-start = (bf16[16,5504]{1,0:T(8,128)(2,1)S(1)}, bf16[16,5504]{1,0:T(8,128)(2,1)S(1)}, u32[]{:S(2)}, u32[]{:S(2)}) collective-permute-start(bf16[16,5504]{1,0:T(8,128)(2,1)S(1)} %get-tuple-element.19.refs_0_), channel_id=1, source_target_pairs={{1,5},{4,0},{5,9},{8,4},{9,13},{12,8},{13,15},{14,12},{15,11},{10,... | collective-permute-start | bytes 528392 | tf_op jit(solution)/shard_map/ppermute | solution.py:130
  4.9 4.2 %shard_map.95.refs_16_ = bf16[1024,5376]{1,0:T(8,128)(2,1)S(1)} custom-call(bf16[1024,5376]{1,0:T(8,128)(2,1)} %head_hbm.1), custom_call_target="tpu_custom_call" | custom-call | bytes 22020096 | tf_op jit(solution)/shard_map/pallas_call | solution.py:224
  9.1 0.0 collective-permute-done.5.refs_2_.refs_9_
  9.1 1.5 %collective-permute-start.8 = (bf16[16,5504]{1,0:T(8,128)(2,1)S(1)}, bf16[16,5504]{1,0:T(8,128)(2,1)S(1)}, u32[]{:S(2)}, u32[]{:S(2)}) collective-permute-start(bf16[16,5504]{1,0:T(8,128)(2,1)S(1)} %collective-permute-done.5.refs_2_.refs_9_), channel_id=1, source_target_pairs={{1,4},{4,1},{5,8},{8,5},{9,12},{12,9},{13,14},{14,13},{15,10},{10,... | collective-permute-start | bytes 528392 | tf_op jit(solution)/shard_map/ppermute | solution.py:130
  10.6 0.0 collective-permute-done.refs_3_.refs_1_
  10.6 0.7 %collective-permute-start.1 = (bf16[16,5504]{1,0:T(8,128)(2,1)S(1)}, bf16[16,5504]{1,0:T(8,128)(2,1)S(1)}, u32[]{:S(2)}, u32[]{:S(2)}) collective-permute-start(bf16[16,5504]{1,0:T(8,128)(2,1)S(1)} %collective-permute-done.refs_3_.refs_1_), channel_id=1, source_target_pairs={{1,4},{4,1},{5,8},{8,5},{9,12},{12,9},{13,14},{14,13},{15,10},{10,... | collective-permute-start | bytes 528392 | tf_op jit(solution)/shard_map/ppermute | solution.py:130
  11.3 0.5 collective-permute-start.4
  11.7 0.1 collective-permute-start.7
  11.8 2.3 %collective-permute-done.8.refs_0_.refs_6_ = bf16[16,5504]{1,0:T(8,128)(2,1)S(1)} collective-permute-done((bf16[16,5504]{1,0:T(8,128)(2,1)S(1)}, bf16[16,5504]{1,0:T(8,128)(2,1)S(1)}, u32[]{:S(2)}, u32[]{:S(2)}) %collective-permute-start.8) | collective-permute-done | bytes 176160 | tf_op jit(solution)/shard_map/ppermute | solution.py:130
  14.1 2.4 %collective-permute-start.9 = (bf16[16,5504]{1,0:T(8,128)(2,1)S(1)}, bf16[16,5504]{1,0:T(8,128)(2,1)S(1)}, u32[]{:S(2)}, u32[]{:S(2)}) collective-permute-start(bf16[16,5504]{1,0:T(8,128)(2,1)S(1)} %collective-permute-done.8.refs_0_.refs_6_), channel_id=1, source_target_pairs={{0,5},{5,0},{4,9},{9,4},{8,13},{13,8},{12,15},{15,12},{14,11},{11,... | collective-permute-start | bytes 528392 | tf_op jit(solution)/shard_map/ppermute | solution.py:130
  16.5 0.0 collective-permute-start.6
  16.5 0.0 collective-permute-done.1.refs_1_.refs_14_
  16.5 1.6 %collective-permute-start.3 = (bf16[16,5504]{1,0:T(8,128)(2,1)S(1)}, bf16[16,5504]{1,0:T(8,128)(2,1)S(1)}, u32[]{:S(2)}, u32[]{:S(2)}) collective-permute-start(bf16[16,5504]{1,0:T(8,128)(2,1)S(1)} %collective-permute-done.1.refs_1_.refs_14_), channel_id=1, source_target_pairs={{0,5},{5,0},{4,9},{9,4},{8,13},{13,8},{12,15},{15,12},{14,11},{11,... | collective-permute-start | bytes 528392 | tf_op jit(solution)/shard_map/ppermute | solution.py:130
  18.1 0.0 collective-permute-done.4.refs_1_.refs_8_
  18.1 0.0 collective-permute-start.2
  18.1 0.0 collective-permute-done.7.refs_5_.refs_15_
  18.1 0.5 %collective-permute-start.11 = (bf16[16,5504]{1,0:T(8,128)(2,1)S(1)}, bf16[16,5504]{1,0:T(8,128)(2,1)S(1)}, u32[]{:S(2)}, u32[]{:S(2)}) collective-permute-start(bf16[16,5504]{1,0:T(8,128)(2,1)S(1)} %collective-permute-done.8.refs_0_.refs_6_), channel_id=1, source_target_pairs={{0,1},{1,0},{2,3},{3,2},{4,5},{5,4},{6,7},{7,6},{8,9},{9,8},{10,11... | collective-permute-start | bytes 528392 | tf_op jit(solution)/shard_map/ppermute | solution.py:130
  18.6 1.0 %collective-permute-done.9.refs_4_.refs_11_ = bf16[16,5504]{1,0:T(8,128)(2,1)S(1)} collective-permute-done((bf16[16,5504]{1,0:T(8,128)(2,1)S(1)}, bf16[16,5504]{1,0:T(8,128)(2,1)S(1)}, u32[]{:S(2)}, u32[]{:S(2)}) %collective-permute-start.9) | collective-permute-done | bytes 176160 | tf_op jit(solution)/shard_map/ppermute | solution.py:130
  19.6 1.3 %collective-permute-start.10 = (bf16[16,5504]{1,0:T(8,128)(2,1)S(1)}, bf16[16,5504]{1,0:T(8,128)(2,1)S(1)}, u32[]{:S(2)}, u32[]{:S(2)}) collective-permute-start(bf16[16,5504]{1,0:T(8,128)(2,1)S(1)} %collective-permute-done.9.refs_4_.refs_11_), channel_id=1, source_target_pairs={{1,4},{4,1},{5,8},{8,5},{9,12},{12,9},{13,14},{14,13},{15,10},{10,... | collective-permute-start | bytes 528392 | tf_op jit(solution)/shard_map/ppermute | solution.py:130
  20.9 0.0 collective-permute-done.6.refs_4_.refs_7_
  20.9 1.0 %shard_map.96.refs_8_ = bf16[256,5376]{1,0:T(8,128)(2,1)S(1)} custom-call(bf16[16,5504]{1,0:T(8,128)(2,1)S(1)} %get-tuple-element.19.refs_0_, bf16[16,5504]{1,0:T(8,128)(2,1)S(1)} %collective-permute-done.4.refs_1_.refs_8_, bf16[16,5504]{1,0:T(8,128)(2,1)S(1)} %collective-permute-done.5.refs_2_.refs_9_, ...), custom_call_target="tpu_custom_call" | custom-call | flops 10321920 | bytes 2064384 | tf_op jit(solution)/shard_map/pallas_call | solution.py:196
  22.0 0.0 collective-permute-done.3.refs_5_.refs_3_
  22.0 0.3 collective-permute-start.14
  22.3 0.3 collective-permute-start.12
  22.6 0.0 collective-permute-done.2.refs_3_.refs_2_
  22.6 0.0 collective-permute-done.11.refs_2_.refs_10_
  22.6 1.0 %shard_map.97.refs_19_ = bf16[256,5376]{1,0:T(8,128)(2,1)S(1)} custom-call(bf16[16,5504]{1,0:T(8,128)(2,1)S(1)} %collective-permute-done.8.refs_0_.refs_6_, bf16[16,5504]{1,0:T(8,128)(2,1)S(1)} %collective-permute-done.1.refs_1_.refs_14_, bf16[16,5504]{1,0:T(8,128)(2,1)S(1)} %collective-permute-done.11.refs_2_.refs_10_, ...), custom_call_target="tpu_custom_call", output_to_operand_aliasing={{}: (8, {})} | custom-call | flops 10321920 | bytes 2064384 | tf_op jit(solution)/shard_map/pallas_call | solution.py:196
  23.6 0.9 %collective-permute-done.10.refs_4_ = bf16[16,5504]{1,0:T(8,128)(2,1)S(1)} collective-permute-done((bf16[16,5504]{1,0:T(8,128)(2,1)S(1)}, bf16[16,5504]{1,0:T(8,128)(2,1)S(1)}, u32[]{:S(2)}, u32[]{:S(2)}) %collective-permute-start.10) | collective-permute-done | bytes 176160 | tf_op jit(solution)/shard_map/ppermute | solution.py:130
  24.5 0.1 collective-permute-start.13
  24.6 0.0 collective-permute-done.12.refs_5_
  24.6 0.0 collective-permute-done.14.refs_13_
  24.6 1.3 %collective-permute-done.13.refs_12_ = bf16[16,5504]{1,0:T(8,128)(2,1)S(1)} collective-permute-done((bf16[16,5504]{1,0:T(8,128)(2,1)S(1)}, bf16[16,5504]{1,0:T(8,128)(2,1)S(1)}, u32[]{:S(2)}, u32[]{:S(2)}) %collective-permute-start.13) | collective-permute-done | bytes 176160 | tf_op jit(solution)/shard_map/ppermute | solution.py:130
  25.9 5.6 %shard_map.98 = (f32[8,2816]{1,0:T(8,128)S(1)}, bf16[272,1024]{1,0:T(8,128)(2,1)S(1)}, bf16[16,256]{1,0:T(8,128)(2,1)S(1)}, f32[1,128]{1,0:T(1,128)S(1)}, bf16[256,5376]{1,0:T(8,128)(2,1)S(1)}) custom-call(bf16[16,5504]{1,0:T(8,128)(2,1)S(1)} %get-tuple-element.19.refs_0_, ...), custom_call_target="tpu_custom_call", output_to_operand_aliasing={{4}: (19, {})} | custom-call | flops 4227858432 | bytes 5505024 | tf_op jit(solution)/shard_map/pallas_call | solution.py:328
  31.5 0.1 collective-permute-start.15
  31.6 2.1 %shard_map.99 = f32[8,2816]{1,0:T(8,128)S(1)} custom-call(bf16[16,5504]{1,0:T(8,128)(2,1)S(1)} %get-tuple-element.19.refs_0_, bf16[16,5504]{1,0:T(8,128)(2,1)S(1)} %collective-permute-done.refs_3_.refs_1_, bf16[16,5504]{1,0:T(8,128)(2,1)S(1)} %collective-permute-done.2.refs_3_.refs_2_, bf16[16,5504]{1,0:T(8,128)(2,1)S(1)} %collective-permute-done.3.refs_5_.refs_3_, ...), custom_call_target="tpu_custom_call" | custom-call | flops 1409286144 | bytes 5505024 | tf_op jit(solution)/shard_map/pallas_call | solution.py:344
  33.8 2.7 %collective-permute-start.18 = (bf16[8,2816]{1,0:T(8,128)(2,1)S(1)}, bf16[8,2816]{1,0:T(8,128)(2,1)S(1)}, u32[]{:S(2)}, u32[]{:S(2)}) collective-permute-start(bf16[8,2816]{1,0:T(8,128)(2,1)S(1)} %fusion), channel_id=1, source_target_pairs={{0,6},{1,7},{2,4},{3,5},{4,2},{5,3},{6,0},{7,1},{8,14},{9,15},{10,... | collective-permute-start | bytes 135176 | tf_op jit(solution)/shard_map/ppermute | solution.py:357
  36.5 0.4 collective-permute-start.17
  36.9 0.7 %collective-permute-start.16 = (bf16[8,2816]{1,0:T(8,128)(2,1)S(1)}, bf16[8,2816]{1,0:T(8,128)(2,1)S(1)}, u32[]{:S(2)}, u32[]{:S(2)}) collective-permute-start(bf16[8,2816]{1,0:T(8,128)(2,1)S(1)} %fusion), channel_id=1, source_target_pairs={{0,2},{1,3},{2,0},{3,1},{4,6},{5,7},{6,4},{7,5},{8,10},{9,11},{10,... | collective-permute-start | bytes 135176 | tf_op jit(solution)/shard_map/ppermute | solution.py:357
  37.6 1.2 %collective-permute-done.18 = bf16[8,2816]{1,0:T(8,128)(2,1)S(1)} collective-permute-done((bf16[8,2816]{1,0:T(8,128)(2,1)S(1)}, bf16[8,2816]{1,0:T(8,128)(2,1)S(1)}, u32[]{:S(2)}, u32[]{:S(2)}) %collective-permute-start.18) | collective-permute-done | bytes 45088 | tf_op jit(solution)/shard_map/ppermute | solution.py:357
  38.8 1.7 %collective-permute-done.17 = bf16[8,2816]{1,0:T(8,128)(2,1)S(1)} collective-permute-done((bf16[8,2816]{1,0:T(8,128)(2,1)S(1)}, bf16[8,2816]{1,0:T(8,128)(2,1)S(1)}, u32[]{:S(2)}, u32[]{:S(2)}) %collective-permute-start.17) | collective-permute-done | bytes 45088 | tf_op jit(solution)/shard_map/ppermute | solution.py:357
  40.5 0.4 collective-permute-done.16
  41.0 2.7 %collective-permute-start.19 = (bf16[8,2816]{1,0:T(8,128)(2,1)S(1)}, bf16[8,2816]{1,0:T(8,128)(2,1)S(1)}, u32[]{:S(2)}, u32[]{:S(2)}) collective-permute-start(bf16[8,2816]{1,0:T(8,128)(2,1)S(1)} %get-tuple-element.35), channel_id=1, source_target_pairs={{0,8},{1,9},{2,10},{3,11},{4,12},{5,13},{6,14},{7,15},{8,0},{9,1},... | collective-permute-start | bytes 135176 | tf_op jit(solution)/shard_map/ppermute | solution.py:357
  43.7 2.3 %collective-permute-done.19 = bf16[8,2816]{1,0:T(8,128)(2,1)S(1)} collective-permute-done((bf16[8,2816]{1,0:T(8,128)(2,1)S(1)}, bf16[8,2816]{1,0:T(8,128)(2,1)S(1)}, u32[]{:S(2)}, u32[]{:S(2)}) %collective-permute-start.19) | collective-permute-done | bytes 45088 | tf_op jit(solution)/shard_map/ppermute | solution.py:357
  46.0 0.1 collective-permute-start.20
  46.1 1.3 %collective-permute-done.20.given = f32[8,2816]{1,0:T(8,128)S(1)} collective-permute-done((f32[8,2816]{1,0:T(8,128)S(1)}, f32[8,2816]{1,0:T(8,128)S(1)}, u32[]{:S(2)}, u32[]{:S(2)}) %collective-permute-start.20) | collective-permute-done | bytes 90144 | tf_op jit(solution)/shard_map/ppermute | solution.py:357
  47.4 0.7 %shard_map.100 = (f32[1,16]{1,0:T(1,128)}, f32[4,5376]{1,0:T(4,128)}, f32[4,5376]{1,0:T(4,128)}) custom-call(f32[8,2816]{1,0:T(8,128)S(1)} %convert_add_fusion.kept, f32[8,2816]{1,0:T(8,128)S(1)} %collective-permute-done.20.given), custom_call_target="tpu_custom_call" | custom-call | tf_op jit(solution)/shard_map/pallas_call | solution.py:401
  (4 shorter events, 0.1 us)
Async XLA Ops:
  1.8 7.4 %collective-permute-start.5 = (bf16[16,5504]{1,0:T(8,128)(2,1)S(1)}, bf16[16,5504]{1,0:T(8,128)(2,1)S(1)}, u32[]{:S(2)}, u32[]{:S(2)}) collective-permute-start(bf16[16,5504]{1,0:T(8,128)(2,1)S(1)} %get-tuple-element.19.refs_0_), channel_id=1, source_target_pairs={{0,5},{5,0},{4,9},{9,4},{8,13},{13,8},{12,15},{15,12},{14,11},{11,... | collective-permute-start | bytes 528392 | tf_op jit(solution)/shard_map/ppermute | solution.py:130
  4.3 6.3 %collective-permute-start = (bf16[16,5504]{1,0:T(8,128)(2,1)S(1)}, bf16[16,5504]{1,0:T(8,128)(2,1)S(1)}, u32[]{:S(2)}, u32[]{:S(2)}) collective-permute-start(bf16[16,5504]{1,0:T(8,128)(2,1)S(1)} %get-tuple-element.19.refs_0_), channel_id=1, source_target_pairs={{1,5},{4,0},{5,9},{8,4},{9,13},{12,8},{13,15},{14,12},{15,11},{10,... | collective-permute-start | bytes 528392 | tf_op jit(solution)/shard_map/ppermute | solution.py:130
  9.1 4.9 %collective-permute-start.8 = (bf16[16,5504]{1,0:T(8,128)(2,1)S(1)}, bf16[16,5504]{1,0:T(8,128)(2,1)S(1)}, u32[]{:S(2)}, u32[]{:S(2)}) collective-permute-start(bf16[16,5504]{1,0:T(8,128)(2,1)S(1)} %collective-permute-done.5.refs_2_.refs_9_), channel_id=1, source_target_pairs={{1,4},{4,1},{5,8},{8,5},{9,12},{12,9},{13,14},{14,13},{15,10},{10,... | collective-permute-start | bytes 528392 | tf_op jit(solution)/shard_map/ppermute | solution.py:130
  10.6 5.9 %collective-permute-start.1 = (bf16[16,5504]{1,0:T(8,128)(2,1)S(1)}, bf16[16,5504]{1,0:T(8,128)(2,1)S(1)}, u32[]{:S(2)}, u32[]{:S(2)}) collective-permute-start(bf16[16,5504]{1,0:T(8,128)(2,1)S(1)} %collective-permute-done.refs_3_.refs_1_), channel_id=1, source_target_pairs={{1,4},{4,1},{5,8},{8,5},{9,12},{12,9},{13,14},{14,13},{15,10},{10,... | collective-permute-start | bytes 528392 | tf_op jit(solution)/shard_map/ppermute | solution.py:130
  11.3 6.8 %collective-permute-start.4 = (bf16[16,5504]{1,0:T(8,128)(2,1)S(1)}, bf16[16,5504]{1,0:T(8,128)(2,1)S(1)}, u32[]{:S(2)}, u32[]{:S(2)}) collective-permute-start(bf16[16,5504]{1,0:T(8,128)(2,1)S(1)} %get-tuple-element.19.refs_0_), channel_id=1, source_target_pairs={{0,1},{1,0},{2,3},{3,2},{4,5},{5,4},{6,7},{7,6},{8,9},{9,8},{10,11... | collective-permute-start | bytes 528392 | tf_op jit(solution)/shard_map/ppermute | solution.py:130
  11.7 6.3 %collective-permute-start.7 = (bf16[16,5504]{1,0:T(8,128)(2,1)S(1)}, bf16[16,5504]{1,0:T(8,128)(2,1)S(1)}, u32[]{:S(2)}, u32[]{:S(2)}) collective-permute-start(bf16[16,5504]{1,0:T(8,128)(2,1)S(1)} %collective-permute-done.refs_3_.refs_1_), channel_id=1, source_target_pairs={{0,1},{1,0},{2,3},{3,2},{4,5},{5,4},{6,7},{7,6},{8,9},{9,8},{10,11... | collective-permute-start | bytes 528392 | tf_op jit(solution)/shard_map/ppermute | solution.py:130
  14.1 5.5 %collective-permute-start.9 = (bf16[16,5504]{1,0:T(8,128)(2,1)S(1)}, bf16[16,5504]{1,0:T(8,128)(2,1)S(1)}, u32[]{:S(2)}, u32[]{:S(2)}) collective-permute-start(bf16[16,5504]{1,0:T(8,128)(2,1)S(1)} %collective-permute-done.8.refs_0_.refs_6_), channel_id=1, source_target_pairs={{0,5},{5,0},{4,9},{9,4},{8,13},{13,8},{12,15},{15,12},{14,11},{11,... | collective-permute-start | bytes 528392 | tf_op jit(solution)/shard_map/ppermute | solution.py:130
  16.5 4.5 %collective-permute-start.6 = (bf16[16,5504]{1,0:T(8,128)(2,1)S(1)}, bf16[16,5504]{1,0:T(8,128)(2,1)S(1)}, u32[]{:S(2)}, u32[]{:S(2)}) collective-permute-start(bf16[16,5504]{1,0:T(8,128)(2,1)S(1)} %collective-permute-done.5.refs_2_.refs_9_), channel_id=1, source_target_pairs={{0,1},{1,0},{2,3},{3,2},{4,5},{5,4},{6,7},{7,6},{8,9},{9,8},{10,11... | collective-permute-start | bytes 528392 | tf_op jit(solution)/shard_map/ppermute | solution.py:130
  16.5 5.5 %collective-permute-start.3 = (bf16[16,5504]{1,0:T(8,128)(2,1)S(1)}, bf16[16,5504]{1,0:T(8,128)(2,1)S(1)}, u32[]{:S(2)}, u32[]{:S(2)}) collective-permute-start(bf16[16,5504]{1,0:T(8,128)(2,1)S(1)} %collective-permute-done.1.refs_1_.refs_14_), channel_id=1, source_target_pairs={{0,5},{5,0},{4,9},{9,4},{8,13},{13,8},{12,15},{15,12},{14,11},{11,... | collective-permute-start | bytes 528392 | tf_op jit(solution)/shard_map/ppermute | solution.py:130
  18.1 4.5 %collective-permute-start.2 = (bf16[16,5504]{1,0:T(8,128)(2,1)S(1)}, bf16[16,5504]{1,0:T(8,128)(2,1)S(1)}, u32[]{:S(2)}, u32[]{:S(2)}) collective-permute-start(bf16[16,5504]{1,0:T(8,128)(2,1)S(1)} %collective-permute-done.1.refs_1_.refs_14_), channel_id=1, source_target_pairs={{0,1},{1,0},{2,3},{3,2},{4,5},{5,4},{6,7},{7,6},{8,9},{9,8},{10,11... | collective-permute-start | bytes 528392 | tf_op jit(solution)/shard_map/ppermute | solution.py:130
  18.1 4.5 %collective-permute-start.11 = (bf16[16,5504]{1,0:T(8,128)(2,1)S(1)}, bf16[16,5504]{1,0:T(8,128)(2,1)S(1)}, u32[]{:S(2)}, u32[]{:S(2)}) collective-permute-start(bf16[16,5504]{1,0:T(8,128)(2,1)S(1)} %collective-permute-done.8.refs_0_.refs_6_), channel_id=1, source_target_pairs={{0,1},{1,0},{2,3},{3,2},{4,5},{5,4},{6,7},{7,6},{8,9},{9,8},{10,11... | collective-permute-start | bytes 528392 | tf_op jit(solution)/shard_map/ppermute | solution.py:130
  19.6 4.9 %collective-permute-start.10 = (bf16[16,5504]{1,0:T(8,128)(2,1)S(1)}, bf16[16,5504]{1,0:T(8,128)(2,1)S(1)}, u32[]{:S(2)}, u32[]{:S(2)}) collective-permute-start(bf16[16,5504]{1,0:T(8,128)(2,1)S(1)} %collective-permute-done.9.refs_4_.refs_11_), channel_id=1, source_target_pairs={{1,4},{4,1},{5,8},{8,5},{9,12},{12,9},{13,14},{14,13},{15,10},{10,... | collective-permute-start | bytes 528392 | tf_op jit(solution)/shard_map/ppermute | solution.py:130
  22.0 2.6 %collective-permute-start.14 = (bf16[16,5504]{1,0:T(8,128)(2,1)S(1)}, bf16[16,5504]{1,0:T(8,128)(2,1)S(1)}, u32[]{:S(2)}, u32[]{:S(2)}) collective-permute-start(bf16[16,5504]{1,0:T(8,128)(2,1)S(1)} %collective-permute-done.3.refs_5_.refs_3_), channel_id=1, source_target_pairs={{0,1},{1,0},{2,3},{3,2},{4,5},{5,4},{6,7},{7,6},{8,9},{9,8},{10,11... | collective-permute-start | bytes 528392 | tf_op jit(solution)/shard_map/ppermute | solution.py:130
  22.3 2.3 %collective-permute-start.12 = (bf16[16,5504]{1,0:T(8,128)(2,1)S(1)}, bf16[16,5504]{1,0:T(8,128)(2,1)S(1)}, u32[]{:S(2)}, u32[]{:S(2)}) collective-permute-start(bf16[16,5504]{1,0:T(8,128)(2,1)S(1)} %collective-permute-done.9.refs_4_.refs_11_), channel_id=1, source_target_pairs={{0,1},{1,0},{2,3},{3,2},{4,5},{5,4},{6,7},{7,6},{8,9},{9,8},{10,11... | collective-permute-start | bytes 528392 | tf_op jit(solution)/shard_map/ppermute | solution.py:130
  24.5 1.4 %collective-permute-start.13 = (bf16[16,5504]{1,0:T(8,128)(2,1)S(1)}, bf16[16,5504]{1,0:T(8,128)(2,1)S(1)}, u32[]{:S(2)}, u32[]{:S(2)}) collective-permute-start(bf16[16,5504]{1,0:T(8,128)(2,1)S(1)} %collective-permute-done.10.refs_4_), channel_id=1, source_target_pairs={{0,1},{1,0},{2,3},{3,2},{4,5},{5,4},{6,7},{7,6},{8,9},{9,8},{10,11... | collective-permute-start | bytes 528392 | tf_op jit(solution)/shard_map/ppermute | solution.py:130
  31.5 2.3 %collective-permute-start.15 = (f32[8,2816]{1,0:T(8,128)S(1)}, f32[8,2816]{1,0:T(8,128)S(1)}, u32[]{:S(2)}, u32[]{:S(2)}) collective-permute-start(f32[8,2816]{1,0:T(8,128)S(1)} %get-tuple-element.31), channel_id=1, source_target_pairs={{0,1},{1,0},{2,3},{3,2},{4,5},{5,4},{6,7},{7,6},{8,9},{9,8},{10,11... | collective-permute-start | bytes 270344 | tf_op jit(solution)/shard_map/ppermute | solution.py:357
  33.8 5.0 %collective-permute-start.18 = (bf16[8,2816]{1,0:T(8,128)(2,1)S(1)}, bf16[8,2816]{1,0:T(8,128)(2,1)S(1)}, u32[]{:S(2)}, u32[]{:S(2)}) collective-permute-start(bf16[8,2816]{1,0:T(8,128)(2,1)S(1)} %fusion), channel_id=1, source_target_pairs={{0,6},{1,7},{2,4},{3,5},{4,2},{5,3},{6,0},{7,1},{8,14},{9,15},{10,... | collective-permute-start | bytes 135176 | tf_op jit(solution)/shard_map/ppermute | solution.py:357
  36.5 4.0 %collective-permute-start.17 = (bf16[8,2816]{1,0:T(8,128)(2,1)S(1)}, bf16[8,2816]{1,0:T(8,128)(2,1)S(1)}, u32[]{:S(2)}, u32[]{:S(2)}) collective-permute-start(bf16[8,2816]{1,0:T(8,128)(2,1)S(1)} %fusion), channel_id=1, source_target_pairs={{0,4},{1,5},{2,6},{3,7},{4,0},{5,1},{6,2},{7,3},{8,12},{9,13},{10,... | collective-permute-start | bytes 135176 | tf_op jit(solution)/shard_map/ppermute | solution.py:357
  36.9 4.0 %collective-permute-start.16 = (bf16[8,2816]{1,0:T(8,128)(2,1)S(1)}, bf16[8,2816]{1,0:T(8,128)(2,1)S(1)}, u32[]{:S(2)}, u32[]{:S(2)}) collective-permute-start(bf16[8,2816]{1,0:T(8,128)(2,1)S(1)} %fusion), channel_id=1, source_target_pairs={{0,2},{1,3},{2,0},{3,1},{4,6},{5,7},{6,4},{7,5},{8,10},{9,11},{10,... | collective-permute-start | bytes 135176 | tf_op jit(solution)/shard_map/ppermute | solution.py:357
  41.0 5.0 %collective-permute-start.19 = (bf16[8,2816]{1,0:T(8,128)(2,1)S(1)}, bf16[8,2816]{1,0:T(8,128)(2,1)S(1)}, u32[]{:S(2)}, u32[]{:S(2)}) collective-permute-start(bf16[8,2816]{1,0:T(8,128)(2,1)S(1)} %get-tuple-element.35), channel_id=1, source_target_pairs={{0,8},{1,9},{2,10},{3,11},{4,12},{5,13},{6,14},{7,15},{8,0},{9,1},... | collective-permute-start | bytes 135176 | tf_op jit(solution)/shard_map/ppermute | solution.py:357
  46.0 1.4 %collective-permute-start.20 = (f32[8,2816]{1,0:T(8,128)S(1)}, f32[8,2816]{1,0:T(8,128)S(1)}, u32[]{:S(2)}, u32[]{:S(2)}) collective-permute-start(f32[8,2816]{1,0:T(8,128)S(1)} %convert_add_fusion.kept), channel_id=1, source_target_pairs={{0,1},{1,0},{2,3},{3,2},{4,5},{5,4},{6,7},{7,6},{8,9},{9,8},{10,11... | collective-permute-start | bytes 270344 | tf_op jit(solution)/shard_map/ppermute | solution.py:357

commit v9 on v8

--- a/solution.py
+++ b/solution.py
@@ -10,6 +10,8 @@
 BF16 = jnp.bfloat16
 F32 = jnp.float32
 LANES = 128
+CUTS = 42
+TOGETHER = 2
 NT = (((1,), (1,)), ((), ()))
 VMEM = pl.BlockSpec(memory_space=pltpu.VMEM)
 HBM = pl.BlockSpec(memory_space=pl.ANY)
@@ -40,11 +42,11 @@
 
 def prep_kernel(
     hidden, exit_depth, teacher, normalizer, depth_gain, depth_bias,
-    out, gain_out, bias_out, row_buf, int_buf, float_buf, sems,
+    out, gain_out, bias_out, int_buf, float_buf, sems,
 ):
     rows, width = hidden.shape
     copies = [
-        pltpu.make_async_copy(hidden, row_buf, sems.at[0]),
+        pltpu.make_async_copy(hidden, out.at[:, pl.ds(0, hidden.shape[1])], sems.at[0]),
         pltpu.make_async_copy(exit_depth, int_buf.at[0], sems.at[1]),
         pltpu.make_async_copy(teacher, int_buf.at[1], sems.at[2]),
         pltpu.make_async_copy(normalizer, float_buf, sems.at[3]),
@@ -53,13 +55,8 @@
     ]
     for copy in copies:
         copy.start()
-    for copy in copies[:4]:
+    for copy in copies[1:4]:
         copy.wait()
-    block = row_buf[...]
-    out[:, :width] = block
-    wide = block.astype(F32)
-    mean = jnp.sum(wide * wide, axis=1, keepdims=True) * (1.0 / width)
-    scale = lax.rsqrt(mean + 1e-06)
     down = lax.broadcasted_iota(jnp.int32, (rows, rows), 0)
     across = lax.broadcasted_iota(jnp.int32, (rows, rows), 1)
 
@@ -68,10 +65,14 @@
         return jnp.sum(jnp.where(down == across, square, 0.0), axis=1, keepdims=True)
 
     token = int_buf[1]
-    columns = pieces(scale) + pieces(column(float_buf[...]))
+    columns = pieces(column(float_buf[...]))
     for digit in (token & 127, (token >> 7) & 127, token >> 14):
         columns.append(column(digit.astype(F32)))
     columns.append(column(int_buf[0].astype(F32)))
+    copies[0].wait()
+    wide = out[:, :width].astype(F32)
+    mean = jnp.sum(wide * wide, axis=1, keepdims=True) * (1.0 / width)
+    columns = pieces(lax.rsqrt(mean + 1e-06)) + columns
     lane = lax.broadcasted_iota(jnp.int32, (rows, LANES), 1)
     meta = jnp.zeros((rows, LANES), F32)
     for i, value in enumerate(columns):
@@ -93,7 +94,6 @@
         in_specs=[HBM] * 6,
         out_specs=(VMEM, VMEM, VMEM),
         scratch_shapes=[
-            pltpu.VMEM((rows, width), BF16),
             pltpu.VMEM((2, 1, rows), jnp.int32),
             pltpu.VMEM((1, rows), F32),
             pltpu.SemaphoreType.DMA((6,)),
@@ -159,33 +159,37 @@
         else:
             blocks[theirs + far] = swap(crossed)
             ready += [mine + far, theirs + far]
-    return blocks, head, mapped, ready[12:] if mapper is not None else ready
-
-
-def map_rows(block, gain, bias, mapped, first):
-    rows, width = block.shape[0], mapped.shape[1]
+            if mapper is not None:
+                mapped = mapper(mapped, {i: blocks[i] for i in ready[12:15]})
+    return blocks, head, mapped, ready[15:] if mapper is not None else ready
+
+
+def map_rows(blocks, places, gain, bias, mapped):
+    size, width = blocks[0].shape[0], mapped.shape[1]
     levels = gain.shape[0]
-    meta = block[:, width:].astype(F32)
-    scale = (meta[:, 0:1] + meta[:, 1:2]) + meta[:, 2:3]
-    depth = meta[:, 9:10]
-    cuts = 3 if width % (3 * LANES) == 0 else 1
-    cut = width // cuts
-    for k in range(cuts):
-        at = slice(k * cut, (k + 1) * cut)
-        g, c = gain[0:1, at], bias[0:1, at]
-        for level in range(1, levels):
-            here = depth == float(level)
-            g = jnp.where(here, gain[level : level + 1, at], g)
-            c = jnp.where(here, bias[level : level + 1, at], c)
-        value = (block[:, at].astype(F32) * scale) * g + c
-        mapped[first : first + rows, at] = value.astype(BF16)
+    cut = width // CUTS if width % (CUTS * LANES) == 0 else LANES
+    for first in range(0, len(blocks), TOGETHER):
+        some = blocks[first : first + TOGETHER]
+        meta = jnp.concatenate([b[:, width:] for b in some], axis=0).astype(F32)
+        scale = (meta[:, 0:1] + meta[:, 1:2]) + meta[:, 2:3]
+        depth = meta[:, 9:10]
+        for start in range(0, width, cut):
+            at = slice(start, start + cut)
+            g, c = gain[0:1, at], bias[0:1, at]
+            for level in range(1, levels):
+                here = depth == float(level)
+                g = jnp.where(here, gain[level : level + 1, at], g)
+                c = jnp.where(here, bias[level : level + 1, at], c)
+            wide = jnp.concatenate([b[:, at] for b in some], axis=0).astype(F32)
+            value = ((wide * scale) * g + c).astype(BF16)
+            for i, place in enumerate(places[first : first + TOGETHER]):
+                mapped[place * size : (place + 1) * size, at] = value[i * size : (i + 1) * size]
 
 
 def map_kernel(places, *refs):
     blocks = refs[: len(places)]
     gain, bias = refs[len(places) : len(places) + 2]
-    for place, block in zip(places, blocks):
-        map_rows(block, gain, bias, refs[-1], place * block.shape[0])
+    map_rows(blocks, places, gain, bias, refs[-1])
 
 
 def map_early(rows, gain, bias, mapped, blocks):
@@ -234,7 +238,7 @@
     )(in_hbm(tied_head))
 
 
-def half_sums(blocks, head, slopes, scaled, mass, which, work, out):
+def half_sums(blocks, head, slopes, scaled, which, work, out):
     levels = out.shape[0] // 2
     rows = sum(b.shape[0] for b in blocks)
     half = head.shape[1] // 2
@@ -250,17 +254,14 @@
         out[levels:, here] = add3(back[rows:])
         done += size
     out[:levels, :half] = add3(jnp.dot(scaled, work[:, :half], preferred_element_type=F32))
-    out[:, half:] = jnp.broadcast_to(mass, (2 * levels, mass.shape[1]))
-
-
-def front_kernel(loop, levels, count, late, *refs):
+
+
+def front_kernel(levels, count, late, *refs):
     blocks = refs[:count]
     head, gain, bias = refs[count : count + 3]
     give, slopes, scaled_out, mass_out, mapped = refs[-5:]
     voc, width = head.shape
     rows = mapped.shape[0]
-    rows_dev = rows // loop
-    chips = loop // 2
     me = lax.axis_index("loop")
     core = me % 2
     meta = jnp.concatenate([b[:, width:] for b in blocks], axis=0).astype(F32)
@@ -270,8 +271,7 @@
     target = (col(6) + 128.0 * col(7) + 16384.0 * col(8)).astype(jnp.int32)
     depth = col(9)
 
-    for i in late:
-        map_rows(blocks[i], gain, bias, mapped, i * blocks[i].shape[0])
+    map_rows([blocks[i] for i in late], late, gain, bias, mapped)
     logits = lax.dot_general(mapped[...], head[...], NT, preferred_element_type=F32)
     prob = jnp.exp(logits - norm)
     columns = me * voc + lax.broadcasted_iota(jnp.int32, (rows, voc), 1)
@@ -280,21 +280,7 @@
     mass = prob[:, :LANES]
     for j in range(1, voc // LANES):
         mass = mass + prob[:, j * LANES : (j + 1) * LANES]
-    mass = jnp.sum(mass.T, axis=0, keepdims=True)
-    index = lax.broadcasted_iota(jnp.int32, (rows, rows), 0)
-    flip = index // (rows // 2)
-    relative = (index - flip * (rows // 2)) // rows_dev
-    place = place_of(me // 2, chips) + jnp.where(core == 0, relative, chips - relative)
-    place = jnp.where(place >= chips, place - chips, place)
-    owner = 2 * chip_at(place, chips) + jnp.where(flip == 0, core, 1 - core)
-    goes_to = owner * rows_dev + index % rows_dev
-    move = goes_to == lax.broadcasted_iota(jnp.int32, (rows, rows), 1)
-    move = jnp.where(move, 1.0, 0.0).astype(BF16)
-    lines = jnp.concatenate(pieces(mass) + [jnp.zeros((13, rows), F32)], axis=0)
-    moved = jnp.dot(lines.astype(BF16), move, preferred_element_type=F32)
-    moved = (moved[0:1] + moved[1:2]) + moved[2:3]
-    low, high = moved[:, : rows // 2], moved[:, rows // 2 :]
-    mass_out[...] = jnp.where(core == 0, low, high)
+    mass_out[...] = mass
 
     lane = lax.broadcasted_iota(jnp.int32, (rows, LANES), 1).astype(F32)
     pick = jnp.where(lane == depth, 1.0, 0.0).T[:levels]
@@ -305,33 +291,53 @@
     sums = jnp.dot(pick.astype(BF16), slopes[:rows, :], preferred_element_type=F32)
     none = jnp.zeros((16 - 3 * levels, voc), F32)
     slopes[rows:, :] = jnp.concatenate(pieces(sums) + [none], axis=0).astype(BF16)
-    other = jnp.where(core == 0, high, low)
-    half_sums(blocks, head, slopes, scaled, other, 1 - core, mapped, give)
-
-
-def back_kernel(count, *refs):
+    half_sums(blocks, head, slopes, scaled, 1 - core, mapped, give)
+    give[:, width // 2 :] = jnp.zeros((2 * levels, rows), F32)
+
+
+def back_kernel(loop, count, *refs):
     blocks = refs[:count]
     head, slopes, scaled, mass, keep, work = refs[count:]
-    core = lax.axis_index("loop") % 2
-    half_sums(blocks, head, slopes, scaled[...], mass[...], core, work, keep)
+    rows, half = work.shape
+    rows_dev = rows // loop
+    chips = loop // 2
+    me = lax.axis_index("loop")
+    core = me % 2
+    half_sums(blocks, head, slopes, scaled[...], core, work, keep)
+
+    index = lax.broadcasted_iota(jnp.int32, (rows, LANES), 0)
+    flip = index // (rows // 2)
+    relative = (index - flip * (rows // 2)) // rows_dev
+    place = place_of(me // 2, chips) + jnp.where(core == 0, relative, chips - relative)
+    place = jnp.where(place >= chips, place - chips, place)
+    owner = 2 * chip_at(place, chips) + jnp.where(flip == 0, core, 1 - core)
+    goes_to = owner * rows_dev + index % rows_dev
+    lane = lax.broadcasted_iota(jnp.int32, (rows, LANES), 1)
+    move = [jnp.where(goes_to == lane + k, 1.0, 0.0) for k in range(0, rows, LANES)]
+    move = jnp.concatenate(move, axis=1).astype(BF16)
+    line = jnp.sum(mass[...].T, axis=0, keepdims=True)
+    lines = jnp.concatenate(pieces(line) + [jnp.zeros((13, rows), F32)], axis=0)
+    moved = jnp.dot(lines.astype(BF16), move, preferred_element_type=F32)
+    moved = (moved[0:1] + moved[1:2]) + moved[2:3]
+    keep[:, half:] = jnp.broadcast_to(moved, (keep.shape[0], rows))
 
 
 def main(blocks, head, gain, bias, mapped, late, loop):
     levels = gain.shape[0]
     voc, width = head.shape
     rows = sum(b.shape[0] for b in blocks)
-    half = pltpu.VMEM((2 * levels, (width + rows) // 2), F32)
+    half = pltpu.VMEM((2 * levels, width // 2 + rows), F32)
     operands = list(blocks) + [head, gain, bias] + ([] if mapped is None else [mapped])
     cost = lambda passes: pl.CostEstimate(
         flops=passes * rows * voc * width, bytes_accessed=voc * width, transcendentals=0
     )
     give, slopes, scaled, mass, _ = pl.pallas_call(
-        functools.partial(front_kernel, loop, levels, len(blocks), late),
+        functools.partial(front_kernel, levels, len(blocks), late),
         out_shape=(
             half,
             pltpu.VMEM((rows + 16, voc), BF16),
             pltpu.VMEM((16, rows), BF16),
-            pltpu.VMEM((1, rows // 2), F32),
+            pltpu.VMEM((rows, LANES), F32),
             pltpu.VMEM((rows, width), BF16),
         ),
         in_specs=[VMEM] * len(operands),
@@ -342,7 +348,7 @@
     )(*operands)
     operands = list(blocks) + [head, slopes, scaled, mass]
     keep = pl.pallas_call(
-        functools.partial(back_kernel, len(blocks)),
+        functools.partial(back_kernel, loop, len(blocks)),
         out_shape=half,
         in_specs=[VMEM] * len(operands),
         out_specs=VMEM,
@@ -377,8 +383,7 @@
     low = jnp.where(me % 2 == 0, kept[...], given[...])
     high = jnp.where(me % 2 == 0, given[...], kept[...])
     buf[:, :cut], buf[:, cut:width] = low[:, :cut], high[:, :cut]
-    buf[:, width:] = jnp.concatenate([low[:, cut:], high[:, cut:]], axis=1)
-    every = buf[0:1, width:]
+    every = kept[0:1, cut:] + given[0:1, cut:]
     spread = lax.broadcasted_iota(jnp.int32, (every.shape[1], LANES), 0)
     target = lax.broadcasted_iota(jnp.int32, (every.shape[1], LANES), 1)
     move = jnp.where(spread - me * rows == target, 1.0, 0.0).astype(BF16)
@@ -386,8 +391,8 @@
     own = jnp.dot(lines.astype(BF16), move, preferred_element_type=F32)
     line[...] = ((own[0:1] + own[1:2]) + own[2:3])[:, :rows]
     copies = [
-        pltpu.make_async_copy(buf.at[pl.ds(0, levels), pl.ds(0, width)], gain_out, sems.at[0]),
-        pltpu.make_async_copy(buf.at[pl.ds(levels, levels), pl.ds(0, width)], bias_out, sems.at[1]),
+        pltpu.make_async_copy(buf.at[pl.ds(0, levels)], gain_out, sems.at[0]),
+        pltpu.make_async_copy(buf.at[pl.ds(levels, levels)], bias_out, sems.at[1]),
         pltpu.make_async_copy(line, mass_out, sems.at[2]),
     ]
     for copy in copies:
@@ -404,7 +409,7 @@
         in_specs=[VMEM, VMEM],
         out_specs=(HBM, HBM, HBM),
         scratch_shapes=[
-            pltpu.VMEM((kept.shape[0], 2 * kept.shape[1]), F32),
+            pltpu.VMEM((2 * levels, width), F32),
             pltpu.VMEM((1, rows), F32),
             pltpu.SemaphoreType.DMA((3,)),
         ],

time: 48.2 us -> 48.1 us (level)
    pallas_call x2 -> x3, Pallas kernels: 2.04 us -> 2.12 us  [map_early(): pl.pallas_call(functools.partial(map_kernel, places), out_shape=pltpu.VME...]
  transfers between devices with their start and end apart: 21 -> 21, of which waited for: 9 -> 9; matrix products, arithmetic and copies ran while one was open for 0% -> 0% of each run, Pallas kernels for 17% -> 18%
where the time goes in v9:
time: 48.1 us; the launch traced here: 48 us
  starting transfers between devices  19.1 us (40%)
  Pallas kernels  15.7 us (33%)
  waiting for transfers between devices  12.3 us (26%)
  between operations  0.73 us (2%)
    ppermute x15, starting transfers between devices, gather_blocks(): send = lambda x, pairs: lax.ppermute(x, 'loop', pairs)  12.3 us
    ppermute x6, waiting for transfers between devices, sum_over_loop(): lax.ppermute(x, 'loop', [(i, i ^ mask) for i in range(loop)])  6.94 us
    ppermute x6, starting transfers between devices, sum_over_loop(): lax.ppermute(x, 'loop', [(i, i ^ mask) for i in range(loop)])  6.79 us
    ppermute x15, waiting for transfers between devices, gather_blocks(): send = lambda x, pairs: lax.ppermute(x, 'loop', pairs)  5.4 us
    pallas_call x1, Pallas kernels, main(): pl.pallas_call(functools.partial(front_kernel, levels, len(blocks), late)...  5.31 us
    pallas_call x1, Pallas kernels, load(): pl.pallas_call(load_kernel, out_shape=pltpu.VMEM(tied_head.shape, BF16),...  4.24 us
    pallas_call x1, Pallas kernels, main(): pl.pallas_call(functools.partial(back_kernel, loop, len(blocks)), out_sha...  2.22 us
    pallas_call x3, Pallas kernels, map_early(): pl.pallas_call(functools.partial(map_kernel, places), out_shape=pltpu.VME...  2.12 us
  transfers between devices with their start and end apart: 21, of which 9 were waited for; matrix products, arithmetic and copies ran while one was open for 0% of the time, Pallas kernels for 18%

profile of v9, /device:TPU:0, one launch (start us, length us, event | category | flops | bytes accessed | tf_op | source)
XLA Modules:
  0.0 48.0 jit_solution(7321121253216603122)
XLA Ops:
  0.6 1.1 %shard_map.94 = (bf16[16,5504]{1,0:T(8,128)(2,1)S(1)}, f32[4,5376]{1,0:T(4,128)S(1)}, f32[4,5376]{1,0:T(4,128)S(1)}) custom-call(bf16[16,5376]{1,0:T(8,128)(2,1)} %hidden.1, s32[1,16]{1,0:T(1,128)} %bitcast.4, s32[1,16]{1,0:T(1,128)} %bitcast.5, f32[1,16]{1,0:T(1,128)} %bitcast.6, f32[4,5376]{1,0:T(4,128)} %depth_gain.1, f32[4,5376]{1,0:T(4,128)} %depth_bias.1), custom_call_target="tpu_custom_call" | custom-call | tf_op jit(solution)/shard_map/pallas_call | solution.py:87
  1.8 2.5 %collective-permute-start.5 = (bf16[16,5504]{1,0:T(8,128)(2,1)S(1)}, bf16[16,5504]{1,0:T(8,128)(2,1)S(1)}, u32[]{:S(2)}, u32[]{:S(2)}) collective-permute-start(bf16[16,5504]{1,0:T(8,128)(2,1)S(1)} %get-tuple-element.19.refs_0_), channel_id=1, source_target_pairs={{0,5},{5,0},{4,9},{9,4},{8,13},{13,8},{12,15},{15,12},{14,11},{11,... | collective-permute-start | bytes 528392 | tf_op jit(solution)/shard_map/ppermute | solution.py:130
  4.3 0.6 %collective-permute-start = (bf16[16,5504]{1,0:T(8,128)(2,1)S(1)}, bf16[16,5504]{1,0:T(8,128)(2,1)S(1)}, u32[]{:S(2)}, u32[]{:S(2)}) collective-permute-start(bf16[16,5504]{1,0:T(8,128)(2,1)S(1)} %get-tuple-element.19.refs_0_), channel_id=1, source_target_pairs={{1,5},{4,0},{5,9},{8,4},{9,13},{12,8},{13,15},{14,12},{15,11},{10,... | collective-permute-start | bytes 528392 | tf_op jit(solution)/shard_map/ppermute | solution.py:130
  4.9 4.2 %shard_map.95.refs_16_ = bf16[1024,5376]{1,0:T(8,128)(2,1)S(1)} custom-call(bf16[1024,5376]{1,0:T(8,128)(2,1)} %head_hbm.1), custom_call_target="tpu_custom_call" | custom-call | bytes 22020096 | tf_op jit(solution)/shard_map/pallas_call | solution.py:228
  9.1 0.0 collective-permute-done.5.refs_2_.refs_9_
  9.1 1.5 %collective-permute-start.8 = (bf16[16,5504]{1,0:T(8,128)(2,1)S(1)}, bf16[16,5504]{1,0:T(8,128)(2,1)S(1)}, u32[]{:S(2)}, u32[]{:S(2)}) collective-permute-start(bf16[16,5504]{1,0:T(8,128)(2,1)S(1)} %collective-permute-done.5.refs_2_.refs_9_), channel_id=1, source_target_pairs={{1,4},{4,1},{5,8},{8,5},{9,12},{12,9},{13,14},{14,13},{15,10},{10,... | collective-permute-start | bytes 528392 | tf_op jit(solution)/shard_map/ppermute | solution.py:130
  10.6 0.0 collective-permute-done.refs_3_.refs_1_
  10.6 0.7 %collective-permute-start.1 = (bf16[16,5504]{1,0:T(8,128)(2,1)S(1)}, bf16[16,5504]{1,0:T(8,128)(2,1)S(1)}, u32[]{:S(2)}, u32[]{:S(2)}) collective-permute-start(bf16[16,5504]{1,0:T(8,128)(2,1)S(1)} %collective-permute-done.refs_3_.refs_1_), channel_id=1, source_target_pairs={{1,4},{4,1},{5,8},{8,5},{9,12},{12,9},{13,14},{14,13},{15,10},{10,... | collective-permute-start | bytes 528392 | tf_op jit(solution)/shard_map/ppermute | solution.py:130
  11.3 0.5 collective-permute-start.4
  11.7 0.1 collective-permute-start.7
  11.8 2.3 %collective-permute-done.8.refs_0_.refs_6_ = bf16[16,5504]{1,0:T(8,128)(2,1)S(1)} collective-permute-done((bf16[16,5504]{1,0:T(8,128)(2,1)S(1)}, bf16[16,5504]{1,0:T(8,128)(2,1)S(1)}, u32[]{:S(2)}, u32[]{:S(2)}) %collective-permute-start.8) | collective-permute-done | bytes 176160 | tf_op jit(solution)/shard_map/ppermute | solution.py:130
  14.1 2.4 %collective-permute-start.9 = (bf16[16,5504]{1,0:T(8,128)(2,1)S(1)}, bf16[16,5504]{1,0:T(8,128)(2,1)S(1)}, u32[]{:S(2)}, u32[]{:S(2)}) collective-permute-start(bf16[16,5504]{1,0:T(8,128)(2,1)S(1)} %collective-permute-done.8.refs_0_.refs_6_), channel_id=1, source_target_pairs={{0,5},{5,0},{4,9},{9,4},{8,13},{13,8},{12,15},{15,12},{14,11},{11,... | collective-permute-start | bytes 528392 | tf_op jit(solution)/shard_map/ppermute | solution.py:130
  16.5 0.0 collective-permute-start.6
  16.5 0.0 collective-permute-done.1.refs_1_.refs_14_
  16.5 1.6 %collective-permute-start.3 = (bf16[16,5504]{1,0:T(8,128)(2,1)S(1)}, bf16[16,5504]{1,0:T(8,128)(2,1)S(1)}, u32[]{:S(2)}, u32[]{:S(2)}) collective-permute-start(bf16[16,5504]{1,0:T(8,128)(2,1)S(1)} %collective-permute-done.1.refs_1_.refs_14_), channel_id=1, source_target_pairs={{0,5},{5,0},{4,9},{9,4},{8,13},{13,8},{12,15},{15,12},{14,11},{11,... | collective-permute-start | bytes 528392 | tf_op jit(solution)/shard_map/ppermute | solution.py:130
  18.1 0.0 collective-permute-done.4.refs_1_.refs_8_
  18.1 0.0 collective-permute-start.2
  18.1 0.0 collective-permute-done.7.refs_5_.refs_15_
  18.1 0.5 %collective-permute-start.11 = (bf16[16,5504]{1,0:T(8,128)(2,1)S(1)}, bf16[16,5504]{1,0:T(8,128)(2,1)S(1)}, u32[]{:S(2)}, u32[]{:S(2)}) collective-permute-start(bf16[16,5504]{1,0:T(8,128)(2,1)S(1)} %collective-permute-done.8.refs_0_.refs_6_), channel_id=1, source_target_pairs={{0,1},{1,0},{2,3},{3,2},{4,5},{5,4},{6,7},{7,6},{8,9},{9,8},{10,11... | collective-permute-start | bytes 528392 | tf_op jit(solution)/shard_map/ppermute | solution.py:130
  18.6 1.0 %collective-permute-done.9.refs_4_.refs_11_ = bf16[16,5504]{1,0:T(8,128)(2,1)S(1)} collective-permute-done((bf16[16,5504]{1,0:T(8,128)(2,1)S(1)}, bf16[16,5504]{1,0:T(8,128)(2,1)S(1)}, u32[]{:S(2)}, u32[]{:S(2)}) %collective-permute-start.9) | collective-permute-done | bytes 176160 | tf_op jit(solution)/shard_map/ppermute | solution.py:130
  19.6 1.3 %collective-permute-start.10 = (bf16[16,5504]{1,0:T(8,128)(2,1)S(1)}, bf16[16,5504]{1,0:T(8,128)(2,1)S(1)}, u32[]{:S(2)}, u32[]{:S(2)}) collective-permute-start(bf16[16,5504]{1,0:T(8,128)(2,1)S(1)} %collective-permute-done.9.refs_4_.refs_11_), channel_id=1, source_target_pairs={{1,4},{4,1},{5,8},{8,5},{9,12},{12,9},{13,14},{14,13},{15,10},{10,... | collective-permute-start | bytes 528392 | tf_op jit(solution)/shard_map/ppermute | solution.py:130
  20.9 0.0 collective-permute-done.6.refs_4_.refs_7_
  20.9 0.8 %shard_map.96.refs_8_ = bf16[256,5376]{1,0:T(8,128)(2,1)S(1)} custom-call(bf16[16,5504]{1,0:T(8,128)(2,1)S(1)} %get-tuple-element.19.refs_0_, bf16[16,5504]{1,0:T(8,128)(2,1)S(1)} %collective-permute-done.4.refs_1_.refs_8_, bf16[16,5504]{1,0:T(8,128)(2,1)S(1)} %collective-permute-done.5.refs_2_.refs_9_, ...), custom_call_target="tpu_custom_call" | custom-call | flops 10321920 | bytes 2064384 | tf_op jit(solution)/shard_map/pallas_call | solution.py:200
  21.8 0.0 collective-permute-done.3.refs_5_.refs_3_
  21.8 0.3 collective-permute-start.14
  22.1 0.3 collective-permute-start.12
  22.4 0.0 collective-permute-done.2.refs_3_.refs_2_
  22.4 0.0 collective-permute-done.11.refs_2_.refs_10_
  22.4 0.8 %shard_map.97.refs_5_ = bf16[256,5376]{1,0:T(8,128)(2,1)S(1)} custom-call(bf16[16,5504]{1,0:T(8,128)(2,1)S(1)} %collective-permute-done.8.refs_0_.refs_6_, bf16[16,5504]{1,0:T(8,128)(2,1)S(1)} %collective-permute-done.1.refs_1_.refs_14_, bf16[16,5504]{1,0:T(8,128)(2,1)S(1)} %collective-permute-done.11.refs_2_.refs_10_, ...), custom_call_target="tpu_custom_call", output_to_operand_aliasing={{}: (8, {})} | custom-call | flops 10321920 | bytes 2064384 | tf_op jit(solution)/shard_map/pallas_call | solution.py:200
  23.2 1.3 %collective-permute-done.10.refs_2_.refs_4_ = bf16[16,5504]{1,0:T(8,128)(2,1)S(1)} collective-permute-done((bf16[16,5504]{1,0:T(8,128)(2,1)S(1)}, bf16[16,5504]{1,0:T(8,128)(2,1)S(1)}, u32[]{:S(2)}, u32[]{:S(2)}) %collective-permute-start.10) | collective-permute-done | bytes 176160 | tf_op jit(solution)/shard_map/ppermute | solution.py:130
  24.5 0.1 collective-permute-start.13
  24.6 0.0 collective-permute-done.12.refs_0_.refs_5_
  24.6 0.5 shard_map.98.refs_19_
  25.1 0.8 %collective-permute-done.13.refs_12_ = bf16[16,5504]{1,0:T(8,128)(2,1)S(1)} collective-permute-done((bf16[16,5504]{1,0:T(8,128)(2,1)S(1)}, bf16[16,5504]{1,0:T(8,128)(2,1)S(1)}, u32[]{:S(2)}, u32[]{:S(2)}) %collective-permute-start.13) | collective-permute-done | bytes 176160 | tf_op jit(solution)/shard_map/ppermute | solution.py:130
  25.9 5.3 %shard_map.99 = (f32[8,2944]{1,0:T(8,128)S(1)}, bf16[272,1024]{1,0:T(8,128)(2,1)S(1)}, bf16[16,256]{1,0:T(8,128)(2,1)S(1)}, f32[256,128]{1,0:T(8,128)S(1)}, bf16[256,5376]{1,0:T(8,128)(2,1)S(1)}) custom-call(bf16[16,5504]{1,0:T(8,128)(2,1)S(1)} %get-tuple-element.19.refs_0_, ...), custom_call_target="tpu_custom_call", output_to_operand_aliasing={{4}: (19, {})} | custom-call | flops 4227858432 | bytes 5505024 | tf_op jit(solution)/shard_map/pallas_call | solution.py:334
  31.2 0.2 collective-permute-start.15
  31.3 2.2 %shard_map.100 = f32[8,2944]{1,0:T(8,128)S(1)} custom-call(bf16[16,5504]{1,0:T(8,128)(2,1)S(1)} %get-tuple-element.19.refs_0_, bf16[16,5504]{1,0:T(8,128)(2,1)S(1)} %collective-permute-done.refs_3_.refs_1_, bf16[16,5504]{1,0:T(8,128)(2,1)S(1)} %collective-permute-done.2.refs_3_.refs_2_, bf16[16,5504]{1,0:T(8,128)(2,1)S(1)} %collective-permute-done.3.refs_5_.refs_3_, ...), custom_call_target="tpu_custom_call" | custom-call | flops 1409286144 | bytes 5505024 | tf_op jit(solution)/shard_map/pallas_call | solution.py:350
  33.6 2.7 %collective-permute-start.18 = (bf16[8,2944]{1,0:T(8,128)(2,1)S(1)}, bf16[8,2944]{1,0:T(8,128)(2,1)S(1)}, u32[]{:S(2)}, u32[]{:S(2)}) collective-permute-start(bf16[8,2944]{1,0:T(8,128)(2,1)S(1)} %fusion), channel_id=1, source_target_pairs={{0,6},{1,7},{2,4},{3,5},{4,2},{5,3},{6,0},{7,1},{8,14},{9,15},{10,... | collective-permute-start | bytes 141320 | tf_op jit(solution)/shard_map/ppermute | solution.py:363
  36.3 0.4 collective-permute-start.17
  36.7 0.7 %collective-permute-start.16 = (bf16[8,2944]{1,0:T(8,128)(2,1)S(1)}, bf16[8,2944]{1,0:T(8,128)(2,1)S(1)}, u32[]{:S(2)}, u32[]{:S(2)}) collective-permute-start(bf16[8,2944]{1,0:T(8,128)(2,1)S(1)} %fusion), channel_id=1, source_target_pairs={{0,2},{1,3},{2,0},{3,1},{4,6},{5,7},{6,4},{7,5},{8,10},{9,11},{10,... | collective-permute-start | bytes 141320 | tf_op jit(solution)/shard_map/ppermute | solution.py:363
  37.4 1.2 %collective-permute-done.18 = bf16[8,2944]{1,0:T(8,128)(2,1)S(1)} collective-permute-done((bf16[8,2944]{1,0:T(8,128)(2,1)S(1)}, bf16[8,2944]{1,0:T(8,128)(2,1)S(1)}, u32[]{:S(2)}, u32[]{:S(2)}) %collective-permute-start.18) | collective-permute-done | bytes 47136 | tf_op jit(solution)/shard_map/ppermute | solution.py:363
  38.6 1.7 %collective-permute-done.17 = bf16[8,2944]{1,0:T(8,128)(2,1)S(1)} collective-permute-done((bf16[8,2944]{1,0:T(8,128)(2,1)S(1)}, bf16[8,2944]{1,0:T(8,128)(2,1)S(1)}, u32[]{:S(2)}, u32[]{:S(2)}) %collective-permute-start.17) | collective-permute-done | bytes 47136 | tf_op jit(solution)/shard_map/ppermute | solution.py:363
  40.3 0.4 collective-permute-done.16
  40.8 2.7 %collective-permute-start.19 = (bf16[8,2944]{1,0:T(8,128)(2,1)S(1)}, bf16[8,2944]{1,0:T(8,128)(2,1)S(1)}, u32[]{:S(2)}, u32[]{:S(2)}) collective-permute-start(bf16[8,2944]{1,0:T(8,128)(2,1)S(1)} %get-tuple-element.35), channel_id=1, source_target_pairs={{0,8},{1,9},{2,10},{3,11},{4,12},{5,13},{6,14},{7,15},{8,0},{9,1},... | collective-permute-start | bytes 141320 | tf_op jit(solution)/shard_map/ppermute | solution.py:363
  43.6 2.3 %collective-permute-done.19 = bf16[8,2944]{1,0:T(8,128)(2,1)S(1)} collective-permute-done((bf16[8,2944]{1,0:T(8,128)(2,1)S(1)}, bf16[8,2944]{1,0:T(8,128)(2,1)S(1)}, u32[]{:S(2)}, u32[]{:S(2)}) %collective-permute-start.19) | collective-permute-done | bytes 47136 | tf_op jit(solution)/shard_map/ppermute | solution.py:363
  45.9 0.1 collective-permute-start.20
  45.9 1.3 %collective-permute-done.20.given = f32[8,2944]{1,0:T(8,128)S(1)} collective-permute-done((f32[8,2944]{1,0:T(8,128)S(1)}, f32[8,2944]{1,0:T(8,128)S(1)}, u32[]{:S(2)}, u32[]{:S(2)}) %collective-permute-start.20) | collective-permute-done | bytes 94240 | tf_op jit(solution)/shard_map/ppermute | solution.py:363
  47.2 0.7 %shard_map.101 = (f32[1,16]{1,0:T(1,128)}, f32[4,5376]{1,0:T(4,128)}, f32[4,5376]{1,0:T(4,128)}) custom-call(f32[8,2944]{1,0:T(8,128)S(1)} %convert_add_fusion.kept, f32[8,2944]{1,0:T(8,128)S(1)} %collective-permute-done.20.given), custom_call_target="tpu_custom_call" | custom-call | tf_op jit(solution)/shard_map/pallas_call | solution.py:406
  (5 shorter events, 0.1 us)
Async XLA Ops:
  1.8 7.4 %collective-permute-start.5 = (bf16[16,5504]{1,0:T(8,128)(2,1)S(1)}, bf16[16,5504]{1,0:T(8,128)(2,1)S(1)}, u32[]{:S(2)}, u32[]{:S(2)}) collective-permute-start(bf16[16,5504]{1,0:T(8,128)(2,1)S(1)} %get-tuple-element.19.refs_0_), channel_id=1, source_target_pairs={{0,5},{5,0},{4,9},{9,4},{8,13},{13,8},{12,15},{15,12},{14,11},{11,... | collective-permute-start | bytes 528392 | tf_op jit(solution)/shard_map/ppermute | solution.py:130
  4.3 6.3 %collective-permute-start = (bf16[16,5504]{1,0:T(8,128)(2,1)S(1)}, bf16[16,5504]{1,0:T(8,128)(2,1)S(1)}, u32[]{:S(2)}, u32[]{:S(2)}) collective-permute-start(bf16[16,5504]{1,0:T(8,128)(2,1)S(1)} %get-tuple-element.19.refs_0_), channel_id=1, source_target_pairs={{1,5},{4,0},{5,9},{8,4},{9,13},{12,8},{13,15},{14,12},{15,11},{10,... | collective-permute-start | bytes 528392 | tf_op jit(solution)/shard_map/ppermute | solution.py:130
  9.1 4.9 %collective-permute-start.8 = (bf16[16,5504]{1,0:T(8,128)(2,1)S(1)}, bf16[16,5504]{1,0:T(8,128)(2,1)S(1)}, u32[]{:S(2)}, u32[]{:S(2)}) collective-permute-start(bf16[16,5504]{1,0:T(8,128)(2,1)S(1)} %collective-permute-done.5.refs_2_.refs_9_), channel_id=1, source_target_pairs={{1,4},{4,1},{5,8},{8,5},{9,12},{12,9},{13,14},{14,13},{15,10},{10,... | collective-permute-start | bytes 528392 | tf_op jit(solution)/shard_map/ppermute | solution.py:130
  10.6 5.9 %collective-permute-start.1 = (bf16[16,5504]{1,0:T(8,128)(2,1)S(1)}, bf16[16,5504]{1,0:T(8,128)(2,1)S(1)}, u32[]{:S(2)}, u32[]{:S(2)}) collective-permute-start(bf16[16,5504]{1,0:T(8,128)(2,1)S(1)} %collective-permute-done.refs_3_.refs_1_), channel_id=1, source_target_pairs={{1,4},{4,1},{5,8},{8,5},{9,12},{12,9},{13,14},{14,13},{15,10},{10,... | collective-permute-start | bytes 528392 | tf_op jit(solution)/shard_map/ppermute | solution.py:130
  11.3 6.8 %collective-permute-start.4 = (bf16[16,5504]{1,0:T(8,128)(2,1)S(1)}, bf16[16,5504]{1,0:T(8,128)(2,1)S(1)}, u32[]{:S(2)}, u32[]{:S(2)}) collective-permute-start(bf16[16,5504]{1,0:T(8,128)(2,1)S(1)} %get-tuple-element.19.refs_0_), channel_id=1, source_target_pairs={{0,1},{1,0},{2,3},{3,2},{4,5},{5,4},{6,7},{7,6},{8,9},{9,8},{10,11... | collective-permute-start | bytes 528392 | tf_op jit(solution)/shard_map/ppermute | solution.py:130
  11.7 6.3 %collective-permute-start.7 = (bf16[16,5504]{1,0:T(8,128)(2,1)S(1)}, bf16[16,5504]{1,0:T(8,128)(2,1)S(1)}, u32[]{:S(2)}, u32[]{:S(2)}) collective-permute-start(bf16[16,5504]{1,0:T(8,128)(2,1)S(1)} %collective-permute-done.refs_3_.refs_1_), channel_id=1, source_target_pairs={{0,1},{1,0},{2,3},{3,2},{4,5},{5,4},{6,7},{7,6},{8,9},{9,8},{10,11... | collective-permute-start | bytes 528392 | tf_op jit(solution)/shard_map/ppermute | solution.py:130
  14.1 5.5 %collective-permute-start.9 = (bf16[16,5504]{1,0:T(8,128)(2,1)S(1)}, bf16[16,5504]{1,0:T(8,128)(2,1)S(1)}, u32[]{:S(2)}, u32[]{:S(2)}) collective-permute-start(bf16[16,5504]{1,0:T(8,128)(2,1)S(1)} %collective-permute-done.8.refs_0_.refs_6_), channel_id=1, source_target_pairs={{0,5},{5,0},{4,9},{9,4},{8,13},{13,8},{12,15},{15,12},{14,11},{11,... | collective-permute-start | bytes 528392 | tf_op jit(solution)/shard_map/ppermute | solution.py:130
  16.5 4.5 %collective-permute-start.6 = (bf16[16,5504]{1,0:T(8,128)(2,1)S(1)}, bf16[16,5504]{1,0:T(8,128)(2,1)S(1)}, u32[]{:S(2)}, u32[]{:S(2)}) collective-permute-start(bf16[16,5504]{1,0:T(8,128)(2,1)S(1)} %collective-permute-done.5.refs_2_.refs_9_), channel_id=1, source_target_pairs={{0,1},{1,0},{2,3},{3,2},{4,5},{5,4},{6,7},{7,6},{8,9},{9,8},{10,11... | collective-permute-start | bytes 528392 | tf_op jit(solution)/shard_map/ppermute | solution.py:130
  16.5 5.3 %collective-permute-start.3 = (bf16[16,5504]{1,0:T(8,128)(2,1)S(1)}, bf16[16,5504]{1,0:T(8,128)(2,1)S(1)}, u32[]{:S(2)}, u32[]{:S(2)}) collective-permute-start(bf16[16,5504]{1,0:T(8,128)(2,1)S(1)} %collective-permute-done.1.refs_1_.refs_14_), channel_id=1, source_target_pairs={{0,5},{5,0},{4,9},{9,4},{8,13},{13,8},{12,15},{15,12},{14,11},{11,... | collective-permute-start | bytes 528392 | tf_op jit(solution)/shard_map/ppermute | solution.py:130
  18.1 4.3 %collective-permute-start.2 = (bf16[16,5504]{1,0:T(8,128)(2,1)S(1)}, bf16[16,5504]{1,0:T(8,128)(2,1)S(1)}, u32[]{:S(2)}, u32[]{:S(2)}) collective-permute-start(bf16[16,5504]{1,0:T(8,128)(2,1)S(1)} %collective-permute-done.1.refs_1_.refs_14_), channel_id=1, source_target_pairs={{0,1},{1,0},{2,3},{3,2},{4,5},{5,4},{6,7},{7,6},{8,9},{9,8},{10,11... | collective-permute-start | bytes 528392 | tf_op jit(solution)/shard_map/ppermute | solution.py:130
  18.1 4.3 %collective-permute-start.11 = (bf16[16,5504]{1,0:T(8,128)(2,1)S(1)}, bf16[16,5504]{1,0:T(8,128)(2,1)S(1)}, u32[]{:S(2)}, u32[]{:S(2)}) collective-permute-start(bf16[16,5504]{1,0:T(8,128)(2,1)S(1)} %collective-permute-done.8.refs_0_.refs_6_), channel_id=1, source_target_pairs={{0,1},{1,0},{2,3},{3,2},{4,5},{5,4},{6,7},{7,6},{8,9},{9,8},{10,11... | collective-permute-start | bytes 528392 | tf_op jit(solution)/shard_map/ppermute | solution.py:130
  19.6 4.9 %collective-permute-start.10 = (bf16[16,5504]{1,0:T(8,128)(2,1)S(1)}, bf16[16,5504]{1,0:T(8,128)(2,1)S(1)}, u32[]{:S(2)}, u32[]{:S(2)}) collective-permute-start(bf16[16,5504]{1,0:T(8,128)(2,1)S(1)} %collective-permute-done.9.refs_4_.refs_11_), channel_id=1, source_target_pairs={{1,4},{4,1},{5,8},{8,5},{9,12},{12,9},{13,14},{14,13},{15,10},{10,... | collective-permute-start | bytes 528392 | tf_op jit(solution)/shard_map/ppermute | solution.py:130
  21.8 2.8 %collective-permute-start.14 = (bf16[16,5504]{1,0:T(8,128)(2,1)S(1)}, bf16[16,5504]{1,0:T(8,128)(2,1)S(1)}, u32[]{:S(2)}, u32[]{:S(2)}) collective-permute-start(bf16[16,5504]{1,0:T(8,128)(2,1)S(1)} %collective-permute-done.3.refs_5_.refs_3_), channel_id=1, source_target_pairs={{0,1},{1,0},{2,3},{3,2},{4,5},{5,4},{6,7},{7,6},{8,9},{9,8},{10,11... | collective-permute-start | bytes 528392 | tf_op jit(solution)/shard_map/ppermute | solution.py:130
  22.1 2.5 %collective-permute-start.12 = (bf16[16,5504]{1,0:T(8,128)(2,1)S(1)}, bf16[16,5504]{1,0:T(8,128)(2,1)S(1)}, u32[]{:S(2)}, u32[]{:S(2)}) collective-permute-start(bf16[16,5504]{1,0:T(8,128)(2,1)S(1)} %collective-permute-done.9.refs_4_.refs_11_), channel_id=1, source_target_pairs={{0,1},{1,0},{2,3},{3,2},{4,5},{5,4},{6,7},{7,6},{8,9},{9,8},{10,11... | collective-permute-start | bytes 528392 | tf_op jit(solution)/shard_map/ppermute | solution.py:130
  24.5 1.4 %collective-permute-start.13 = (bf16[16,5504]{1,0:T(8,128)(2,1)S(1)}, bf16[16,5504]{1,0:T(8,128)(2,1)S(1)}, u32[]{:S(2)}, u32[]{:S(2)}) collective-permute-start(bf16[16,5504]{1,0:T(8,128)(2,1)S(1)} %collective-permute-done.10.refs_2_.refs_4_), channel_id=1, source_target_pairs={{0,1},{1,0},{2,3},{3,2},{4,5},{5,4},{6,7},{7,6},{8,9},{9,8},{10,11... | collective-permute-start | bytes 528392 | tf_op jit(solution)/shard_map/ppermute | solution.py:130
  31.2 2.4 %collective-permute-start.15 = (f32[8,2944]{1,0:T(8,128)S(1)}, f32[8,2944]{1,0:T(8,128)S(1)}, u32[]{:S(2)}, u32[]{:S(2)}) collective-permute-start(f32[8,2944]{1,0:T(8,128)S(1)} %get-tuple-element.31), channel_id=1, source_target_pairs={{0,1},{1,0},{2,3},{3,2},{4,5},{5,4},{6,7},{7,6},{8,9},{9,8},{10,11... | collective-permute-start | bytes 282632 | tf_op jit(solution)/shard_map/ppermute | solution.py:363
  33.6 5.0 %collective-permute-start.18 = (bf16[8,2944]{1,0:T(8,128)(2,1)S(1)}, bf16[8,2944]{1,0:T(8,128)(2,1)S(1)}, u32[]{:S(2)}, u32[]{:S(2)}) collective-permute-start(bf16[8,2944]{1,0:T(8,128)(2,1)S(1)} %fusion), channel_id=1, source_target_pairs={{0,6},{1,7},{2,4},{3,5},{4,2},{5,3},{6,0},{7,1},{8,14},{9,15},{10,... | collective-permute-start | bytes 141320 | tf_op jit(solution)/shard_map/ppermute | solution.py:363
  36.3 4.1 %collective-permute-start.17 = (bf16[8,2944]{1,0:T(8,128)(2,1)S(1)}, bf16[8,2944]{1,0:T(8,128)(2,1)S(1)}, u32[]{:S(2)}, u32[]{:S(2)}) collective-permute-start(bf16[8,2944]{1,0:T(8,128)(2,1)S(1)} %fusion), channel_id=1, source_target_pairs={{0,4},{1,5},{2,6},{3,7},{4,0},{5,1},{6,2},{7,3},{8,12},{9,13},{10,... | collective-permute-start | bytes 141320 | tf_op jit(solution)/shard_map/ppermute | solution.py:363
  36.7 4.1 %collective-permute-start.16 = (bf16[8,2944]{1,0:T(8,128)(2,1)S(1)}, bf16[8,2944]{1,0:T(8,128)(2,1)S(1)}, u32[]{:S(2)}, u32[]{:S(2)}) collective-permute-start(bf16[8,2944]{1,0:T(8,128)(2,1)S(1)} %fusion), channel_id=1, source_target_pairs={{0,2},{1,3},{2,0},{3,1},{4,6},{5,7},{6,4},{7,5},{8,10},{9,11},{10,... | collective-permute-start | bytes 141320 | tf_op jit(solution)/shard_map/ppermute | solution.py:363
  40.8 5.0 %collective-permute-start.19 = (bf16[8,2944]{1,0:T(8,128)(2,1)S(1)}, bf16[8,2944]{1,0:T(8,128)(2,1)S(1)}, u32[]{:S(2)}, u32[]{:S(2)}) collective-permute-start(bf16[8,2944]{1,0:T(8,128)(2,1)S(1)} %get-tuple-element.35), channel_id=1, source_target_pairs={{0,8},{1,9},{2,10},{3,11},{4,12},{5,13},{6,14},{7,15},{8,0},{9,1},... | collective-permute-start | bytes 141320 | tf_op jit(solution)/shard_map/ppermute | solution.py:363
  45.9 1.4 %collective-permute-start.20 = (f32[8,2944]{1,0:T(8,128)S(1)}, f32[8,2944]{1,0:T(8,128)S(1)}, u32[]{:S(2)}, u32[]{:S(2)}) collective-permute-start(f32[8,2944]{1,0:T(8,128)S(1)} %convert_add_fusion.kept), channel_id=1, source_target_pairs={{0,1},{1,0},{2,3},{3,2},{4,5},{5,4},{6,7},{7,6},{8,9},{9,8},{10,11... | collective-permute-start | bytes 282632 | tf_op jit(solution)/shard_map/ppermute | solution.py:363

commit v10 on v9

--- a/solution.py
+++ b/solution.py
@@ -109,16 +109,13 @@
     )
 
 
-def hop_pairs(order, step, cross):
+def hop_pairs(order, step):
     chips = len(order)
     first = 1 - step % 2
     pairs = []
     for i in range(chips):
         here, after = 2 * order[i], 2 * order[(i + 1) % chips]
-        if cross:
-            pairs += [(here + first, after + 1 - first), (after + 1 - first, here + first)]
-        else:
-            pairs += [(here + 1 - first, after + 1 - first), (after + first, here + first)]
+        pairs += [(here + first, after + 1 - first), (after + 1 - first, here + first)]
     return pairs
 
 
@@ -130,16 +127,17 @@
     send = lambda x, pairs: lax.ppermute(x, "loop", pairs)
     swap = lambda x: send(x, [(i, i ^ 1) for i in range(loop)])
     blocks = [None] * loop
-    blocks[0], blocks[chips] = block, swap(block)
-    crossed = plain = block
+    first = swap(block)
+    blocks[0], blocks[chips] = block, first
+    crossed, plain = block, first
     ready = [0, chips]
     mapped = None
     for step in range(1, half + 1):
-        crossed = send(crossed, hop_pairs(order, step, True))
+        crossed = send(crossed, hop_pairs(order, step))
         if step < half:
-            plain = send(plain, hop_pairs(order, step, step > 1))
-        if step == 1:
-            head = load(tied_head)
+            plain = send(plain, hop_pairs(order, step))
+        if step <= 2:
+            head = load(tied_head, step - 1, min(2, half), head if step > 1 else None)
             crossed, head = tie(crossed, head)
         if mapper is not None and step == 3:
             mapped = mapper(None, {i: blocks[i] for i in ready[:6]})
@@ -210,12 +208,13 @@
     )(*operands)
 
 
-def load_kernel(head_hbm, head, sems):
+def load_kernel(part, parts, head_hbm, *refs):
+    head, sems = refs[-2:]
     count = sems.shape[0]
-    size = head.shape[0] // count
+    size = head.shape[0] // (parts * count)
     copies = []
     for k in range(count):
-        at = pl.ds(k * size, size)
+        at = pl.ds((part * count + k) * size, size)
         copies.append(pltpu.make_async_copy(head_hbm.at[at], head.at[at], sems.at[k]))
     for copy in copies:
         copy.start()
@@ -223,19 +222,21 @@
         copy.wait()
 
 
-def load(tied_head):
+def load(tied_head, part, parts, loaded):
+    operands = [in_hbm(tied_head)] + ([] if loaded is None else [loaded])
     voc, width = tied_head.shape
     return pl.pallas_call(
-        load_kernel,
+        functools.partial(load_kernel, part, parts),
         out_shape=pltpu.VMEM(tied_head.shape, BF16),
-        in_specs=[HBM],
+        in_specs=[HBM] + [VMEM] * (len(operands) - 1),
         out_specs=VMEM,
+        input_output_aliases={} if loaded is None else {1: 0},
         scratch_shapes=[pltpu.SemaphoreType.DMA((4,))],
         compiler_params=pltpu.CompilerParams(vmem_limit_bytes=16 << 20),
         cost_estimate=pl.CostEstimate(
-            flops=0, bytes_accessed=4 * voc * width, transcendentals=0
+            flops=0, bytes_accessed=4 * voc * width // parts, transcendentals=0
         ),
-    )(in_hbm(tied_head))
+    )(*operands)
 
 
 def half_sums(blocks, head, slopes, scaled, which, work, out):

time: 48.1 us -> 48.4 us (level)
  waiting for transfers between devices: 12.3 us -> 10.2 us
  starting transfers between devices: 19.1 us -> 20.5 us
  Pallas kernels: 15.7 us -> 16.7 us
    ppermute x15, waiting for transfers between devices: 5.4 us -> 2.95 us  [gather_blocks(): send = lambda x, pairs: lax.ppermute(x, 'loop', pairs)]
    ppermute x15, starting transfers between devices: 12.3 us -> 13.8 us  [gather_blocks(): send = lambda x, pairs: lax.ppermute(x, 'loop', pairs)]
    pallas_call x1 -> x2, Pallas kernels: 4.24 us -> 5.23 us  [load(): pl.pallas_call(functools.partial(load_kernel, part, parts), out_shape=plt...]
  transfers between devices with their start and end apart: 21 -> 21, of which waited for: 9 -> 8; matrix products, arithmetic and copies ran while one was open for 0% -> 0% of each run, Pallas kernels for 18% -> 20%
where the time goes in v10:
time: 48.4 us; the launch traced here: 48.3 us
  starting transfers between devices  20.5 us (42%)
  Pallas kernels  16.7 us (35%)
  waiting for transfers between devices  10.2 us (21%)
  between operations  0.75 us (2%)
    ppermute x15, starting transfers between devices, gather_blocks(): send = lambda x, pairs: lax.ppermute(x, 'loop', pairs)  13.8 us
    ppermute x6, waiting for transfers between devices, sum_over_loop(): lax.ppermute(x, 'loop', [(i, i ^ mask) for i in range(loop)])  7.28 us
    ppermute x6, starting transfers between devices, sum_over_loop(): lax.ppermute(x, 'loop', [(i, i ^ mask) for i in range(loop)])  6.66 us
    pallas_call x1, Pallas kernels, main(): pl.pallas_call(functools.partial(front_kernel, levels, len(blocks), late)...  5.31 us
    pallas_call x2, Pallas kernels, load(): pl.pallas_call(functools.partial(load_kernel, part, parts), out_shape=plt...  5.23 us
    ppermute x15, waiting for transfers between devices, gather_blocks(): send = lambda x, pairs: lax.ppermute(x, 'loop', pairs)  2.95 us
    pallas_call x1, Pallas kernels, main(): pl.pallas_call(functools.partial(back_kernel, loop, len(blocks)), out_sha...  2.21 us
    pallas_call x3, Pallas kernels, map_early(): pl.pallas_call(functools.partial(map_kernel, places), out_shape=pltpu.VME...  2.11 us
  transfers between devices with their start and end apart: 21, of which 8 were waited for; matrix products, arithmetic and copies ran while one was open for 0% of the time, Pallas kernels for 20%

profile of v10, /device:TPU:0, one launch (start us, length us, event | category | flops | bytes accessed | tf_op | source)
XLA Modules:
  0.0 48.3 jit_solution(2168114482239256600)
XLA Ops:
  0.6 1.1 %shard_map.94 = (bf16[16,5504]{1,0:T(8,128)(2,1)S(1)}, f32[4,5376]{1,0:T(4,128)S(1)}, f32[4,5376]{1,0:T(4,128)S(1)}) custom-call(bf16[16,5376]{1,0:T(8,128)(2,1)} %hidden.1, s32[1,16]{1,0:T(1,128)} %bitcast.4, s32[1,16]{1,0:T(1,128)} %bitcast.5, f32[1,16]{1,0:T(1,128)} %bitcast.6, f32[4,5376]{1,0:T(4,128)} %depth_gain.1, f32[4,5376]{1,0:T(4,128)} %depth_bias.1), custom_call_target="tpu_custom_call" | custom-call | tf_op jit(solution)/shard_map/pallas_call | solution.py:87
  1.8 0.5 %collective-permute-start = (bf16[16,5504]{1,0:T(8,128)(2,1)S(1)}, bf16[16,5504]{1,0:T(8,128)(2,1)S(1)}, u32[]{:S(2)}, u32[]{:S(2)}) collective-permute-start(bf16[16,5504]{1,0:T(8,128)(2,1)S(1)} %get-tuple-element.21.refs_0_), channel_id=1, source_target_pairs={{0,1},{1,0},{2,3},{3,2},{4,5},{5,4},{6,7},{7,6},{8,9},{9,8},{10,11... | collective-permute-start | bytes 528392 | tf_op jit(solution)/shard_map/ppermute | solution.py:127
  2.3 2.7 %collective-permute-start.5 = (bf16[16,5504]{1,0:T(8,128)(2,1)S(1)}, bf16[16,5504]{1,0:T(8,128)(2,1)S(1)}, u32[]{:S(2)}, u32[]{:S(2)}) collective-permute-start(bf16[16,5504]{1,0:T(8,128)(2,1)S(1)} %get-tuple-element.21.refs_0_), channel_id=1, source_target_pairs={{0,5},{5,0},{4,9},{9,4},{8,13},{13,8},{12,15},{15,12},{14,11},{11,... | collective-permute-start | bytes 528392 | tf_op jit(solution)/shard_map/ppermute | solution.py:127
  5.0 0.0 collective-permute-done.refs_1_.refs_8_
  5.0 1.0 %collective-permute-start.1 = (bf16[16,5504]{1,0:T(8,128)(2,1)S(1)}, bf16[16,5504]{1,0:T(8,128)(2,1)S(1)}, u32[]{:S(2)}, u32[]{:S(2)}) collective-permute-start(bf16[16,5504]{1,0:T(8,128)(2,1)S(1)} %collective-permute-done.refs_1_.refs_8_), channel_id=1, source_target_pairs={{0,5},{5,0},{4,9},{9,4},{8,13},{13,8},{12,15},{15,12},{14,11},{11,... | collective-permute-start | bytes 528392 | tf_op jit(solution)/shard_map/ppermute | solution.py:127
  6.0 2.6 %shard_map.95.refs_0_ = bf16[1024,5376]{1,0:T(8,128)(2,1)S(1)} custom-call(bf16[1024,5376]{1,0:T(8,128)(2,1)} %head_hbm.3), custom_call_target="tpu_custom_call" | custom-call | bytes 11010048 | tf_op jit(solution)/shard_map/pallas_call | solution.py:228
  8.6 0.0 collective-permute-done.5.refs_2_.refs_9_
  8.6 1.6 %collective-permute-start.8 = (bf16[16,5504]{1,0:T(8,128)(2,1)S(1)}, bf16[16,5504]{1,0:T(8,128)(2,1)S(1)}, u32[]{:S(2)}, u32[]{:S(2)}) collective-permute-start(bf16[16,5504]{1,0:T(8,128)(2,1)S(1)} %collective-permute-done.5.refs_2_.refs_9_), channel_id=1, source_target_pairs={{1,4},{4,1},{5,8},{8,5},{9,12},{12,9},{13,14},{14,13},{15,10},{10,... | collective-permute-start | bytes 528392 | tf_op jit(solution)/shard_map/ppermute | solution.py:127
  10.2 0.0 collective-permute-done.1.refs_3_.refs_1_
  10.2 1.5 %collective-permute-start.2 = (bf16[16,5504]{1,0:T(8,128)(2,1)S(1)}, bf16[16,5504]{1,0:T(8,128)(2,1)S(1)}, u32[]{:S(2)}, u32[]{:S(2)}) collective-permute-start(bf16[16,5504]{1,0:T(8,128)(2,1)S(1)} %collective-permute-done.1.refs_3_.refs_1_), channel_id=1, source_target_pairs={{1,4},{4,1},{5,8},{8,5},{9,12},{12,9},{13,14},{14,13},{15,10},{10,... | collective-permute-start | bytes 528392 | tf_op jit(solution)/shard_map/ppermute | solution.py:127
  11.7 0.1 collective-permute-start.6
  11.8 2.6 %shard_map.97.refs_16_ = bf16[1024,5376]{1,0:T(8,128)(2,1)S(1)} custom-call(bf16[1024,5376]{1,0:T(8,128)(2,1)} %head_hbm.3, bf16[1024,5376]{1,0:T(8,128)(2,1)S(1)} %shard_map.95.refs_0_), custom_call_target="tpu_custom_call", output_to_operand_aliasing={{}: (1, {})} | custom-call | bytes 11010048 | tf_op jit(solution)/shard_map/pallas_call | solution.py:228
  14.4 1.2 %collective-permute-start.9 = (bf16[16,5504]{1,0:T(8,128)(2,1)S(1)}, bf16[16,5504]{1,0:T(8,128)(2,1)S(1)}, u32[]{:S(2)}, u32[]{:S(2)}) collective-permute-start(bf16[16,5504]{1,0:T(8,128)(2,1)S(1)} %collective-permute-done.8.refs_0_.refs_6_), channel_id=1, source_target_pairs={{0,5},{5,0},{4,9},{9,4},{8,13},{13,8},{12,15},{15,12},{14,11},{11,... | collective-permute-start | bytes 528392 | tf_op jit(solution)/shard_map/ppermute | solution.py:127
  15.7 0.4 collective-permute-start.7
  16.1 0.0 collective-permute-done.2.refs_1_.refs_14_
  16.1 1.3 %collective-permute-start.4 = (bf16[16,5504]{1,0:T(8,128)(2,1)S(1)}, bf16[16,5504]{1,0:T(8,128)(2,1)S(1)}, u32[]{:S(2)}, u32[]{:S(2)}) collective-permute-start(bf16[16,5504]{1,0:T(8,128)(2,1)S(1)} %collective-permute-done.2.refs_1_.refs_14_), channel_id=1, source_target_pairs={{0,5},{5,0},{4,9},{9,4},{8,13},{13,8},{12,15},{15,12},{14,11},{11,... | collective-permute-start | bytes 528392 | tf_op jit(solution)/shard_map/ppermute | solution.py:127
  17.4 0.4 collective-permute-start.11
  17.8 0.0 collective-permute-done.6.refs_4_.refs_7_
  17.8 0.1 collective-permute-start.3
  17.9 1.5 %collective-permute-done.9.refs_4_.refs_11_ = bf16[16,5504]{1,0:T(8,128)(2,1)S(1)} collective-permute-done((bf16[16,5504]{1,0:T(8,128)(2,1)S(1)}, bf16[16,5504]{1,0:T(8,128)(2,1)S(1)}, u32[]{:S(2)}, u32[]{:S(2)}) %collective-permute-start.9) | collective-permute-done | bytes 176160 | tf_op jit(solution)/shard_map/ppermute | solution.py:127
  19.4 1.9 %collective-permute-start.10 = (bf16[16,5504]{1,0:T(8,128)(2,1)S(1)}, bf16[16,5504]{1,0:T(8,128)(2,1)S(1)}, u32[]{:S(2)}, u32[]{:S(2)}) collective-permute-start(bf16[16,5504]{1,0:T(8,128)(2,1)S(1)} %collective-permute-done.9.refs_4_.refs_11_), channel_id=1, source_target_pairs={{1,4},{4,1},{5,8},{8,5},{9,12},{12,9},{13,14},{14,13},{15,10},{10,... | collective-permute-start | bytes 528392 | tf_op jit(solution)/shard_map/ppermute | solution.py:127
  21.2 0.0 collective-permute-done.7.refs_5_.refs_15_
  21.2 0.0 collective-permute-start.12
  21.2 0.8 %shard_map.96.refs_8_ = bf16[256,5376]{1,0:T(8,128)(2,1)S(1)} custom-call(bf16[16,5504]{1,0:T(8,128)(2,1)S(1)} %get-tuple-element.21.refs_0_, bf16[16,5504]{1,0:T(8,128)(2,1)S(1)} %collective-permute-done.refs_1_.refs_8_, bf16[16,5504]{1,0:T(8,128)(2,1)S(1)} %collective-permute-done.5.refs_2_.refs_9_, ...), custom_call_target="tpu_custom_call" | custom-call | flops 10321920 | bytes 2064384 | tf_op jit(solution)/shard_map/pallas_call | solution.py:198
  22.1 0.6 %collective-permute-start.14 = (bf16[16,5504]{1,0:T(8,128)(2,1)S(1)}, bf16[16,5504]{1,0:T(8,128)(2,1)S(1)}, u32[]{:S(2)}, u32[]{:S(2)}) collective-permute-start(bf16[16,5504]{1,0:T(8,128)(2,1)S(1)} %collective-permute-done.4.refs_5_.refs_3_), channel_id=1, source_target_pairs={{0,1},{1,0},{2,3},{3,2},{4,5},{5,4},{6,7},{7,6},{8,9},{9,8},{10,11... | collective-permute-start | bytes 528392 | tf_op jit(solution)/shard_map/ppermute | solution.py:127
  22.7 0.0 collective-permute-done.11.refs_2_.refs_10_
  22.7 0.0 collective-permute-done.3.refs_3_.refs_2_
  22.7 0.8 %shard_map.98.refs_5_ = bf16[256,5376]{1,0:T(8,128)(2,1)S(1)} custom-call(bf16[16,5504]{1,0:T(8,128)(2,1)S(1)} %collective-permute-done.8.refs_0_.refs_6_, bf16[16,5504]{1,0:T(8,128)(2,1)S(1)} %collective-permute-done.2.refs_1_.refs_14_, bf16[16,5504]{1,0:T(8,128)(2,1)S(1)} %collective-permute-done.11.refs_2_.refs_10_, ...), custom_call_target="tpu_custom_call", output_to_operand_aliasing={{}: (8, {})} | custom-call | flops 10321920 | bytes 2064384 | tf_op jit(solution)/shard_map/pallas_call | solution.py:198
  23.5 0.9 %collective-permute-done.10.refs_2_.refs_4_ = bf16[16,5504]{1,0:T(8,128)(2,1)S(1)} collective-permute-done((bf16[16,5504]{1,0:T(8,128)(2,1)S(1)}, bf16[16,5504]{1,0:T(8,128)(2,1)S(1)}, u32[]{:S(2)}, u32[]{:S(2)}) %collective-permute-start.10) | collective-permute-done | bytes 176160 | tf_op jit(solution)/shard_map/ppermute | solution.py:127
  24.4 0.6 %collective-permute-start.13 = (bf16[16,5504]{1,0:T(8,128)(2,1)S(1)}, bf16[16,5504]{1,0:T(8,128)(2,1)S(1)}, u32[]{:S(2)}, u32[]{:S(2)}) collective-permute-start(bf16[16,5504]{1,0:T(8,128)(2,1)S(1)} %collective-permute-done.10.refs_2_.refs_4_), channel_id=1, source_target_pairs={{0,1},{1,0},{2,3},{3,2},{4,5},{5,4},{6,7},{7,6},{8,9},{9,8},{10,11... | collective-permute-start | bytes 528392 | tf_op jit(solution)/shard_map/ppermute | solution.py:127
  24.9 0.0 collective-permute-done.12.refs_0_.refs_5_
  24.9 0.0 collective-permute-done.14.refs_1_.refs_13_
  24.9 0.5 shard_map.99.refs_19_
  25.4 0.6 %collective-permute-done.13.refs_12_ = bf16[16,5504]{1,0:T(8,128)(2,1)S(1)} collective-permute-done((bf16[16,5504]{1,0:T(8,128)(2,1)S(1)}, bf16[16,5504]{1,0:T(8,128)(2,1)S(1)}, u32[]{:S(2)}, u32[]{:S(2)}) %collective-permute-start.13) | collective-permute-done | bytes 176160 | tf_op jit(solution)/shard_map/ppermute | solution.py:127
  26.0 5.3 %shard_map.100 = (f32[8,2944]{1,0:T(8,128)S(1)}, bf16[272,1024]{1,0:T(8,128)(2,1)S(1)}, bf16[16,256]{1,0:T(8,128)(2,1)S(1)}, f32[256,128]{1,0:T(8,128)S(1)}, bf16[256,5376]{1,0:T(8,128)(2,1)S(1)}) custom-call(bf16[16,5504]{1,0:T(8,128)(2,1)S(1)} %get-tuple-element.21.refs_0_, ...), custom_call_target="tpu_custom_call", output_to_operand_aliasing={{4}: (19, {})} | custom-call | flops 4227858432 | bytes 5505024 | tf_op jit(solution)/shard_map/pallas_call | solution.py:335
  31.3 0.4 collective-permute-start.15
  31.7 2.2 %shard_map.101 = f32[8,2944]{1,0:T(8,128)S(1)} custom-call(bf16[16,5504]{1,0:T(8,128)(2,1)S(1)} %get-tuple-element.21.refs_0_, bf16[16,5504]{1,0:T(8,128)(2,1)S(1)} %collective-permute-done.1.refs_3_.refs_1_, bf16[16,5504]{1,0:T(8,128)(2,1)S(1)} %collective-permute-done.3.refs_3_.refs_2_, bf16[16,5504]{1,0:T(8,128)(2,1)S(1)} %collective-permute-done.4.refs_5_.refs_3_, ...), custom_call_target="tpu_custom_call" | custom-call | flops 1409286144 | bytes 5505024 | tf_op jit(solution)/shard_map/pallas_call | solution.py:351
  33.9 2.6 %collective-permute-start.18 = (bf16[8,2944]{1,0:T(8,128)(2,1)S(1)}, bf16[8,2944]{1,0:T(8,128)(2,1)S(1)}, u32[]{:S(2)}, u32[]{:S(2)}) collective-permute-start(bf16[8,2944]{1,0:T(8,128)(2,1)S(1)} %fusion), channel_id=1, source_target_pairs={{0,6},{1,7},{2,4},{3,5},{4,2},{5,3},{6,0},{7,1},{8,14},{9,15},{10,... | collective-permute-start | bytes 141320 | tf_op jit(solution)/shard_map/ppermute | solution.py:364
  36.6 0.5 collective-permute-start.17
  37.0 0.5 collective-permute-start.16
  37.5 1.8 %collective-permute-done.18 = bf16[8,2944]{1,0:T(8,128)(2,1)S(1)} collective-permute-done((bf16[8,2944]{1,0:T(8,128)(2,1)S(1)}, bf16[8,2944]{1,0:T(8,128)(2,1)S(1)}, u32[]{:S(2)}, u32[]{:S(2)}) %collective-permute-start.18) | collective-permute-done | bytes 47136 | tf_op jit(solution)/shard_map/ppermute | solution.py:364
  39.3 1.4 %collective-permute-done.17 = bf16[8,2944]{1,0:T(8,128)(2,1)S(1)} collective-permute-done((bf16[8,2944]{1,0:T(8,128)(2,1)S(1)}, bf16[8,2944]{1,0:T(8,128)(2,1)S(1)}, u32[]{:S(2)}, u32[]{:S(2)}) %collective-permute-start.17) | collective-permute-done | bytes 47136 | tf_op jit(solution)/shard_map/ppermute | solution.py:364
  40.6 0.5 collective-permute-done.16
  41.1 2.7 %collective-permute-start.19 = (bf16[8,2944]{1,0:T(8,128)(2,1)S(1)}, bf16[8,2944]{1,0:T(8,128)(2,1)S(1)}, u32[]{:S(2)}, u32[]{:S(2)}) collective-permute-start(bf16[8,2944]{1,0:T(8,128)(2,1)S(1)} %get-tuple-element.39), channel_id=1, source_target_pairs={{0,8},{1,9},{2,10},{3,11},{4,12},{5,13},{6,14},{7,15},{8,0},{9,1},... | collective-permute-start | bytes 141320 | tf_op jit(solution)/shard_map/ppermute | solution.py:364
  43.8 2.4 %collective-permute-done.19 = bf16[8,2944]{1,0:T(8,128)(2,1)S(1)} collective-permute-done((bf16[8,2944]{1,0:T(8,128)(2,1)S(1)}, bf16[8,2944]{1,0:T(8,128)(2,1)S(1)}, u32[]{:S(2)}, u32[]{:S(2)}) %collective-permute-start.19) | collective-permute-done | bytes 47136 | tf_op jit(solution)/shard_map/ppermute | solution.py:364
  46.2 0.1 collective-permute-start.20
  46.2 1.3 %collective-permute-done.20.given = f32[8,2944]{1,0:T(8,128)S(1)} collective-permute-done((f32[8,2944]{1,0:T(8,128)S(1)}, f32[8,2944]{1,0:T(8,128)S(1)}, u32[]{:S(2)}, u32[]{:S(2)}) %collective-permute-start.20) | collective-permute-done | bytes 94240 | tf_op jit(solution)/shard_map/ppermute | solution.py:364
  47.5 0.7 %shard_map.102 = (f32[1,16]{1,0:T(1,128)}, f32[4,5376]{1,0:T(4,128)}, f32[4,5376]{1,0:T(4,128)}) custom-call(f32[8,2944]{1,0:T(8,128)S(1)} %convert_add_fusion.kept, f32[8,2944]{1,0:T(8,128)S(1)} %collective-permute-done.20.given), custom_call_target="tpu_custom_call" | custom-call | tf_op jit(solution)/shard_map/pallas_call | solution.py:407
  (6 shorter events, 0.1 us)
Async XLA Ops:
  1.8 3.2 %collective-permute-start = (bf16[16,5504]{1,0:T(8,128)(2,1)S(1)}, bf16[16,5504]{1,0:T(8,128)(2,1)S(1)}, u32[]{:S(2)}, u32[]{:S(2)}) collective-permute-start(bf16[16,5504]{1,0:T(8,128)(2,1)S(1)} %get-tuple-element.21.refs_0_), channel_id=1, source_target_pairs={{0,1},{1,0},{2,3},{3,2},{4,5},{5,4},{6,7},{7,6},{8,9},{9,8},{10,11... | collective-permute-start | bytes 528392 | tf_op jit(solution)/shard_map/ppermute | solution.py:127
  2.3 6.4 %collective-permute-start.5 = (bf16[16,5504]{1,0:T(8,128)(2,1)S(1)}, bf16[16,5504]{1,0:T(8,128)(2,1)S(1)}, u32[]{:S(2)}, u32[]{:S(2)}) collective-permute-start(bf16[16,5504]{1,0:T(8,128)(2,1)S(1)} %get-tuple-element.21.refs_0_), channel_id=1, source_target_pairs={{0,5},{5,0},{4,9},{9,4},{8,13},{13,8},{12,15},{15,12},{14,11},{11,... | collective-permute-start | bytes 528392 | tf_op jit(solution)/shard_map/ppermute | solution.py:127
  5.0 5.2 %collective-permute-start.1 = (bf16[16,5504]{1,0:T(8,128)(2,1)S(1)}, bf16[16,5504]{1,0:T(8,128)(2,1)S(1)}, u32[]{:S(2)}, u32[]{:S(2)}) collective-permute-start(bf16[16,5504]{1,0:T(8,128)(2,1)S(1)} %collective-permute-done.refs_1_.refs_8_), channel_id=1, source_target_pairs={{0,5},{5,0},{4,9},{9,4},{8,13},{13,8},{12,15},{15,12},{14,11},{11,... | collective-permute-start | bytes 528392 | tf_op jit(solution)/shard_map/ppermute | solution.py:127
  8.6 5.8 %collective-permute-start.8 = (bf16[16,5504]{1,0:T(8,128)(2,1)S(1)}, bf16[16,5504]{1,0:T(8,128)(2,1)S(1)}, u32[]{:S(2)}, u32[]{:S(2)}) collective-permute-start(bf16[16,5504]{1,0:T(8,128)(2,1)S(1)} %collective-permute-done.5.refs_2_.refs_9_), channel_id=1, source_target_pairs={{1,4},{4,1},{5,8},{8,5},{9,12},{12,9},{13,14},{14,13},{15,10},{10,... | collective-permute-start | bytes 528392 | tf_op jit(solution)/shard_map/ppermute | solution.py:127
  10.2 5.9 %collective-permute-start.2 = (bf16[16,5504]{1,0:T(8,128)(2,1)S(1)}, bf16[16,5504]{1,0:T(8,128)(2,1)S(1)}, u32[]{:S(2)}, u32[]{:S(2)}) collective-permute-start(bf16[16,5504]{1,0:T(8,128)(2,1)S(1)} %collective-permute-done.1.refs_3_.refs_1_), channel_id=1, source_target_pairs={{1,4},{4,1},{5,8},{8,5},{9,12},{12,9},{13,14},{14,13},{15,10},{10,... | collective-permute-start | bytes 528392 | tf_op jit(solution)/shard_map/ppermute | solution.py:127
  11.7 6.1 %collective-permute-start.6 = (bf16[16,5504]{1,0:T(8,128)(2,1)S(1)}, bf16[16,5504]{1,0:T(8,128)(2,1)S(1)}, u32[]{:S(2)}, u32[]{:S(2)}) collective-permute-start(bf16[16,5504]{1,0:T(8,128)(2,1)S(1)} %collective-permute-done.5.refs_2_.refs_9_), channel_id=1, source_target_pairs={{0,1},{1,0},{2,3},{3,2},{4,5},{5,4},{6,7},{7,6},{8,9},{9,8},{10,11... | collective-permute-start | bytes 528392 | tf_op jit(solution)/shard_map/ppermute | solution.py:127
  14.4 4.9 %collective-permute-start.9 = (bf16[16,5504]{1,0:T(8,128)(2,1)S(1)}, bf16[16,5504]{1,0:T(8,128)(2,1)S(1)}, u32[]{:S(2)}, u32[]{:S(2)}) collective-permute-start(bf16[16,5504]{1,0:T(8,128)(2,1)S(1)} %collective-permute-done.8.refs_0_.refs_6_), channel_id=1, source_target_pairs={{0,5},{5,0},{4,9},{9,4},{8,13},{13,8},{12,15},{15,12},{14,11},{11,... | collective-permute-start | bytes 528392 | tf_op jit(solution)/shard_map/ppermute | solution.py:127
  15.7 5.5 %collective-permute-start.7 = (bf16[16,5504]{1,0:T(8,128)(2,1)S(1)}, bf16[16,5504]{1,0:T(8,128)(2,1)S(1)}, u32[]{:S(2)}, u32[]{:S(2)}) collective-permute-start(bf16[16,5504]{1,0:T(8,128)(2,1)S(1)} %collective-permute-done.1.refs_3_.refs_1_), channel_id=1, source_target_pairs={{0,1},{1,0},{2,3},{3,2},{4,5},{5,4},{6,7},{7,6},{8,9},{9,8},{10,11... | collective-permute-start | bytes 528392 | tf_op jit(solution)/shard_map/ppermute | solution.py:127
  16.1 6.0 %collective-permute-start.4 = (bf16[16,5504]{1,0:T(8,128)(2,1)S(1)}, bf16[16,5504]{1,0:T(8,128)(2,1)S(1)}, u32[]{:S(2)}, u32[]{:S(2)}) collective-permute-start(bf16[16,5504]{1,0:T(8,128)(2,1)S(1)} %collective-permute-done.2.refs_1_.refs_14_), channel_id=1, source_target_pairs={{0,5},{5,0},{4,9},{9,4},{8,13},{13,8},{12,15},{15,12},{14,11},{11,... | collective-permute-start | bytes 528392 | tf_op jit(solution)/shard_map/ppermute | solution.py:127
  17.4 5.3 %collective-permute-start.11 = (bf16[16,5504]{1,0:T(8,128)(2,1)S(1)}, bf16[16,5504]{1,0:T(8,128)(2,1)S(1)}, u32[]{:S(2)}, u32[]{:S(2)}) collective-permute-start(bf16[16,5504]{1,0:T(8,128)(2,1)S(1)} %collective-permute-done.8.refs_0_.refs_6_), channel_id=1, source_target_pairs={{0,1},{1,0},{2,3},{3,2},{4,5},{5,4},{6,7},{7,6},{8,9},{9,8},{10,11... | collective-permute-start | bytes 528392 | tf_op jit(solution)/shard_map/ppermute | solution.py:127
  17.8 4.9 %collective-permute-start.3 = (bf16[16,5504]{1,0:T(8,128)(2,1)S(1)}, bf16[16,5504]{1,0:T(8,128)(2,1)S(1)}, u32[]{:S(2)}, u32[]{:S(2)}) collective-permute-start(bf16[16,5504]{1,0:T(8,128)(2,1)S(1)} %collective-permute-done.2.refs_1_.refs_14_), channel_id=1, source_target_pairs={{0,1},{1,0},{2,3},{3,2},{4,5},{5,4},{6,7},{7,6},{8,9},{9,8},{10,11... | collective-permute-start | bytes 528392 | tf_op jit(solution)/shard_map/ppermute | solution.py:127
  19.4 5.0 %collective-permute-start.10 = (bf16[16,5504]{1,0:T(8,128)(2,1)S(1)}, bf16[16,5504]{1,0:T(8,128)(2,1)S(1)}, u32[]{:S(2)}, u32[]{:S(2)}) collective-permute-start(bf16[16,5504]{1,0:T(8,128)(2,1)S(1)} %collective-permute-done.9.refs_4_.refs_11_), channel_id=1, source_target_pairs={{1,4},{4,1},{5,8},{8,5},{9,12},{12,9},{13,14},{14,13},{15,10},{10,... | collective-permute-start | bytes 528392 | tf_op jit(solution)/shard_map/ppermute | solution.py:127
  21.2 3.7 %collective-permute-start.12 = (bf16[16,5504]{1,0:T(8,128)(2,1)S(1)}, bf16[16,5504]{1,0:T(8,128)(2,1)S(1)}, u32[]{:S(2)}, u32[]{:S(2)}) collective-permute-start(bf16[16,5504]{1,0:T(8,128)(2,1)S(1)} %collective-permute-done.9.refs_4_.refs_11_), channel_id=1, source_target_pairs={{0,1},{1,0},{2,3},{3,2},{4,5},{5,4},{6,7},{7,6},{8,9},{9,8},{10,11... | collective-permute-start | bytes 528392 | tf_op jit(solution)/shard_map/ppermute | solution.py:127
  22.1 2.8 %collective-permute-start.14 = (bf16[16,5504]{1,0:T(8,128)(2,1)S(1)}, bf16[16,5504]{1,0:T(8,128)(2,1)S(1)}, u32[]{:S(2)}, u32[]{:S(2)}) collective-permute-start(bf16[16,5504]{1,0:T(8,128)(2,1)S(1)} %collective-permute-done.4.refs_5_.refs_3_), channel_id=1, source_target_pairs={{0,1},{1,0},{2,3},{3,2},{4,5},{5,4},{6,7},{7,6},{8,9},{9,8},{10,11... | collective-permute-start | bytes 528392 | tf_op jit(solution)/shard_map/ppermute | solution.py:127
  24.4 1.6 %collective-permute-start.13 = (bf16[16,5504]{1,0:T(8,128)(2,1)S(1)}, bf16[16,5504]{1,0:T(8,128)(2,1)S(1)}, u32[]{:S(2)}, u32[]{:S(2)}) collective-permute-start(bf16[16,5504]{1,0:T(8,128)(2,1)S(1)} %collective-permute-done.10.refs_2_.refs_4_), channel_id=1, source_target_pairs={{0,1},{1,0},{2,3},{3,2},{4,5},{5,4},{6,7},{7,6},{8,9},{9,8},{10,11... | collective-permute-start | bytes 528392 | tf_op jit(solution)/shard_map/ppermute | solution.py:127
  31.3 2.6 %collective-permute-start.15 = (f32[8,2944]{1,0:T(8,128)S(1)}, f32[8,2944]{1,0:T(8,128)S(1)}, u32[]{:S(2)}, u32[]{:S(2)}) collective-permute-start(f32[8,2944]{1,0:T(8,128)S(1)} %get-tuple-element.35), channel_id=1, source_target_pairs={{0,1},{1,0},{2,3},{3,2},{4,5},{5,4},{6,7},{7,6},{8,9},{9,8},{10,11... | collective-permute-start | bytes 282632 | tf_op jit(solution)/shard_map/ppermute | solution.py:364
  33.9 5.4 %collective-permute-start.18 = (bf16[8,2944]{1,0:T(8,128)(2,1)S(1)}, bf16[8,2944]{1,0:T(8,128)(2,1)S(1)}, u32[]{:S(2)}, u32[]{:S(2)}) collective-permute-start(bf16[8,2944]{1,0:T(8,128)(2,1)S(1)} %fusion), channel_id=1, source_target_pairs={{0,6},{1,7},{2,4},{3,5},{4,2},{5,3},{6,0},{7,1},{8,14},{9,15},{10,... | collective-permute-start | bytes 141320 | tf_op jit(solution)/shard_map/ppermute | solution.py:364
  36.6 4.1 %collective-permute-start.17 = (bf16[8,2944]{1,0:T(8,128)(2,1)S(1)}, bf16[8,2944]{1,0:T(8,128)(2,1)S(1)}, u32[]{:S(2)}, u32[]{:S(2)}) collective-permute-start(bf16[8,2944]{1,0:T(8,128)(2,1)S(1)} %fusion), channel_id=1, source_target_pairs={{0,4},{1,5},{2,6},{3,7},{4,0},{5,1},{6,2},{7,3},{8,12},{9,13},{10,... | collective-permute-start | bytes 141320 | tf_op jit(solution)/shard_map/ppermute | solution.py:364
  37.0 4.1 %collective-permute-start.16 = (bf16[8,2944]{1,0:T(8,128)(2,1)S(1)}, bf16[8,2944]{1,0:T(8,128)(2,1)S(1)}, u32[]{:S(2)}, u32[]{:S(2)}) collective-permute-start(bf16[8,2944]{1,0:T(8,128)(2,1)S(1)} %fusion), channel_id=1, source_target_pairs={{0,2},{1,3},{2,0},{3,1},{4,6},{5,7},{6,4},{7,5},{8,10},{9,11},{10,... | collective-permute-start | bytes 141320 | tf_op jit(solution)/shard_map/ppermute | solution.py:364
  41.1 5.0 %collective-permute-start.19 = (bf16[8,2944]{1,0:T(8,128)(2,1)S(1)}, bf16[8,2944]{1,0:T(8,128)(2,1)S(1)}, u32[]{:S(2)}, u32[]{:S(2)}) collective-permute-start(bf16[8,2944]{1,0:T(8,128)(2,1)S(1)} %get-tuple-element.39), channel_id=1, source_target_pairs={{0,8},{1,9},{2,10},{3,11},{4,12},{5,13},{6,14},{7,15},{8,0},{9,1},... | collective-permute-start | bytes 141320 | tf_op jit(solution)/shard_map/ppermute | solution.py:364
  46.2 1.4 %collective-permute-start.20 = (f32[8,2944]{1,0:T(8,128)S(1)}, f32[8,2944]{1,0:T(8,128)S(1)}, u32[]{:S(2)}, u32[]{:S(2)}) collective-permute-start(f32[8,2944]{1,0:T(8,128)S(1)} %convert_add_fusion.kept), channel_id=1, source_target_pairs={{0,1},{1,0},{2,3},{3,2},{4,5},{5,4},{6,7},{7,6},{8,9},{9,8},{10,11... | collective-permute-start | bytes 282632 | tf_op jit(solution)/shard_map/ppermute | solution.py:364

commit v11 on v10

--- a/solution.py
+++ b/solution.py
@@ -12,6 +12,7 @@
 LANES = 128
 CUTS = 42
 TOGETHER = 2
+LOADS = ((0, 3), (3, 4))
 NT = (((1,), (1,)), ((), ()))
 VMEM = pl.BlockSpec(memory_space=pltpu.VMEM)
 HBM = pl.BlockSpec(memory_space=pl.ANY)
@@ -137,7 +138,7 @@
         if step < half:
             plain = send(plain, hop_pairs(order, step))
         if step <= 2:
-            head = load(tied_head, step - 1, min(2, half), head if step > 1 else None)
+            head = load(tied_head, *(LOADS[step - 1]), head if step > 1 else None)
             crossed, head = tie(crossed, head)
         if mapper is not None and step == 3:
             mapped = mapper(None, {i: blocks[i] for i in ready[:6]})
@@ -208,13 +209,13 @@
     )(*operands)
 
 
-def load_kernel(part, parts, head_hbm, *refs):
+def load_kernel(first, last, head_hbm, *refs):
     head, sems = refs[-2:]
-    count = sems.shape[0]
-    size = head.shape[0] // (parts * count)
+    quarter = head.shape[0] // 4
+    size = quarter if last - first > 1 else quarter // 4
     copies = []
-    for k in range(count):
-        at = pl.ds((part * count + k) * size, size)
+    for k, start in enumerate(range(first * quarter, last * quarter, size)):
+        at = pl.ds(start, size)
         copies.append(pltpu.make_async_copy(head_hbm.at[at], head.at[at], sems.at[k]))
     for copy in copies:
         copy.start()
@@ -222,11 +223,11 @@
         copy.wait()
 
 
-def load(tied_head, part, parts, loaded):
+def load(tied_head, first, last, loaded):
     operands = [in_hbm(tied_head)] + ([] if loaded is None else [loaded])
     voc, width = tied_head.shape
     return pl.pallas_call(
-        functools.partial(load_kernel, part, parts),
+        functools.partial(load_kernel, first, last),
         out_shape=pltpu.VMEM(tied_head.shape, BF16),
         in_specs=[HBM] + [VMEM] * (len(operands) - 1),
         out_specs=VMEM,
@@ -234,7 +235,7 @@
         scratch_shapes=[pltpu.SemaphoreType.DMA((4,))],
         compiler_params=pltpu.CompilerParams(vmem_limit_bytes=16 << 20),
         cost_estimate=pl.CostEstimate(
-            flops=0, bytes_accessed=4 * voc * width // parts, transcendentals=0
+            flops=0, bytes_accessed=voc * width * (last - first), transcendentals=0
         ),
     )(*operands)
 

time: 48.4 us -> 48.6 us (level)
  waiting for transfers between devices: 10.2 us -> 11.2 us
  starting transfers between devices: 20.5 us -> 19.7 us
    ppermute x15, waiting for transfers between devices: 2.95 us -> 3.94 us  [gather_blocks(): send = lambda x, pairs: lax.ppermute(x, 'loop', pairs)]
    ppermute x15, starting transfers between devices: 13.8 us -> 13 us  [gather_blocks(): send = lambda x, pairs: lax.ppermute(x, 'loop', pairs)]
  transfers between devices with their start and end apart: 21 -> 21, of which waited for: 8 -> 10; matrix products, arithmetic and copies ran while one was open for 0% -> 0% of each run, Pallas kernels for 20% -> 20%
where the time goes in v11:
time: 48.6 us; the launch traced here: 48.4 us
  starting transfers between devices  19.7 us (41%)
  Pallas kernels  16.7 us (34%)
  waiting for transfers between devices  11.2 us (23%)
  between operations  0.74 us (2%)
    ppermute x15, starting transfers between devices, gather_blocks(): send = lambda x, pairs: lax.ppermute(x, 'loop', pairs)  13 us
    ppermute x6, waiting for transfers between devices, sum_over_loop(): lax.ppermute(x, 'loop', [(i, i ^ mask) for i in range(loop)])  7.28 us
    ppermute x6, starting transfers between devices, sum_over_loop(): lax.ppermute(x, 'loop', [(i, i ^ mask) for i in range(loop)])  6.65 us
    pallas_call x1, Pallas kernels, main(): pl.pallas_call(functools.partial(front_kernel, levels, len(blocks), late)...  5.31 us
    pallas_call x2, Pallas kernels, load(): pl.pallas_call(functools.partial(load_kernel, first, last), out_shape=plt...  5.21 us
    ppermute x15, waiting for transfers between devices, gather_blocks(): send = lambda x, pairs: lax.ppermute(x, 'loop', pairs)  3.94 us
    pallas_call x1, Pallas kernels, main(): pl.pallas_call(functools.partial(back_kernel, loop, len(blocks)), out_sha...  2.21 us
    pallas_call x3, Pallas kernels, map_early(): pl.pallas_call(functools.partial(map_kernel, places), out_shape=pltpu.VME...  2.11 us
  transfers between devices with their start and end apart: 21, of which 10 were waited for; matrix products, arithmetic and copies ran while one was open for 0% of the time, Pallas kernels for 20%

profile of v11, /device:TPU:0, one launch (start us, length us, event | category | flops | bytes accessed | tf_op | source)
XLA Modules:
  0.0 48.4 jit_solution(15943232419218797399)
XLA Ops:
  0.6 1.1 %shard_map.94 = (bf16[16,5504]{1,0:T(8,128)(2,1)S(1)}, f32[4,5376]{1,0:T(4,128)S(1)}, f32[4,5376]{1,0:T(4,128)S(1)}) custom-call(bf16[16,5376]{1,0:T(8,128)(2,1)} %hidden.1, s32[1,16]{1,0:T(1,128)} %bitcast.4, s32[1,16]{1,0:T(1,128)} %bitcast.5, f32[1,16]{1,0:T(1,128)} %bitcast.6, f32[4,5376]{1,0:T(4,128)} %depth_gain.1, f32[4,5376]{1,0:T(4,128)} %depth_bias.1), custom_call_target="tpu_custom_call" | custom-call | tf_op jit(solution)/shard_map/pallas_call | solution.py:88
  1.8 0.5 %collective-permute-start = (bf16[16,5504]{1,0:T(8,128)(2,1)S(1)}, bf16[16,5504]{1,0:T(8,128)(2,1)S(1)}, u32[]{:S(2)}, u32[]{:S(2)}) collective-permute-start(bf16[16,5504]{1,0:T(8,128)(2,1)S(1)} %get-tuple-element.21.refs_0_), channel_id=1, source_target_pairs={{0,1},{1,0},{2,3},{3,2},{4,5},{5,4},{6,7},{7,6},{8,9},{9,8},{10,11... | collective-permute-start | bytes 528392 | tf_op jit(solution)/shard_map/ppermute | solution.py:128
  2.3 2.7 %collective-permute-start.5 = (bf16[16,5504]{1,0:T(8,128)(2,1)S(1)}, bf16[16,5504]{1,0:T(8,128)(2,1)S(1)}, u32[]{:S(2)}, u32[]{:S(2)}) collective-permute-start(bf16[16,5504]{1,0:T(8,128)(2,1)S(1)} %get-tuple-element.21.refs_0_), channel_id=1, source_target_pairs={{0,5},{5,0},{4,9},{9,4},{8,13},{13,8},{12,15},{15,12},{14,11},{11,... | collective-permute-start | bytes 528392 | tf_op jit(solution)/shard_map/ppermute | solution.py:128
  5.0 1.0 %collective-permute-start.1 = (bf16[16,5504]{1,0:T(8,128)(2,1)S(1)}, bf16[16,5504]{1,0:T(8,128)(2,1)S(1)}, u32[]{:S(2)}, u32[]{:S(2)}) collective-permute-start(bf16[16,5504]{1,0:T(8,128)(2,1)S(1)} %collective-permute-done.refs_1_.refs_8_), channel_id=1, source_target_pairs={{0,5},{5,0},{4,9},{9,4},{8,13},{13,8},{12,15},{15,12},{14,11},{11,... | collective-permute-start | bytes 528392 | tf_op jit(solution)/shard_map/ppermute | solution.py:128
  6.0 3.5 %shard_map.95.refs_0_ = bf16[1024,5376]{1,0:T(8,128)(2,1)S(1)} custom-call(bf16[1024,5376]{1,0:T(8,128)(2,1)} %head_hbm.3), custom_call_target="tpu_custom_call" | custom-call | bytes 16515072 | tf_op jit(solution)/shard_map/pallas_call | solution.py:229
  9.5 1.6 %collective-permute-start.8 = (bf16[16,5504]{1,0:T(8,128)(2,1)S(1)}, bf16[16,5504]{1,0:T(8,128)(2,1)S(1)}, u32[]{:S(2)}, u32[]{:S(2)}) collective-permute-start(bf16[16,5504]{1,0:T(8,128)(2,1)S(1)} %collective-permute-done.5.refs_2_.refs_9_), channel_id=1, source_target_pairs={{1,4},{4,1},{5,8},{8,5},{9,12},{12,9},{13,14},{14,13},{15,10},{10,... | collective-permute-start | bytes 528392 | tf_op jit(solution)/shard_map/ppermute | solution.py:128
  11.1 0.0 collective-permute-done.1.refs_3_.refs_1_
  11.1 0.6 %collective-permute-start.2 = (bf16[16,5504]{1,0:T(8,128)(2,1)S(1)}, bf16[16,5504]{1,0:T(8,128)(2,1)S(1)}, u32[]{:S(2)}, u32[]{:S(2)}) collective-permute-start(bf16[16,5504]{1,0:T(8,128)(2,1)S(1)} %collective-permute-done.1.refs_3_.refs_1_), channel_id=1, source_target_pairs={{1,4},{4,1},{5,8},{8,5},{9,12},{12,9},{13,14},{14,13},{15,10},{10,... | collective-permute-start | bytes 528392 | tf_op jit(solution)/shard_map/ppermute | solution.py:128
  11.7 0.1 collective-permute-start.6
  11.8 1.8 %shard_map.97.refs_16_ = bf16[1024,5376]{1,0:T(8,128)(2,1)S(1)} custom-call(bf16[1024,5376]{1,0:T(8,128)(2,1)} %head_hbm.3, bf16[1024,5376]{1,0:T(8,128)(2,1)S(1)} %shard_map.95.refs_0_), custom_call_target="tpu_custom_call", output_to_operand_aliasing={{}: (1, {})} | custom-call | bytes 5505024 | tf_op jit(solution)/shard_map/pallas_call | solution.py:229
  13.6 0.9 %collective-permute-done.8.refs_0_.refs_6_ = bf16[16,5504]{1,0:T(8,128)(2,1)S(1)} collective-permute-done((bf16[16,5504]{1,0:T(8,128)(2,1)S(1)}, bf16[16,5504]{1,0:T(8,128)(2,1)S(1)}, u32[]{:S(2)}, u32[]{:S(2)}) %collective-permute-start.8) | collective-permute-done | bytes 176160 | tf_op jit(solution)/shard_map/ppermute | solution.py:128
  14.4 1.4 %collective-permute-start.9 = (bf16[16,5504]{1,0:T(8,128)(2,1)S(1)}, bf16[16,5504]{1,0:T(8,128)(2,1)S(1)}, u32[]{:S(2)}, u32[]{:S(2)}) collective-permute-start(bf16[16,5504]{1,0:T(8,128)(2,1)S(1)} %collective-permute-done.8.refs_0_.refs_6_), channel_id=1, source_target_pairs={{0,5},{5,0},{4,9},{9,4},{8,13},{13,8},{12,15},{15,12},{14,11},{11,... | collective-permute-start | bytes 528392 | tf_op jit(solution)/shard_map/ppermute | solution.py:128
  15.9 0.0 collective-permute-start.7
  15.9 0.4 collective-permute-done.2.refs_1_.refs_14_
  16.3 1.3 %collective-permute-start.4 = (bf16[16,5504]{1,0:T(8,128)(2,1)S(1)}, bf16[16,5504]{1,0:T(8,128)(2,1)S(1)}, u32[]{:S(2)}, u32[]{:S(2)}) collective-permute-start(bf16[16,5504]{1,0:T(8,128)(2,1)S(1)} %collective-permute-done.2.refs_1_.refs_14_), channel_id=1, source_target_pairs={{0,5},{5,0},{4,9},{9,4},{8,13},{13,8},{12,15},{15,12},{14,11},{11,... | collective-permute-start | bytes 528392 | tf_op jit(solution)/shard_map/ppermute | solution.py:128
  17.6 0.1 collective-permute-start.11
  17.8 0.0 collective-permute-done.6.refs_4_.refs_7_
  17.8 0.4 collective-permute-start.3
  18.1 1.2 %collective-permute-done.9.refs_4_.refs_11_ = bf16[16,5504]{1,0:T(8,128)(2,1)S(1)} collective-permute-done((bf16[16,5504]{1,0:T(8,128)(2,1)S(1)}, bf16[16,5504]{1,0:T(8,128)(2,1)S(1)}, u32[]{:S(2)}, u32[]{:S(2)}) %collective-permute-start.9) | collective-permute-done | bytes 176160 | tf_op jit(solution)/shard_map/ppermute | solution.py:128
  19.3 2.1 %collective-permute-start.10 = (bf16[16,5504]{1,0:T(8,128)(2,1)S(1)}, bf16[16,5504]{1,0:T(8,128)(2,1)S(1)}, u32[]{:S(2)}, u32[]{:S(2)}) collective-permute-start(bf16[16,5504]{1,0:T(8,128)(2,1)S(1)} %collective-permute-done.9.refs_4_.refs_11_), channel_id=1, source_target_pairs={{1,4},{4,1},{5,8},{8,5},{9,12},{12,9},{13,14},{14,13},{15,10},{10,... | collective-permute-start | bytes 528392 | tf_op jit(solution)/shard_map/ppermute | solution.py:128
  21.4 0.0 collective-permute-done.7.refs_5_.refs_15_
  21.4 0.0 collective-permute-start.12
  21.4 0.8 %shard_map.96.refs_8_ = bf16[256,5376]{1,0:T(8,128)(2,1)S(1)} custom-call(bf16[16,5504]{1,0:T(8,128)(2,1)S(1)} %get-tuple-element.21.refs_0_, bf16[16,5504]{1,0:T(8,128)(2,1)S(1)} %collective-permute-done.refs_1_.refs_8_, bf16[16,5504]{1,0:T(8,128)(2,1)S(1)} %collective-permute-done.5.refs_2_.refs_9_, ...), custom_call_target="tpu_custom_call" | custom-call | flops 10321920 | bytes 2064384 | tf_op jit(solution)/shard_map/pallas_call | solution.py:199
  22.2 0.6 %collective-permute-start.14 = (bf16[16,5504]{1,0:T(8,128)(2,1)S(1)}, bf16[16,5504]{1,0:T(8,128)(2,1)S(1)}, u32[]{:S(2)}, u32[]{:S(2)}) collective-permute-start(bf16[16,5504]{1,0:T(8,128)(2,1)S(1)} %collective-permute-done.4.refs_5_.refs_3_), channel_id=1, source_target_pairs={{0,1},{1,0},{2,3},{3,2},{4,5},{5,4},{6,7},{7,6},{8,9},{9,8},{10,11... | collective-permute-start | bytes 528392 | tf_op jit(solution)/shard_map/ppermute | solution.py:128
  22.8 0.0 collective-permute-done.11.refs_2_.refs_10_
  22.8 0.0 collective-permute-done.3.refs_3_.refs_2_
  22.8 0.8 %shard_map.98.refs_5_ = bf16[256,5376]{1,0:T(8,128)(2,1)S(1)} custom-call(bf16[16,5504]{1,0:T(8,128)(2,1)S(1)} %collective-permute-done.8.refs_0_.refs_6_, bf16[16,5504]{1,0:T(8,128)(2,1)S(1)} %collective-permute-done.2.refs_1_.refs_14_, bf16[16,5504]{1,0:T(8,128)(2,1)S(1)} %collective-permute-done.11.refs_2_.refs_10_, ...), custom_call_target="tpu_custom_call", output_to_operand_aliasing={{}: (8, {})} | custom-call | flops 10321920 | bytes 2064384 | tf_op jit(solution)/shard_map/pallas_call | solution.py:199
  23.7 0.9 %collective-permute-done.10.refs_2_.refs_4_ = bf16[16,5504]{1,0:T(8,128)(2,1)S(1)} collective-permute-done((bf16[16,5504]{1,0:T(8,128)(2,1)S(1)}, bf16[16,5504]{1,0:T(8,128)(2,1)S(1)}, u32[]{:S(2)}, u32[]{:S(2)}) %collective-permute-start.10) | collective-permute-done | bytes 176160 | tf_op jit(solution)/shard_map/ppermute | solution.py:128
  24.5 0.6 %collective-permute-start.13 = (bf16[16,5504]{1,0:T(8,128)(2,1)S(1)}, bf16[16,5504]{1,0:T(8,128)(2,1)S(1)}, u32[]{:S(2)}, u32[]{:S(2)}) collective-permute-start(bf16[16,5504]{1,0:T(8,128)(2,1)S(1)} %collective-permute-done.10.refs_2_.refs_4_), channel_id=1, source_target_pairs={{0,1},{1,0},{2,3},{3,2},{4,5},{5,4},{6,7},{7,6},{8,9},{9,8},{10,11... | collective-permute-start | bytes 528392 | tf_op jit(solution)/shard_map/ppermute | solution.py:128
  25.1 0.0 collective-permute-done.12.refs_0_.refs_5_
  25.1 0.0 collective-permute-done.14.refs_1_.refs_13_
  25.1 0.5 shard_map.99.refs_19_
  25.6 0.6 %collective-permute-done.13.refs_12_ = bf16[16,5504]{1,0:T(8,128)(2,1)S(1)} collective-permute-done((bf16[16,5504]{1,0:T(8,128)(2,1)S(1)}, bf16[16,5504]{1,0:T(8,128)(2,1)S(1)}, u32[]{:S(2)}, u32[]{:S(2)}) %collective-permute-start.13) | collective-permute-done | bytes 176160 | tf_op jit(solution)/shard_map/ppermute | solution.py:128
  26.1 5.3 %shard_map.100 = (f32[8,2944]{1,0:T(8,128)S(1)}, bf16[272,1024]{1,0:T(8,128)(2,1)S(1)}, bf16[16,256]{1,0:T(8,128)(2,1)S(1)}, f32[256,128]{1,0:T(8,128)S(1)}, bf16[256,5376]{1,0:T(8,128)(2,1)S(1)}) custom-call(bf16[16,5504]{1,0:T(8,128)(2,1)S(1)} %get-tuple-element.21.refs_0_, ...), custom_call_target="tpu_custom_call", output_to_operand_aliasing={{4}: (19, {})} | custom-call | flops 4227858432 | bytes 5505024 | tf_op jit(solution)/shard_map/pallas_call | solution.py:336
  31.4 0.4 collective-permute-start.15
  31.8 2.2 %shard_map.101 = f32[8,2944]{1,0:T(8,128)S(1)} custom-call(bf16[16,5504]{1,0:T(8,128)(2,1)S(1)} %get-tuple-element.21.refs_0_, bf16[16,5504]{1,0:T(8,128)(2,1)S(1)} %collective-permute-done.1.refs_3_.refs_1_, bf16[16,5504]{1,0:T(8,128)(2,1)S(1)} %collective-permute-done.3.refs_3_.refs_2_, bf16[16,5504]{1,0:T(8,128)(2,1)S(1)} %collective-permute-done.4.refs_5_.refs_3_, ...), custom_call_target="tpu_custom_call" | custom-call | flops 1409286144 | bytes 5505024 | tf_op jit(solution)/shard_map/pallas_call | solution.py:352
  34.0 0.0 collective-permute-done.15
  34.1 2.7 %collective-permute-start.18 = (bf16[8,2944]{1,0:T(8,128)(2,1)S(1)}, bf16[8,2944]{1,0:T(8,128)(2,1)S(1)}, u32[]{:S(2)}, u32[]{:S(2)}) collective-permute-start(bf16[8,2944]{1,0:T(8,128)(2,1)S(1)} %fusion), channel_id=1, source_target_pairs={{0,6},{1,7},{2,4},{3,5},{4,2},{5,3},{6,0},{7,1},{8,14},{9,15},{10,... | collective-permute-start | bytes 141320 | tf_op jit(solution)/shard_map/ppermute | solution.py:365
  36.7 0.4 collective-permute-start.17
  37.2 0.4 collective-permute-start.16
  37.6 1.9 %collective-permute-done.18 = bf16[8,2944]{1,0:T(8,128)(2,1)S(1)} collective-permute-done((bf16[8,2944]{1,0:T(8,128)(2,1)S(1)}, bf16[8,2944]{1,0:T(8,128)(2,1)S(1)}, u32[]{:S(2)}, u32[]{:S(2)}) %collective-permute-start.18) | collective-permute-done | bytes 47136 | tf_op jit(solution)/shard_map/ppermute | solution.py:365
  39.5 1.3 %collective-permute-done.17 = bf16[8,2944]{1,0:T(8,128)(2,1)S(1)} collective-permute-done((bf16[8,2944]{1,0:T(8,128)(2,1)S(1)}, bf16[8,2944]{1,0:T(8,128)(2,1)S(1)}, u32[]{:S(2)}, u32[]{:S(2)}) %collective-permute-start.17) | collective-permute-done | bytes 47136 | tf_op jit(solution)/shard_map/ppermute | solution.py:365
  40.8 0.4 collective-permute-done.16
  41.3 2.7 %collective-permute-start.19 = (bf16[8,2944]{1,0:T(8,128)(2,1)S(1)}, bf16[8,2944]{1,0:T(8,128)(2,1)S(1)}, u32[]{:S(2)}, u32[]{:S(2)}) collective-permute-start(bf16[8,2944]{1,0:T(8,128)(2,1)S(1)} %get-tuple-element.39), channel_id=1, source_target_pairs={{0,8},{1,9},{2,10},{3,11},{4,12},{5,13},{6,14},{7,15},{8,0},{9,1},... | collective-permute-start | bytes 141320 | tf_op jit(solution)/shard_map/ppermute | solution.py:365
  43.9 2.4 %collective-permute-done.19 = bf16[8,2944]{1,0:T(8,128)(2,1)S(1)} collective-permute-done((bf16[8,2944]{1,0:T(8,128)(2,1)S(1)}, bf16[8,2944]{1,0:T(8,128)(2,1)S(1)}, u32[]{:S(2)}, u32[]{:S(2)}) %collective-permute-start.19) | collective-permute-done | bytes 47136 | tf_op jit(solution)/shard_map/ppermute | solution.py:365
  46.3 0.1 collective-permute-start.20
  46.4 1.3 %collective-permute-done.20.given = f32[8,2944]{1,0:T(8,128)S(1)} collective-permute-done((f32[8,2944]{1,0:T(8,128)S(1)}, f32[8,2944]{1,0:T(8,128)S(1)}, u32[]{:S(2)}, u32[]{:S(2)}) %collective-permute-start.20) | collective-permute-done | bytes 94240 | tf_op jit(solution)/shard_map/ppermute | solution.py:365
  47.7 0.7 %shard_map.102 = (f32[1,16]{1,0:T(1,128)}, f32[4,5376]{1,0:T(4,128)}, f32[4,5376]{1,0:T(4,128)}) custom-call(f32[8,2944]{1,0:T(8,128)S(1)} %convert_add_fusion.kept, f32[8,2944]{1,0:T(8,128)S(1)} %collective-permute-done.20.given), custom_call_target="tpu_custom_call" | custom-call | tf_op jit(solution)/shard_map/pallas_call | solution.py:408
  (6 shorter events, 0.1 us)
Async XLA Ops:
  1.8 3.2 %collective-permute-start = (bf16[16,5504]{1,0:T(8,128)(2,1)S(1)}, bf16[16,5504]{1,0:T(8,128)(2,1)S(1)}, u32[]{:S(2)}, u32[]{:S(2)}) collective-permute-start(bf16[16,5504]{1,0:T(8,128)(2,1)S(1)} %get-tuple-element.21.refs_0_), channel_id=1, source_target_pairs={{0,1},{1,0},{2,3},{3,2},{4,5},{5,4},{6,7},{7,6},{8,9},{9,8},{10,11... | collective-permute-start | bytes 528392 | tf_op jit(solution)/shard_map/ppermute | solution.py:128
  2.3 7.2 %collective-permute-start.5 = (bf16[16,5504]{1,0:T(8,128)(2,1)S(1)}, bf16[16,5504]{1,0:T(8,128)(2,1)S(1)}, u32[]{:S(2)}, u32[]{:S(2)}) collective-permute-start(bf16[16,5504]{1,0:T(8,128)(2,1)S(1)} %get-tuple-element.21.refs_0_), channel_id=1, source_target_pairs={{0,5},{5,0},{4,9},{9,4},{8,13},{13,8},{12,15},{15,12},{14,11},{11,... | collective-permute-start | bytes 528392 | tf_op jit(solution)/shard_map/ppermute | solution.py:128
  5.0 6.1 %collective-permute-start.1 = (bf16[16,5504]{1,0:T(8,128)(2,1)S(1)}, bf16[16,5504]{1,0:T(8,128)(2,1)S(1)}, u32[]{:S(2)}, u32[]{:S(2)}) collective-permute-start(bf16[16,5504]{1,0:T(8,128)(2,1)S(1)} %collective-permute-done.refs_1_.refs_8_), channel_id=1, source_target_pairs={{0,5},{5,0},{4,9},{9,4},{8,13},{13,8},{12,15},{15,12},{14,11},{11,... | collective-permute-start | bytes 528392 | tf_op jit(solution)/shard_map/ppermute | solution.py:128
  9.5 4.9 %collective-permute-start.8 = (bf16[16,5504]{1,0:T(8,128)(2,1)S(1)}, bf16[16,5504]{1,0:T(8,128)(2,1)S(1)}, u32[]{:S(2)}, u32[]{:S(2)}) collective-permute-start(bf16[16,5504]{1,0:T(8,128)(2,1)S(1)} %collective-permute-done.5.refs_2_.refs_9_), channel_id=1, source_target_pairs={{1,4},{4,1},{5,8},{8,5},{9,12},{12,9},{13,14},{14,13},{15,10},{10,... | collective-permute-start | bytes 528392 | tf_op jit(solution)/shard_map/ppermute | solution.py:128
  11.1 5.3 %collective-permute-start.2 = (bf16[16,5504]{1,0:T(8,128)(2,1)S(1)}, bf16[16,5504]{1,0:T(8,128)(2,1)S(1)}, u32[]{:S(2)}, u32[]{:S(2)}) collective-permute-start(bf16[16,5504]{1,0:T(8,128)(2,1)S(1)} %collective-permute-done.1.refs_3_.refs_1_), channel_id=1, source_target_pairs={{1,4},{4,1},{5,8},{8,5},{9,12},{12,9},{13,14},{14,13},{15,10},{10,... | collective-permute-start | bytes 528392 | tf_op jit(solution)/shard_map/ppermute | solution.py:128
  11.7 6.1 %collective-permute-start.6 = (bf16[16,5504]{1,0:T(8,128)(2,1)S(1)}, bf16[16,5504]{1,0:T(8,128)(2,1)S(1)}, u32[]{:S(2)}, u32[]{:S(2)}) collective-permute-start(bf16[16,5504]{1,0:T(8,128)(2,1)S(1)} %collective-permute-done.5.refs_2_.refs_9_), channel_id=1, source_target_pairs={{0,1},{1,0},{2,3},{3,2},{4,5},{5,4},{6,7},{7,6},{8,9},{9,8},{10,11... | collective-permute-start | bytes 528392 | tf_op jit(solution)/shard_map/ppermute | solution.py:128
  14.4 4.9 %collective-permute-start.9 = (bf16[16,5504]{1,0:T(8,128)(2,1)S(1)}, bf16[16,5504]{1,0:T(8,128)(2,1)S(1)}, u32[]{:S(2)}, u32[]{:S(2)}) collective-permute-start(bf16[16,5504]{1,0:T(8,128)(2,1)S(1)} %collective-permute-done.8.refs_0_.refs_6_), channel_id=1, source_target_pairs={{0,5},{5,0},{4,9},{9,4},{8,13},{13,8},{12,15},{15,12},{14,11},{11,... | collective-permute-start | bytes 528392 | tf_op jit(solution)/shard_map/ppermute | solution.py:128
  15.9 5.5 %collective-permute-start.7 = (bf16[16,5504]{1,0:T(8,128)(2,1)S(1)}, bf16[16,5504]{1,0:T(8,128)(2,1)S(1)}, u32[]{:S(2)}, u32[]{:S(2)}) collective-permute-start(bf16[16,5504]{1,0:T(8,128)(2,1)S(1)} %collective-permute-done.1.refs_3_.refs_1_), channel_id=1, source_target_pairs={{0,1},{1,0},{2,3},{3,2},{4,5},{5,4},{6,7},{7,6},{8,9},{9,8},{10,11... | collective-permute-start | bytes 528392 | tf_op jit(solution)/shard_map/ppermute | solution.py:128
  16.3 5.9 %collective-permute-start.4 = (bf16[16,5504]{1,0:T(8,128)(2,1)S(1)}, bf16[16,5504]{1,0:T(8,128)(2,1)S(1)}, u32[]{:S(2)}, u32[]{:S(2)}) collective-permute-start(bf16[16,5504]{1,0:T(8,128)(2,1)S(1)} %collective-permute-done.2.refs_1_.refs_14_), channel_id=1, source_target_pairs={{0,5},{5,0},{4,9},{9,4},{8,13},{13,8},{12,15},{15,12},{14,11},{11,... | collective-permute-start | bytes 528392 | tf_op jit(solution)/shard_map/ppermute | solution.py:128
  17.6 5.2 %collective-permute-start.11 = (bf16[16,5504]{1,0:T(8,128)(2,1)S(1)}, bf16[16,5504]{1,0:T(8,128)(2,1)S(1)}, u32[]{:S(2)}, u32[]{:S(2)}) collective-permute-start(bf16[16,5504]{1,0:T(8,128)(2,1)S(1)} %collective-permute-done.8.refs_0_.refs_6_), channel_id=1, source_target_pairs={{0,1},{1,0},{2,3},{3,2},{4,5},{5,4},{6,7},{7,6},{8,9},{9,8},{10,11... | collective-permute-start | bytes 528392 | tf_op jit(solution)/shard_map/ppermute | solution.py:128
  17.8 5.1 %collective-permute-start.3 = (bf16[16,5504]{1,0:T(8,128)(2,1)S(1)}, bf16[16,5504]{1,0:T(8,128)(2,1)S(1)}, u32[]{:S(2)}, u32[]{:S(2)}) collective-permute-start(bf16[16,5504]{1,0:T(8,128)(2,1)S(1)} %collective-permute-done.2.refs_1_.refs_14_), channel_id=1, source_target_pairs={{0,1},{1,0},{2,3},{3,2},{4,5},{5,4},{6,7},{7,6},{8,9},{9,8},{10,11... | collective-permute-start | bytes 528392 | tf_op jit(solution)/shard_map/ppermute | solution.py:128
  19.3 5.2 %collective-permute-start.10 = (bf16[16,5504]{1,0:T(8,128)(2,1)S(1)}, bf16[16,5504]{1,0:T(8,128)(2,1)S(1)}, u32[]{:S(2)}, u32[]{:S(2)}) collective-permute-start(bf16[16,5504]{1,0:T(8,128)(2,1)S(1)} %collective-permute-done.9.refs_4_.refs_11_), channel_id=1, source_target_pairs={{1,4},{4,1},{5,8},{8,5},{9,12},{12,9},{13,14},{14,13},{15,10},{10,... | collective-permute-start | bytes 528392 | tf_op jit(solution)/shard_map/ppermute | solution.py:128
  21.4 3.7 %collective-permute-start.12 = (bf16[16,5504]{1,0:T(8,128)(2,1)S(1)}, bf16[16,5504]{1,0:T(8,128)(2,1)S(1)}, u32[]{:S(2)}, u32[]{:S(2)}) collective-permute-start(bf16[16,5504]{1,0:T(8,128)(2,1)S(1)} %collective-permute-done.9.refs_4_.refs_11_), channel_id=1, source_target_pairs={{0,1},{1,0},{2,3},{3,2},{4,5},{5,4},{6,7},{7,6},{8,9},{9,8},{10,11... | collective-permute-start | bytes 528392 | tf_op jit(solution)/shard_map/ppermute | solution.py:128
  22.2 2.8 %collective-permute-start.14 = (bf16[16,5504]{1,0:T(8,128)(2,1)S(1)}, bf16[16,5504]{1,0:T(8,128)(2,1)S(1)}, u32[]{:S(2)}, u32[]{:S(2)}) collective-permute-start(bf16[16,5504]{1,0:T(8,128)(2,1)S(1)} %collective-permute-done.4.refs_5_.refs_3_), channel_id=1, source_target_pairs={{0,1},{1,0},{2,3},{3,2},{4,5},{5,4},{6,7},{7,6},{8,9},{9,8},{10,11... | collective-permute-start | bytes 528392 | tf_op jit(solution)/shard_map/ppermute | solution.py:128
  24.5 1.6 %collective-permute-start.13 = (bf16[16,5504]{1,0:T(8,128)(2,1)S(1)}, bf16[16,5504]{1,0:T(8,128)(2,1)S(1)}, u32[]{:S(2)}, u32[]{:S(2)}) collective-permute-start(bf16[16,5504]{1,0:T(8,128)(2,1)S(1)} %collective-permute-done.10.refs_2_.refs_4_), channel_id=1, source_target_pairs={{0,1},{1,0},{2,3},{3,2},{4,5},{5,4},{6,7},{7,6},{8,9},{9,8},{10,11... | collective-permute-start | bytes 528392 | tf_op jit(solution)/shard_map/ppermute | solution.py:128
  31.4 2.6 %collective-permute-start.15 = (f32[8,2944]{1,0:T(8,128)S(1)}, f32[8,2944]{1,0:T(8,128)S(1)}, u32[]{:S(2)}, u32[]{:S(2)}) collective-permute-start(f32[8,2944]{1,0:T(8,128)S(1)} %get-tuple-element.35), channel_id=1, source_target_pairs={{0,1},{1,0},{2,3},{3,2},{4,5},{5,4},{6,7},{7,6},{8,9},{9,8},{10,11... | collective-permute-start | bytes 282632 | tf_op jit(solution)/shard_map/ppermute | solution.py:365
  34.1 5.4 %collective-permute-start.18 = (bf16[8,2944]{1,0:T(8,128)(2,1)S(1)}, bf16[8,2944]{1,0:T(8,128)(2,1)S(1)}, u32[]{:S(2)}, u32[]{:S(2)}) collective-permute-start(bf16[8,2944]{1,0:T(8,128)(2,1)S(1)} %fusion), channel_id=1, source_target_pairs={{0,6},{1,7},{2,4},{3,5},{4,2},{5,3},{6,0},{7,1},{8,14},{9,15},{10,... | collective-permute-start | bytes 141320 | tf_op jit(solution)/shard_map/ppermute | solution.py:365
  36.7 4.1 %collective-permute-start.17 = (bf16[8,2944]{1,0:T(8,128)(2,1)S(1)}, bf16[8,2944]{1,0:T(8,128)(2,1)S(1)}, u32[]{:S(2)}, u32[]{:S(2)}) collective-permute-start(bf16[8,2944]{1,0:T(8,128)(2,1)S(1)} %fusion), channel_id=1, source_target_pairs={{0,4},{1,5},{2,6},{3,7},{4,0},{5,1},{6,2},{7,3},{8,12},{9,13},{10,... | collective-permute-start | bytes 141320 | tf_op jit(solution)/shard_map/ppermute | solution.py:365
  37.2 4.1 %collective-permute-start.16 = (bf16[8,2944]{1,0:T(8,128)(2,1)S(1)}, bf16[8,2944]{1,0:T(8,128)(2,1)S(1)}, u32[]{:S(2)}, u32[]{:S(2)}) collective-permute-start(bf16[8,2944]{1,0:T(8,128)(2,1)S(1)} %fusion), channel_id=1, source_target_pairs={{0,2},{1,3},{2,0},{3,1},{4,6},{5,7},{6,4},{7,5},{8,10},{9,11},{10,... | collective-permute-start | bytes 141320 | tf_op jit(solution)/shard_map/ppermute | solution.py:365
  41.3 5.0 %collective-permute-start.19 = (bf16[8,2944]{1,0:T(8,128)(2,1)S(1)}, bf16[8,2944]{1,0:T(8,128)(2,1)S(1)}, u32[]{:S(2)}, u32[]{:S(2)}) collective-permute-start(bf16[8,2944]{1,0:T(8,128)(2,1)S(1)} %get-tuple-element.39), channel_id=1, source_target_pairs={{0,8},{1,9},{2,10},{3,11},{4,12},{5,13},{6,14},{7,15},{8,0},{9,1},... | collective-permute-start | bytes 141320 | tf_op jit(solution)/shard_map/ppermute | solution.py:365
  46.3 1.4 %collective-permute-start.20 = (f32[8,2944]{1,0:T(8,128)S(1)}, f32[8,2944]{1,0:T(8,128)S(1)}, u32[]{:S(2)}, u32[]{:S(2)}) collective-permute-start(f32[8,2944]{1,0:T(8,128)S(1)} %convert_add_fusion.kept), channel_id=1, source_target_pairs={{0,1},{1,0},{2,3},{3,2},{4,5},{5,4},{6,7},{7,6},{8,9},{9,8},{10,11... | collective-permute-start | bytes 282632 | tf_op jit(solution)/shard_map/ppermute | solution.py:365

commit v12 on v10

--- a/solution.py
+++ b/solution.py
@@ -136,15 +136,15 @@
         crossed = send(crossed, hop_pairs(order, step))
         if step < half:
             plain = send(plain, hop_pairs(order, step))
-        if step <= 2:
-            head = load(tied_head, step - 1, min(2, half), head if step > 1 else None)
+        if step == 1:
+            head = load(tied_head, 0, 2, None)
             crossed, head = tie(crossed, head)
         if mapper is not None and step == 3:
             mapped = mapper(None, {i: blocks[i] for i in ready[:6]})
             plain, mapped = tie(plain, mapped)
-        if mapper is not None and step == half:
-            mapped = mapper(mapped, {i: blocks[i] for i in ready[6:12]})
-            crossed, mapped = tie(crossed, mapped)
+        if step == half:
+            head = load(tied_head, 1, 2, head)
+            crossed, head = tie(crossed, head)
         far = step if step % 2 else chips - step
         near = chips - far
         mine, theirs = (chips, 0) if step % 2 else (0, chips)
@@ -158,7 +158,7 @@
             blocks[theirs + far] = swap(crossed)
             ready += [mine + far, theirs + far]
             if mapper is not None:
-                mapped = mapper(mapped, {i: blocks[i] for i in ready[12:15]})
+                mapped = mapper(mapped, {i: blocks[i] for i in ready[6:15]})
     return blocks, head, mapped, ready[15:] if mapper is not None else ready
 
 

time: 48.4 us -> 49 us (1.012)
  waiting for transfers between devices: 10.2 us -> 10.9 us
    ppermute x15, waiting for transfers between devices: 2.95 us -> 3.51 us  [gather_blocks(): send = lambda x, pairs: lax.ppermute(x, 'loop', pairs)]
    pallas_call x3 -> x2, Pallas kernels: 2.11 us -> 2.03 us  [map_early(): pl.pallas_call(functools.partial(map_kernel, places), out_shape=pltpu.VME...]
  transfers between devices with their start and end apart: 21 -> 21, of which waited for: 8 -> 8; matrix products, arithmetic and copies ran while one was open for 0% -> 0% of each run, Pallas kernels for 20% -> 19%
where the time goes in v12:
time: 49 us; the launch traced here: 48.9 us
  starting transfers between devices  20.5 us (42%)
  Pallas kernels  16.6 us (34%)
  waiting for transfers between devices  10.9 us (22%)
  between operations  0.75 us (2%)
    ppermute x15, starting transfers between devices, gather_blocks(): send = lambda x, pairs: lax.ppermute(x, 'loop', pairs)  14 us
    ppermute x6, waiting for transfers between devices, sum_over_loop(): lax.ppermute(x, 'loop', [(i, i ^ mask) for i in range(loop)])  7.4 us
    ppermute x6, starting transfers between devices, sum_over_loop(): lax.ppermute(x, 'loop', [(i, i ^ mask) for i in range(loop)])  6.52 us
    pallas_call x1, Pallas kernels, main(): pl.pallas_call(functools.partial(front_kernel, levels, len(blocks), late)...  5.3 us
    pallas_call x2, Pallas kernels, load(): pl.pallas_call(functools.partial(load_kernel, part, parts), out_shape=plt...  5.23 us
    ppermute x15, waiting for transfers between devices, gather_blocks(): send = lambda x, pairs: lax.ppermute(x, 'loop', pairs)  3.51 us
    pallas_call x1, Pallas kernels, main(): pl.pallas_call(functools.partial(back_kernel, loop, len(blocks)), out_sha...  2.21 us
    pallas_call x2, Pallas kernels, map_early(): pl.pallas_call(functools.partial(map_kernel, places), out_shape=pltpu.VME...  2.03 us
  transfers between devices with their start and end apart: 21, of which 8 were waited for; matrix products, arithmetic and copies ran while one was open for 0% of the time, Pallas kernels for 19%

profile of v12, /device:TPU:0, one launch (start us, length us, event | category | flops | bytes accessed | tf_op | source)
XLA Modules:
  0.0 48.9 jit_solution(1396928640844144882)
XLA Ops:
  0.6 1.1 %shard_map.94 = (bf16[16,5504]{1,0:T(8,128)(2,1)S(1)}, f32[4,5376]{1,0:T(4,128)S(1)}, f32[4,5376]{1,0:T(4,128)S(1)}) custom-call(bf16[16,5376]{1,0:T(8,128)(2,1)} %hidden.1, s32[1,16]{1,0:T(1,128)} %bitcast.4, s32[1,16]{1,0:T(1,128)} %bitcast.5, f32[1,16]{1,0:T(1,128)} %bitcast.6, f32[4,5376]{1,0:T(4,128)} %depth_gain.1, f32[4,5376]{1,0:T(4,128)} %depth_bias.1), custom_call_target="tpu_custom_call" | custom-call | tf_op jit(solution)/shard_map/pallas_call | solution.py:87
  1.8 0.5 %collective-permute-start = (bf16[16,5504]{1,0:T(8,128)(2,1)S(1)}, bf16[16,5504]{1,0:T(8,128)(2,1)S(1)}, u32[]{:S(2)}, u32[]{:S(2)}) collective-permute-start(bf16[16,5504]{1,0:T(8,128)(2,1)S(1)} %get-tuple-element.19.refs_0_), channel_id=1, source_target_pairs={{0,1},{1,0},{2,3},{3,2},{4,5},{5,4},{6,7},{7,6},{8,9},{9,8},{10,11... | collective-permute-start | bytes 528392 | tf_op jit(solution)/shard_map/ppermute | solution.py:127
  2.3 2.7 %collective-permute-start.5 = (bf16[16,5504]{1,0:T(8,128)(2,1)S(1)}, bf16[16,5504]{1,0:T(8,128)(2,1)S(1)}, u32[]{:S(2)}, u32[]{:S(2)}) collective-permute-start(bf16[16,5504]{1,0:T(8,128)(2,1)S(1)} %get-tuple-element.19.refs_0_), channel_id=1, source_target_pairs={{0,5},{5,0},{4,9},{9,4},{8,13},{13,8},{12,15},{15,12},{14,11},{11,... | collective-permute-start | bytes 528392 | tf_op jit(solution)/shard_map/ppermute | solution.py:127
  5.0 0.0 collective-permute-done.refs_1_.refs_8_
  5.0 1.0 %collective-permute-start.1 = (bf16[16,5504]{1,0:T(8,128)(2,1)S(1)}, bf16[16,5504]{1,0:T(8,128)(2,1)S(1)}, u32[]{:S(2)}, u32[]{:S(2)}) collective-permute-start(bf16[16,5504]{1,0:T(8,128)(2,1)S(1)} %collective-permute-done.refs_1_.refs_8_), channel_id=1, source_target_pairs={{0,5},{5,0},{4,9},{9,4},{8,13},{13,8},{12,15},{15,12},{14,11},{11,... | collective-permute-start | bytes 528392 | tf_op jit(solution)/shard_map/ppermute | solution.py:127
  6.0 2.6 %shard_map.95.refs_0_ = bf16[1024,5376]{1,0:T(8,128)(2,1)S(1)} custom-call(bf16[1024,5376]{1,0:T(8,128)(2,1)} %head_hbm.3), custom_call_target="tpu_custom_call" | custom-call | bytes 11010048 | tf_op jit(solution)/shard_map/pallas_call | solution.py:228
  8.6 0.0 collective-permute-done.5.refs_2_.refs_9_
  8.6 1.6 %collective-permute-start.8 = (bf16[16,5504]{1,0:T(8,128)(2,1)S(1)}, bf16[16,5504]{1,0:T(8,128)(2,1)S(1)}, u32[]{:S(2)}, u32[]{:S(2)}) collective-permute-start(bf16[16,5504]{1,0:T(8,128)(2,1)S(1)} %collective-permute-done.5.refs_2_.refs_9_), channel_id=1, source_target_pairs={{1,4},{4,1},{5,8},{8,5},{9,12},{12,9},{13,14},{14,13},{15,10},{10,... | collective-permute-start | bytes 528392 | tf_op jit(solution)/shard_map/ppermute | solution.py:127
  10.2 0.0 collective-permute-done.1.refs_3_.refs_1_
  10.2 1.5 %collective-permute-start.2 = (bf16[16,5504]{1,0:T(8,128)(2,1)S(1)}, bf16[16,5504]{1,0:T(8,128)(2,1)S(1)}, u32[]{:S(2)}, u32[]{:S(2)}) collective-permute-start(bf16[16,5504]{1,0:T(8,128)(2,1)S(1)} %collective-permute-done.1.refs_3_.refs_1_), channel_id=1, source_target_pairs={{1,4},{4,1},{5,8},{8,5},{9,12},{12,9},{13,14},{14,13},{15,10},{10,... | collective-permute-start | bytes 528392 | tf_op jit(solution)/shard_map/ppermute | solution.py:127
  11.7 1.9 %collective-permute-done.8.refs_0_.refs_6_ = bf16[16,5504]{1,0:T(8,128)(2,1)S(1)} collective-permute-done((bf16[16,5504]{1,0:T(8,128)(2,1)S(1)}, bf16[16,5504]{1,0:T(8,128)(2,1)S(1)}, u32[]{:S(2)}, u32[]{:S(2)}) %collective-permute-start.8) | collective-permute-done | bytes 176160 | tf_op jit(solution)/shard_map/ppermute | solution.py:127
  13.6 1.7 %collective-permute-start.9 = (bf16[16,5504]{1,0:T(8,128)(2,1)S(1)}, bf16[16,5504]{1,0:T(8,128)(2,1)S(1)}, u32[]{:S(2)}, u32[]{:S(2)}) collective-permute-start(bf16[16,5504]{1,0:T(8,128)(2,1)S(1)} %collective-permute-done.8.refs_0_.refs_6_), channel_id=1, source_target_pairs={{0,5},{5,0},{4,9},{9,4},{8,13},{13,8},{12,15},{15,12},{14,11},{11,... | collective-permute-start | bytes 528392 | tf_op jit(solution)/shard_map/ppermute | solution.py:127
  15.3 0.0 collective-permute-start.6
  15.3 0.5 %collective-permute-start.7 = (bf16[16,5504]{1,0:T(8,128)(2,1)S(1)}, bf16[16,5504]{1,0:T(8,128)(2,1)S(1)}, u32[]{:S(2)}, u32[]{:S(2)}) collective-permute-start(bf16[16,5504]{1,0:T(8,128)(2,1)S(1)} %collective-permute-done.1.refs_3_.refs_1_), channel_id=1, source_target_pairs={{0,1},{1,0},{2,3},{3,2},{4,5},{5,4},{6,7},{7,6},{8,9},{9,8},{10,11... | collective-permute-start | bytes 528392 | tf_op jit(solution)/shard_map/ppermute | solution.py:127
  15.8 0.0 collective-permute-done.2.refs_1_.refs_14_
  15.8 1.2 %collective-permute-start.4 = (bf16[16,5504]{1,0:T(8,128)(2,1)S(1)}, bf16[16,5504]{1,0:T(8,128)(2,1)S(1)}, u32[]{:S(2)}, u32[]{:S(2)}) collective-permute-start(bf16[16,5504]{1,0:T(8,128)(2,1)S(1)} %collective-permute-done.2.refs_1_.refs_14_), channel_id=1, source_target_pairs={{0,5},{5,0},{4,9},{9,4},{8,13},{13,8},{12,15},{15,12},{14,11},{11,... | collective-permute-start | bytes 528392 | tf_op jit(solution)/shard_map/ppermute | solution.py:127
  17.0 1.5 %collective-permute-done.9.refs_4_.refs_11_ = bf16[16,5504]{1,0:T(8,128)(2,1)S(1)} collective-permute-done((bf16[16,5504]{1,0:T(8,128)(2,1)S(1)}, bf16[16,5504]{1,0:T(8,128)(2,1)S(1)}, u32[]{:S(2)}, u32[]{:S(2)}) %collective-permute-start.9) | collective-permute-done | bytes 176160 | tf_op jit(solution)/shard_map/ppermute | solution.py:127
  18.5 2.1 %collective-permute-start.10 = (bf16[16,5504]{1,0:T(8,128)(2,1)S(1)}, bf16[16,5504]{1,0:T(8,128)(2,1)S(1)}, u32[]{:S(2)}, u32[]{:S(2)}) collective-permute-start(bf16[16,5504]{1,0:T(8,128)(2,1)S(1)} %collective-permute-done.9.refs_4_.refs_11_), channel_id=1, source_target_pairs={{1,4},{4,1},{5,8},{8,5},{9,12},{12,9},{13,14},{14,13},{15,10},{10,... | collective-permute-start | bytes 528392 | tf_op jit(solution)/shard_map/ppermute | solution.py:127
  20.5 0.0 collective-permute-start.12
  20.6 0.0 collective-permute-done.6.refs_4_.refs_7_
  20.6 0.5 %collective-permute-start.3 = (bf16[16,5504]{1,0:T(8,128)(2,1)S(1)}, bf16[16,5504]{1,0:T(8,128)(2,1)S(1)}, u32[]{:S(2)}, u32[]{:S(2)}) collective-permute-start(bf16[16,5504]{1,0:T(8,128)(2,1)S(1)} %collective-permute-done.2.refs_1_.refs_14_), channel_id=1, source_target_pairs={{0,1},{1,0},{2,3},{3,2},{4,5},{5,4},{6,7},{7,6},{8,9},{9,8},{10,11... | collective-permute-start | bytes 528392 | tf_op jit(solution)/shard_map/ppermute | solution.py:127
  21.1 0.1 collective-permute-start.11
  21.1 0.8 %shard_map.96.refs_11_ = bf16[256,5376]{1,0:T(8,128)(2,1)S(1)} custom-call(bf16[16,5504]{1,0:T(8,128)(2,1)S(1)} %get-tuple-element.19.refs_0_, bf16[16,5504]{1,0:T(8,128)(2,1)S(1)} %collective-permute-done.refs_1_.refs_8_, bf16[16,5504]{1,0:T(8,128)(2,1)S(1)} %collective-permute-done.5.refs_2_.refs_9_, ...), custom_call_target="tpu_custom_call" | custom-call | flops 10321920 | bytes 2064384 | tf_op jit(solution)/shard_map/pallas_call | solution.py:198
  22.0 0.0 collective-permute-done.4.refs_5_.refs_3_
  22.0 0.5 %collective-permute-start.14 = (bf16[16,5504]{1,0:T(8,128)(2,1)S(1)}, bf16[16,5504]{1,0:T(8,128)(2,1)S(1)}, u32[]{:S(2)}, u32[]{:S(2)}) collective-permute-start(bf16[16,5504]{1,0:T(8,128)(2,1)S(1)} %collective-permute-done.4.refs_5_.refs_3_), channel_id=1, source_target_pairs={{0,1},{1,0},{2,3},{3,2},{4,5},{5,4},{6,7},{7,6},{8,9},{9,8},{10,11... | collective-permute-start | bytes 528392 | tf_op jit(solution)/shard_map/ppermute | solution.py:127
  22.5 2.6 %shard_map.97.refs_16_ = bf16[1024,5376]{1,0:T(8,128)(2,1)S(1)} custom-call(bf16[1024,5376]{1,0:T(8,128)(2,1)} %head_hbm.3, bf16[1024,5376]{1,0:T(8,128)(2,1)S(1)} %shard_map.95.refs_0_), custom_call_target="tpu_custom_call", output_to_operand_aliasing={{}: (1, {})} | custom-call | bytes 11010048 | tf_op jit(solution)/shard_map/pallas_call | solution.py:228
  25.1 0.0 collective-permute-done.10.refs_8_.refs_4_
  25.1 0.1 collective-permute-start.13
  25.3 0.0 collective-permute-done.12.refs_2_.refs_10_
  25.3 0.0 collective-permute-done.3.refs_3_.refs_2_
  25.3 0.0 collective-permute-done.11.refs_6_.refs_5_
  25.3 1.2 %shard_map.98.refs_19_ = bf16[256,5376]{1,0:T(8,128)(2,1)S(1)} custom-call(bf16[16,5504]{1,0:T(8,128)(2,1)S(1)} %collective-permute-done.8.refs_0_.refs_6_, bf16[16,5504]{1,0:T(8,128)(2,1)S(1)} %collective-permute-done.2.refs_1_.refs_14_, bf16[16,5504]{1,0:T(8,128)(2,1)S(1)} %collective-permute-done.12.refs_2_.refs_10_, ...), custom_call_target="tpu_custom_call", output_to_operand_aliasing={{}: (11, {})} | custom-call | flops 15482880 | bytes 3096576 | tf_op jit(solution)/shard_map/pallas_call | solution.py:198
  26.5 0.1 collective-permute-done.13.refs_12_
  26.6 5.3 %shard_map.99 = (f32[8,2944]{1,0:T(8,128)S(1)}, bf16[272,1024]{1,0:T(8,128)(2,1)S(1)}, bf16[16,256]{1,0:T(8,128)(2,1)S(1)}, f32[256,128]{1,0:T(8,128)S(1)}, bf16[256,5376]{1,0:T(8,128)(2,1)S(1)}) custom-call(bf16[16,5504]{1,0:T(8,128)(2,1)S(1)} %get-tuple-element.19.refs_0_, ...), custom_call_target="tpu_custom_call", output_to_operand_aliasing={{4}: (19, {})} | custom-call | flops 4227858432 | bytes 5505024 | tf_op jit(solution)/shard_map/pallas_call | solution.py:335
  31.9 0.4 collective-permute-start.15
  32.3 2.2 %shard_map.100 = f32[8,2944]{1,0:T(8,128)S(1)} custom-call(bf16[16,5504]{1,0:T(8,128)(2,1)S(1)} %get-tuple-element.19.refs_0_, bf16[16,5504]{1,0:T(8,128)(2,1)S(1)} %collective-permute-done.1.refs_3_.refs_1_, bf16[16,5504]{1,0:T(8,128)(2,1)S(1)} %collective-permute-done.3.refs_3_.refs_2_, bf16[16,5504]{1,0:T(8,128)(2,1)S(1)} %collective-permute-done.4.refs_5_.refs_3_, ...), custom_call_target="tpu_custom_call" | custom-call | flops 1409286144 | bytes 5505024 | tf_op jit(solution)/shard_map/pallas_call | solution.py:351
  34.5 0.0 collective-permute-done.15
  34.5 2.6 %collective-permute-start.18 = (bf16[8,2944]{1,0:T(8,128)(2,1)S(1)}, bf16[8,2944]{1,0:T(8,128)(2,1)S(1)}, u32[]{:S(2)}, u32[]{:S(2)}) collective-permute-start(bf16[8,2944]{1,0:T(8,128)(2,1)S(1)} %fusion), channel_id=1, source_target_pairs={{0,6},{1,7},{2,4},{3,5},{4,2},{5,3},{6,0},{7,1},{8,14},{9,15},{10,... | collective-permute-start | bytes 141320 | tf_op jit(solution)/shard_map/ppermute | solution.py:364
  37.2 0.5 collective-permute-start.17
  37.6 0.5 collective-permute-start.16
  38.1 2.0 %collective-permute-done.18 = bf16[8,2944]{1,0:T(8,128)(2,1)S(1)} collective-permute-done((bf16[8,2944]{1,0:T(8,128)(2,1)S(1)}, bf16[8,2944]{1,0:T(8,128)(2,1)S(1)}, u32[]{:S(2)}, u32[]{:S(2)}) %collective-permute-start.18) | collective-permute-done | bytes 47136 | tf_op jit(solution)/shard_map/ppermute | solution.py:364
  40.1 1.1 %collective-permute-done.17 = bf16[8,2944]{1,0:T(8,128)(2,1)S(1)} collective-permute-done((bf16[8,2944]{1,0:T(8,128)(2,1)S(1)}, bf16[8,2944]{1,0:T(8,128)(2,1)S(1)}, u32[]{:S(2)}, u32[]{:S(2)}) %collective-permute-start.17) | collective-permute-done | bytes 47136 | tf_op jit(solution)/shard_map/ppermute | solution.py:364
  41.2 0.5 collective-permute-done.16
  41.7 2.5 %collective-permute-start.19 = (bf16[8,2944]{1,0:T(8,128)(2,1)S(1)}, bf16[8,2944]{1,0:T(8,128)(2,1)S(1)}, u32[]{:S(2)}, u32[]{:S(2)}) collective-permute-start(bf16[8,2944]{1,0:T(8,128)(2,1)S(1)} %get-tuple-element.35), channel_id=1, source_target_pairs={{0,8},{1,9},{2,10},{3,11},{4,12},{5,13},{6,14},{7,15},{8,0},{9,1},... | collective-permute-start | bytes 141320 | tf_op jit(solution)/shard_map/ppermute | solution.py:364
  44.3 2.5 %collective-permute-done.19 = bf16[8,2944]{1,0:T(8,128)(2,1)S(1)} collective-permute-done((bf16[8,2944]{1,0:T(8,128)(2,1)S(1)}, bf16[8,2944]{1,0:T(8,128)(2,1)S(1)}, u32[]{:S(2)}, u32[]{:S(2)}) %collective-permute-start.19) | collective-permute-done | bytes 47136 | tf_op jit(solution)/shard_map/ppermute | solution.py:364
  46.8 0.1 collective-permute-start.20
  46.9 1.3 %collective-permute-done.20.given = f32[8,2944]{1,0:T(8,128)S(1)} collective-permute-done((f32[8,2944]{1,0:T(8,128)S(1)}, f32[8,2944]{1,0:T(8,128)S(1)}, u32[]{:S(2)}, u32[]{:S(2)}) %collective-permute-start.20) | collective-permute-done | bytes 94240 | tf_op jit(solution)/shard_map/ppermute | solution.py:364
  48.1 0.7 %shard_map.101 = (f32[1,16]{1,0:T(1,128)}, f32[4,5376]{1,0:T(4,128)}, f32[4,5376]{1,0:T(4,128)}) custom-call(f32[8,2944]{1,0:T(8,128)S(1)} %convert_add_fusion.kept, f32[8,2944]{1,0:T(8,128)S(1)} %collective-permute-done.20.given), custom_call_target="tpu_custom_call" | custom-call | tf_op jit(solution)/shard_map/pallas_call | solution.py:407
  (5 shorter events, 0.1 us)
Async XLA Ops:
  1.8 3.2 %collective-permute-start = (bf16[16,5504]{1,0:T(8,128)(2,1)S(1)}, bf16[16,5504]{1,0:T(8,128)(2,1)S(1)}, u32[]{:S(2)}, u32[]{:S(2)}) collective-permute-start(bf16[16,5504]{1,0:T(8,128)(2,1)S(1)} %get-tuple-element.19.refs_0_), channel_id=1, source_target_pairs={{0,1},{1,0},{2,3},{3,2},{4,5},{5,4},{6,7},{7,6},{8,9},{9,8},{10,11... | collective-permute-start | bytes 528392 | tf_op jit(solution)/shard_map/ppermute | solution.py:127
  2.3 6.4 %collective-permute-start.5 = (bf16[16,5504]{1,0:T(8,128)(2,1)S(1)}, bf16[16,5504]{1,0:T(8,128)(2,1)S(1)}, u32[]{:S(2)}, u32[]{:S(2)}) collective-permute-start(bf16[16,5504]{1,0:T(8,128)(2,1)S(1)} %get-tuple-element.19.refs_0_), channel_id=1, source_target_pairs={{0,5},{5,0},{4,9},{9,4},{8,13},{13,8},{12,15},{15,12},{14,11},{11,... | collective-permute-start | bytes 528392 | tf_op jit(solution)/shard_map/ppermute | solution.py:127
  5.0 5.2 %collective-permute-start.1 = (bf16[16,5504]{1,0:T(8,128)(2,1)S(1)}, bf16[16,5504]{1,0:T(8,128)(2,1)S(1)}, u32[]{:S(2)}, u32[]{:S(2)}) collective-permute-start(bf16[16,5504]{1,0:T(8,128)(2,1)S(1)} %collective-permute-done.refs_1_.refs_8_), channel_id=1, source_target_pairs={{0,5},{5,0},{4,9},{9,4},{8,13},{13,8},{12,15},{15,12},{14,11},{11,... | collective-permute-start | bytes 528392 | tf_op jit(solution)/shard_map/ppermute | solution.py:127
  8.6 4.9 %collective-permute-start.8 = (bf16[16,5504]{1,0:T(8,128)(2,1)S(1)}, bf16[16,5504]{1,0:T(8,128)(2,1)S(1)}, u32[]{:S(2)}, u32[]{:S(2)}) collective-permute-start(bf16[16,5504]{1,0:T(8,128)(2,1)S(1)} %collective-permute-done.5.refs_2_.refs_9_), channel_id=1, source_target_pairs={{1,4},{4,1},{5,8},{8,5},{9,12},{12,9},{13,14},{14,13},{15,10},{10,... | collective-permute-start | bytes 528392 | tf_op jit(solution)/shard_map/ppermute | solution.py:127
  10.2 5.6 %collective-permute-start.2 = (bf16[16,5504]{1,0:T(8,128)(2,1)S(1)}, bf16[16,5504]{1,0:T(8,128)(2,1)S(1)}, u32[]{:S(2)}, u32[]{:S(2)}) collective-permute-start(bf16[16,5504]{1,0:T(8,128)(2,1)S(1)} %collective-permute-done.1.refs_3_.refs_1_), channel_id=1, source_target_pairs={{1,4},{4,1},{5,8},{8,5},{9,12},{12,9},{13,14},{14,13},{15,10},{10,... | collective-permute-start | bytes 528392 | tf_op jit(solution)/shard_map/ppermute | solution.py:127
  13.6 4.9 %collective-permute-start.9 = (bf16[16,5504]{1,0:T(8,128)(2,1)S(1)}, bf16[16,5504]{1,0:T(8,128)(2,1)S(1)}, u32[]{:S(2)}, u32[]{:S(2)}) collective-permute-start(bf16[16,5504]{1,0:T(8,128)(2,1)S(1)} %collective-permute-done.8.refs_0_.refs_6_), channel_id=1, source_target_pairs={{0,5},{5,0},{4,9},{9,4},{8,13},{13,8},{12,15},{15,12},{14,11},{11,... | collective-permute-start | bytes 528392 | tf_op jit(solution)/shard_map/ppermute | solution.py:127
  15.3 5.2 %collective-permute-start.6 = (bf16[16,5504]{1,0:T(8,128)(2,1)S(1)}, bf16[16,5504]{1,0:T(8,128)(2,1)S(1)}, u32[]{:S(2)}, u32[]{:S(2)}) collective-permute-start(bf16[16,5504]{1,0:T(8,128)(2,1)S(1)} %collective-permute-done.5.refs_2_.refs_9_), channel_id=1, source_target_pairs={{0,1},{1,0},{2,3},{3,2},{4,5},{5,4},{6,7},{7,6},{8,9},{9,8},{10,11... | collective-permute-start | bytes 528392 | tf_op jit(solution)/shard_map/ppermute | solution.py:127
  15.3 5.8 %collective-permute-start.7 = (bf16[16,5504]{1,0:T(8,128)(2,1)S(1)}, bf16[16,5504]{1,0:T(8,128)(2,1)S(1)}, u32[]{:S(2)}, u32[]{:S(2)}) collective-permute-start(bf16[16,5504]{1,0:T(8,128)(2,1)S(1)} %collective-permute-done.1.refs_3_.refs_1_), channel_id=1, source_target_pairs={{0,1},{1,0},{2,3},{3,2},{4,5},{5,4},{6,7},{7,6},{8,9},{9,8},{10,11... | collective-permute-start | bytes 528392 | tf_op jit(solution)/shard_map/ppermute | solution.py:127
  15.8 6.1 %collective-permute-start.4 = (bf16[16,5504]{1,0:T(8,128)(2,1)S(1)}, bf16[16,5504]{1,0:T(8,128)(2,1)S(1)}, u32[]{:S(2)}, u32[]{:S(2)}) collective-permute-start(bf16[16,5504]{1,0:T(8,128)(2,1)S(1)} %collective-permute-done.2.refs_1_.refs_14_), channel_id=1, source_target_pairs={{0,5},{5,0},{4,9},{9,4},{8,13},{13,8},{12,15},{15,12},{14,11},{11,... | collective-permute-start | bytes 528392 | tf_op jit(solution)/shard_map/ppermute | solution.py:127
  18.5 6.6 %collective-permute-start.10 = (bf16[16,5504]{1,0:T(8,128)(2,1)S(1)}, bf16[16,5504]{1,0:T(8,128)(2,1)S(1)}, u32[]{:S(2)}, u32[]{:S(2)}) collective-permute-start(bf16[16,5504]{1,0:T(8,128)(2,1)S(1)} %collective-permute-done.9.refs_4_.refs_11_), channel_id=1, source_target_pairs={{1,4},{4,1},{5,8},{8,5},{9,12},{12,9},{13,14},{14,13},{15,10},{10,... | collective-permute-start | bytes 528392 | tf_op jit(solution)/shard_map/ppermute | solution.py:127
  20.5 4.7 %collective-permute-start.12 = (bf16[16,5504]{1,0:T(8,128)(2,1)S(1)}, bf16[16,5504]{1,0:T(8,128)(2,1)S(1)}, u32[]{:S(2)}, u32[]{:S(2)}) collective-permute-start(bf16[16,5504]{1,0:T(8,128)(2,1)S(1)} %collective-permute-done.8.refs_0_.refs_6_), channel_id=1, source_target_pairs={{0,1},{1,0},{2,3},{3,2},{4,5},{5,4},{6,7},{7,6},{8,9},{9,8},{10,11... | collective-permute-start | bytes 528392 | tf_op jit(solution)/shard_map/ppermute | solution.py:127
  20.6 4.7 %collective-permute-start.3 = (bf16[16,5504]{1,0:T(8,128)(2,1)S(1)}, bf16[16,5504]{1,0:T(8,128)(2,1)S(1)}, u32[]{:S(2)}, u32[]{:S(2)}) collective-permute-start(bf16[16,5504]{1,0:T(8,128)(2,1)S(1)} %collective-permute-done.2.refs_1_.refs_14_), channel_id=1, source_target_pairs={{0,1},{1,0},{2,3},{3,2},{4,5},{5,4},{6,7},{7,6},{8,9},{9,8},{10,11... | collective-permute-start | bytes 528392 | tf_op jit(solution)/shard_map/ppermute | solution.py:127
  21.1 4.2 %collective-permute-start.11 = (bf16[16,5504]{1,0:T(8,128)(2,1)S(1)}, bf16[16,5504]{1,0:T(8,128)(2,1)S(1)}, u32[]{:S(2)}, u32[]{:S(2)}) collective-permute-start(bf16[16,5504]{1,0:T(8,128)(2,1)S(1)} %collective-permute-done.9.refs_4_.refs_11_), channel_id=1, source_target_pairs={{0,1},{1,0},{2,3},{3,2},{4,5},{5,4},{6,7},{7,6},{8,9},{9,8},{10,11... | collective-permute-start | bytes 528392 | tf_op jit(solution)/shard_map/ppermute | solution.py:127
  22.0 3.3 %collective-permute-start.14 = (bf16[16,5504]{1,0:T(8,128)(2,1)S(1)}, bf16[16,5504]{1,0:T(8,128)(2,1)S(1)}, u32[]{:S(2)}, u32[]{:S(2)}) collective-permute-start(bf16[16,5504]{1,0:T(8,128)(2,1)S(1)} %collective-permute-done.4.refs_5_.refs_3_), channel_id=1, source_target_pairs={{0,1},{1,0},{2,3},{3,2},{4,5},{5,4},{6,7},{7,6},{8,9},{9,8},{10,11... | collective-permute-start | bytes 528392 | tf_op jit(solution)/shard_map/ppermute | solution.py:127
  25.1 1.5 %collective-permute-start.13 = (bf16[16,5504]{1,0:T(8,128)(2,1)S(1)}, bf16[16,5504]{1,0:T(8,128)(2,1)S(1)}, u32[]{:S(2)}, u32[]{:S(2)}) collective-permute-start(bf16[16,5504]{1,0:T(8,128)(2,1)S(1)} %collective-permute-done.10.refs_8_.refs_4_), channel_id=1, source_target_pairs={{0,1},{1,0},{2,3},{3,2},{4,5},{5,4},{6,7},{7,6},{8,9},{9,8},{10,11... | collective-permute-start | bytes 528392 | tf_op jit(solution)/shard_map/ppermute | solution.py:127
  31.9 2.6 %collective-permute-start.15 = (f32[8,2944]{1,0:T(8,128)S(1)}, f32[8,2944]{1,0:T(8,128)S(1)}, u32[]{:S(2)}, u32[]{:S(2)}) collective-permute-start(f32[8,2944]{1,0:T(8,128)S(1)} %get-tuple-element.31), channel_id=1, source_target_pairs={{0,1},{1,0},{2,3},{3,2},{4,5},{5,4},{6,7},{7,6},{8,9},{9,8},{10,11... | collective-permute-start | bytes 282632 | tf_op jit(solution)/shard_map/ppermute | solution.py:364
  34.5 5.6 %collective-permute-start.18 = (bf16[8,2944]{1,0:T(8,128)(2,1)S(1)}, bf16[8,2944]{1,0:T(8,128)(2,1)S(1)}, u32[]{:S(2)}, u32[]{:S(2)}) collective-permute-start(bf16[8,2944]{1,0:T(8,128)(2,1)S(1)} %fusion), channel_id=1, source_target_pairs={{0,6},{1,7},{2,4},{3,5},{4,2},{5,3},{6,0},{7,1},{8,14},{9,15},{10,... | collective-permute-start | bytes 141320 | tf_op jit(solution)/shard_map/ppermute | solution.py:364
  37.2 4.1 %collective-permute-start.17 = (bf16[8,2944]{1,0:T(8,128)(2,1)S(1)}, bf16[8,2944]{1,0:T(8,128)(2,1)S(1)}, u32[]{:S(2)}, u32[]{:S(2)}) collective-permute-start(bf16[8,2944]{1,0:T(8,128)(2,1)S(1)} %fusion), channel_id=1, source_target_pairs={{0,4},{1,5},{2,6},{3,7},{4,0},{5,1},{6,2},{7,3},{8,12},{9,13},{10,... | collective-permute-start | bytes 141320 | tf_op jit(solution)/shard_map/ppermute | solution.py:364
  37.6 4.1 %collective-permute-start.16 = (bf16[8,2944]{1,0:T(8,128)(2,1)S(1)}, bf16[8,2944]{1,0:T(8,128)(2,1)S(1)}, u32[]{:S(2)}, u32[]{:S(2)}) collective-permute-start(bf16[8,2944]{1,0:T(8,128)(2,1)S(1)} %fusion), channel_id=1, source_target_pairs={{0,2},{1,3},{2,0},{3,1},{4,6},{5,7},{6,4},{7,5},{8,10},{9,11},{10,... | collective-permute-start | bytes 141320 | tf_op jit(solution)/shard_map/ppermute | solution.py:364
  41.7 5.0 %collective-permute-start.19 = (bf16[8,2944]{1,0:T(8,128)(2,1)S(1)}, bf16[8,2944]{1,0:T(8,128)(2,1)S(1)}, u32[]{:S(2)}, u32[]{:S(2)}) collective-permute-start(bf16[8,2944]{1,0:T(8,128)(2,1)S(1)} %get-tuple-element.35), channel_id=1, source_target_pairs={{0,8},{1,9},{2,10},{3,11},{4,12},{5,13},{6,14},{7,15},{8,0},{9,1},... | collective-permute-start | bytes 141320 | tf_op jit(solution)/shard_map/ppermute | solution.py:364
  46.8 1.4 %collective-permute-start.20 = (f32[8,2944]{1,0:T(8,128)S(1)}, f32[8,2944]{1,0:T(8,128)S(1)}, u32[]{:S(2)}, u32[]{:S(2)}) collective-permute-start(f32[8,2944]{1,0:T(8,128)S(1)} %convert_add_fusion.kept), channel_id=1, source_target_pairs={{0,1},{1,0},{2,3},{3,2},{4,5},{5,4},{6,7},{7,6},{8,9},{9,8},{10,11... | collective-permute-start | bytes 282632 | tf_op jit(solution)/shard_map/ppermute | solution.py:364

commit v13 on v10

--- a/solution.py
+++ b/solution.py
@@ -12,6 +12,7 @@
 LANES = 128
 CUTS = 42
 TOGETHER = 2
+FLOPS_HINT = 4_000_000_000
 NT = (((1,), (1,)), ((), ()))
 VMEM = pl.BlockSpec(memory_space=pltpu.VMEM)
 HBM = pl.BlockSpec(memory_space=pl.ANY)
@@ -119,7 +120,7 @@
     return pairs
 
 
-def gather_blocks(block, loop, tied_head, mapper):
+def gather_blocks(block, loop, mapper):
     chips = loop // 2
     order = ring_of(chips)
     half = chips // 2
@@ -136,9 +137,6 @@
         crossed = send(crossed, hop_pairs(order, step))
         if step < half:
             plain = send(plain, hop_pairs(order, step))
-        if step <= 2:
-            head = load(tied_head, step - 1, min(2, half), head if step > 1 else None)
-            crossed, head = tie(crossed, head)
         if mapper is not None and step == 3:
             mapped = mapper(None, {i: blocks[i] for i in ready[:6]})
             plain, mapped = tie(plain, mapped)
@@ -159,7 +157,7 @@
             ready += [mine + far, theirs + far]
             if mapper is not None:
                 mapped = mapper(mapped, {i: blocks[i] for i in ready[12:15]})
-    return blocks, head, mapped, ready[15:] if mapper is not None else ready
+    return blocks, mapped, ready[15:] if mapper is not None else ready
 
 
 def map_rows(blocks, places, gain, bias, mapped):
@@ -203,38 +201,7 @@
         input_output_aliases={} if mapped is None else {len(operands) - 1: 0},
         compiler_params=pltpu.CompilerParams(vmem_limit_bytes=8 << 20),
         cost_estimate=pl.CostEstimate(
-            flops=20 * count * width, bytes_accessed=4 * count * width, transcendentals=0
-        ),
-    )(*operands)
-
-
-def load_kernel(part, parts, head_hbm, *refs):
-    head, sems = refs[-2:]
-    count = sems.shape[0]
-    size = head.shape[0] // (parts * count)
-    copies = []
-    for k in range(count):
-        at = pl.ds((part * count + k) * size, size)
-        copies.append(pltpu.make_async_copy(head_hbm.at[at], head.at[at], sems.at[k]))
-    for copy in copies:
-        copy.start()
-    for copy in copies:
-        copy.wait()
-
-
-def load(tied_head, part, parts, loaded):
-    operands = [in_hbm(tied_head)] + ([] if loaded is None else [loaded])
-    voc, width = tied_head.shape
-    return pl.pallas_call(
-        functools.partial(load_kernel, part, parts),
-        out_shape=pltpu.VMEM(tied_head.shape, BF16),
-        in_specs=[HBM] + [VMEM] * (len(operands) - 1),
-        out_specs=VMEM,
-        input_output_aliases={} if loaded is None else {1: 0},
-        scratch_shapes=[pltpu.SemaphoreType.DMA((4,))],
-        compiler_params=pltpu.CompilerParams(vmem_limit_bytes=16 << 20),
-        cost_estimate=pl.CostEstimate(
-            flops=0, bytes_accessed=4 * voc * width // parts, transcendentals=0
+            flops=FLOPS_HINT if mapped is None else 0, bytes_accessed=4 * count * width, transcendentals=0
         ),
     )(*operands)
 
@@ -426,12 +393,12 @@
     rows = rows_dev * loop
     early = rows_dev % 16 == 0 and loop == 16
     mapper = functools.partial(map_early, rows, gain, bias) if early else None
-    blocks, head, mapped, late = gather_blocks(block, loop, tied_head, mapper)
+    blocks, mapped, late = gather_blocks(block, loop, mapper)
     if rows_dev % 16:
         whole = jnp.concatenate(blocks, axis=0)
         blocks = [whole[i : i + 16] for i in range(0, rows, 16)]
         late = range(len(blocks))
-    keep, give = main(blocks, head, gain, bias, mapped, late, loop)
+    keep, give = main(blocks, tied_head, gain, bias, mapped, late, loop)
     return last(*sum_over_loop(keep, give, loop), levels, width, rows_dev)
 
 

time: 48.4 us -> 52.8 us (1.091)
  waiting for transfers between devices: 10.2 us -> 17.9 us
  Pallas kernels: 16.7 us -> 11.5 us
  starting transfers between devices: 20.5 us -> 22.4 us
    ppermute x15, waiting for transfers between devices: 2.95 us -> 10.8 us  [gather_blocks(): send = lambda x, pairs: lax.ppermute(x, 'loop', pairs)]
    pallas_call x2 -> x0, Pallas kernels: 5.23 us -> none  [load(): pl.pallas_call(functools.partial(load_kernel, part, parts), out_shape=plt...]
    ppermute x15, starting transfers between devices: 13.8 us -> 15 us  [gather_blocks(): send = lambda x, pairs: lax.ppermute(x, 'loop', pairs)]
    ppermute x6, starting transfers between devices: 6.66 us -> 7.4 us  [sum_over_loop(): lax.ppermute(x, 'loop', [(i, i ^ mask) for i in range(loop)])]
  transfers between devices with their start and end apart: 21 -> 21, of which waited for: 8 -> 10; matrix products, arithmetic and copies ran while one was open for 0% -> 0% of each run, Pallas kernels for 20% -> 8%
where the time goes in v13:
time: 52.8 us; the launch traced here: 52.7 us
  starting transfers between devices  22.4 us (42%)
  waiting for transfers between devices  17.9 us (34%)
  Pallas kernels  11.5 us (22%)
  between operations  0.74 us (1%)
    ppermute x15, starting transfers between devices, gather_blocks(): send = lambda x, pairs: lax.ppermute(x, 'loop', pairs)  15 us
    ppermute x15, waiting for transfers between devices, gather_blocks(): send = lambda x, pairs: lax.ppermute(x, 'loop', pairs)  10.8 us
    ppermute x6, starting transfers between devices, sum_over_loop(): lax.ppermute(x, 'loop', [(i, i ^ mask) for i in range(loop)])  7.4 us
    ppermute x6, waiting for transfers between devices, sum_over_loop(): lax.ppermute(x, 'loop', [(i, i ^ mask) for i in range(loop)])  7.04 us
    pallas_call x1, Pallas kernels, main(): pl.pallas_call(functools.partial(front_kernel, levels, len(blocks), late)...  5.33 us
    pallas_call x1, Pallas kernels, main(): pl.pallas_call(functools.partial(back_kernel, loop, len(blocks)), out_sha...  2.23 us
    pallas_call x3, Pallas kernels, map_early(): pl.pallas_call(functools.partial(map_kernel, places), out_shape=pltpu.VME...  2.14 us
    pallas_call x1, Pallas kernels, prep(): pl.pallas_call(prep_kernel, out_shape=(pltpu.VMEM((rows, width + LANES),...  1.12 us
  transfers between devices with their start and end apart: 21, of which 10 were waited for; matrix products, arithmetic and copies ran while one was open for 0% of the time, Pallas kernels for 8%

profile of v13, /device:TPU:0, one launch (start us, length us, event | category | flops | bytes accessed | tf_op | source)
XLA Modules:
  0.0 52.7 jit_solution(2766615423512405384)
XLA Ops:
  0.6 1.1 %shard_map.94 = (bf16[16,5504]{1,0:T(8,128)(2,1)S(1)}, f32[4,5376]{1,0:T(4,128)S(1)}, f32[4,5376]{1,0:T(4,128)S(1)}) custom-call(bf16[16,5376]{1,0:T(8,128)(2,1)} %hidden.1, s32[1,16]{1,0:T(1,128)} %bitcast.6, s32[1,16]{1,0:T(1,128)} %bitcast.7, f32[1,16]{1,0:T(1,128)} %bitcast.8, f32[4,5376]{1,0:T(4,128)} %depth_gain.1, f32[4,5376]{1,0:T(4,128)} %depth_bias.1), custom_call_target="tpu_custom_call" | custom-call | tf_op jit(solution)/shard_map/pallas_call | solution.py:88
  1.8 2.5 %collective-permute-start.5 = (bf16[16,5504]{1,0:T(8,128)(2,1)S(1)}, bf16[16,5504]{1,0:T(8,128)(2,1)S(1)}, u32[]{:S(2)}, u32[]{:S(2)}) collective-permute-start(bf16[16,5504]{1,0:T(8,128)(2,1)S(1)} %get-tuple-element.17.refs_0_), channel_id=1, source_target_pairs={{0,5},{5,0},{4,9},{9,4},{8,13},{13,8},{12,15},{15,12},{14,11},{11,... | collective-permute-start | bytes 528392 | tf_op jit(solution)/shard_map/ppermute | solution.py:128
  4.3 0.6 %collective-permute-start = (bf16[16,5504]{1,0:T(8,128)(2,1)S(1)}, bf16[16,5504]{1,0:T(8,128)(2,1)S(1)}, u32[]{:S(2)}, u32[]{:S(2)}) collective-permute-start(bf16[16,5504]{1,0:T(8,128)(2,1)S(1)} %get-tuple-element.17.refs_0_), channel_id=1, source_target_pairs={{0,1},{1,0},{2,3},{3,2},{4,5},{5,4},{6,7},{7,6},{8,9},{9,8},{10,11... | collective-permute-start | bytes 528392 | tf_op jit(solution)/shard_map/ppermute | solution.py:128
  4.9 2.5 %collective-permute-done.5.refs_2_.refs_9_ = bf16[16,5504]{1,0:T(8,128)(2,1)S(1)} collective-permute-done((bf16[16,5504]{1,0:T(8,128)(2,1)S(1)}, bf16[16,5504]{1,0:T(8,128)(2,1)S(1)}, u32[]{:S(2)}, u32[]{:S(2)}) %collective-permute-start.5) | collective-permute-done | bytes 176160 | tf_op jit(solution)/shard_map/ppermute | solution.py:128
  7.4 2.0 %collective-permute-start.8 = (bf16[16,5504]{1,0:T(8,128)(2,1)S(1)}, bf16[16,5504]{1,0:T(8,128)(2,1)S(1)}, u32[]{:S(2)}, u32[]{:S(2)}) collective-permute-start(bf16[16,5504]{1,0:T(8,128)(2,1)S(1)} %collective-permute-done.5.refs_2_.refs_9_), channel_id=1, source_target_pairs={{1,4},{4,1},{5,8},{8,5},{9,12},{12,9},{13,14},{14,13},{15,10},{10,... | collective-permute-start | bytes 528392 | tf_op jit(solution)/shard_map/ppermute | solution.py:128
  9.4 0.0 collective-permute-done.refs_1_.refs_8_
  9.4 1.6 %collective-permute-start.1 = (bf16[16,5504]{1,0:T(8,128)(2,1)S(1)}, bf16[16,5504]{1,0:T(8,128)(2,1)S(1)}, u32[]{:S(2)}, u32[]{:S(2)}) collective-permute-start(bf16[16,5504]{1,0:T(8,128)(2,1)S(1)} %collective-permute-done.refs_1_.refs_8_), channel_id=1, source_target_pairs={{0,5},{5,0},{4,9},{9,4},{8,13},{13,8},{12,15},{15,12},{14,11},{11,... | collective-permute-start | bytes 528392 | tf_op jit(solution)/shard_map/ppermute | solution.py:128
  11.0 2.2 %collective-permute-done.8.refs_0_.refs_6_ = bf16[16,5504]{1,0:T(8,128)(2,1)S(1)} collective-permute-done((bf16[16,5504]{1,0:T(8,128)(2,1)S(1)}, bf16[16,5504]{1,0:T(8,128)(2,1)S(1)}, u32[]{:S(2)}, u32[]{:S(2)}) %collective-permute-start.8) | collective-permute-done | bytes 176160 | tf_op jit(solution)/shard_map/ppermute | solution.py:128
  13.2 2.4 %collective-permute-start.9 = (bf16[16,5504]{1,0:T(8,128)(2,1)S(1)}, bf16[16,5504]{1,0:T(8,128)(2,1)S(1)}, u32[]{:S(2)}, u32[]{:S(2)}) collective-permute-start(bf16[16,5504]{1,0:T(8,128)(2,1)S(1)} %collective-permute-done.8.refs_0_.refs_6_), channel_id=1, source_target_pairs={{0,5},{5,0},{4,9},{9,4},{8,13},{13,8},{12,15},{15,12},{14,11},{11,... | collective-permute-start | bytes 528392 | tf_op jit(solution)/shard_map/ppermute | solution.py:128
  15.7 0.0 collective-permute-start.6
  15.7 0.0 collective-permute-done.1.refs_3_.refs_1_
  15.7 0.6 %collective-permute-start.2 = (bf16[16,5504]{1,0:T(8,128)(2,1)S(1)}, bf16[16,5504]{1,0:T(8,128)(2,1)S(1)}, u32[]{:S(2)}, u32[]{:S(2)}) collective-permute-start(bf16[16,5504]{1,0:T(8,128)(2,1)S(1)} %collective-permute-done.1.refs_3_.refs_1_), channel_id=1, source_target_pairs={{1,4},{4,1},{5,8},{8,5},{9,12},{12,9},{13,14},{14,13},{15,10},{10,... | collective-permute-start | bytes 528392 | tf_op jit(solution)/shard_map/ppermute | solution.py:128
  16.2 1.2 %collective-permute-start.7 = (bf16[16,5504]{1,0:T(8,128)(2,1)S(1)}, bf16[16,5504]{1,0:T(8,128)(2,1)S(1)}, u32[]{:S(2)}, u32[]{:S(2)}) collective-permute-start(bf16[16,5504]{1,0:T(8,128)(2,1)S(1)} %collective-permute-done.1.refs_3_.refs_1_), channel_id=1, source_target_pairs={{0,1},{1,0},{2,3},{3,2},{4,5},{5,4},{6,7},{7,6},{8,9},{9,8},{10,11... | collective-permute-start | bytes 528392 | tf_op jit(solution)/shard_map/ppermute | solution.py:128
  17.5 0.0 collective-permute-start.11
  17.5 2.0 %collective-permute-done.9.refs_4_.refs_11_ = bf16[16,5504]{1,0:T(8,128)(2,1)S(1)} collective-permute-done((bf16[16,5504]{1,0:T(8,128)(2,1)S(1)}, bf16[16,5504]{1,0:T(8,128)(2,1)S(1)}, u32[]{:S(2)}, u32[]{:S(2)}) %collective-permute-start.9) | collective-permute-done | bytes 176160 | tf_op jit(solution)/shard_map/ppermute | solution.py:128
  19.4 0.1 collective-permute-start.12
  19.5 0.0 collective-permute-done.6.refs_4_.refs_7_
  19.5 2.1 %collective-permute-start.10 = (bf16[16,5504]{1,0:T(8,128)(2,1)S(1)}, bf16[16,5504]{1,0:T(8,128)(2,1)S(1)}, u32[]{:S(2)}, u32[]{:S(2)}) collective-permute-start(bf16[16,5504]{1,0:T(8,128)(2,1)S(1)} %collective-permute-done.9.refs_4_.refs_11_), channel_id=1, source_target_pairs={{1,4},{4,1},{5,8},{8,5},{9,12},{12,9},{13,14},{14,13},{15,10},{10,... | collective-permute-start | bytes 528392 | tf_op jit(solution)/shard_map/ppermute | solution.py:128
  21.6 0.0 collective-permute-done.2.refs_1_.refs_14_
  21.6 1.3 %collective-permute-start.4 = (bf16[16,5504]{1,0:T(8,128)(2,1)S(1)}, bf16[16,5504]{1,0:T(8,128)(2,1)S(1)}, u32[]{:S(2)}, u32[]{:S(2)}) collective-permute-start(bf16[16,5504]{1,0:T(8,128)(2,1)S(1)} %collective-permute-done.2.refs_1_.refs_14_), channel_id=1, source_target_pairs={{0,5},{5,0},{4,9},{9,4},{8,13},{13,8},{12,15},{15,12},{14,11},{11,... | collective-permute-start | bytes 528392 | tf_op jit(solution)/shard_map/ppermute | solution.py:128
  22.9 0.0 collective-permute-done.7.refs_5_.refs_15_
  22.9 0.0 slice-start.1
  23.0 0.8 %shard_map.95.refs_8_ = bf16[256,5376]{1,0:T(8,128)(2,1)S(1)} custom-call(bf16[16,5504]{1,0:T(8,128)(2,1)S(1)} %get-tuple-element.17.refs_0_, bf16[16,5504]{1,0:T(8,128)(2,1)S(1)} %collective-permute-done.refs_1_.refs_8_, bf16[16,5504]{1,0:T(8,128)(2,1)S(1)} %collective-permute-done.5.refs_2_.refs_9_, ...), custom_call_target="tpu_custom_call" | custom-call | flops 4000000000 | bytes 2064384 | tf_op jit(solution)/shard_map/pallas_call | solution.py:196
  23.8 0.0 slice-start.2
  23.8 3.5 %collective-permute-done.4.refs_5_.refs_3_ = bf16[16,5504]{1,0:T(8,128)(2,1)S(1)} collective-permute-done((bf16[16,5504]{1,0:T(8,128)(2,1)S(1)}, bf16[16,5504]{1,0:T(8,128)(2,1)S(1)}, u32[]{:S(2)}, u32[]{:S(2)}) %collective-permute-start.4) | collective-permute-done | bytes 176160 | tf_op jit(solution)/shard_map/ppermute | solution.py:128
  27.4 0.0 collective-permute-start.14
  27.4 0.0 collective-permute-done.11.refs_2_.refs_10_
  27.4 0.8 %shard_map.96.refs_5_ = bf16[256,5376]{1,0:T(8,128)(2,1)S(1)} custom-call(bf16[16,5504]{1,0:T(8,128)(2,1)S(1)} %collective-permute-done.8.refs_0_.refs_6_, bf16[16,5504]{1,0:T(8,128)(2,1)S(1)} %collective-permute-done.2.refs_1_.refs_14_, bf16[16,5504]{1,0:T(8,128)(2,1)S(1)} %collective-permute-done.11.refs_2_.refs_10_, ...), custom_call_target="tpu_custom_call", output_to_operand_aliasing={{}: (8, {})} | custom-call | bytes 2064384 | tf_op jit(solution)/shard_map/pallas_call | solution.py:196
  28.2 0.0 collective-permute-done.10.refs_2_.refs_4_
  28.2 0.6 %collective-permute-start.13 = (bf16[16,5504]{1,0:T(8,128)(2,1)S(1)}, bf16[16,5504]{1,0:T(8,128)(2,1)S(1)}, u32[]{:S(2)}, u32[]{:S(2)}) collective-permute-start(bf16[16,5504]{1,0:T(8,128)(2,1)S(1)} %collective-permute-done.10.refs_2_.refs_4_), channel_id=1, source_target_pairs={{0,1},{1,0},{2,3},{3,2},{4,5},{5,4},{6,7},{7,6},{8,9},{9,8},{10,11... | collective-permute-start | bytes 528392 | tf_op jit(solution)/shard_map/ppermute | solution.py:128
  28.8 0.0 collective-permute-done.12.refs_0_.refs_5_
  28.8 0.0 collective-permute-done.14.refs_1_.refs_13_
  28.8 0.5 shard_map.97.refs_19_
  29.3 0.6 %collective-permute-done.13.refs_12_ = bf16[16,5504]{1,0:T(8,128)(2,1)S(1)} collective-permute-done((bf16[16,5504]{1,0:T(8,128)(2,1)S(1)}, bf16[16,5504]{1,0:T(8,128)(2,1)S(1)}, u32[]{:S(2)}, u32[]{:S(2)}) %collective-permute-start.13) | collective-permute-done | bytes 176160 | tf_op jit(solution)/shard_map/ppermute | solution.py:128
  29.8 5.3 %shard_map.98 = (f32[8,2944]{1,0:T(8,128)S(1)}, bf16[272,1024]{1,0:T(8,128)(2,1)S(1)}, bf16[16,256]{1,0:T(8,128)(2,1)S(1)}, f32[256,128]{1,0:T(8,128)S(1)}, bf16[256,5376]{1,0:T(8,128)(2,1)S(1)}) custom-call(bf16[16,5504]{1,0:T(8,128)(2,1)S(1)} %get-tuple-element.17.refs_0_, ...), custom_call_target="tpu_custom_call", output_to_operand_aliasing={{4}: (19, {})} | custom-call | flops 4227858432 | bytes 5505024 | tf_op jit(solution)/shard_map/pallas_call | solution.py:302
  35.2 0.4 collective-permute-start.15
  35.6 2.2 %shard_map.99 = f32[8,2944]{1,0:T(8,128)S(1)} custom-call(bf16[16,5504]{1,0:T(8,128)(2,1)S(1)} %get-tuple-element.17.refs_0_, bf16[16,5504]{1,0:T(8,128)(2,1)S(1)} %collective-permute-done.1.refs_3_.refs_1_, bf16[16,5504]{1,0:T(8,128)(2,1)S(1)} %collective-permute-done.3.refs_3_.refs_2_, bf16[16,5504]{1,0:T(8,128)(2,1)S(1)} %collective-permute-done.4.refs_5_.refs_3_, ...), custom_call_target="tpu_custom_call" | custom-call | flops 1409286144 | bytes 5505024 | tf_op jit(solution)/shard_map/pallas_call | solution.py:318
  37.8 2.8 %collective-permute-start.18 = (bf16[8,2944]{1,0:T(8,128)(2,1)S(1)}, bf16[8,2944]{1,0:T(8,128)(2,1)S(1)}, u32[]{:S(2)}, u32[]{:S(2)}) collective-permute-start(bf16[8,2944]{1,0:T(8,128)(2,1)S(1)} %fusion), channel_id=1, source_target_pairs={{0,6},{1,7},{2,4},{3,5},{4,2},{5,3},{6,0},{7,1},{8,14},{9,15},{10,... | collective-permute-start | bytes 141320 | tf_op jit(solution)/shard_map/ppermute | solution.py:331
  40.6 0.3 collective-permute-start.17
  41.0 0.4 collective-permute-start.16
  41.4 1.5 %collective-permute-done.18 = bf16[8,2944]{1,0:T(8,128)(2,1)S(1)} collective-permute-done((bf16[8,2944]{1,0:T(8,128)(2,1)S(1)}, bf16[8,2944]{1,0:T(8,128)(2,1)S(1)}, u32[]{:S(2)}, u32[]{:S(2)}) %collective-permute-start.18) | collective-permute-done | bytes 47136 | tf_op jit(solution)/shard_map/ppermute | solution.py:331
  42.9 1.8 %collective-permute-done.17 = bf16[8,2944]{1,0:T(8,128)(2,1)S(1)} collective-permute-done((bf16[8,2944]{1,0:T(8,128)(2,1)S(1)}, bf16[8,2944]{1,0:T(8,128)(2,1)S(1)}, u32[]{:S(2)}, u32[]{:S(2)}) %collective-permute-start.17) | collective-permute-done | bytes 47136 | tf_op jit(solution)/shard_map/ppermute | solution.py:331
  44.7 0.3 collective-permute-done.16
  45.1 3.4 %collective-permute-start.19 = (bf16[8,2944]{1,0:T(8,128)(2,1)S(1)}, bf16[8,2944]{1,0:T(8,128)(2,1)S(1)}, u32[]{:S(2)}, u32[]{:S(2)}) collective-permute-start(bf16[8,2944]{1,0:T(8,128)(2,1)S(1)} %get-tuple-element.31), channel_id=1, source_target_pairs={{0,8},{1,9},{2,10},{3,11},{4,12},{5,13},{6,14},{7,15},{8,0},{9,1},... | collective-permute-start | bytes 141320 | tf_op jit(solution)/shard_map/ppermute | solution.py:331
  48.5 2.1 %collective-permute-done.19 = bf16[8,2944]{1,0:T(8,128)(2,1)S(1)} collective-permute-done((bf16[8,2944]{1,0:T(8,128)(2,1)S(1)}, bf16[8,2944]{1,0:T(8,128)(2,1)S(1)}, u32[]{:S(2)}, u32[]{:S(2)}) %collective-permute-start.19) | collective-permute-done | bytes 47136 | tf_op jit(solution)/shard_map/ppermute | solution.py:331
  50.6 0.1 collective-permute-start.20
  50.7 1.3 %collective-permute-done.20.given = f32[8,2944]{1,0:T(8,128)S(1)} collective-permute-done((f32[8,2944]{1,0:T(8,128)S(1)}, f32[8,2944]{1,0:T(8,128)S(1)}, u32[]{:S(2)}, u32[]{:S(2)}) %collective-permute-start.20) | collective-permute-done | bytes 94240 | tf_op jit(solution)/shard_map/ppermute | solution.py:331
  51.9 0.7 %shard_map.100 = (f32[1,16]{1,0:T(1,128)}, f32[4,5376]{1,0:T(4,128)}, f32[4,5376]{1,0:T(4,128)}) custom-call(f32[8,2944]{1,0:T(8,128)S(1)} %convert_add_fusion.kept, f32[8,2944]{1,0:T(8,128)S(1)} %collective-permute-done.20.given), custom_call_target="tpu_custom_call" | custom-call | tf_op jit(solution)/shard_map/pallas_call | solution.py:374
  (11 shorter events, 0.1 us)
Async XLA Ops:
  1.8 5.7 %collective-permute-start.5 = (bf16[16,5504]{1,0:T(8,128)(2,1)S(1)}, bf16[16,5504]{1,0:T(8,128)(2,1)S(1)}, u32[]{:S(2)}, u32[]{:S(2)}) collective-permute-start(bf16[16,5504]{1,0:T(8,128)(2,1)S(1)} %get-tuple-element.17.refs_0_), channel_id=1, source_target_pairs={{0,5},{5,0},{4,9},{9,4},{8,13},{13,8},{12,15},{15,12},{14,11},{11,... | collective-permute-start | bytes 528392 | tf_op jit(solution)/shard_map/ppermute | solution.py:128
  4.3 5.1 %collective-permute-start = (bf16[16,5504]{1,0:T(8,128)(2,1)S(1)}, bf16[16,5504]{1,0:T(8,128)(2,1)S(1)}, u32[]{:S(2)}, u32[]{:S(2)}) collective-permute-start(bf16[16,5504]{1,0:T(8,128)(2,1)S(1)} %get-tuple-element.17.refs_0_), channel_id=1, source_target_pairs={{0,1},{1,0},{2,3},{3,2},{4,5},{5,4},{6,7},{7,6},{8,9},{9,8},{10,11... | collective-permute-start | bytes 528392 | tf_op jit(solution)/shard_map/ppermute | solution.py:128
  7.4 5.8 %collective-permute-start.8 = (bf16[16,5504]{1,0:T(8,128)(2,1)S(1)}, bf16[16,5504]{1,0:T(8,128)(2,1)S(1)}, u32[]{:S(2)}, u32[]{:S(2)}) collective-permute-start(bf16[16,5504]{1,0:T(8,128)(2,1)S(1)} %collective-permute-done.5.refs_2_.refs_9_), channel_id=1, source_target_pairs={{1,4},{4,1},{5,8},{8,5},{9,12},{12,9},{13,14},{14,13},{15,10},{10,... | collective-permute-start | bytes 528392 | tf_op jit(solution)/shard_map/ppermute | solution.py:128
  9.4 6.3 %collective-permute-start.1 = (bf16[16,5504]{1,0:T(8,128)(2,1)S(1)}, bf16[16,5504]{1,0:T(8,128)(2,1)S(1)}, u32[]{:S(2)}, u32[]{:S(2)}) collective-permute-start(bf16[16,5504]{1,0:T(8,128)(2,1)S(1)} %collective-permute-done.refs_1_.refs_8_), channel_id=1, source_target_pairs={{0,5},{5,0},{4,9},{9,4},{8,13},{13,8},{12,15},{15,12},{14,11},{11,... | collective-permute-start | bytes 528392 | tf_op jit(solution)/shard_map/ppermute | solution.py:128
  13.2 6.2 %collective-permute-start.9 = (bf16[16,5504]{1,0:T(8,128)(2,1)S(1)}, bf16[16,5504]{1,0:T(8,128)(2,1)S(1)}, u32[]{:S(2)}, u32[]{:S(2)}) collective-permute-start(bf16[16,5504]{1,0:T(8,128)(2,1)S(1)} %collective-permute-done.8.refs_0_.refs_6_), channel_id=1, source_target_pairs={{0,5},{5,0},{4,9},{9,4},{8,13},{13,8},{12,15},{15,12},{14,11},{11,... | collective-permute-start | bytes 528392 | tf_op jit(solution)/shard_map/ppermute | solution.py:128
  15.7 3.8 %collective-permute-start.6 = (bf16[16,5504]{1,0:T(8,128)(2,1)S(1)}, bf16[16,5504]{1,0:T(8,128)(2,1)S(1)}, u32[]{:S(2)}, u32[]{:S(2)}) collective-permute-start(bf16[16,5504]{1,0:T(8,128)(2,1)S(1)} %collective-permute-done.5.refs_2_.refs_9_), channel_id=1, source_target_pairs={{0,1},{1,0},{2,3},{3,2},{4,5},{5,4},{6,7},{7,6},{8,9},{9,8},{10,11... | collective-permute-start | bytes 528392 | tf_op jit(solution)/shard_map/ppermute | solution.py:128
  15.7 5.9 %collective-permute-start.2 = (bf16[16,5504]{1,0:T(8,128)(2,1)S(1)}, bf16[16,5504]{1,0:T(8,128)(2,1)S(1)}, u32[]{:S(2)}, u32[]{:S(2)}) collective-permute-start(bf16[16,5504]{1,0:T(8,128)(2,1)S(1)} %collective-permute-done.1.refs_3_.refs_1_), channel_id=1, source_target_pairs={{1,4},{4,1},{5,8},{8,5},{9,12},{12,9},{13,14},{14,13},{15,10},{10,... | collective-permute-start | bytes 528392 | tf_op jit(solution)/shard_map/ppermute | solution.py:128
  16.2 6.7 %collective-permute-start.7 = (bf16[16,5504]{1,0:T(8,128)(2,1)S(1)}, bf16[16,5504]{1,0:T(8,128)(2,1)S(1)}, u32[]{:S(2)}, u32[]{:S(2)}) collective-permute-start(bf16[16,5504]{1,0:T(8,128)(2,1)S(1)} %collective-permute-done.1.refs_3_.refs_1_), channel_id=1, source_target_pairs={{0,1},{1,0},{2,3},{3,2},{4,5},{5,4},{6,7},{7,6},{8,9},{9,8},{10,11... | collective-permute-start | bytes 528392 | tf_op jit(solution)/shard_map/ppermute | solution.py:128
  17.5 9.9 %collective-permute-start.11 = (bf16[16,5504]{1,0:T(8,128)(2,1)S(1)}, bf16[16,5504]{1,0:T(8,128)(2,1)S(1)}, u32[]{:S(2)}, u32[]{:S(2)}) collective-permute-start(bf16[16,5504]{1,0:T(8,128)(2,1)S(1)} %collective-permute-done.8.refs_0_.refs_6_), channel_id=1, source_target_pairs={{0,1},{1,0},{2,3},{3,2},{4,5},{5,4},{6,7},{7,6},{8,9},{9,8},{10,11... | collective-permute-start | bytes 528392 | tf_op jit(solution)/shard_map/ppermute | solution.py:128
  19.4 9.4 %collective-permute-start.12 = (bf16[16,5504]{1,0:T(8,128)(2,1)S(1)}, bf16[16,5504]{1,0:T(8,128)(2,1)S(1)}, u32[]{:S(2)}, u32[]{:S(2)}) collective-permute-start(bf16[16,5504]{1,0:T(8,128)(2,1)S(1)} %collective-permute-done.9.refs_4_.refs_11_), channel_id=1, source_target_pairs={{0,1},{1,0},{2,3},{3,2},{4,5},{5,4},{6,7},{7,6},{8,9},{9,8},{10,11... | collective-permute-start | bytes 528392 | tf_op jit(solution)/shard_map/ppermute | solution.py:128
  19.5 8.7 %collective-permute-start.10 = (bf16[16,5504]{1,0:T(8,128)(2,1)S(1)}, bf16[16,5504]{1,0:T(8,128)(2,1)S(1)}, u32[]{:S(2)}, u32[]{:S(2)}) collective-permute-start(bf16[16,5504]{1,0:T(8,128)(2,1)S(1)} %collective-permute-done.9.refs_4_.refs_11_), channel_id=1, source_target_pairs={{1,4},{4,1},{5,8},{8,5},{9,12},{12,9},{13,14},{14,13},{15,10},{10,... | collective-permute-start | bytes 528392 | tf_op jit(solution)/shard_map/ppermute | solution.py:128
  21.6 5.7 %collective-permute-start.4 = (bf16[16,5504]{1,0:T(8,128)(2,1)S(1)}, bf16[16,5504]{1,0:T(8,128)(2,1)S(1)}, u32[]{:S(2)}, u32[]{:S(2)}) collective-permute-start(bf16[16,5504]{1,0:T(8,128)(2,1)S(1)} %collective-permute-done.2.refs_1_.refs_14_), channel_id=1, source_target_pairs={{0,5},{5,0},{4,9},{9,4},{8,13},{13,8},{12,15},{15,12},{14,11},{11,... | collective-permute-start | bytes 528392 | tf_op jit(solution)/shard_map/ppermute | solution.py:128
  22.9 4.4 %collective-permute-start.3 = (bf16[16,5504]{1,0:T(8,128)(2,1)S(1)}, bf16[16,5504]{1,0:T(8,128)(2,1)S(1)}, u32[]{:S(2)}, u32[]{:S(2)}) collective-permute-start(bf16[16,5504]{1,0:T(8,128)(2,1)S(1)} %collective-permute-done.2.refs_1_.refs_14_), channel_id=1, source_target_pairs={{0,1},{1,0},{2,3},{3,2},{4,5},{5,4},{6,7},{7,6},{8,9},{9,8},{10,11... | collective-permute-start | bytes 528392 | tf_op jit(solution)/shard_map/ppermute | solution.py:128
  22.9 6.9 %slice-start = ((s8[11010048]{0:T(1024)(128)(4,1)}), s8[4194304]{0:T(1024)(128)(4,1)S(1)}, s32[]{:S(2)}) async-start(s8[11010048]{0:T(1024)(128)(4,1)} %bitcast.4), calls=%async_computation | async-start | bytes 8388608
  22.9 6.9 %slice-start.1 = ((s8[11010048]{0:T(1024)(128)(4,1)}), s8[4194304]{0:T(1024)(128)(4,1)S(1)}, s32[]{:S(2)}) async-start(s8[11010048]{0:T(1024)(128)(4,1)} %bitcast.4), calls=%async_computation.1 | async-start | bytes 8388608
  23.8 6.0 %slice-start.2 = ((s8[11010048]{0:T(1024)(128)(4,1)}), s8[2621440]{0:T(1024)(128)(4,1)S(1)}, s32[]{:S(2)}) async-start(s8[11010048]{0:T(1024)(128)(4,1)} %bitcast.4), calls=%async_computation.2 | async-start | bytes 5242880
  27.4 1.4 %collective-permute-start.14 = (bf16[16,5504]{1,0:T(8,128)(2,1)S(1)}, bf16[16,5504]{1,0:T(8,128)(2,1)S(1)}, u32[]{:S(2)}, u32[]{:S(2)}) collective-permute-start(bf16[16,5504]{1,0:T(8,128)(2,1)S(1)} %collective-permute-done.4.refs_5_.refs_3_), channel_id=1, source_target_pairs={{0,1},{1,0},{2,3},{3,2},{4,5},{5,4},{6,7},{7,6},{8,9},{9,8},{10,11... | collective-permute-start | bytes 528392 | tf_op jit(solution)/shard_map/ppermute | solution.py:128
  28.2 1.6 %collective-permute-start.13 = (bf16[16,5504]{1,0:T(8,128)(2,1)S(1)}, bf16[16,5504]{1,0:T(8,128)(2,1)S(1)}, u32[]{:S(2)}, u32[]{:S(2)}) collective-permute-start(bf16[16,5504]{1,0:T(8,128)(2,1)S(1)} %collective-permute-done.10.refs_2_.refs_4_), channel_id=1, source_target_pairs={{0,1},{1,0},{2,3},{3,2},{4,5},{5,4},{6,7},{7,6},{8,9},{9,8},{10,11... | collective-permute-start | bytes 528392 | tf_op jit(solution)/shard_map/ppermute | solution.py:128
  35.2 2.6 %collective-permute-start.15 = (f32[8,2944]{1,0:T(8,128)S(1)}, f32[8,2944]{1,0:T(8,128)S(1)}, u32[]{:S(2)}, u32[]{:S(2)}) collective-permute-start(f32[8,2944]{1,0:T(8,128)S(1)} %get-tuple-element.27), channel_id=1, source_target_pairs={{0,1},{1,0},{2,3},{3,2},{4,5},{5,4},{6,7},{7,6},{8,9},{9,8},{10,11... | collective-permute-start | bytes 282632 | tf_op jit(solution)/shard_map/ppermute | solution.py:331
  37.8 5.0 %collective-permute-start.18 = (bf16[8,2944]{1,0:T(8,128)(2,1)S(1)}, bf16[8,2944]{1,0:T(8,128)(2,1)S(1)}, u32[]{:S(2)}, u32[]{:S(2)}) collective-permute-start(bf16[8,2944]{1,0:T(8,128)(2,1)S(1)} %fusion), channel_id=1, source_target_pairs={{0,6},{1,7},{2,4},{3,5},{4,2},{5,3},{6,0},{7,1},{8,14},{9,15},{10,... | collective-permute-start | bytes 141320 | tf_op jit(solution)/shard_map/ppermute | solution.py:331
  40.6 4.1 %collective-permute-start.17 = (bf16[8,2944]{1,0:T(8,128)(2,1)S(1)}, bf16[8,2944]{1,0:T(8,128)(2,1)S(1)}, u32[]{:S(2)}, u32[]{:S(2)}) collective-permute-start(bf16[8,2944]{1,0:T(8,128)(2,1)S(1)} %fusion), channel_id=1, source_target_pairs={{0,4},{1,5},{2,6},{3,7},{4,0},{5,1},{6,2},{7,3},{8,12},{9,13},{10,... | collective-permute-start | bytes 141320 | tf_op jit(solution)/shard_map/ppermute | solution.py:331
  41.0 4.1 %collective-permute-start.16 = (bf16[8,2944]{1,0:T(8,128)(2,1)S(1)}, bf16[8,2944]{1,0:T(8,128)(2,1)S(1)}, u32[]{:S(2)}, u32[]{:S(2)}) collective-permute-start(bf16[8,2944]{1,0:T(8,128)(2,1)S(1)} %fusion), channel_id=1, source_target_pairs={{0,2},{1,3},{2,0},{3,1},{4,6},{5,7},{6,4},{7,5},{8,10},{9,11},{10,... | collective-permute-start | bytes 141320 | tf_op jit(solution)/shard_map/ppermute | solution.py:331
  45.1 5.5 %collective-permute-start.19 = (bf16[8,2944]{1,0:T(8,128)(2,1)S(1)}, bf16[8,2944]{1,0:T(8,128)(2,1)S(1)}, u32[]{:S(2)}, u32[]{:S(2)}) collective-permute-start(bf16[8,2944]{1,0:T(8,128)(2,1)S(1)} %get-tuple-element.31), channel_id=1, source_target_pairs={{0,8},{1,9},{2,10},{3,11},{4,12},{5,13},{6,14},{7,15},{8,0},{9,1},... | collective-permute-start | bytes 141320 | tf_op jit(solution)/shard_map/ppermute | solution.py:331
  50.6 1.4 %collective-permute-start.20 = (f32[8,2944]{1,0:T(8,128)S(1)}, f32[8,2944]{1,0:T(8,128)S(1)}, u32[]{:S(2)}, u32[]{:S(2)}) collective-permute-start(f32[8,2944]{1,0:T(8,128)S(1)} %convert_add_fusion.kept), channel_id=1, source_target_pairs={{0,1},{1,0},{2,3},{3,2},{4,5},{5,4},{6,7},{7,6},{8,9},{9,8},{10,11... | collective-permute-start | bytes 282632 | tf_op jit(solution)/shard_map/ppermute | solution.py:331

commit v14 on v13

--- a/solution.py
+++ b/solution.py
@@ -110,13 +110,16 @@
     )
 
 
-def hop_pairs(order, step):
+def hop_pairs(order, step, cross):
     chips = len(order)
     first = 1 - step % 2
     pairs = []
     for i in range(chips):
         here, after = 2 * order[i], 2 * order[(i + 1) % chips]
-        pairs += [(here + first, after + 1 - first), (after + 1 - first, here + first)]
+        if cross:
+            pairs += [(here + first, after + 1 - first), (after + 1 - first, here + first)]
+        else:
+            pairs += [(here + 1 - first, after + 1 - first), (after + first, here + first)]
     return pairs
 
 
@@ -128,15 +131,16 @@
     send = lambda x, pairs: lax.ppermute(x, "loop", pairs)
     swap = lambda x: send(x, [(i, i ^ 1) for i in range(loop)])
     blocks = [None] * loop
-    first = swap(block)
-    blocks[0], blocks[chips] = block, first
-    crossed, plain = block, first
+    blocks[0], blocks[chips] = block, swap(block)
+    crossed = plain = block
     ready = [0, chips]
     mapped = None
     for step in range(1, half + 1):
-        crossed = send(crossed, hop_pairs(order, step))
+        crossed = send(crossed, hop_pairs(order, step, True))
         if step < half:
-            plain = send(plain, hop_pairs(order, step))
+            plain = send(plain, hop_pairs(order, step, step > 1))
+        if step == 1:
+            crossed, plain = tie(crossed, plain)
         if mapper is not None and step == 3:
             mapped = mapper(None, {i: blocks[i] for i in ready[:6]})
             plain, mapped = tie(plain, mapped)

time: 52.8 us -> 48.9 us (0.926)
  starting transfers between devices: 22.4 us -> 20 us
  waiting for transfers between devices: 17.9 us -> 16.4 us
    ppermute x15, starting transfers between devices: 15 us -> 13.4 us  [gather_blocks(): send = lambda x, pairs: lax.ppermute(x, 'loop', pairs)]
    ppermute x15, waiting for transfers between devices: 10.8 us -> 9.43 us  [gather_blocks(): send = lambda x, pairs: lax.ppermute(x, 'loop', pairs)]
    ppermute x6, starting transfers between devices: 7.4 us -> 6.6 us  [sum_over_loop(): lax.ppermute(x, 'loop', [(i, i ^ mask) for i in range(loop)])]
  transfers between devices with their start and end apart: 21 -> 21, of which waited for: 10 -> 11; matrix products, arithmetic and copies ran while one was open for 0% -> 0% of each run, Pallas kernels for 8% -> 9%
where the time goes in v14:
time: 48.9 us; the launch traced here: 48.8 us
  starting transfers between devices  20 us (41%)
  waiting for transfers between devices  16.4 us (34%)
  Pallas kernels  11.5 us (24%)
  between operations  0.73 us (1%)
    ppermute x15, starting transfers between devices, gather_blocks(): send = lambda x, pairs: lax.ppermute(x, 'loop', pairs)  13.4 us
    ppermute x15, waiting for transfers between devices, gather_blocks(): send = lambda x, pairs: lax.ppermute(x, 'loop', pairs)  9.43 us
    ppermute x6, waiting for transfers between devices, sum_over_loop(): lax.ppermute(x, 'loop', [(i, i ^ mask) for i in range(loop)])  6.98 us
    ppermute x6, starting transfers between devices, sum_over_loop(): lax.ppermute(x, 'loop', [(i, i ^ mask) for i in range(loop)])  6.6 us
    pallas_call x1, Pallas kernels, main(): pl.pallas_call(functools.partial(front_kernel, levels, len(blocks), late)...  5.33 us
    pallas_call x1, Pallas kernels, main(): pl.pallas_call(functools.partial(back_kernel, loop, len(blocks)), out_sha...  2.22 us
    pallas_call x3, Pallas kernels, map_early(): pl.pallas_call(functools.partial(map_kernel, places), out_shape=pltpu.VME...  2.12 us
    pallas_call x1, Pallas kernels, prep(): pl.pallas_call(prep_kernel, out_shape=(pltpu.VMEM((rows, width + LANES),...  1.12 us
  transfers between devices with their start and end apart: 21, of which 11 were waited for; matrix products, arithmetic and copies ran while one was open for 0% of the time, Pallas kernels for 9%

profile of v14, /device:TPU:0, one launch (start us, length us, event | category | flops | bytes accessed | tf_op | source)
XLA Modules:
  0.0 48.8 jit_solution(15896256374479915417)
XLA Ops:
  0.6 1.1 %shard_map.94 = (bf16[16,5504]{1,0:T(8,128)(2,1)S(1)}, f32[4,5376]{1,0:T(4,128)S(1)}, f32[4,5376]{1,0:T(4,128)S(1)}) custom-call(bf16[16,5376]{1,0:T(8,128)(2,1)} %hidden.1, s32[1,16]{1,0:T(1,128)} %bitcast.6, s32[1,16]{1,0:T(1,128)} %bitcast.7, f32[1,16]{1,0:T(1,128)} %bitcast.8, f32[4,5376]{1,0:T(4,128)} %depth_gain.1, f32[4,5376]{1,0:T(4,128)} %depth_bias.1), custom_call_target="tpu_custom_call" | custom-call | tf_op jit(solution)/shard_map/pallas_call | solution.py:88
  1.8 3.0 %collective-permute-start.1 = (bf16[16,5504]{1,0:T(8,128)(2,1)S(1)}, bf16[16,5504]{1,0:T(8,128)(2,1)S(1)}, u32[]{:S(2)}, u32[]{:S(2)}) collective-permute-start(bf16[16,5504]{1,0:T(8,128)(2,1)S(1)} %get-tuple-element.19.refs_0_), channel_id=1, source_target_pairs={{1,5},{4,0},{5,9},{8,4},{9,13},{12,8},{13,15},{14,12},{15,11},{10,... | collective-permute-start | bytes 528392 | tf_op jit(solution)/shard_map/ppermute | solution.py:131
  4.8 0.8 %collective-permute-start = (bf16[16,5504]{1,0:T(8,128)(2,1)S(1)}, bf16[16,5504]{1,0:T(8,128)(2,1)S(1)}, u32[]{:S(2)}, u32[]{:S(2)}) collective-permute-start(bf16[16,5504]{1,0:T(8,128)(2,1)S(1)} %get-tuple-element.19.refs_0_), channel_id=1, source_target_pairs={{0,5},{5,0},{4,9},{9,4},{8,13},{13,8},{12,15},{15,12},{14,11},{11,... | collective-permute-start | bytes 528392 | tf_op jit(solution)/shard_map/ppermute | solution.py:131
  5.6 3.1 %collective-permute-done.1.refs_3_.refs_1_ = bf16[16,5504]{1,0:T(8,128)(2,1)S(1)} collective-permute-done((bf16[16,5504]{1,0:T(8,128)(2,1)S(1)}, bf16[16,5504]{1,0:T(8,128)(2,1)S(1)}, u32[]{:S(2)}, u32[]{:S(2)}) %collective-permute-start.1) | collective-permute-done | bytes 176160 | tf_op jit(solution)/shard_map/ppermute | solution.py:131
  8.7 1.4 %collective-permute-done.refs_2_.refs_9_ = bf16[16,5504]{1,0:T(8,128)(2,1)S(1)} collective-permute-done((bf16[16,5504]{1,0:T(8,128)(2,1)S(1)}, bf16[16,5504]{1,0:T(8,128)(2,1)S(1)}, u32[]{:S(2)}, u32[]{:S(2)}) %collective-permute-start) | collective-permute-done | bytes 176160 | tf_op jit(solution)/shard_map/ppermute | solution.py:131
  10.2 0.9 %collective-permute-start.8 = (bf16[16,5504]{1,0:T(8,128)(2,1)S(1)}, bf16[16,5504]{1,0:T(8,128)(2,1)S(1)}, u32[]{:S(2)}, u32[]{:S(2)}) collective-permute-start(bf16[16,5504]{1,0:T(8,128)(2,1)S(1)} %collective-permute-done.refs_2_.refs_9_), channel_id=1, source_target_pairs={{1,4},{4,1},{5,8},{8,5},{9,12},{12,9},{13,14},{14,13},{15,10},{10,... | collective-permute-start | bytes 528392 | tf_op jit(solution)/shard_map/ppermute | solution.py:131
  11.1 0.8 %collective-permute-start.2 = (bf16[16,5504]{1,0:T(8,128)(2,1)S(1)}, bf16[16,5504]{1,0:T(8,128)(2,1)S(1)}, u32[]{:S(2)}, u32[]{:S(2)}) collective-permute-start(bf16[16,5504]{1,0:T(8,128)(2,1)S(1)} %collective-permute-done.1.refs_3_.refs_1_), channel_id=1, source_target_pairs={{1,4},{4,1},{5,8},{8,5},{9,12},{12,9},{13,14},{14,13},{15,10},{10,... | collective-permute-start | bytes 528392 | tf_op jit(solution)/shard_map/ppermute | solution.py:131
  11.9 0.4 collective-permute-start.5
  12.3 0.1 collective-permute-start.7
  12.4 2.6 %collective-permute-done.8.refs_0_.refs_6_ = bf16[16,5504]{1,0:T(8,128)(2,1)S(1)} collective-permute-done((bf16[16,5504]{1,0:T(8,128)(2,1)S(1)}, bf16[16,5504]{1,0:T(8,128)(2,1)S(1)}, u32[]{:S(2)}, u32[]{:S(2)}) %collective-permute-start.8) | collective-permute-done | bytes 176160 | tf_op jit(solution)/shard_map/ppermute | solution.py:131
  15.0 1.8 %collective-permute-start.9 = (bf16[16,5504]{1,0:T(8,128)(2,1)S(1)}, bf16[16,5504]{1,0:T(8,128)(2,1)S(1)}, u32[]{:S(2)}, u32[]{:S(2)}) collective-permute-start(bf16[16,5504]{1,0:T(8,128)(2,1)S(1)} %collective-permute-done.8.refs_0_.refs_6_), channel_id=1, source_target_pairs={{0,5},{5,0},{4,9},{9,4},{8,13},{13,8},{12,15},{15,12},{14,11},{11,... | collective-permute-start | bytes 528392 | tf_op jit(solution)/shard_map/ppermute | solution.py:131
  16.8 0.3 collective-permute-start.6
  17.1 0.0 collective-permute-done.2.refs_1_.refs_14_
  17.1 1.5 %collective-permute-start.4 = (bf16[16,5504]{1,0:T(8,128)(2,1)S(1)}, bf16[16,5504]{1,0:T(8,128)(2,1)S(1)}, u32[]{:S(2)}, u32[]{:S(2)}) collective-permute-start(bf16[16,5504]{1,0:T(8,128)(2,1)S(1)} %collective-permute-done.2.refs_1_.refs_14_), channel_id=1, source_target_pairs={{0,5},{5,0},{4,9},{9,4},{8,13},{13,8},{12,15},{15,12},{14,11},{11,... | collective-permute-start | bytes 528392 | tf_op jit(solution)/shard_map/ppermute | solution.py:131
  18.7 0.0 collective-permute-done.5.refs_1_.refs_8_
  18.7 0.3 collective-permute-start.3
  19.0 0.0 collective-permute-done.7.refs_5_.refs_15_
  19.0 0.2 collective-permute-start.11
  19.2 0.8 %collective-permute-done.9.refs_4_.refs_11_ = bf16[16,5504]{1,0:T(8,128)(2,1)S(1)} collective-permute-done((bf16[16,5504]{1,0:T(8,128)(2,1)S(1)}, bf16[16,5504]{1,0:T(8,128)(2,1)S(1)}, u32[]{:S(2)}, u32[]{:S(2)}) %collective-permute-start.9) | collective-permute-done | bytes 176160 | tf_op jit(solution)/shard_map/ppermute | solution.py:131
  20.0 1.7 %collective-permute-start.10 = (bf16[16,5504]{1,0:T(8,128)(2,1)S(1)}, bf16[16,5504]{1,0:T(8,128)(2,1)S(1)}, u32[]{:S(2)}, u32[]{:S(2)}) collective-permute-start(bf16[16,5504]{1,0:T(8,128)(2,1)S(1)} %collective-permute-done.9.refs_4_.refs_11_), channel_id=1, source_target_pairs={{1,4},{4,1},{5,8},{8,5},{9,12},{12,9},{13,14},{14,13},{15,10},{10,... | collective-permute-start | bytes 528392 | tf_op jit(solution)/shard_map/ppermute | solution.py:131
  21.7 0.8 %shard_map.95.refs_8_ = bf16[256,5376]{1,0:T(8,128)(2,1)S(1)} custom-call(bf16[16,5504]{1,0:T(8,128)(2,1)S(1)} %get-tuple-element.19.refs_0_, bf16[16,5504]{1,0:T(8,128)(2,1)S(1)} %collective-permute-done.5.refs_1_.refs_8_, bf16[16,5504]{1,0:T(8,128)(2,1)S(1)} %collective-permute-done.refs_2_.refs_9_, ...), custom_call_target="tpu_custom_call" | custom-call | flops 4000000000 | bytes 2064384 | tf_op jit(solution)/shard_map/pallas_call | solution.py:200
  22.6 0.0 slice-start.2
  22.6 0.0 collective-permute-done.4.refs_5_.refs_3_
  22.6 0.4 collective-permute-start.14
  23.0 0.2 collective-permute-start.12
  23.2 0.0 collective-permute-done.3.refs_3_.refs_2_
  23.2 0.0 collective-permute-done.11.refs_2_.refs_10_
  23.2 0.8 %shard_map.96.refs_5_ = bf16[256,5376]{1,0:T(8,128)(2,1)S(1)} custom-call(bf16[16,5504]{1,0:T(8,128)(2,1)S(1)} %collective-permute-done.8.refs_0_.refs_6_, bf16[16,5504]{1,0:T(8,128)(2,1)S(1)} %collective-permute-done.2.refs_1_.refs_14_, bf16[16,5504]{1,0:T(8,128)(2,1)S(1)} %collective-permute-done.11.refs_2_.refs_10_, ...), custom_call_target="tpu_custom_call", output_to_operand_aliasing={{}: (8, {})} | custom-call | bytes 2064384 | tf_op jit(solution)/shard_map/pallas_call | solution.py:200
  24.0 0.8 %collective-permute-done.10.refs_2_.refs_4_ = bf16[16,5504]{1,0:T(8,128)(2,1)S(1)} collective-permute-done((bf16[16,5504]{1,0:T(8,128)(2,1)S(1)}, bf16[16,5504]{1,0:T(8,128)(2,1)S(1)}, u32[]{:S(2)}, u32[]{:S(2)}) %collective-permute-start.10) | collective-permute-done | bytes 176160 | tf_op jit(solution)/shard_map/ppermute | solution.py:131
  24.9 0.9 %collective-permute-start.13 = (bf16[16,5504]{1,0:T(8,128)(2,1)S(1)}, bf16[16,5504]{1,0:T(8,128)(2,1)S(1)}, u32[]{:S(2)}, u32[]{:S(2)}) collective-permute-start(bf16[16,5504]{1,0:T(8,128)(2,1)S(1)} %collective-permute-done.10.refs_2_.refs_4_), channel_id=1, source_target_pairs={{0,1},{1,0},{2,3},{3,2},{4,5},{5,4},{6,7},{7,6},{8,9},{9,8},{10,11... | collective-permute-start | bytes 528392 | tf_op jit(solution)/shard_map/ppermute | solution.py:131
  25.8 0.0 collective-permute-done.14.refs_1_.refs_13_
  25.8 0.5 shard_map.97.refs_19_
  26.3 0.6 %collective-permute-done.13.refs_12_ = bf16[16,5504]{1,0:T(8,128)(2,1)S(1)} collective-permute-done((bf16[16,5504]{1,0:T(8,128)(2,1)S(1)}, bf16[16,5504]{1,0:T(8,128)(2,1)S(1)}, u32[]{:S(2)}, u32[]{:S(2)}) %collective-permute-start.13) | collective-permute-done | bytes 176160 | tf_op jit(solution)/shard_map/ppermute | solution.py:131
  26.8 5.3 %shard_map.98 = (f32[8,2944]{1,0:T(8,128)S(1)}, bf16[272,1024]{1,0:T(8,128)(2,1)S(1)}, bf16[16,256]{1,0:T(8,128)(2,1)S(1)}, f32[256,128]{1,0:T(8,128)S(1)}, bf16[256,5376]{1,0:T(8,128)(2,1)S(1)}) custom-call(bf16[16,5504]{1,0:T(8,128)(2,1)S(1)} %get-tuple-element.19.refs_0_, ...), custom_call_target="tpu_custom_call", output_to_operand_aliasing={{4}: (19, {})} | custom-call | flops 4227858432 | bytes 5505024 | tf_op jit(solution)/shard_map/pallas_call | solution.py:306
  32.2 0.4 collective-permute-start.15
  32.5 2.2 %shard_map.99 = f32[8,2944]{1,0:T(8,128)S(1)} custom-call(bf16[16,5504]{1,0:T(8,128)(2,1)S(1)} %get-tuple-element.19.refs_0_, bf16[16,5504]{1,0:T(8,128)(2,1)S(1)} %collective-permute-done.1.refs_3_.refs_1_, bf16[16,5504]{1,0:T(8,128)(2,1)S(1)} %collective-permute-done.3.refs_3_.refs_2_, bf16[16,5504]{1,0:T(8,128)(2,1)S(1)} %collective-permute-done.4.refs_5_.refs_3_, ...), custom_call_target="tpu_custom_call" | custom-call | flops 1409286144 | bytes 5505024 | tf_op jit(solution)/shard_map/pallas_call | solution.py:322
  34.8 0.0 collective-permute-done.15
  34.8 2.3 %collective-permute-start.18 = (bf16[8,2944]{1,0:T(8,128)(2,1)S(1)}, bf16[8,2944]{1,0:T(8,128)(2,1)S(1)}, u32[]{:S(2)}, u32[]{:S(2)}) collective-permute-start(bf16[8,2944]{1,0:T(8,128)(2,1)S(1)} %fusion), channel_id=1, source_target_pairs={{0,6},{1,7},{2,4},{3,5},{4,2},{5,3},{6,0},{7,1},{8,14},{9,15},{10,... | collective-permute-start | bytes 141320 | tf_op jit(solution)/shard_map/ppermute | solution.py:335
  37.1 0.4 collective-permute-start.17
  37.5 0.8 %collective-permute-start.16 = (bf16[8,2944]{1,0:T(8,128)(2,1)S(1)}, bf16[8,2944]{1,0:T(8,128)(2,1)S(1)}, u32[]{:S(2)}, u32[]{:S(2)}) collective-permute-start(bf16[8,2944]{1,0:T(8,128)(2,1)S(1)} %fusion), channel_id=1, source_target_pairs={{0,2},{1,3},{2,0},{3,1},{4,6},{5,7},{6,4},{7,5},{8,10},{9,11},{10,... | collective-permute-start | bytes 141320 | tf_op jit(solution)/shard_map/ppermute | solution.py:335
  38.3 1.6 %collective-permute-done.18 = bf16[8,2944]{1,0:T(8,128)(2,1)S(1)} collective-permute-done((bf16[8,2944]{1,0:T(8,128)(2,1)S(1)}, bf16[8,2944]{1,0:T(8,128)(2,1)S(1)}, u32[]{:S(2)}, u32[]{:S(2)}) %collective-permute-start.18) | collective-permute-done | bytes 47136 | tf_op jit(solution)/shard_map/ppermute | solution.py:335
  40.0 1.2 %collective-permute-done.17 = bf16[8,2944]{1,0:T(8,128)(2,1)S(1)} collective-permute-done((bf16[8,2944]{1,0:T(8,128)(2,1)S(1)}, bf16[8,2944]{1,0:T(8,128)(2,1)S(1)}, u32[]{:S(2)}, u32[]{:S(2)}) %collective-permute-start.17) | collective-permute-done | bytes 47136 | tf_op jit(solution)/shard_map/ppermute | solution.py:335
  41.2 0.4 collective-permute-done.16
  41.6 2.6 %collective-permute-start.19 = (bf16[8,2944]{1,0:T(8,128)(2,1)S(1)}, bf16[8,2944]{1,0:T(8,128)(2,1)S(1)}, u32[]{:S(2)}, u32[]{:S(2)}) collective-permute-start(bf16[8,2944]{1,0:T(8,128)(2,1)S(1)} %get-tuple-element.35), channel_id=1, source_target_pairs={{0,8},{1,9},{2,10},{3,11},{4,12},{5,13},{6,14},{7,15},{8,0},{9,1},... | collective-permute-start | bytes 141320 | tf_op jit(solution)/shard_map/ppermute | solution.py:335
  44.2 2.4 %collective-permute-done.19 = bf16[8,2944]{1,0:T(8,128)(2,1)S(1)} collective-permute-done((bf16[8,2944]{1,0:T(8,128)(2,1)S(1)}, bf16[8,2944]{1,0:T(8,128)(2,1)S(1)}, u32[]{:S(2)}, u32[]{:S(2)}) %collective-permute-start.19) | collective-permute-done | bytes 47136 | tf_op jit(solution)/shard_map/ppermute | solution.py:335
  46.7 0.1 collective-permute-start.20
  46.8 1.3 %collective-permute-done.20.given = f32[8,2944]{1,0:T(8,128)S(1)} collective-permute-done((f32[8,2944]{1,0:T(8,128)S(1)}, f32[8,2944]{1,0:T(8,128)S(1)}, u32[]{:S(2)}, u32[]{:S(2)}) %collective-permute-start.20) | collective-permute-done | bytes 94240 | tf_op jit(solution)/shard_map/ppermute | solution.py:335
  48.1 0.7 %shard_map.100 = (f32[1,16]{1,0:T(1,128)}, f32[4,5376]{1,0:T(4,128)}, f32[4,5376]{1,0:T(4,128)}) custom-call(f32[8,2944]{1,0:T(8,128)S(1)} %convert_add_fusion.kept, f32[8,2944]{1,0:T(8,128)S(1)} %collective-permute-done.20.given), custom_call_target="tpu_custom_call" | custom-call | tf_op jit(solution)/shard_map/pallas_call | solution.py:378
  (11 shorter events, 0.1 us)
Async XLA Ops:
  1.8 6.9 %collective-permute-start.1 = (bf16[16,5504]{1,0:T(8,128)(2,1)S(1)}, bf16[16,5504]{1,0:T(8,128)(2,1)S(1)}, u32[]{:S(2)}, u32[]{:S(2)}) collective-permute-start(bf16[16,5504]{1,0:T(8,128)(2,1)S(1)} %get-tuple-element.19.refs_0_), channel_id=1, source_target_pairs={{1,5},{4,0},{5,9},{8,4},{9,13},{12,8},{13,15},{14,12},{15,11},{10,... | collective-permute-start | bytes 528392 | tf_op jit(solution)/shard_map/ppermute | solution.py:131
  4.8 5.4 %collective-permute-start = (bf16[16,5504]{1,0:T(8,128)(2,1)S(1)}, bf16[16,5504]{1,0:T(8,128)(2,1)S(1)}, u32[]{:S(2)}, u32[]{:S(2)}) collective-permute-start(bf16[16,5504]{1,0:T(8,128)(2,1)S(1)} %get-tuple-element.19.refs_0_), channel_id=1, source_target_pairs={{0,5},{5,0},{4,9},{9,4},{8,13},{13,8},{12,15},{15,12},{14,11},{11,... | collective-permute-start | bytes 528392 | tf_op jit(solution)/shard_map/ppermute | solution.py:131
  10.2 4.9 %collective-permute-start.8 = (bf16[16,5504]{1,0:T(8,128)(2,1)S(1)}, bf16[16,5504]{1,0:T(8,128)(2,1)S(1)}, u32[]{:S(2)}, u32[]{:S(2)}) collective-permute-start(bf16[16,5504]{1,0:T(8,128)(2,1)S(1)} %collective-permute-done.refs_2_.refs_9_), channel_id=1, source_target_pairs={{1,4},{4,1},{5,8},{8,5},{9,12},{12,9},{13,14},{14,13},{15,10},{10,... | collective-permute-start | bytes 528392 | tf_op jit(solution)/shard_map/ppermute | solution.py:131
  11.1 6.0 %collective-permute-start.2 = (bf16[16,5504]{1,0:T(8,128)(2,1)S(1)}, bf16[16,5504]{1,0:T(8,128)(2,1)S(1)}, u32[]{:S(2)}, u32[]{:S(2)}) collective-permute-start(bf16[16,5504]{1,0:T(8,128)(2,1)S(1)} %collective-permute-done.1.refs_3_.refs_1_), channel_id=1, source_target_pairs={{1,4},{4,1},{5,8},{8,5},{9,12},{12,9},{13,14},{14,13},{15,10},{10,... | collective-permute-start | bytes 528392 | tf_op jit(solution)/shard_map/ppermute | solution.py:131
  11.9 6.8 %collective-permute-start.5 = (bf16[16,5504]{1,0:T(8,128)(2,1)S(1)}, bf16[16,5504]{1,0:T(8,128)(2,1)S(1)}, u32[]{:S(2)}, u32[]{:S(2)}) collective-permute-start(bf16[16,5504]{1,0:T(8,128)(2,1)S(1)} %get-tuple-element.19.refs_0_), channel_id=1, source_target_pairs={{0,1},{1,0},{2,3},{3,2},{4,5},{5,4},{6,7},{7,6},{8,9},{9,8},{10,11... | collective-permute-start | bytes 528392 | tf_op jit(solution)/shard_map/ppermute | solution.py:131
  12.3 6.7 %collective-permute-start.7 = (bf16[16,5504]{1,0:T(8,128)(2,1)S(1)}, bf16[16,5504]{1,0:T(8,128)(2,1)S(1)}, u32[]{:S(2)}, u32[]{:S(2)}) collective-permute-start(bf16[16,5504]{1,0:T(8,128)(2,1)S(1)} %collective-permute-done.1.refs_3_.refs_1_), channel_id=1, source_target_pairs={{0,1},{1,0},{2,3},{3,2},{4,5},{5,4},{6,7},{7,6},{8,9},{9,8},{10,11... | collective-permute-start | bytes 528392 | tf_op jit(solution)/shard_map/ppermute | solution.py:131
  15.0 4.9 %collective-permute-start.9 = (bf16[16,5504]{1,0:T(8,128)(2,1)S(1)}, bf16[16,5504]{1,0:T(8,128)(2,1)S(1)}, u32[]{:S(2)}, u32[]{:S(2)}) collective-permute-start(bf16[16,5504]{1,0:T(8,128)(2,1)S(1)} %collective-permute-done.8.refs_0_.refs_6_), channel_id=1, source_target_pairs={{0,5},{5,0},{4,9},{9,4},{8,13},{13,8},{12,15},{15,12},{14,11},{11,... | collective-permute-start | bytes 528392 | tf_op jit(solution)/shard_map/ppermute | solution.py:131
  16.8 4.9 %collective-permute-start.6 = (bf16[16,5504]{1,0:T(8,128)(2,1)S(1)}, bf16[16,5504]{1,0:T(8,128)(2,1)S(1)}, u32[]{:S(2)}, u32[]{:S(2)}) collective-permute-start(bf16[16,5504]{1,0:T(8,128)(2,1)S(1)} %collective-permute-done.refs_2_.refs_9_), channel_id=1, source_target_pairs={{0,1},{1,0},{2,3},{3,2},{4,5},{5,4},{6,7},{7,6},{8,9},{9,8},{10,11... | collective-permute-start | bytes 528392 | tf_op jit(solution)/shard_map/ppermute | solution.py:131
  17.1 5.5 %collective-permute-start.4 = (bf16[16,5504]{1,0:T(8,128)(2,1)S(1)}, bf16[16,5504]{1,0:T(8,128)(2,1)S(1)}, u32[]{:S(2)}, u32[]{:S(2)}) collective-permute-start(bf16[16,5504]{1,0:T(8,128)(2,1)S(1)} %collective-permute-done.2.refs_1_.refs_14_), channel_id=1, source_target_pairs={{0,5},{5,0},{4,9},{9,4},{8,13},{13,8},{12,15},{15,12},{14,11},{11,... | collective-permute-start | bytes 528392 | tf_op jit(solution)/shard_map/ppermute | solution.py:131
  18.7 4.5 %collective-permute-start.3 = (bf16[16,5504]{1,0:T(8,128)(2,1)S(1)}, bf16[16,5504]{1,0:T(8,128)(2,1)S(1)}, u32[]{:S(2)}, u32[]{:S(2)}) collective-permute-start(bf16[16,5504]{1,0:T(8,128)(2,1)S(1)} %collective-permute-done.2.refs_1_.refs_14_), channel_id=1, source_target_pairs={{0,1},{1,0},{2,3},{3,2},{4,5},{5,4},{6,7},{7,6},{8,9},{9,8},{10,11... | collective-permute-start | bytes 528392 | tf_op jit(solution)/shard_map/ppermute | solution.py:131
  19.0 4.2 %collective-permute-start.11 = (bf16[16,5504]{1,0:T(8,128)(2,1)S(1)}, bf16[16,5504]{1,0:T(8,128)(2,1)S(1)}, u32[]{:S(2)}, u32[]{:S(2)}) collective-permute-start(bf16[16,5504]{1,0:T(8,128)(2,1)S(1)} %collective-permute-done.8.refs_0_.refs_6_), channel_id=1, source_target_pairs={{0,1},{1,0},{2,3},{3,2},{4,5},{5,4},{6,7},{7,6},{8,9},{9,8},{10,11... | collective-permute-start | bytes 528392 | tf_op jit(solution)/shard_map/ppermute | solution.py:131
  20.0 4.9 %collective-permute-start.10 = (bf16[16,5504]{1,0:T(8,128)(2,1)S(1)}, bf16[16,5504]{1,0:T(8,128)(2,1)S(1)}, u32[]{:S(2)}, u32[]{:S(2)}) collective-permute-start(bf16[16,5504]{1,0:T(8,128)(2,1)S(1)} %collective-permute-done.9.refs_4_.refs_11_), channel_id=1, source_target_pairs={{1,4},{4,1},{5,8},{8,5},{9,12},{12,9},{13,14},{14,13},{15,10},{10,... | collective-permute-start | bytes 528392 | tf_op jit(solution)/shard_map/ppermute | solution.py:131
  21.7 5.1 %slice-start = ((s8[11010048]{0:T(1024)(128)(4,1)}), s8[4194304]{0:T(1024)(128)(4,1)S(1)}, s32[]{:S(2)}) async-start(s8[11010048]{0:T(1024)(128)(4,1)} %bitcast.4), calls=%async_computation | async-start | bytes 8388608
  21.7 5.1 %slice-start.1 = ((s8[11010048]{0:T(1024)(128)(4,1)}), s8[4194304]{0:T(1024)(128)(4,1)S(1)}, s32[]{:S(2)}) async-start(s8[11010048]{0:T(1024)(128)(4,1)} %bitcast.4), calls=%async_computation.1 | async-start | bytes 8388608
  22.6 4.3 %slice-start.2 = ((s8[11010048]{0:T(1024)(128)(4,1)}), s8[2621440]{0:T(1024)(128)(4,1)S(1)}, s32[]{:S(2)}) async-start(s8[11010048]{0:T(1024)(128)(4,1)} %bitcast.4), calls=%async_computation.2 | async-start | bytes 5242880
  22.6 3.2 %collective-permute-start.14 = (bf16[16,5504]{1,0:T(8,128)(2,1)S(1)}, bf16[16,5504]{1,0:T(8,128)(2,1)S(1)}, u32[]{:S(2)}, u32[]{:S(2)}) collective-permute-start(bf16[16,5504]{1,0:T(8,128)(2,1)S(1)} %collective-permute-done.4.refs_5_.refs_3_), channel_id=1, source_target_pairs={{0,1},{1,0},{2,3},{3,2},{4,5},{5,4},{6,7},{7,6},{8,9},{9,8},{10,11... | collective-permute-start | bytes 528392 | tf_op jit(solution)/shard_map/ppermute | solution.py:131
  23.0 2.8 %collective-permute-start.12 = (bf16[16,5504]{1,0:T(8,128)(2,1)S(1)}, bf16[16,5504]{1,0:T(8,128)(2,1)S(1)}, u32[]{:S(2)}, u32[]{:S(2)}) collective-permute-start(bf16[16,5504]{1,0:T(8,128)(2,1)S(1)} %collective-permute-done.9.refs_4_.refs_11_), channel_id=1, source_target_pairs={{0,1},{1,0},{2,3},{3,2},{4,5},{5,4},{6,7},{7,6},{8,9},{9,8},{10,11... | collective-permute-start | bytes 528392 | tf_op jit(solution)/shard_map/ppermute | solution.py:131
  24.9 2.0 %collective-permute-start.13 = (bf16[16,5504]{1,0:T(8,128)(2,1)S(1)}, bf16[16,5504]{1,0:T(8,128)(2,1)S(1)}, u32[]{:S(2)}, u32[]{:S(2)}) collective-permute-start(bf16[16,5504]{1,0:T(8,128)(2,1)S(1)} %collective-permute-done.10.refs_2_.refs_4_), channel_id=1, source_target_pairs={{0,1},{1,0},{2,3},{3,2},{4,5},{5,4},{6,7},{7,6},{8,9},{9,8},{10,11... | collective-permute-start | bytes 528392 | tf_op jit(solution)/shard_map/ppermute | solution.py:131
  32.2 2.6 %collective-permute-start.15 = (f32[8,2944]{1,0:T(8,128)S(1)}, f32[8,2944]{1,0:T(8,128)S(1)}, u32[]{:S(2)}, u32[]{:S(2)}) collective-permute-start(f32[8,2944]{1,0:T(8,128)S(1)} %get-tuple-element.31), channel_id=1, source_target_pairs={{0,1},{1,0},{2,3},{3,2},{4,5},{5,4},{6,7},{7,6},{8,9},{9,8},{10,11... | collective-permute-start | bytes 282632 | tf_op jit(solution)/shard_map/ppermute | solution.py:335
  34.8 5.2 %collective-permute-start.18 = (bf16[8,2944]{1,0:T(8,128)(2,1)S(1)}, bf16[8,2944]{1,0:T(8,128)(2,1)S(1)}, u32[]{:S(2)}, u32[]{:S(2)}) collective-permute-start(bf16[8,2944]{1,0:T(8,128)(2,1)S(1)} %fusion), channel_id=1, source_target_pairs={{0,6},{1,7},{2,4},{3,5},{4,2},{5,3},{6,0},{7,1},{8,14},{9,15},{10,... | collective-permute-start | bytes 141320 | tf_op jit(solution)/shard_map/ppermute | solution.py:335
  37.1 4.1 %collective-permute-start.17 = (bf16[8,2944]{1,0:T(8,128)(2,1)S(1)}, bf16[8,2944]{1,0:T(8,128)(2,1)S(1)}, u32[]{:S(2)}, u32[]{:S(2)}) collective-permute-start(bf16[8,2944]{1,0:T(8,128)(2,1)S(1)} %fusion), channel_id=1, source_target_pairs={{0,4},{1,5},{2,6},{3,7},{4,0},{5,1},{6,2},{7,3},{8,12},{9,13},{10,... | collective-permute-start | bytes 141320 | tf_op jit(solution)/shard_map/ppermute | solution.py:335
  37.5 4.1 %collective-permute-start.16 = (bf16[8,2944]{1,0:T(8,128)(2,1)S(1)}, bf16[8,2944]{1,0:T(8,128)(2,1)S(1)}, u32[]{:S(2)}, u32[]{:S(2)}) collective-permute-start(bf16[8,2944]{1,0:T(8,128)(2,1)S(1)} %fusion), channel_id=1, source_target_pairs={{0,2},{1,3},{2,0},{3,1},{4,6},{5,7},{6,4},{7,5},{8,10},{9,11},{10,... | collective-permute-start | bytes 141320 | tf_op jit(solution)/shard_map/ppermute | solution.py:335
  41.6 5.0 %collective-permute-start.19 = (bf16[8,2944]{1,0:T(8,128)(2,1)S(1)}, bf16[8,2944]{1,0:T(8,128)(2,1)S(1)}, u32[]{:S(2)}, u32[]{:S(2)}) collective-permute-start(bf16[8,2944]{1,0:T(8,128)(2,1)S(1)} %get-tuple-element.35), channel_id=1, source_target_pairs={{0,8},{1,9},{2,10},{3,11},{4,12},{5,13},{6,14},{7,15},{8,0},{9,1},... | collective-permute-start | bytes 141320 | tf_op jit(solution)/shard_map/ppermute | solution.py:335
  46.7 1.4 %collective-permute-start.20 = (f32[8,2944]{1,0:T(8,128)S(1)}, f32[8,2944]{1,0:T(8,128)S(1)}, u32[]{:S(2)}, u32[]{:S(2)}) collective-permute-start(f32[8,2944]{1,0:T(8,128)S(1)} %convert_add_fusion.kept), channel_id=1, source_target_pairs={{0,1},{1,0},{2,3},{3,2},{4,5},{5,4},{6,7},{7,6},{8,9},{9,8},{10,11... | collective-permute-start | bytes 282632 | tf_op jit(solution)/shard_map/ppermute | solution.py:335
